TPU v7x, 32 devices: a whole 2x2x4 slice. The times are simulated.
32 devices in a mesh: dp: 8 (over z, x), ep: 4 (over y, core).
Axes of the slice: x: 2, y: 2, z: 4, core: 2. Of those that a mesh axis runs over, the one named last changes fastest.
Arguments:
- hidden: bfloat16 [2, 512, 3584], P(None, ('dp', 'ep')), may hold values from -6 to 6
- routes: int32 [2, 512, 8], P(None, ('dp', 'ep')), may hold values from 0 to 31, all different within a row; in each aligned block of 16 rows (0 to 15, 16 to 31, ..., all dimensions but the last counted through in order) at most 8 rows name the same one
- route_weights: float32 [2, 512, 8], P(None, ('dp', 'ep')), may hold values from 0.1 to 0.6
- expert_in: bfloat16 [32, 3584, 2048], P(('dp', 'ep')), may hold values from -0.09375 to 0.09375
- expert_out: bfloat16 [32, 1024, 3584], P(('dp', 'ep')), may hold values from -0.1875 to 0.1875
- queries: bfloat16 [512, 64, 576], P(('dp', 'ep')), may hold values from -6 to 6
- fresh_key: bfloat16 [512, 576], P(('dp', 'ep')), may hold values from -4 to 4
- latent_cache: bfloat16 [512, 128, 576], P(('dp', 'ep')), may hold values from -4 to 4
- lengths: int32 [512], replicated, may hold values from 2 to 128, as said below
- swapped: int32 [512], P(('dp', 'ep')), may hold values from 0 to 1, as said below
Outputs:
- mixed: bfloat16 [2, 512, 3584], P(None, ('dp', 'ep'))
- context: bfloat16 [512, 64, 512], P(('dp', 'ep'))
Inputs may be any that keep to these rules, and one draw needn't show every extreme that they name: `routes`: in each step the 8 experts of a token differ; the 16 tokens of one device name one expert at most 8 times, a bound that some block reaches. `lengths`: some request holds exactly 128 positions. `swapped`: A marked slot trades with the slot at the same position on the device of the same ep index whose dp index differs by half the dp axis; both devices of such a pair carry the same marks; a device carries at most 4 marks, and some device exactly 4.
All inputs are finite; a program needn't handle non-finite values.
Results may differ from a plain program's by a relative error of at most 0.0058.
Values may be sent and summed in bfloat16 or wider, within the bound.
No kernel may reach another device: no remote copies, remote signals or barrier semaphores. Data moves between devices by JAX's collectives and lax.ppermute only.
A program may use at most 128 MiB of HBM per device.

v0:
```python
import jax
import jax.numpy as jnp
from jax import lax
from jax.sharding import PartitionSpec as P

LATENT = 512
STEPS = 2
MOVE = 4


SOFTMAX_SCALE = 192.0 ** (-0.5)


def swapped_2(value, axis, apart):
    mask = 2**apart
    pairs = [(source, source ^ mask) for source in range(lax.axis_size(axis))]
    return lax.ppermute(value, axis, pairs)


def expert_rows(picked, expert_in, expert_out):
    projected = jnp.dot(picked, expert_in, preferred_element_type=jnp.float32)
    half_width = projected.shape[1] // 2
    activated = (jax.nn.silu(projected[:, :half_width]) * projected[:, half_width:]).astype(
        jnp.bfloat16
    )
    return jnp.dot(activated, expert_out, preferred_element_type=jnp.float32).astype(jnp.bfloat16)


def serve_slots(received, expert_in, expert_out):
    source_count, slot_count, row_width = received.shape
    finished = expert_rows(
        received.reshape(source_count * slot_count, row_width), expert_in[0], expert_out[0]
    )
    return finished.reshape(source_count, slot_count, row_width)


def route_rows(buffer, expert_in, expert_out):
    finished = serve_slots(
        lax.all_to_all(buffer, ("dp", "ep"), split_axis=0, concat_axis=0, tiled=True),
        expert_in,
        expert_out,
    )
    return lax.all_to_all(finished, ("dp", "ep"), split_axis=0, concat_axis=0, tiled=True)


def pack_rows(tokens, experts, expert_count, slot_cap):
    token_count, pick_count = experts.shape
    flat_ids = experts.reshape(-1)
    onehot = (flat_ids[:, None] == jnp.arange(expert_count, dtype=jnp.int32)[None, :]).astype(
        jnp.int32
    )
    earlier = jnp.cumsum(onehot, axis=0) - onehot
    within = jnp.sum(earlier * onehot, axis=1)
    target = (flat_ids * slot_cap + within).reshape(token_count, pick_count)
    places = jnp.arange(expert_count * slot_cap, dtype=jnp.int32)
    select = jnp.any(target[None, :, :] == places[:, None, None], axis=2).astype(jnp.bfloat16)
    packed = jnp.dot(select, tokens, preferred_element_type=jnp.float32).astype(jnp.bfloat16)
    return (packed.reshape(expert_count, slot_cap, tokens.shape[1]), target)


def unpack_rows(returned, target, gate_values):
    flat_rows = returned.reshape(-1, returned.shape[2])
    picked = jnp.take(flat_rows, target.reshape(-1), axis=0).reshape(
        target.shape + (returned.shape[2],)
    )
    summed = jnp.sum(picked.astype(jnp.float32) * gate_values[:, :, None], axis=1)
    return summed.astype(jnp.bfloat16)


def attend_block(query_rows, cache_rows, live_lengths, fresh_rows):
    scores = (
        jnp.einsum("nhc,nlc->nhl", query_rows, cache_rows, preferred_element_type=jnp.float32)
        * SOFTMAX_SCALE
    )
    own_score = (
        jnp.einsum("nhc,nc->nh", query_rows, fresh_rows, preferred_element_type=jnp.float32)
        * SOFTMAX_SCALE
    )
    positions = jnp.arange(cache_rows.shape[1], dtype=jnp.int32)
    scores = jnp.where(positions[None, None, :] < live_lengths[:, None, None], scores, -jnp.inf)
    row_top = jnp.maximum(jnp.max(scores, axis=2), own_score)
    weights = jnp.exp(scores - row_top[:, :, None])
    own_weight = jnp.exp(own_score - row_top)
    summed = jnp.sum(weights, axis=2) + own_weight
    blended = jnp.einsum(
        "nhl,nlc->nhc",
        weights.astype(jnp.bfloat16),
        cache_rows[:, :, :LATENT],
        preferred_element_type=jnp.float32,
    )
    own_rounded = lax.optimization_barrier(own_weight.astype(jnp.bfloat16))
    blended = blended + own_rounded.astype(jnp.float32)[:, :, None] * fresh_rows[
        :, None, :LATENT
    ].astype(jnp.float32)
    return (blended / summed[:, :, None]).astype(jnp.bfloat16)


def per_device(
    hidden,
    routes,
    route_weights,
    expert_in,
    expert_out,
    queries,
    fresh_key,
    latent_cache,
    lengths,
    swapped,
):
    expert_count = lax.axis_size("dp") * lax.axis_size("ep")
    token_count = hidden.shape[1]
    slot_cap = max(2, 2 * token_count * routes.shape[2] // expert_count)
    packs = [pack_rows(hidden[step], routes[step], expert_count, slot_cap) for step in range(STEPS)]
    returned = [route_rows(entry[0], expert_in, expert_out) for entry in packs]
    mixed = jnp.stack(
        [unpack_rows(returned[step], packs[step][1], route_weights[step]) for step in range(STEPS)]
    )
    row_count = swapped.shape[0]
    top_bit = lax.axis_size("dp").bit_length() - 2
    outgoing = jnp.argsort(1 - swapped, stable=True)[:MOVE]
    arrival = jnp.clip(jnp.cumsum(swapped) - 1, 0, MOVE - 1)
    is_moved = swapped == 1
    device_rows = lax.axis_index(("dp", "ep")) * row_count + jnp.arange(row_count, dtype=jnp.int32)
    total_rows = expert_count * row_count
    anchor = jnp.where(is_moved, (device_rows + total_rows // 2) % total_rows, device_rows)
    incoming_cache = swapped_2(latent_cache[outgoing], "dp", top_bit)
    merged_cache = jnp.where(is_moved[:, None, None], incoming_cache[arrival], latent_cache)
    context = attend_block(queries, merged_cache, lengths[anchor], fresh_key)
    return (mixed, context)


def solution(mesh):
    in_specs = (
        P(None, ("dp", "ep"), None),
        P(None, ("dp", "ep"), None),
        P(None, ("dp", "ep"), None),
        P(("dp", "ep"), None, None),
        P(("dp", "ep"), None, None),
        P(("dp", "ep"), None, None),
        P(("dp", "ep"), None),
        P(("dp", "ep"), None, None),
        P(),
        P(("dp", "ep")),
    )
    out_specs = (P(None, ("dp", "ep"), None), P(("dp", "ep"), None, None))
    return jax.shard_map(
        per_device, mesh=mesh, in_specs=in_specs, out_specs=out_specs, check_vma=False
    )
```

profile of v0, /device:TPU:0, one launch (start us, length us, event | category | flops | bytes accessed | tf_op | source)
XLA Modules:
  0.0 222.9 jit_solution(14331302242819246893)
XLA Ops:
  0.6 0.8 fusion.59
  1.5 0.1 eq.65
  1.6 0.1 fusion.49
  1.7 0.2 reduce_window_sum.24
  1.9 0.2 select_reduce_fusion.1
  2.2 0.1 fusion.42
  2.3 2.8 %fusion.14 = bf16[32,8,3584]{2,1,0:T(8,128)(2,1)} fusion(pred[256,16]{0,1:T(8,128)(4,1)S(1)} %fusion.42, bf16[2,16,3584]{2,1,0:T(8,128)(2,1)} %param.12), kind=kOutput, calls=%fused_computation.17 | convolution fusion | flops 30277632 | bytes 1953792 | tf_op jit(solution)/shard_map/dot_general | solution.py:57
  5.1 7.3 %all-to-all-start = ((bf16[32,8,3584]{2,1,0:T(8,128)(2,1)}), bf16[32,8,3584]{2,1,0:T(8,128)(2,1)S(1)}, u32[]{:S(2)}, u32[]{:S(2)}) async-start(bf16[32,8,3584]{2,1,0:T(8,128)(2,1)} %fusion.14), calls=%async_computation | async-start | bytes 3670016 | tf_op jit(solution)/shard_map/all_to_all | solution.py:39
  12.5 0.1 eq.73
  12.6 0.1 fusion.48
  12.7 0.2 reduce_window_sum.25
  12.9 0.2 select_reduce_fusion
  13.0 0.1 reduce_sum.53
  13.1 0.1 fusion.43
  13.3 1.9 fusion.15
  15.2 40.4 %all-to-all-done = bf16[32,8,3584]{2,1,0:T(8,128)(2,1)S(1)} async-done(((bf16[32,8,3584]{2,1,0:T(8,128)(2,1)}), bf16[32,8,3584]{2,1,0:T(8,128)(2,1)S(1)}, u32[]{:S(2)}, u32[]{:S(2)}) %all-to-all-start) | async-done | bytes 1835040 | tf_op jit(solution)/shard_map/all_to_all | solution.py:39
  55.6 1.3 copy-done.4
  56.8 3.9 %all-to-all-start.2 = ((bf16[32,8,3584]{2,1,0:T(8,128)(2,1)}), bf16[32,8,3584]{2,1,0:T(8,128)(2,1)S(1)}, u32[]{:S(2)}, u32[]{:S(2)}) async-start(bf16[32,8,3584]{2,1,0:T(8,128)(2,1)} %fusion.15), calls=%async_computation.2 | async-start | bytes 3670016 | tf_op jit(solution)/shard_map/all_to_all | solution.py:39
  60.7 7.8 %fusion.2 = f32[256,2048]{1,0:T(8,128)S(1)} fusion(bf16[1,3584,2048]{2,1,0:T(8,128)(2,1)} %param.15, bf16[32,8,3584]{2,1,0:T(8,128)(2,1)} %copy-done.4), kind=kOutput, calls=%fused_computation.7 | convolution fusion | flops 3758096384 | bytes 18612224 | tf_op jit(solution)/shard_map/dot_general | solution.py:21
  68.5 6.4 %fusion.19 = bf16[32,8,3584]{2,1,0:T(8,128)(2,1)} fusion(bf16[1,1024,3584]{2,1,0:T(8,128)(2,1)} %param.16, f32[256,2048]{1,0:T(8,128)S(1)} %fusion.2), kind=kOutput, calls=%fused_computation.20 | convolution fusion | flops 1881538560 | bytes 11272192 | tf_op jit(solution)/shard_map/dot_general | solution.py:26
  74.9 28.9 %all-to-all-done.2 = bf16[32,8,3584]{2,1,0:T(8,128)(2,1)S(1)} async-done(((bf16[32,8,3584]{2,1,0:T(8,128)(2,1)}), bf16[32,8,3584]{2,1,0:T(8,128)(2,1)S(1)}, u32[]{:S(2)}, u32[]{:S(2)}) %all-to-all-start.2) | async-done | bytes 1835040 | tf_op jit(solution)/shard_map/all_to_all | solution.py:39
  103.8 1.2 copy-done.3
  105.1 3.9 %all-to-all-start.1 = ((bf16[32,8,3584]{2,1,0:T(8,128)(2,1)}), bf16[32,8,3584]{2,1,0:T(8,128)(2,1)S(1)}, u32[]{:S(2)}, u32[]{:S(2)}) async-start(bf16[32,8,3584]{2,1,0:T(8,128)(2,1)} %fusion.19), calls=%async_computation.1 | async-start | bytes 3670016 | tf_op jit(solution)/shard_map/all_to_all | solution.py:43
  109.0 1.2 sort.17
  110.3 3.1 %gather_fusion.1 = bf16[4,128,576]{1,2,0:T(8,128)(2,1)} fusion(bf16[16,128,576]{1,2,0:T(8,128)(2,1)} %param.19, s32[1024]{0:T(1024)S(1)} %pad_clamp_fusion.1), kind=kCustom, calls=%fused_computation.3 | custom fusion | bytes 1179664 | tf_op jit(solution)/shard_map/gather | solution.py:126
  113.4 2.7 %collective-permute-start = (bf16[4,128,576]{1,2,0:T(8,128)(2,1)}, bf16[4,128,576]{1,2,0:T(8,128)(2,1)}, u32[]{:S(2)}, u32[]{:S(2)}) collective-permute-start(bf16[4,128,576]{1,2,0:T(8,128)(2,1)} %gather_fusion.1), channel_id=1, source_target_pairs={{0,16},{4,20},{8,24},{12,28},{16,0},{20,4},{24,8},{28,12},{1,17},{... | collective-permute-start | bytes 1769480 | tf_op jit(solution)/shard_map/ppermute | solution.py:17
  116.0 0.1 copy.43
  116.2 0.1 fusion.52
  116.3 7.8 %fusion = f32[256,2048]{1,0:T(8,128)S(1)} fusion(bf16[1,3584,2048]{2,1,0:T(8,128)(2,1)} %param.15, bf16[32,8,3584]{2,1,0:T(8,128)(2,1)} %copy-done.3), kind=kOutput, calls=%fused_computation.5 | convolution fusion | flops 3758096384 | bytes 18612224 | tf_op jit(solution)/shard_map/dot_general | solution.py:21
  124.1 6.5 %fusion.16 = bf16[32,8,3584]{2,1,0:T(8,128)(2,1)} fusion(bf16[1,1024,3584]{2,1,0:T(8,128)(2,1)} %param.16, f32[256,2048]{1,0:T(8,128)S(1)} %fusion), kind=kOutput, calls=%fused_computation.19 | convolution fusion | flops 1881538560 | bytes 11272192 | tf_op jit(solution)/shard_map/dot_general | solution.py:26
  130.6 34.6 %all-to-all-done.1 = bf16[32,8,3584]{2,1,0:T(8,128)(2,1)S(1)} async-done(((bf16[32,8,3584]{2,1,0:T(8,128)(2,1)}), bf16[32,8,3584]{2,1,0:T(8,128)(2,1)S(1)}, u32[]{:S(2)}, u32[]{:S(2)}) %all-to-all-start.1) | async-done | bytes 1835040 | tf_op jit(solution)/shard_map/all_to_all | solution.py:43
  165.2 3.7 %all-to-all-start.3 = ((bf16[32,8,3584]{2,1,0:T(8,128)(2,1)}), bf16[32,8,3584]{2,1,0:T(8,128)(2,1)}, u32[]{:S(2)}, u32[]{:S(2)}) async-start(bf16[32,8,3584]{2,1,0:T(8,128)(2,1)} %fusion.16), calls=%async_computation.3 | async-start | bytes 3670016 | tf_op jit(solution)/shard_map/all_to_all | solution.py:43
  169.0 4.3 %copy.45 = bf16[16,128,576]{2,1,0:T(8,128)(2,1)} copy(bf16[16,128,576]{1,2,0:T(8,128)(2,1)} %param.19) | data formatting | bytes 4718592 | tf_op args[7]
  173.5 0.7 gather_fusion
  174.3 0.5 fusion.50
  174.8 10.7 %collective-permute-done = bf16[4,128,576]{1,2,0:T(8,128)(2,1)} collective-permute-done((bf16[4,128,576]{1,2,0:T(8,128)(2,1)}, bf16[4,128,576]{1,2,0:T(8,128)(2,1)}, u32[]{:S(2)}, u32[]{:S(2)}) %collective-permute-start) | collective-permute-done | bytes 589856 | tf_op jit(solution)/shard_map/ppermute | solution.py:17
  185.5 3.4 %gather_fusion.2 = bf16[16,128,576]{1,2,0:T(8,128)(2,1)} fusion(bf16[4,128,576]{1,2,0:T(8,128)(2,1)} %collective-permute-done, s32[1024]{0:T(1024)S(1)} %pad_clamp_fusion), kind=kCustom, calls=%fused_computation.4 | custom fusion | bytes 4718656 | tf_op jit(solution)/shard_map/gather | solution.py:127
  188.9 4.4 %copy.44 = bf16[16,128,576]{2,1,0:T(8,128)(2,1)} copy(bf16[16,128,576]{1,2,0:T(8,128)(2,1)} %gather_fusion.2) | data formatting | bytes 4718592 | tf_op jit(solution)/shard_map/gather | solution.py:127
  193.2 2.9 %broadcast_select_fusion = bf16[16,128,576]{2,1,0:T(8,128)(2,1)S(1)} fusion(bf16[16,128,576]{2,1,0:T(8,128)(2,1)} %copy.44, bf16[16,128,576]{2,1,0:T(8,128)(2,1)} %copy.45, pred[16]{0:T(512)(128)(4,1)S(1)} %broadcast_compare_fusion), kind=kLoop, calls=%fused_computation.21 | loop fusion | flops 1179648 | bytes 7077904 | tf_op jit(solution)/shard_map/jit(_where)/select_n | solution.py:127
  196.1 1.3 fusion.60
  197.4 0.4 fusion.38
  197.8 1.6 divide_convert_fusion
  199.4 2.1 gather_fusion.3
  201.4 15.4 %all-to-all-done.3 = bf16[32,8,3584]{2,1,0:T(8,128)(2,1)} async-done(((bf16[32,8,3584]{2,1,0:T(8,128)(2,1)}), bf16[32,8,3584]{2,1,0:T(8,128)(2,1)}, u32[]{:S(2)}, u32[]{:S(2)}) %all-to-all-start.3) | async-done | bytes 1835040 | tf_op jit(solution)/shard_map/all_to_all | solution.py:43
  216.8 3.8 %gather_fusion.4 = bf16[128,3584]{1,0:T(8,128)(2,1)S(1)} fusion(bf16[256,3584]{1,0:T(8,128)(2,1)} %bitcast.16, s32[1024]{0:T(1024)S(1)} %pad_clamp_fusion.3), kind=kCustom, calls=%fused_computation.1.clone | custom fusion | bytes 1835520 | tf_op jit(solution)/shard_map/jit(_take)/gather | solution.py:63
  220.7 0.7 fusion.25
  221.4 0.7 fusion.24
  222.2 0.7 pad_maximum_fusion
  (41 shorter events, 0.7 us)
Async XLA Ops:
  0.6 173.7 %copy-start = (bf16[16,64,576]{2,1,0:T(8,128)(2,1)S(1)}, bf16[16,64,576]{2,1,0:T(8,128)(2,1)}, u32[]{:S(2)}) copy-start(bf16[16,64,576]{2,1,0:T(8,128)(2,1)} %param.17) | copy-start | bytes 3538948
  5.1 8.1 %copy-start.5 = (bf16[2,16,3584]{2,1,0:T(8,128)(2,1)S(1)}, bf16[2,16,3584]{2,1,0:T(8,128)(2,1)}, u32[]{:S(2)}) copy-start(bf16[2,16,3584]{2,1,0:T(8,128)(2,1)} %param.12) | copy-start | bytes 688132
  5.1 50.4 %all-to-all-start = ((bf16[32,8,3584]{2,1,0:T(8,128)(2,1)}), bf16[32,8,3584]{2,1,0:T(8,128)(2,1)S(1)}, u32[]{:S(2)}, u32[]{:S(2)}) async-start(bf16[32,8,3584]{2,1,0:T(8,128)(2,1)} %fusion.14), calls=%async_computation | async-start | bytes 3670016 | tf_op jit(solution)/shard_map/all_to_all | solution.py:39
  55.6 1.3 copy-start.4
  56.8 47.0 %all-to-all-start.2 = ((bf16[32,8,3584]{2,1,0:T(8,128)(2,1)}), bf16[32,8,3584]{2,1,0:T(8,128)(2,1)S(1)}, u32[]{:S(2)}, u32[]{:S(2)}) async-start(bf16[32,8,3584]{2,1,0:T(8,128)(2,1)} %fusion.15), calls=%async_computation.2 | async-start | bytes 3670016 | tf_op jit(solution)/shard_map/all_to_all | solution.py:39
  74.9 34.0 %copy-start.8 = (s32[16]{0:T(128)S(1)}, s32[16]{0:T(128)}, u32[]{:S(2)}) copy-start(s32[16]{0:T(128)} %param.21) | copy-start | bytes 196
  74.9 41.3 %copy-start.7 = (f32[2,16,8]{1,2,0:T(8,128)S(1)}, f32[2,16,8]{1,2,0:T(8,128)}, u32[]{:S(2)}) copy-start(f32[2,16,8]{1,2,0:T(8,128)} %param.14) | copy-start | bytes 3076
  103.8 1.2 copy-start.3
  105.1 60.1 %all-to-all-start.1 = ((bf16[32,8,3584]{2,1,0:T(8,128)(2,1)}), bf16[32,8,3584]{2,1,0:T(8,128)(2,1)S(1)}, u32[]{:S(2)}, u32[]{:S(2)}) async-start(bf16[32,8,3584]{2,1,0:T(8,128)(2,1)} %fusion.19), calls=%async_computation.1 | async-start | bytes 3670016 | tf_op jit(solution)/shard_map/all_to_all | solution.py:43
  113.4 72.1 %collective-permute-start = (bf16[4,128,576]{1,2,0:T(8,128)(2,1)}, bf16[4,128,576]{1,2,0:T(8,128)(2,1)}, u32[]{:S(2)}, u32[]{:S(2)}) collective-permute-start(bf16[4,128,576]{1,2,0:T(8,128)(2,1)} %gather_fusion.1), channel_id=1, source_target_pairs={{0,16},{4,20},{8,24},{12,28},{16,0},{20,4},{24,8},{28,12},{1,17},{... | collective-permute-start | bytes 1769480 | tf_op jit(solution)/shard_map/ppermute | solution.py:17
  165.2 51.6 %all-to-all-start.3 = ((bf16[32,8,3584]{2,1,0:T(8,128)(2,1)}), bf16[32,8,3584]{2,1,0:T(8,128)(2,1)}, u32[]{:S(2)}, u32[]{:S(2)}) async-start(bf16[32,8,3584]{2,1,0:T(8,128)(2,1)} %fusion.16), calls=%async_computation.3 | async-start | bytes 3670016 | tf_op jit(solution)/shard_map/all_to_all | solution.py:43
  169.0 4.5 %copy-start.1 = (s32[512]{0:T(512)S(1)}, s32[512]{0:T(512)}, u32[]{:S(2)}) copy-start(s32[512]{0:T(512)} %param.20) | copy-start | bytes 6148
  169.0 5.3 %copy-start.6 = (bf16[16,576]{1,0:T(8,128)(2,1)S(1)}, bf16[16,576]{1,0:T(8,128)(2,1)}, u32[]{:S(2)}) copy-start(bf16[16,576]{1,0:T(8,128)(2,1)} %param.18) | copy-start | bytes 55300
  216.8 3.9 %copy-start.2 = (bf16[128,3584]{1,0:T(8,128)(2,1)S(1)}, bf16[128,3584]{1,0:T(8,128)(2,1)}, u32[]{:S(2)}) copy-start(bf16[128,3584]{1,0:T(8,128)(2,1)} %gather_fusion.3) | copy-start | bytes 2752516
where the time goes:
time: 224 us; the launch traced here: 223 us
  waiting for transfers between devices  130 us (58%)
  matrix products  36.6 us (16%)
  local copies, waits for them, and re-layouts  25.8 us (12%)
  starting transfers between devices  21.5 us (10%)
  other arithmetic  8.18 us (4%)
    all_to_all x2, waiting for transfers between devices, route_rows(): lax.all_to_all(buffer, ('dp', 'ep'), split_axis=0, concat_axis=0, tiled=T...  69.3 us
    all_to_all x2, waiting for transfers between devices, route_rows(): lax.all_to_all(finished, ('dp', 'ep'), split_axis=0, concat_axis=0, tiled...  50 us
    dot_general x2, matrix products, expert_rows(): projected = jnp.dot(picked, expert_in, preferred_element_type=jnp.float32)  15.6 us
    dot_general x2, matrix products, expert_rows(): jnp.dot(activated, expert_out, preferred_element_type=jnp.float32)  12.9 us
    all_to_all x2, starting transfers between devices, route_rows(): lax.all_to_all(buffer, ('dp', 'ep'), split_axis=0, concat_axis=0, tiled=T...  11.2 us
    ppermute x1, waiting for transfers between devices, swapped_2(): return lax.ppermute(value, axis, pairs)  10.7 us
    gather x2, local copies, waits for them, and re-layouts, per_device(): incoming_cache[arrival]  7.72 us
    all_to_all x2, starting transfers between devices, route_rows(): lax.all_to_all(finished, ('dp', 'ep'), split_axis=0, concat_axis=0, tiled...  7.62 us
  transfers between devices with their start and end apart: 5, of which 5 were waited for; matrix products, arithmetic and copies ran while one was open for 26% of the time, Pallas kernels for 0%

commit v1 on v0

v1 whole, which is shorter than its diff:
```python
import functools

import jax
import jax.numpy as jnp
from jax import lax
from jax.experimental import pallas as pl
from jax.experimental.pallas import tpu as pltpu
from jax.sharding import PartitionSpec as P

AXES = ("dp", "ep")
LATENT = 512
STEPS = 2
MOVE = 4
Z_BITS = 2

SOFTMAX_SCALE = 192.0 ** (-0.5)
VMEM_BYTES = 56 * 1024 * 1024


def exchange(value, masks):
    count = lax.axis_size(AXES)
    pairs = [(source, source ^ masks[source % 2]) for source in range(count)]
    return lax.ppermute(value, AXES, pairs)


def swap_halves(index, bits):
    low = index & ((1 << bits) - 1)
    return (low << bits) | (index >> bits)


def ffn_body(line_count, up_steps, down_steps, *refs):
    refs = list(refs)
    core_ref = refs.pop(0)
    del core_ref
    pieces = [refs.pop(0) for _ in range(2 * line_count)]
    gate_own, gate_sib, up_own, up_sib, down_ref, scale_ref = [refs.pop(0) for _ in range(6)]
    theirs = [refs.pop(0) for _ in range(line_count)]
    mine = [refs.pop(0) for _ in range(line_count)]
    rows_ref, act_ref, sems = refs
    step = pl.program_id(0)
    line_rows, half = pieces[0].shape
    block = gate_own.shape[2]
    half_bits = (line_count.bit_length() - 1) // 2

    def copies():
        made = []
        for index in range(line_count):
            made.append(
                pltpu.make_async_copy(
                    pieces[index],
                    rows_ref.at[pl.ds(index * line_rows, line_rows), pl.ds(0, half)],
                    sems.at[index],
                )
            )
            place = swap_halves(index, half_bits)
            made.append(
                pltpu.make_async_copy(
                    pieces[line_count + index],
                    rows_ref.at[pl.ds(place * line_rows, line_rows), pl.ds(half, half)],
                    sems.at[line_count + index],
                )
            )
        return made

    @pl.when(step == 0)
    def _():
        made = copies()
        for copy in made:
            copy.start()
        for copy in made:
            copy.wait()

    @pl.when(step < up_steps)
    def _():
        own = rows_ref[:, :half]
        sib = rows_ref[:, half:]
        gate = jnp.dot(own, gate_own[0], preferred_element_type=jnp.float32)
        gate += jnp.dot(sib, gate_sib[0], preferred_element_type=jnp.float32)
        up = jnp.dot(own, up_own[0], preferred_element_type=jnp.float32)
        up += jnp.dot(sib, up_sib[0], preferred_element_type=jnp.float32)
        value = (gate / (1.0 + jnp.exp(-gate)) * up).astype(jnp.bfloat16)
        act_ref[:, pl.ds(pl.multiple_of(step * block, block), block)] = value

    def down(outs, places):
        answer = jnp.dot(act_ref[...], down_ref[...], preferred_element_type=jnp.float32)
        weighed = answer.astype(jnp.bfloat16).astype(jnp.float32) * scale_ref[...]
        weighed = weighed.astype(jnp.bfloat16)
        for index, out in enumerate(outs):
            place = places(index)
            out[...] = weighed[place * line_rows : (place + 1) * line_rows]

    @pl.when((step >= up_steps) & (step < up_steps + down_steps))
    def _():
        down(theirs, lambda index: swap_halves(index, half_bits))

    @pl.when(step >= up_steps + down_steps)
    def _():
        down(mine, lambda index: index)


def expert_ffn(core, own_pieces, sib_pieces, expert_in, expert_out, scales):
    line_count = len(own_pieces)
    line_rows, half = own_pieces[0].shape
    width = 2 * half
    hidden_units = expert_out.shape[0]
    rows = line_count * line_rows
    block = 256
    up_steps = hidden_units // block
    down_steps = half // block
    halves = expert_in.reshape(2, half, 2 * hidden_units)
    clip = lambda value, low, high: jnp.minimum(jnp.maximum(value, low), high)
    up_at = lambda i: jnp.minimum(i, up_steps - 1)
    they_at = lambda i: clip(i - up_steps, 0, down_steps - 1)
    mine_at = lambda i: clip(i - up_steps - down_steps, 0, down_steps - 1)

    def out_at(i, core_ref):
        is_mine = (i >= up_steps + down_steps).astype(jnp.int32)
        side = jnp.where(is_mine == 1, core_ref[0], 1 - core_ref[0])
        return (0, side * down_steps + jnp.where(is_mine == 1, mine_at(i), they_at(i)))

    line = lambda place: pl.BlockSpec((line_rows, block), lambda i, c: (0, place(i)))
    return pl.pallas_call(
        functools.partial(ffn_body, line_count, up_steps, down_steps),
        grid_spec=pltpu.PrefetchScalarGridSpec(
            num_scalar_prefetch=1,
            grid=(up_steps + 2 * down_steps,),
            in_specs=[pl.BlockSpec(memory_space=pl.ANY)] * (2 * line_count)
            + [
                pl.BlockSpec((1, half, block), lambda i, c: (c[0], 0, up_at(i))),
                pl.BlockSpec((1, half, block), lambda i, c: (1 - c[0], 0, up_at(i))),
                pl.BlockSpec((1, half, block), lambda i, c: (c[0], 0, up_steps + up_at(i))),
                pl.BlockSpec((1, half, block), lambda i, c: (1 - c[0], 0, up_steps + up_at(i))),
                pl.BlockSpec((hidden_units, block), out_at),
                pl.BlockSpec((rows, 1), lambda i, c: (0, 0)),
            ],
            out_specs=[line(they_at)] * line_count + [line(mine_at)] * line_count,
            scratch_shapes=[
                pltpu.VMEM((rows, width), jnp.bfloat16),
                pltpu.VMEM((rows, hidden_units), jnp.bfloat16),
                pltpu.SemaphoreType.DMA((2 * line_count,)),
            ],
        ),
        out_shape=[jax.ShapeDtypeStruct((line_rows, half), jnp.bfloat16)] * (2 * line_count),
        compiler_params=pltpu.CompilerParams(
            dimension_semantics=("arbitrary",), vmem_limit_bytes=VMEM_BYTES
        ),
        cost_estimate=pl.CostEstimate(
            flops=6 * rows * width * hidden_units,
            bytes_accessed=6 * width * hidden_units + 4 * rows * width,
            transcendentals=rows * hidden_units,
        ),
        name="expert_ffn",
    )(
        core.reshape(1),
        *own_pieces,
        *sib_pieces,
        halves,
        halves,
        halves,
        halves,
        expert_out,
        scales,
    )


def pick_body(index_ref, cache_ref, out_ref):
    out_ref[...] = cache_ref[...]


def pick_caches(outgoing, cache):
    count = outgoing.shape[0]
    shape = (1,) + cache.shape[1:]
    return pl.pallas_call(
        pick_body,
        grid_spec=pltpu.PrefetchScalarGridSpec(
            num_scalar_prefetch=1,
            grid=(count,),
            in_specs=[pl.BlockSpec(shape, lambda i, index: (index[i], 0, 0))],
            out_specs=pl.BlockSpec(shape, lambda i, index: (i, 0, 0)),
        ),
        out_shape=jax.ShapeDtypeStruct((count,) + cache.shape[1:], cache.dtype),
        name="pick_caches",
    )(outgoing, cache)


def attend_body(group, moved_ref, arrival_ref, length_ref, query_ref, cache_ref, came_ref, fresh_ref, out_ref):
    first = pl.program_id(0) * group
    for slot in range(group):
        request = first + slot
        query = query_ref[slot]
        cache = jnp.where(moved_ref[request] == 1, came_ref[arrival_ref[request]], cache_ref[slot])
        fresh = fresh_ref[slot].astype(jnp.float32)
        scores = jnp.dot(query, cache, preferred_element_type=jnp.float32) * SOFTMAX_SCALE
        own = jnp.sum(query.astype(jnp.float32) * fresh, axis=1, keepdims=True) * SOFTMAX_SCALE
        positions = lax.broadcasted_iota(jnp.int32, scores.shape, 1)
        scores = jnp.where(positions < length_ref[request], scores, -jnp.inf)
        top = jnp.maximum(jnp.max(scores, axis=1, keepdims=True), own)
        weights = jnp.exp(scores - top)
        own_weight = jnp.exp(own - top)
        summed = jnp.sum(weights, axis=1, keepdims=True) + own_weight
        blended = lax.dot_general(
            weights.astype(jnp.bfloat16),
            cache[:LATENT],
            (((1,), (1,)), ((), ())),
            preferred_element_type=jnp.float32,
        )
        own_rounded = own_weight.astype(jnp.bfloat16).astype(jnp.float32)
        blended = blended + own_rounded * fresh[:, :LATENT]
        out_ref[slot] = (blended / summed).astype(jnp.bfloat16)


def attend(moved, arrival, live, queries, cache, came, fresh):
    count, heads, full = queries.shape
    positions = cache.shape[2]
    group = 4
    return pl.pallas_call(
        functools.partial(attend_body, group),
        grid_spec=pltpu.PrefetchScalarGridSpec(
            num_scalar_prefetch=3,
            grid=(count // group,),
            in_specs=[
                pl.BlockSpec((group, heads, full), lambda i, *_: (i, 0, 0)),
                pl.BlockSpec((group, full, positions), lambda i, *_: (i, 0, 0)),
                pl.BlockSpec(came.shape, lambda i, *_: (0, 0, 0)),
                pl.BlockSpec((group, 1, full), lambda i, *_: (i, 0, 0)),
            ],
            out_specs=pl.BlockSpec((group, heads, LATENT), lambda i, *_: (i, 0, 0)),
        ),
        out_shape=jax.ShapeDtypeStruct((count, heads, LATENT), jnp.bfloat16),
        compiler_params=pltpu.CompilerParams(
            dimension_semantics=("arbitrary",), vmem_limit_bytes=32 * 1024 * 1024
        ),
        cost_estimate=pl.CostEstimate(
            flops=4 * count * heads * full * positions,
            bytes_accessed=2 * count * (heads * (full + LATENT) + full * positions),
            transcendentals=count * heads * positions,
        ),
        name="attend",
    )(moved, arrival, live, queries, cache, came, fresh[:, None, :])


def per_device(
    hidden,
    routes,
    route_weights,
    expert_in,
    expert_out,
    queries,
    fresh_key,
    latent_cache,
    lengths,
    swapped,
):
    dp_count, ep_count = lax.axis_size("dp"), lax.axis_size("ep")
    device_count = dp_count * ep_count
    token_count, width = hidden.shape[1], hidden.shape[2]
    half = width // 2
    me = lax.axis_index(AXES)
    core = me % 2
    dp_bits, ep_bits = dp_count.bit_length() - 1, ep_count.bit_length() - 1
    x_masks = [ep_count << bit for bit in range(dp_bits - Z_BITS)]
    z_unit = ep_count << (dp_bits - Z_BITS)
    y_masks = [1 << bit for bit in range(1, ep_bits)]
    z_masks = [z_unit * step for step in range(1 << Z_BITS)]
    orders = (x_masks + y_masks, y_masks + x_masks)
    level_masks = list(zip(*orders))
    line_count = 1 << len(level_masks)
    sibling = (1, 1)

    meta = jnp.concatenate([routes.astype(jnp.float32), route_weights], axis=2)
    all_meta = lax.all_gather(meta, AXES, axis=0, tiled=False)
    pick_count = routes.shape[2]
    chosen = all_meta[..., :pick_count] == me.astype(jnp.float32)
    gates = jnp.sum(jnp.where(chosen, all_meta[..., pick_count:], 0.0), axis=3)
    line_masks = []
    for order in orders:
        line_masks.append(
            [
                sum(mask for bit, mask in enumerate(order) if index >> bit & 1)
                for index in range(line_count)
            ]
        )
    by_core = jnp.where(
        core == 0, jnp.array(line_masks[0], jnp.int32), jnp.array(line_masks[1], jnp.int32)
    )
    sources = (
        (me - core)
        ^ by_core[:, None, None]
        ^ jnp.array(z_masks, jnp.int32)[None, :, None]
        ^ jnp.arange(2, dtype=jnp.int32)[None, None, :]
    ).reshape(-1)
    scales = jnp.take(gates, sources, axis=0).transpose(1, 0, 2).reshape(STEPS, -1, 1)

    row_count = swapped.shape[0]
    is_moved = swapped == 1
    rank = jnp.cumsum(swapped) - 1
    arrival = jnp.clip(rank, 0, MOVE - 1)
    slots = jnp.arange(row_count, dtype=jnp.int32)
    outgoing = jnp.sum(
        jnp.where(
            is_moved[None, :] & (rank[None, :] == jnp.arange(MOVE, dtype=jnp.int32)[:, None]),
            slots[None, :],
            0,
        ),
        axis=1,
    )
    device_rows = me * row_count + slots
    total_rows = device_count * row_count
    anchor = jnp.where(is_moved, (device_rows + total_rows // 2) % total_rows, device_rows)
    live = lengths[anchor]
    stored = jnp.swapaxes(latent_cache, 1, 2)
    leaving = pick_caches(outgoing, stored)

    own_half = lax.dynamic_slice_in_dim(hidden, core * half, half, axis=2)
    other_half = lax.dynamic_slice_in_dim(hidden, (1 - core) * half, half, axis=2)
    came_half = exchange(other_half, sibling)
    pair = jnp.where(
        core == 0,
        jnp.concatenate([own_half, came_half], axis=1),
        jnp.concatenate([came_half, own_half], axis=1),
    )

    mixed = []
    z_done = None
    for step in range(STEPS):
        block = pair[step]
        if z_done is not None:
            block, z_done = lax.optimization_barrier((block, z_done))
        parts = [block] + [exchange(block, (mask, mask)) for mask in z_masks[1:]]
        z_done = parts[-1]
        pieces = [jnp.concatenate(parts, axis=0)]
        for masks in level_masks:
            pieces = pieces + [exchange(piece, masks) for piece in pieces]
        sib_pieces = [exchange(piece, sibling) for piece in pieces]
        outs = expert_ffn(core, pieces, sib_pieces, expert_in[0], expert_out[0], scales[step])
        theirs, mine = outs[:line_count], outs[line_count:]
        sums = [None] * line_count
        for index in reversed(range(line_count)):
            sums[index] = mine[index].astype(jnp.float32) + exchange(theirs[index], sibling).astype(
                jnp.float32
            )
        for masks in reversed(level_masks):
            kept = len(sums) // 2
            for index in reversed(range(kept)):
                came = exchange(sums[kept + index].astype(jnp.bfloat16), masks)
                sums[index] = sums[index] + came.astype(jnp.float32)
            sums = sums[:kept]
        parts = sums[0].reshape(len(z_masks), 2 * token_count, half)
        total = parts[0]
        for place in range(1, len(z_masks)):
            mask = z_masks[place]
            came = exchange(parts[place].astype(jnp.bfloat16), (mask, mask))
            total = total + came.astype(jnp.float32)
        total = total.astype(jnp.bfloat16).reshape(2, token_count, half)
        kept = lax.dynamic_index_in_dim(total, core, 0, keepdims=False)
        sent = lax.dynamic_index_in_dim(total, 1 - core, 0, keepdims=False)
        came = exchange(sent, sibling)
        mixed.append(
            jnp.where(
                core == 0,
                jnp.concatenate([kept, came], axis=1),
                jnp.concatenate([came, kept], axis=1),
            )
        )

    leaving, z_done = lax.optimization_barrier((leaving, z_done))
    far = device_count // 2
    came_cache = exchange(leaving, (far, far))
    context = attend(
        swapped, arrival, live, queries, stored, came_cache, fresh_key
    )
    return (jnp.stack(mixed), context)


def solution(mesh):
    in_specs = (
        P(None, ("dp", "ep"), None),
        P(None, ("dp", "ep"), None),
        P(None, ("dp", "ep"), None),
        P(("dp", "ep"), None, None),
        P(("dp", "ep"), None, None),
        P(("dp", "ep"), None, None),
        P(("dp", "ep"), None),
        P(("dp", "ep"), None, None),
        P(),
        P(("dp", "ep")),
    )
    out_specs = (P(None, ("dp", "ep"), None), P(("dp", "ep"), None, None))
    return jax.shard_map(
        per_device, mesh=mesh, in_specs=in_specs, out_specs=out_specs, check_vma=False
    )
```

time: 224 us -> 238 us (1.062)
  Pallas kernels: 0 us -> 61.9 us
  waiting for transfers between devices: 130 us -> 73 us
  blocking collectives: 0 us -> 44.4 us
  matrix products: 36.6 us -> 0 us
  starting transfers between devices: 21.5 us -> 36.8 us
  local copies, waits for them, and re-layouts: 25.8 us -> 10.7 us
    all_to_all x4 -> x0, waiting for transfers between devices: 119 us -> none  [the longest x2 69.3 us: route_rows(): lax.all_to_all(buffer, ('dp', 'ep'), split_axis=0, concat_axis=0, tiled=T...]
    ppermute x1 -> x44, waiting for transfers between devices: 10.7 us -> 73 us  [exchange(): return lax.ppermute(value, AXES, pairs)]
    pallas_call x0 -> x4, Pallas kernels: none -> 61.9 us  [the longest x2 52.1 us: expert_ffn(): pl.pallas_call(functools.partial(ffn_body, line_count, up_steps, down_ste...]
    all_gather x0 -> x1, blocking collectives: none -> 44.4 us  [per_device(): all_meta = lax.all_gather(meta, AXES, axis=0, tiled=False)]
    dot_general x9 -> x0, matrix products: 36.6 us -> none  [the longest x2 15.6 us: expert_rows(): projected = jnp.dot(picked, expert_in, preferred_element_type=jnp.float32)]
    ppermute x1 -> x44, starting transfers between devices: 2.67 us -> 36.8 us  [exchange(): return lax.ppermute(value, AXES, pairs)]
    all_to_all x4 -> x0, starting transfers between devices: 18.8 us -> none  [the longest x2 11.2 us: route_rows(): lax.all_to_all(buffer, ('dp', 'ep'), split_axis=0, concat_axis=0, tiled=T...]
    gather x6 -> x2, local copies, waits for them, and re-layouts: 17.4 us -> 1.27 us  [the longest x1 0.67 us: per_device(): live = lengths[anchor]]
  transfers between devices with their start and end apart: 5 -> 44, of which waited for: 5 -> 15; matrix products, arithmetic and copies ran while one was open for 26% -> 6% of each run, Pallas kernels for 0% -> 26%
where the time goes in v1:
time: 238 us; the launch traced here: 237 us
  waiting for transfers between devices  73 us (31%)
  Pallas kernels  61.9 us (26%)
  blocking collectives  44.4 us (19%)
  starting transfers between devices  36.8 us (15%)
  local copies, waits for them, and re-layouts  10.7 us (4%)
  other arithmetic  8.6 us (4%)
    ppermute x44, waiting for transfers between devices, exchange(): return lax.ppermute(value, AXES, pairs)  73 us
    pallas_call x2, Pallas kernels, expert_ffn(): pl.pallas_call(functools.partial(ffn_body, line_count, up_steps, down_ste...  52.1 us
    all_gather x1, blocking collectives, per_device(): all_meta = lax.all_gather(meta, AXES, axis=0, tiled=False)  44.4 us
    ppermute x44, starting transfers between devices, exchange(): return lax.ppermute(value, AXES, pairs)  36.8 us
    pallas_call x1, Pallas kernels, attend(): pl.pallas_call(functools.partial(attend_body, group), grid_spec=pltpu.Pre...  5.96 us
  transfers between devices with their start and end apart: 44, of which 15 were waited for; matrix products, arithmetic and copies ran while one was open for 6% of the time, Pallas kernels for 26%

profile of v1, /device:TPU:0, one launch (start us, length us, event | category | flops | bytes accessed | tf_op | source)
XLA Modules:
  0.0 236.5 jit_solution(12295789769984039516)
XLA Ops:
  0.7 1.1 constant_dynamic-slice_fusion.3
  2.4 0.7 fusion.9
  3.4 0.7 convert_element_type.120
  4.1 0.7 pad_maximum_fusion.2
  4.8 0.7 broadcast_compare_fusion
  5.5 0.7 copy.35
  6.4 0.7 select_reduce_fusion.index_ref
  7.1 3.9 %pick_caches.1 = bf16[4,576,128]{2,1,0:T(8,128)(2,1)} custom-call(s32[4]{0:T(128)} %select_reduce_fusion.index_ref, bf16[16,576,128]{2,1,0:T(8,128)(2,1)} %bitcast.23), custom_call_target="tpu_custom_call" | custom-call | tf_op jit(solution)/shard_map/pick_caches/pallas_call | solution.py:173
  10.9 44.4 %all-gather = f32[64,16,16]{2,1,0:T(8,128)S(1)} all-gather(f32[2,16,16]{2,1,0:T(8,128)S(1)} %copy.32), channel_id=2, replica_groups=mesh['dp'=8,'ep'=4] {'dp','ep'}, dimensions={0}, use_global_device_ids=true | all-gather | bytes 67584 | tf_op jit(solution)/shard_map/all_gather | solution.py:271
  55.6 4.3 %collective-permute-start.3 = (bf16[32,1792]{1,0:T(8,128)(2,1)S(1)}, bf16[32,1792]{1,0:T(8,128)(2,1)S(1)}, u32[]{:S(2)}, u32[]{:S(2)}) collective-permute-start(bf16[32,1792]{1,0:T(8,128)(2,1)S(1)} %get-tuple-element.50), channel_id=1, source_target_pairs={{0,24},{1,25},{2,26},{3,27},{4,28},{5,29},{6,30},{7,31},{8,16},{9,... | collective-permute-start | bytes 344072 | tf_op jit(solution)/shard_map/ppermute | solution.py:23
  60.3 1.7 collective-permute-done.1
  62.0 5.3 %collective-permute-done.2 = bf16[32,1792]{1,0:T(8,128)(2,1)S(1)} collective-permute-done((bf16[32,1792]{1,0:T(8,128)(2,1)S(1)}, bf16[32,1792]{1,0:T(8,128)(2,1)S(1)}, u32[]{:S(2)}, u32[]{:S(2)}) %collective-permute-start.2) | collective-permute-done | bytes 114720 | tf_op jit(solution)/shard_map/ppermute | solution.py:23
  67.7 2.5 %collective-permute-start.22 = (bf16[32,1792]{1,0:T(8,128)(2,1)S(1)}, bf16[32,1792]{1,0:T(8,128)(2,1)S(1)}, u32[]{:S(2)}, u32[]{:S(2)}) collective-permute-start(bf16[32,1792]{1,0:T(8,128)(2,1)S(1)} %get-tuple-element.28), channel_id=1, source_target_pairs={{0,8},{1,9},{2,10},{3,11},{4,12},{5,13},{6,14},{7,15},{8,0},{9,1},... | collective-permute-start | bytes 344072 | tf_op jit(solution)/shard_map/ppermute | solution.py:23
  70.2 1.3 collective-permute-start.24
  72.2 5.4 %collective-permute-done.24 = bf16[32,1792]{1,0:T(8,128)(2,1)S(1)} collective-permute-done((bf16[32,1792]{1,0:T(8,128)(2,1)S(1)}, bf16[32,1792]{1,0:T(8,128)(2,1)S(1)}, u32[]{:S(2)}, u32[]{:S(2)}) %collective-permute-start.24) | collective-permute-done | bytes 114720 | tf_op jit(solution)/shard_map/ppermute | solution.py:23
  77.6 2.9 %collective-permute-start.43 = (bf16[4,576,128]{2,1,0:T(8,128)(2,1)}, bf16[4,576,128]{2,1,0:T(8,128)(2,1)S(1)}, u32[]{:S(2)}, u32[]{:S(2)}) collective-permute-start(bf16[4,576,128]{2,1,0:T(8,128)(2,1)} %pick_caches.1), channel_id=1, source_target_pairs={{0,16},{1,17},{2,18},{3,19},{4,20},{5,21},{6,22},{7,23},{8,24},{9,... | collective-permute-start | bytes 1769480 | tf_op jit(solution)/shard_map/ppermute | solution.py:23
  80.5 0.7 constant_dynamic-update-slice_fusion.2
  81.2 17.2 %collective-permute-done.23 = bf16[32,1792]{1,0:T(8,128)(2,1)S(1)} collective-permute-done((bf16[32,1792]{1,0:T(8,128)(2,1)S(1)}, bf16[32,1792]{1,0:T(8,128)(2,1)S(1)}, u32[]{:S(2)}, u32[]{:S(2)}) %collective-permute-start.23) | collective-permute-done | bytes 114720 | tf_op jit(solution)/shard_map/ppermute | solution.py:23
  99.7 1.9 collective-permute-start.25
  101.5 2.0 collective-permute-start.6
  104.5 8.5 %collective-permute-done.25.refs_2_ = bf16[128,1792]{1,0:T(8,128)(2,1)} collective-permute-done((bf16[128,1792]{1,0:T(8,128)(2,1)}, bf16[128,1792]{1,0:T(8,128)(2,1)}, u32[]{:S(2)}, u32[]{:S(2)}) %collective-permute-start.25) | collective-permute-done | bytes 458784 | tf_op jit(solution)/shard_map/ppermute | solution.py:23
  113.0 2.3 collective-permute-start.27
  115.4 0.9 squeeze.40.refs_14_
  116.3 0.9 squeeze.41.refs_14_
  117.2 0.7 gather_fusion.1
  117.9 1.3 copy-done.2
  119.2 6.0 %attend.1 = bf16[16,64,512]{2,1,0:T(8,128)(2,1)} custom-call(s32[16]{0:T(128)S(1)} %copy-done.3, s32[16]{0:T(128)S(1)} %broadcast_clamp_fusion.arrival_ref, s32[16]{0:T(128)S(1)} %gather_fusion.1, bf16[16,64,576]{2,1,0:T(8,128)(2,1)S(1)} %copy-done.2, bf16[16,576,128]{2,1,0:T(8,128)(2,1)S(1)} %bitcast.24, ...), custom_call_target="tpu_custom_call" | custom-call | flops 301989888 | bytes 4587520 | tf_op jit(solution)/shard_map/attend/pallas_call | solution.py:216
  126.3 26.1 %expert_ffn.2 = (bf16[128,1792]{1,0:T(8,128)(2,1)}, bf16[128,1792]{1,0:T(8,128)(2,1)}, bf16[128,1792]{1,0:T(8,128)(2,1)}, bf16[128,1792]{1,0:T(8,128)(2,1)}, bf1...) custom-call(s32[1]{0:T(128)} %bitcast.refs_0_, ...), custom_call_target="tpu_custom_call" | custom-call | flops 11274289152 | bytes 29360128 | tf_op jit(solution)/shard_map/expert_ffn/pallas_call | solution.py:122
  154.2 0.8 copy-done.14
  155.0 26.0 %expert_ffn.3 = (bf16[128,1792]{1,0:T(8,128)(2,1)}, bf16[128,1792]{1,0:T(8,128)(2,1)}, bf16[128,1792]{1,0:T(8,128)(2,1)}, bf16[128,1792]{1,0:T(8,128)(2,1)}, bf1...) custom-call(s32[1]{0:T(128)} %bitcast.refs_0_, ...), custom_call_target="tpu_custom_call" | custom-call | flops 11274289152 | bytes 29360128 | tf_op jit(solution)/shard_map/expert_ffn/pallas_call | solution.py:122
  182.1 1.1 collective-permute-done.33
  183.3 1.1 add_convert_fusion.2
  184.5 2.1 collective-permute-start.16
  186.6 1.2 add_convert_fusion.1
  187.8 5.2 %collective-permute-done.16 = bf16[128,1792]{1,0:T(8,128)(2,1)S(1)} collective-permute-done((bf16[128,1792]{1,0:T(8,128)(2,1)S(1)}, bf16[128,1792]{1,0:T(8,128)(2,1)S(1)}, u32[]{:S(2)}, u32[]{:S(2)}) %collective-permute-start.16) | collective-permute-done | bytes 458784 | tf_op jit(solution)/shard_map/ppermute | solution.py:23
  193.0 2.0 collective-permute-start.37
  195.4 7.5 %collective-permute-done.37 = bf16[128,1792]{1,0:T(8,128)(2,1)S(1)} collective-permute-done((bf16[128,1792]{1,0:T(8,128)(2,1)S(1)}, bf16[128,1792]{1,0:T(8,128)(2,1)S(1)}, u32[]{:S(2)}, u32[]{:S(2)}) %collective-permute-start.37) | collective-permute-done | bytes 458784 | tf_op jit(solution)/shard_map/ppermute | solution.py:23
  202.9 1.9 collective-permute-start.17
  205.2 7.1 %collective-permute-done.17 = bf16[128,1792]{1,0:T(8,128)(2,1)S(1)} collective-permute-done((bf16[128,1792]{1,0:T(8,128)(2,1)S(1)}, bf16[128,1792]{1,0:T(8,128)(2,1)S(1)}, u32[]{:S(2)}, u32[]{:S(2)}) %collective-permute-start.17) | collective-permute-done | bytes 458784 | tf_op jit(solution)/shard_map/ppermute | solution.py:23
  212.7 1.7 collective-permute-start.19
  214.3 2.7 %collective-permute-start.20 = (bf16[32,1792]{1,0:T(8,128)(2,1)S(1)}, bf16[32,1792]{1,0:T(8,128)(2,1)S(1)}, u32[]{:S(2)}, u32[]{:S(2)}) collective-permute-start(bf16[32,1792]{1,0:T(8,128)(2,1)S(1)} %get-tuple-element.45), channel_id=1, source_target_pairs={{0,24},{1,25},{2,26},{3,27},{4,28},{5,29},{6,30},{7,31},{8,16},{9,... | collective-permute-start | bytes 344072 | tf_op jit(solution)/shard_map/ppermute | solution.py:23
  217.6 1.7 collective-permute-start.40
  219.4 2.5 %collective-permute-start.41 = (bf16[32,1792]{1,0:T(8,128)(2,1)S(1)}, bf16[32,1792]{1,0:T(8,128)(2,1)S(1)}, u32[]{:S(2)}, u32[]{:S(2)}) collective-permute-start(bf16[32,1792]{1,0:T(8,128)(2,1)S(1)} %get-tuple-element.48), channel_id=1, source_target_pairs={{0,24},{1,25},{2,26},{3,27},{4,28},{5,29},{6,30},{7,31},{8,16},{9,... | collective-permute-start | bytes 344072 | tf_op jit(solution)/shard_map/ppermute | solution.py:23
  221.9 2.6 %collective-permute-done.19 = bf16[32,1792]{1,0:T(8,128)(2,1)S(1)} collective-permute-done((bf16[32,1792]{1,0:T(8,128)(2,1)S(1)}, bf16[32,1792]{1,0:T(8,128)(2,1)S(1)}, u32[]{:S(2)}, u32[]{:S(2)}) %collective-permute-start.19) | collective-permute-done | bytes 114720 | tf_op jit(solution)/shard_map/ppermute | solution.py:23
  224.7 1.7 collective-permute-done.39
  226.4 8.0 %collective-permute-done.40 = bf16[32,1792]{1,0:T(8,128)(2,1)S(1)} collective-permute-done((bf16[32,1792]{1,0:T(8,128)(2,1)S(1)}, bf16[32,1792]{1,0:T(8,128)(2,1)S(1)}, u32[]{:S(2)}, u32[]{:S(2)}) %collective-permute-start.40) | collective-permute-done | bytes 114720 | tf_op jit(solution)/shard_map/ppermute | solution.py:23
  234.6 1.2 collective-permute-done.42
  235.8 0.7 pad_maximum_fusion.1
  (129 shorter events, 11.1 us)
Async XLA Ops:
  0.6 116.6 %copy-start = (s32[512]{0:T(512)S(1)}, s32[512]{0:T(512)}, u32[]{:S(2)}) copy-start(s32[512]{0:T(512)} %param.21) | copy-start | bytes 6148
  0.6 103.5 %copy-start.3 = (s32[16]{0:T(128)S(1)}, s32[16]{0:T(128)}, u32[]{:S(2)}) copy-start(s32[16]{0:T(128)} %moved_ref.1) | copy-start | bytes 196
  0.7 117.2 %copy-start.1 = (bf16[16,128,576]{1,2,0:T(8,128)(2,1)S(1)}, bf16[16,128,576]{1,2,0:T(8,128)(2,1)}, u32[]{:S(2)}) copy-start(bf16[16,128,576]{1,2,0:T(8,128)(2,1)} %param.20) | copy-start | bytes 7077892
  0.7 116.5 %copy-start.15 = (bf16[16,576]{1,0:T(8,128)(2,1)S(1)}, bf16[16,576]{1,0:T(8,128)(2,1)}, u32[]{:S(2)}) copy-start(bf16[16,576]{1,0:T(8,128)(2,1)} %param.19) | copy-start | bytes 55300
  1.8 53.5 %collective-permute-start = (bf16[2,16,1792]{2,1,0:T(8,128)(2,1)S(1)}, bf16[2,16,1792]{2,1,0:T(8,128)(2,1)S(1)}, u32[]{:S(2)}, u32[]{:S(2)}) collective-permute-start(bf16[2,16,1792]{2,1,0:T(8,128)(2,1)S(1)} %get-tuple-element.53), channel_id=1, source_target_pairs={{0,1},{1,0},{2,3},{3,2},{4,5},{5,4},{6,7},{7,6},{8,9},{9,8},{10,11... | collective-permute-start | bytes 344072 | tf_op jit(solution)/shard_map/ppermute | solution.py:23
  55.4 6.6 %collective-permute-start.1 = (bf16[32,1792]{1,0:T(8,128)(2,1)S(1)}, bf16[32,1792]{1,0:T(8,128)(2,1)S(1)}, u32[]{:S(2)}, u32[]{:S(2)}) collective-permute-start(bf16[32,1792]{1,0:T(8,128)(2,1)S(1)} %get-tuple-element.50), channel_id=1, source_target_pairs={{0,8},{1,9},{2,10},{3,11},{4,12},{5,13},{6,14},{7,15},{8,0},{9,1},... | collective-permute-start | bytes 344072 | tf_op jit(solution)/shard_map/ppermute | solution.py:23
  55.5 11.9 %collective-permute-start.2 = (bf16[32,1792]{1,0:T(8,128)(2,1)S(1)}, bf16[32,1792]{1,0:T(8,128)(2,1)S(1)}, u32[]{:S(2)}, u32[]{:S(2)}) collective-permute-start(bf16[32,1792]{1,0:T(8,128)(2,1)S(1)} %get-tuple-element.50), channel_id=1, source_target_pairs={{0,16},{1,17},{2,18},{3,19},{4,20},{5,21},{6,22},{7,23},{8,24},{9,... | collective-permute-start | bytes 344072 | tf_op jit(solution)/shard_map/ppermute | solution.py:23
  55.6 11.8 %collective-permute-start.3 = (bf16[32,1792]{1,0:T(8,128)(2,1)S(1)}, bf16[32,1792]{1,0:T(8,128)(2,1)S(1)}, u32[]{:S(2)}, u32[]{:S(2)}) collective-permute-start(bf16[32,1792]{1,0:T(8,128)(2,1)S(1)} %get-tuple-element.50), channel_id=1, source_target_pairs={{0,24},{1,25},{2,26},{3,27},{4,28},{5,29},{6,30},{7,31},{8,16},{9,... | collective-permute-start | bytes 344072 | tf_op jit(solution)/shard_map/ppermute | solution.py:23
  67.4 34.1 %collective-permute-start.4 = (bf16[128,1792]{1,0:T(8,128)(2,1)S(1)}, bf16[128,1792]{1,0:T(8,128)(2,1)}, u32[]{:S(2)}, u32[]{:S(2)}) collective-permute-start(bf16[128,1792]{1,0:T(8,128)(2,1)S(1)} %pad_maximum_fusion.refs_1_), channel_id=1, source_target_pairs={{0,4},{1,3},{2,6},{3,1},{4,0},{5,7},{6,2},{7,5},{8,12},{9,11},{10,... | collective-permute-start | bytes 1376264 | tf_op jit(solution)/shard_map/ppermute | solution.py:23
  67.5 36.8 %collective-permute-start.5 = (bf16[128,1792]{1,0:T(8,128)(2,1)S(1)}, bf16[128,1792]{1,0:T(8,128)(2,1)}, u32[]{:S(2)}, u32[]{:S(2)}) collective-permute-start(bf16[128,1792]{1,0:T(8,128)(2,1)S(1)} %pad_maximum_fusion.refs_1_), channel_id=1, source_target_pairs={{0,2},{1,5},{2,0},{3,7},{4,6},{5,1},{6,4},{7,3},{8,10},{9,13},{10,... | collective-permute-start | bytes 1376264 | tf_op jit(solution)/shard_map/ppermute | solution.py:23
  67.6 36.8 %collective-permute-start.7 = (bf16[128,1792]{1,0:T(8,128)(2,1)S(1)}, bf16[128,1792]{1,0:T(8,128)(2,1)}, u32[]{:S(2)}, u32[]{:S(2)}) collective-permute-start(bf16[128,1792]{1,0:T(8,128)(2,1)S(1)} %pad_maximum_fusion.refs_1_), channel_id=1, source_target_pairs={{0,1},{1,0},{2,3},{3,2},{4,5},{5,4},{6,7},{7,6},{8,9},{9,8},{10,11... | collective-permute-start | bytes 1376264 | tf_op jit(solution)/shard_map/ppermute | solution.py:23
  67.7 9.9 %collective-permute-start.22 = (bf16[32,1792]{1,0:T(8,128)(2,1)S(1)}, bf16[32,1792]{1,0:T(8,128)(2,1)S(1)}, u32[]{:S(2)}, u32[]{:S(2)}) collective-permute-start(bf16[32,1792]{1,0:T(8,128)(2,1)S(1)} %get-tuple-element.28), channel_id=1, source_target_pairs={{0,8},{1,9},{2,10},{3,11},{4,12},{5,13},{6,14},{7,15},{8,0},{9,1},... | collective-permute-start | bytes 344072 | tf_op jit(solution)/shard_map/ppermute | solution.py:23
  70.2 7.4 %collective-permute-start.24 = (bf16[32,1792]{1,0:T(8,128)(2,1)S(1)}, bf16[32,1792]{1,0:T(8,128)(2,1)S(1)}, u32[]{:S(2)}, u32[]{:S(2)}) collective-permute-start(bf16[32,1792]{1,0:T(8,128)(2,1)S(1)} %get-tuple-element.28), channel_id=1, source_target_pairs={{0,24},{1,25},{2,26},{3,27},{4,28},{5,29},{6,30},{7,31},{8,16},{9,... | collective-permute-start | bytes 344072 | tf_op jit(solution)/shard_map/ppermute | solution.py:23
  77.6 20.8 %collective-permute-start.23 = (bf16[32,1792]{1,0:T(8,128)(2,1)S(1)}, bf16[32,1792]{1,0:T(8,128)(2,1)S(1)}, u32[]{:S(2)}, u32[]{:S(2)}) collective-permute-start(bf16[32,1792]{1,0:T(8,128)(2,1)S(1)} %get-tuple-element.28), channel_id=1, source_target_pairs={{0,16},{1,17},{2,18},{3,19},{4,20},{5,21},{6,22},{7,23},{8,24},{9,... | collective-permute-start | bytes 344072 | tf_op jit(solution)/shard_map/ppermute | solution.py:23
  77.6 35.4 %collective-permute-start.43 = (bf16[4,576,128]{2,1,0:T(8,128)(2,1)}, bf16[4,576,128]{2,1,0:T(8,128)(2,1)S(1)}, u32[]{:S(2)}, u32[]{:S(2)}) collective-permute-start(bf16[4,576,128]{2,1,0:T(8,128)(2,1)} %pick_caches.1), channel_id=1, source_target_pairs={{0,16},{1,17},{2,18},{3,19},{4,20},{5,21},{6,22},{7,23},{8,24},{9,... | collective-permute-start | bytes 1769480 | tf_op jit(solution)/shard_map/ppermute | solution.py:23
  99.7 13.3 %collective-permute-start.25 = (bf16[128,1792]{1,0:T(8,128)(2,1)}, bf16[128,1792]{1,0:T(8,128)(2,1)}, u32[]{:S(2)}, u32[]{:S(2)}) collective-permute-start(bf16[128,1792]{1,0:T(8,128)(2,1)} %constant_dynamic-update-slice_fusion.refs_1_), channel_id=1, source_target_pairs={{0,4},{1,3},{2,6},{3,1},{4,0},{5,7},{6,2},{7,5},{8,12},{9,11},{10,... | collective-permute-start | bytes 1376264 | tf_op jit(solution)/shard_map/ppermute | solution.py:23
  101.5 13.8 %collective-permute-start.6 = (bf16[128,1792]{1,0:T(8,128)(2,1)}, bf16[128,1792]{1,0:T(8,128)(2,1)}, u32[]{:S(2)}, u32[]{:S(2)}) collective-permute-start(bf16[128,1792]{1,0:T(8,128)(2,1)} %collective-permute-done.4.refs_2_), channel_id=1, source_target_pairs={{0,2},{1,5},{2,0},{3,7},{4,6},{5,1},{6,4},{7,3},{8,10},{9,13},{10,... | collective-permute-start | bytes 1376264 | tf_op jit(solution)/shard_map/ppermute | solution.py:23
  104.3 20.9 %collective-permute-start.26 = (bf16[128,1792]{1,0:T(8,128)(2,1)}, bf16[128,1792]{1,0:T(8,128)(2,1)}, u32[]{:S(2)}, u32[]{:S(2)}) collective-permute-start(bf16[128,1792]{1,0:T(8,128)(2,1)} %constant_dynamic-update-slice_fusion.refs_1_), channel_id=1, source_target_pairs={{0,2},{1,5},{2,0},{3,7},{4,6},{5,1},{6,4},{7,3},{8,10},{9,13},{10,... | collective-permute-start | bytes 1376264 | tf_op jit(solution)/shard_map/ppermute | solution.py:23
  104.4 21.3 %collective-permute-start.8 = (bf16[128,1792]{1,0:T(8,128)(2,1)}, bf16[128,1792]{1,0:T(8,128)(2,1)}, u32[]{:S(2)}, u32[]{:S(2)}) collective-permute-start(bf16[128,1792]{1,0:T(8,128)(2,1)} %collective-permute-done.4.refs_2_), channel_id=1, source_target_pairs={{0,1},{1,0},{2,3},{3,2},{4,5},{5,4},{6,7},{7,6},{8,9},{9,8},{10,11... | collective-permute-start | bytes 1376264 | tf_op jit(solution)/shard_map/ppermute | solution.py:23
  113.0 12.8 %collective-permute-start.9 = (bf16[128,1792]{1,0:T(8,128)(2,1)}, bf16[128,1792]{1,0:T(8,128)(2,1)}, u32[]{:S(2)}, u32[]{:S(2)}) collective-permute-start(bf16[128,1792]{1,0:T(8,128)(2,1)} %collective-permute-done.5.refs_3_), channel_id=1, source_target_pairs={{0,1},{1,0},{2,3},{3,2},{4,5},{5,4},{6,7},{7,6},{8,9},{9,8},{10,11... | collective-permute-start | bytes 1376264 | tf_op jit(solution)/shard_map/ppermute | solution.py:23
  113.0 13.2 %collective-permute-start.27 = (bf16[128,1792]{1,0:T(8,128)(2,1)}, bf16[128,1792]{1,0:T(8,128)(2,1)}, u32[]{:S(2)}, u32[]{:S(2)}) collective-permute-start(bf16[128,1792]{1,0:T(8,128)(2,1)} %collective-permute-done.25.refs_2_), channel_id=1, source_target_pairs={{0,2},{1,5},{2,0},{3,7},{4,6},{5,1},{6,4},{7,3},{8,10},{9,13},{10,... | collective-permute-start | bytes 1376264 | tf_op jit(solution)/shard_map/ppermute | solution.py:23
  115.3 11.0 %collective-permute-start.10 = (bf16[128,1792]{1,0:T(8,128)(2,1)}, bf16[128,1792]{1,0:T(8,128)(2,1)}, u32[]{:S(2)}, u32[]{:S(2)}) collective-permute-start(bf16[128,1792]{1,0:T(8,128)(2,1)} %collective-permute-done.6.refs_4_), channel_id=1, source_target_pairs={{0,1},{1,0},{2,3},{3,2},{4,5},{5,4},{6,7},{7,6},{8,9},{9,8},{10,11... | collective-permute-start | bytes 1376264 | tf_op jit(solution)/shard_map/ppermute | solution.py:23
  125.2 27.7 %collective-permute-start.28 = (bf16[128,1792]{1,0:T(8,128)(2,1)}, bf16[128,1792]{1,0:T(8,128)(2,1)S(1)}, u32[]{:S(2)}, u32[]{:S(2)}) collective-permute-start(bf16[128,1792]{1,0:T(8,128)(2,1)} %constant_dynamic-update-slice_fusion.refs_1_), channel_id=1, source_target_pairs={{0,1},{1,0},{2,3},{3,2},{4,5},{5,4},{6,7},{7,6},{8,9},{9,8},{10,11... | collective-permute-start | bytes 1376264 | tf_op jit(solution)/shard_map/ppermute | solution.py:23
  125.7 27.3 %collective-permute-start.29 = (bf16[128,1792]{1,0:T(8,128)(2,1)}, bf16[128,1792]{1,0:T(8,128)(2,1)S(1)}, u32[]{:S(2)}, u32[]{:S(2)}) collective-permute-start(bf16[128,1792]{1,0:T(8,128)(2,1)} %collective-permute-done.25.refs_2_), channel_id=1, source_target_pairs={{0,1},{1,0},{2,3},{3,2},{4,5},{5,4},{6,7},{7,6},{8,9},{9,8},{10,11... | collective-permute-start | bytes 1376264 | tf_op jit(solution)/shard_map/ppermute | solution.py:23
  125.8 27.6 %collective-permute-start.30 = (bf16[128,1792]{1,0:T(8,128)(2,1)}, bf16[128,1792]{1,0:T(8,128)(2,1)S(1)}, u32[]{:S(2)}, u32[]{:S(2)}) collective-permute-start(bf16[128,1792]{1,0:T(8,128)(2,1)} %collective-permute-done.26.refs_3_), channel_id=1, source_target_pairs={{0,1},{1,0},{2,3},{3,2},{4,5},{5,4},{6,7},{7,6},{8,9},{9,8},{10,11... | collective-permute-start | bytes 1376264 | tf_op jit(solution)/shard_map/ppermute | solution.py:23
  126.2 27.4 %collective-permute-start.31 = (bf16[128,1792]{1,0:T(8,128)(2,1)}, bf16[128,1792]{1,0:T(8,128)(2,1)S(1)}, u32[]{:S(2)}, u32[]{:S(2)}) collective-permute-start(bf16[128,1792]{1,0:T(8,128)(2,1)} %collective-permute-done.27.refs_4_), channel_id=1, source_target_pairs={{0,1},{1,0},{2,3},{3,2},{4,5},{5,4},{6,7},{7,6},{8,9},{9,8},{10,11... | collective-permute-start | bytes 1376264 | tf_op jit(solution)/shard_map/ppermute | solution.py:23
  152.4 28.9 %collective-permute-start.12 = (bf16[128,1792]{1,0:T(8,128)(2,1)}, bf16[128,1792]{1,0:T(8,128)(2,1)S(1)}, u32[]{:S(2)}, u32[]{:S(2)}) collective-permute-start(bf16[128,1792]{1,0:T(8,128)(2,1)} %get-tuple-element.23), channel_id=1, source_target_pairs={{0,1},{1,0},{2,3},{3,2},{4,5},{5,4},{6,7},{7,6},{8,9},{9,8},{10,11... | collective-permute-start | bytes 1376264 | tf_op jit(solution)/shard_map/ppermute | solution.py:23
  152.9 28.9 %collective-permute-start.15 = (bf16[128,1792]{1,0:T(8,128)(2,1)}, bf16[128,1792]{1,0:T(8,128)(2,1)S(1)}, u32[]{:S(2)}, u32[]{:S(2)}) collective-permute-start(bf16[128,1792]{1,0:T(8,128)(2,1)} %get-tuple-element.27), channel_id=1, source_target_pairs={{0,1},{1,0},{2,3},{3,2},{4,5},{5,4},{6,7},{7,6},{8,9},{9,8},{10,11... | collective-permute-start | bytes 1376264 | tf_op jit(solution)/shard_map/ppermute | solution.py:23
  153.0 34.8 %collective-permute-start.14 = (bf16[128,1792]{1,0:T(8,128)(2,1)}, bf16[128,1792]{1,0:T(8,128)(2,1)S(1)}, u32[]{:S(2)}, u32[]{:S(2)}) collective-permute-start(bf16[128,1792]{1,0:T(8,128)(2,1)} %get-tuple-element.25), channel_id=1, source_target_pairs={{0,1},{1,0},{2,3},{3,2},{4,5},{5,4},{6,7},{7,6},{8,9},{9,8},{10,11... | collective-permute-start | bytes 1376264 | tf_op jit(solution)/shard_map/ppermute | solution.py:23
  153.4 51.6 %collective-permute-start.11 = (bf16[128,1792]{1,0:T(8,128)(2,1)}, bf16[128,1792]{1,0:T(8,128)(2,1)S(1)}, u32[]{:S(2)}, u32[]{:S(2)}) collective-permute-start(bf16[128,1792]{1,0:T(8,128)(2,1)} %get-tuple-element.21), channel_id=1, source_target_pairs={{0,1},{1,0},{2,3},{3,2},{4,5},{5,4},{6,7},{7,6},{8,9},{9,8},{10,11... | collective-permute-start | bytes 1376264 | tf_op jit(solution)/shard_map/ppermute | solution.py:23
  181.1 2.1 collective-permute-start.33
  181.3 3.2 %collective-permute-start.36 = (bf16[128,1792]{1,0:T(8,128)(2,1)}, bf16[128,1792]{1,0:T(8,128)(2,1)S(1)}, u32[]{:S(2)}, u32[]{:S(2)}) collective-permute-start(bf16[128,1792]{1,0:T(8,128)(2,1)} %get-tuple-element.36), channel_id=1, source_target_pairs={{0,1},{1,0},{2,3},{3,2},{4,5},{5,4},{6,7},{7,6},{8,9},{9,8},{10,11... | collective-permute-start | bytes 1376264 | tf_op jit(solution)/shard_map/ppermute | solution.py:23
  181.8 13.5 %collective-permute-start.35 = (bf16[128,1792]{1,0:T(8,128)(2,1)}, bf16[128,1792]{1,0:T(8,128)(2,1)S(1)}, u32[]{:S(2)}, u32[]{:S(2)}) collective-permute-start(bf16[128,1792]{1,0:T(8,128)(2,1)} %get-tuple-element.34), channel_id=1, source_target_pairs={{0,1},{1,0},{2,3},{3,2},{4,5},{5,4},{6,7},{7,6},{8,9},{9,8},{10,11... | collective-permute-start | bytes 1376264 | tf_op jit(solution)/shard_map/ppermute | solution.py:23
  183.2 31.1 %collective-permute-start.32 = (bf16[128,1792]{1,0:T(8,128)(2,1)}, bf16[128,1792]{1,0:T(8,128)(2,1)S(1)}, u32[]{:S(2)}, u32[]{:S(2)}) collective-permute-start(bf16[128,1792]{1,0:T(8,128)(2,1)} %get-tuple-element.30), channel_id=1, source_target_pairs={{0,1},{1,0},{2,3},{3,2},{4,5},{5,4},{6,7},{7,6},{8,9},{9,8},{10,11... | collective-permute-start | bytes 1376264 | tf_op jit(solution)/shard_map/ppermute | solution.py:23
  184.5 8.6 %collective-permute-start.16 = (bf16[128,1792]{1,0:T(8,128)(2,1)S(1)}, bf16[128,1792]{1,0:T(8,128)(2,1)S(1)}, u32[]{:S(2)}, u32[]{:S(2)}) collective-permute-start(bf16[128,1792]{1,0:T(8,128)(2,1)S(1)} %add_convert_fusion.4), channel_id=1, source_target_pairs={{0,2},{1,5},{2,0},{3,7},{4,6},{5,1},{6,4},{7,3},{8,10},{9,13},{10,... | collective-permute-start | bytes 1376264 | tf_op jit(solution)/shard_map/ppermute | solution.py:23
  187.8 17.4 %collective-permute-start.13 = (bf16[128,1792]{1,0:T(8,128)(2,1)S(1)}, bf16[128,1792]{1,0:T(8,128)(2,1)S(1)}, u32[]{:S(2)}, u32[]{:S(2)}) collective-permute-start(bf16[128,1792]{1,0:T(8,128)(2,1)S(1)} %add_convert_fusion.5), channel_id=1, source_target_pairs={{0,2},{1,5},{2,0},{3,7},{4,6},{5,1},{6,4},{7,3},{8,10},{9,13},{10,... | collective-permute-start | bytes 1376264 | tf_op jit(solution)/shard_map/ppermute | solution.py:23
  193.0 9.8 %collective-permute-start.37 = (bf16[128,1792]{1,0:T(8,128)(2,1)S(1)}, bf16[128,1792]{1,0:T(8,128)(2,1)S(1)}, u32[]{:S(2)}, u32[]{:S(2)}) collective-permute-start(bf16[128,1792]{1,0:T(8,128)(2,1)S(1)} %add_convert_fusion.1), channel_id=1, source_target_pairs={{0,2},{1,5},{2,0},{3,7},{4,6},{5,1},{6,4},{7,3},{8,10},{9,13},{10,... | collective-permute-start | bytes 1376264 | tf_op jit(solution)/shard_map/ppermute | solution.py:23
  195.3 21.8 %collective-permute-start.34 = (bf16[128,1792]{1,0:T(8,128)(2,1)S(1)}, bf16[128,1792]{1,0:T(8,128)(2,1)S(1)}, u32[]{:S(2)}, u32[]{:S(2)}) collective-permute-start(bf16[128,1792]{1,0:T(8,128)(2,1)S(1)} %add_convert_fusion.2), channel_id=1, source_target_pairs={{0,2},{1,5},{2,0},{3,7},{4,6},{5,1},{6,4},{7,3},{8,10},{9,13},{10,... | collective-permute-start | bytes 1376264 | tf_op jit(solution)/shard_map/ppermute | solution.py:23
  202.9 9.4 %collective-permute-start.17 = (bf16[128,1792]{1,0:T(8,128)(2,1)S(1)}, bf16[128,1792]{1,0:T(8,128)(2,1)S(1)}, u32[]{:S(2)}, u32[]{:S(2)}) collective-permute-start(bf16[128,1792]{1,0:T(8,128)(2,1)S(1)} %add_convert_fusion.3), channel_id=1, source_target_pairs={{0,4},{1,3},{2,6},{3,1},{4,0},{5,7},{6,2},{7,5},{8,12},{9,11},{10,... | collective-permute-start | bytes 1376264 | tf_op jit(solution)/shard_map/ppermute | solution.py:23
  205.0 12.2 %collective-permute-start.38 = (bf16[128,1792]{1,0:T(8,128)(2,1)S(1)}, bf16[128,1792]{1,0:T(8,128)(2,1)S(1)}, u32[]{:S(2)}, u32[]{:S(2)}) collective-permute-start(bf16[128,1792]{1,0:T(8,128)(2,1)S(1)} %add_convert_fusion), channel_id=1, source_target_pairs={{0,4},{1,3},{2,6},{3,1},{4,0},{5,7},{6,2},{7,5},{8,12},{9,11},{10,... | collective-permute-start | bytes 1376264 | tf_op jit(solution)/shard_map/ppermute | solution.py:23
  212.6 6.8 %collective-permute-start.18 = (bf16[32,1792]{1,0:T(8,128)(2,1)S(1)}, bf16[32,1792]{1,0:T(8,128)(2,1)S(1)}, u32[]{:S(2)}, u32[]{:S(2)}) collective-permute-start(bf16[32,1792]{1,0:T(8,128)(2,1)S(1)} %get-tuple-element.44), channel_id=1, source_target_pairs={{0,8},{1,9},{2,10},{3,11},{4,12},{5,13},{6,14},{7,15},{8,0},{9,1},... | collective-permute-start | bytes 344072 | tf_op jit(solution)/shard_map/ppermute | solution.py:23
  212.7 11.9 %collective-permute-start.19 = (bf16[32,1792]{1,0:T(8,128)(2,1)S(1)}, bf16[32,1792]{1,0:T(8,128)(2,1)S(1)}, u32[]{:S(2)}, u32[]{:S(2)}) collective-permute-start(bf16[32,1792]{1,0:T(8,128)(2,1)S(1)} %get-tuple-element.46), channel_id=1, source_target_pairs={{0,16},{1,17},{2,18},{3,19},{4,20},{5,21},{6,22},{7,23},{8,24},{9,... | collective-permute-start | bytes 344072 | tf_op jit(solution)/shard_map/ppermute | solution.py:23
  214.3 10.3 %collective-permute-start.20 = (bf16[32,1792]{1,0:T(8,128)(2,1)S(1)}, bf16[32,1792]{1,0:T(8,128)(2,1)S(1)}, u32[]{:S(2)}, u32[]{:S(2)}) collective-permute-start(bf16[32,1792]{1,0:T(8,128)(2,1)S(1)} %get-tuple-element.45), channel_id=1, source_target_pairs={{0,24},{1,25},{2,26},{3,27},{4,28},{5,29},{6,30},{7,31},{8,16},{9,... | collective-permute-start | bytes 344072 | tf_op jit(solution)/shard_map/ppermute | solution.py:23
  217.5 8.9 %collective-permute-start.39 = (bf16[32,1792]{1,0:T(8,128)(2,1)S(1)}, bf16[32,1792]{1,0:T(8,128)(2,1)S(1)}, u32[]{:S(2)}, u32[]{:S(2)}) collective-permute-start(bf16[32,1792]{1,0:T(8,128)(2,1)S(1)} %get-tuple-element.47), channel_id=1, source_target_pairs={{0,8},{1,9},{2,10},{3,11},{4,12},{5,13},{6,14},{7,15},{8,0},{9,1},... | collective-permute-start | bytes 344072 | tf_op jit(solution)/shard_map/ppermute | solution.py:23
  217.6 16.8 %collective-permute-start.40 = (bf16[32,1792]{1,0:T(8,128)(2,1)S(1)}, bf16[32,1792]{1,0:T(8,128)(2,1)S(1)}, u32[]{:S(2)}, u32[]{:S(2)}) collective-permute-start(bf16[32,1792]{1,0:T(8,128)(2,1)S(1)} %get-tuple-element.49), channel_id=1, source_target_pairs={{0,16},{1,17},{2,18},{3,19},{4,20},{5,21},{6,22},{7,23},{8,24},{9,... | collective-permute-start | bytes 344072 | tf_op jit(solution)/shard_map/ppermute | solution.py:23
  219.4 15.0 %collective-permute-start.41 = (bf16[32,1792]{1,0:T(8,128)(2,1)S(1)}, bf16[32,1792]{1,0:T(8,128)(2,1)S(1)}, u32[]{:S(2)}, u32[]{:S(2)}) collective-permute-start(bf16[32,1792]{1,0:T(8,128)(2,1)S(1)} %get-tuple-element.48), channel_id=1, source_target_pairs={{0,24},{1,25},{2,26},{3,27},{4,28},{5,29},{6,30},{7,31},{8,16},{9,... | collective-permute-start | bytes 344072 | tf_op jit(solution)/shard_map/ppermute | solution.py:23
  224.7 9.9 %collective-permute-start.21 = (bf16[16,1792]{1,0:T(8,128)(2,1)S(1)}, bf16[16,1792]{1,0:T(8,128)(2,1)S(1)}, u32[]{:S(2)}, u32[]{:S(2)}) collective-permute-start(bf16[16,1792]{1,0:T(8,128)(2,1)S(1)} %get-tuple-element.55), channel_id=1, source_target_pairs={{0,1},{1,0},{2,3},{3,2},{4,5},{5,4},{6,7},{7,6},{8,9},{9,8},{10,11... | collective-permute-start | bytes 172040 | tf_op jit(solution)/shard_map/ppermute | solution.py:23
  234.5 1.3 collective-permute-start.42
  (12 other events, 253.0 us)

commit v2 on v1

v2 whole, which is shorter than its diff:
```python
import functools

import jax
import jax.numpy as jnp
from jax import lax
from jax.experimental import pallas as pl
from jax.experimental.pallas import tpu as pltpu
from jax.sharding import PartitionSpec as P

AXES = ("dp", "ep")
LATENT = 512
STEPS = 2
MOVE = 4
LANES = 128
META_PICKS = 8
Z_BITS = 2

SOFTMAX_SCALE = 192.0 ** (-0.5)


def exchange(value, masks):
    count = lax.axis_size(AXES)
    pairs = [(source, source ^ masks[source % 2]) for source in range(count)]
    return lax.ppermute(value, AXES, pairs)


def swap_halves(index, bits):
    low = index & ((1 << bits) - 1)
    return (low << bits) | (index >> bits)


def up_body(line_rows, piece_counts, with_meta, block, spot_ref, *refs):
    refs = list(refs)
    own = [refs.pop(0) for _ in piece_counts]
    sib = [refs.pop(0) for _ in piece_counts]
    weight_ref, act_ref = refs.pop(0), refs.pop(0)
    scale_refs = [refs.pop(0) for _ in range(STEPS if with_meta else 0)]
    own_rows, sib_rows, weights, act, row_sems, weight_sems, act_sems = refs
    line_count = sum(piece_counts)
    half_bits = (line_count.bit_length() - 1) // 2
    half = weight_ref.shape[0] // 2
    hidden_units = weight_ref.shape[1] // 2
    steps = hidden_units // block
    core = spot_ref[0]

    def row_copies(side):
        made = []
        line = 0
        for piece, count in zip(sib if side else own, piece_counts):
            for index in range(count):
                place = swap_halves(line, half_bits) if side else line
                made.append(
                    pltpu.make_async_copy(
                        piece.at[pl.ds(index * line_rows, line_rows)],
                        (sib_rows if side else own_rows).at[pl.ds(place * line_rows, line_rows)],
                        row_sems.at[side, line],
                    )
                )
                line += 1
        return made

    def weight_copies(step, side):
        first = pl.multiple_of((1 - core if side else core) * half, half)
        return [
            pltpu.make_async_copy(
                weight_ref.at[
                    pl.ds(first, half),
                    pl.ds(pl.multiple_of(part * hidden_units + step * block, block), block),
                ],
                weights.at[step % 2, 2 * side + part],
                weight_sems.at[step % 2, 2 * side + part],
            )
            for part in range(2)
        ]

    def act_copy(step):
        columns = pl.ds(pl.multiple_of(step * block, block), block)
        return pltpu.make_async_copy(act.at[:, columns], act_ref.at[:, columns], act_sems.at[step])

    def start(copies):
        for copy in copies:
            copy.start()

    def wait(copies):
        for copy in copies:
            copy.wait()

    for side in range(2):
        start(row_copies(side) + weight_copies(0, side))

    @pl.loop(0, steps)
    def _(step):
        slot = step % 2

        @pl.when(step == 0)
        def _():
            wait(row_copies(0))

        wait(weight_copies(step, 0))

        @pl.when(step + 1 < steps)
        def _():
            start(weight_copies(step + 1, 0) + weight_copies(step + 1, 1))

        own_value = own_rows[:, :half]
        gate = jnp.dot(own_value, weights[slot, 0], preferred_element_type=jnp.float32)
        up = jnp.dot(own_value, weights[slot, 1], preferred_element_type=jnp.float32)

        @pl.when(step == 0)
        def _():
            wait(row_copies(1))

        wait(weight_copies(step, 1))
        sib_value = sib_rows[:, :half]
        gate += jnp.dot(sib_value, weights[slot, 2], preferred_element_type=jnp.float32)
        up += jnp.dot(sib_value, weights[slot, 3], preferred_element_type=jnp.float32)
        value = (gate / (1.0 + jnp.exp(-gate)) * up).astype(jnp.bfloat16)
        act[:, pl.ds(pl.multiple_of(step * block, block), block)] = value
        act_copy(step).start()

    if with_meta:
        meta = own_rows[:, half:].astype(jnp.float32) + sib_rows[:, half:].astype(jnp.float32)
        me = spot_ref[1].astype(jnp.float32)
        lanes = lax.broadcasted_iota(jnp.int32, meta.shape, 1)
        for step, scale_ref in enumerate(scale_refs):
            base = step * 4 * META_PICKS
            value = jnp.zeros_like(meta)
            for part in range(1, 4):
                low = base + part * META_PICKS
                named = pltpu.roll(meta, part * META_PICKS, 1) == me
                inside = (lanes >= low) & (lanes < low + META_PICKS)
                value = value + jnp.where(named & inside, meta, 0.0)
            total = jnp.sum(value, axis=1, keepdims=True)
            scale_ref[...] = jnp.broadcast_to(total, scale_ref.shape)
    for step in range(steps):
        act_copy(step).wait()


def expert_up(spot, own_pieces, sib_pieces, expert_in, line_rows, with_meta):
    piece_counts = [piece.shape[0] // line_rows for piece in own_pieces]
    wide = own_pieces[0].shape[1]
    half = expert_in.shape[0] // 2
    hidden_units = expert_in.shape[1] // 2
    rows = sum(piece_counts) * line_rows
    block = 256
    out_specs = [pl.BlockSpec(memory_space=pl.ANY)]
    out_shape = [jax.ShapeDtypeStruct((rows, hidden_units), jnp.bfloat16)]
    if with_meta:
        out_specs += [pl.BlockSpec((rows, LANES), lambda i, c: (0, 0))] * STEPS
        out_shape += [jax.ShapeDtypeStruct((rows, LANES), jnp.float32)] * STEPS
    held = 2 * rows * (2 * wide + hidden_units) + 16 * half * block
    return pl.pallas_call(
        functools.partial(up_body, line_rows, piece_counts, with_meta, block),
        grid_spec=pltpu.PrefetchScalarGridSpec(
            num_scalar_prefetch=1,
            grid=(1,),
            in_specs=[pl.BlockSpec(memory_space=pl.ANY)] * (2 * len(own_pieces) + 1),
            out_specs=out_specs,
            scratch_shapes=[
                pltpu.VMEM((rows, wide), jnp.bfloat16),
                pltpu.VMEM((rows, wide), jnp.bfloat16),
                pltpu.VMEM((2, 4, half, block), jnp.bfloat16),
                pltpu.VMEM((rows, hidden_units), jnp.bfloat16),
                pltpu.SemaphoreType.DMA((2, sum(piece_counts))),
                pltpu.SemaphoreType.DMA((2, 4)),
                pltpu.SemaphoreType.DMA((hidden_units // block,)),
            ],
        ),
        out_shape=out_shape,
        compiler_params=pltpu.CompilerParams(
            dimension_semantics=("arbitrary",), vmem_limit_bytes=max(50 << 20, held + 24 * rows * block + (4 << 20))
        ),
        cost_estimate=pl.CostEstimate(
            flops=8 * rows * half * hidden_units,
            bytes_accessed=8 * half * hidden_units + 4 * rows * wide + 2 * rows * hidden_units,
            transcendentals=rows * hidden_units,
        ),
        name="expert_up",
    )(spot, *own_pieces, *sib_pieces, expert_in)


def down_body(line_rows, places, spot_ref, act_ref, down_ref, scale_ref, low_ref, high_ref):
    del spot_ref
    answer = jnp.dot(act_ref[...], down_ref[...], preferred_element_type=jnp.float32)
    scale = scale_ref[...]
    half_lines = len(places) // 2
    for column in range(0, answer.shape[1], LANES):
        value = answer[:, column : column + LANES].astype(jnp.bfloat16).astype(jnp.float32)
        value = (value * scale).astype(jnp.bfloat16)
        for index, place in enumerate(places):
            out = low_ref if index < half_lines else high_ref
            at = index % half_lines * line_rows
            out[at : at + line_rows, column : column + LANES] = value[
                place * line_rows : (place + 1) * line_rows
            ]


def expert_down(spot, act, expert_out, scale, line_rows, side):
    rows, hidden_units = act.shape
    half = expert_out.shape[1] // 2
    line_count = rows // line_rows
    half_bits = (line_count.bit_length() - 1) // 2
    places = [swap_halves(index, half_bits) if side else index for index in range(line_count)]
    block = 896
    steps = half // block
    out = pl.BlockSpec((rows // 2, block), lambda i, c: (0, i))
    return pl.pallas_call(
        functools.partial(down_body, line_rows, places),
        grid_spec=pltpu.PrefetchScalarGridSpec(
            num_scalar_prefetch=1,
            grid=(steps,),
            in_specs=[
                pl.BlockSpec((rows, hidden_units), lambda i, c: (0, 0)),
                pl.BlockSpec(
                    (hidden_units, block),
                    lambda i, c: (0, (1 - c[0] if side else c[0]) * steps + i),
                ),
                pl.BlockSpec((rows, LANES), lambda i, c: (0, 0)),
            ],
            out_specs=[out, out],
        ),
        out_shape=[jax.ShapeDtypeStruct((rows // 2, half), jnp.bfloat16)] * 2,
        compiler_params=pltpu.CompilerParams(
            dimension_semantics=("arbitrary",),
            vmem_limit_bytes=4 * (rows + block) * hidden_units + 24 * rows * block + (2 << 20),
        ),
        cost_estimate=pl.CostEstimate(
            flops=2 * rows * half * hidden_units,
            bytes_accessed=2 * half * hidden_units + 2 * rows * (half + hidden_units),
            transcendentals=0,
        ),
        name="expert_down",
    )(spot, act, expert_out, scale)


def meta_body(route_ref, weight_ref, meta_ref):
    token_count, wide = meta_ref.shape
    total = jnp.zeros((token_count, wide), jnp.float32)
    lanes = lax.broadcasted_iota(jnp.int32, (META_PICKS, wide), 1)
    picks = lax.broadcasted_iota(jnp.int32, (META_PICKS, wide), 0)
    for step in range(STEPS):
        weight = weight_ref[step]
        top = weight.astype(jnp.bfloat16)
        rest = weight - top.astype(jnp.float32)
        middle = rest.astype(jnp.bfloat16)
        last = (rest - middle.astype(jnp.float32)).astype(jnp.bfloat16)
        ids = route_ref[step].astype(jnp.float32).astype(jnp.bfloat16)
        for part, value in enumerate((ids, top, middle, last)):
            place = (step * 4 + part) * META_PICKS
            spots = (lanes == picks + place).astype(jnp.bfloat16)
            total += lax.dot_general(
                value, spots, (((0,), (0,)), ((), ())), preferred_element_type=jnp.float32
            )
    meta_ref[...] = total.astype(jnp.bfloat16)


def meta_columns(routes, weights):
    return pl.pallas_call(
        meta_body,
        out_shape=jax.ShapeDtypeStruct((routes.shape[2], LANES), jnp.bfloat16),
        name="meta_columns",
    )(routes, weights)


def pick_body(index_ref, cache_ref, out_ref):
    out_ref[...] = cache_ref[...]


def pick_caches(outgoing, cache):
    count = outgoing.shape[0]
    shape = (1,) + cache.shape[1:]
    return pl.pallas_call(
        pick_body,
        grid_spec=pltpu.PrefetchScalarGridSpec(
            num_scalar_prefetch=1,
            grid=(count,),
            in_specs=[pl.BlockSpec(shape, lambda i, index: (index[i], 0, 0))],
            out_specs=pl.BlockSpec(shape, lambda i, index: (i, 0, 0)),
        ),
        out_shape=jax.ShapeDtypeStruct((count,) + cache.shape[1:], cache.dtype),
        name="pick_caches",
    )(outgoing, cache)


def attend_body(group, moved_ref, arrival_ref, length_ref, query_ref, cache_ref, came_ref, fresh_ref, out_ref):
    first = pl.program_id(0) * group
    for slot in range(group):
        request = first + slot
        query = query_ref[slot]
        cache = jnp.where(moved_ref[request] == 1, came_ref[arrival_ref[request]], cache_ref[slot])
        fresh = fresh_ref[slot].astype(jnp.float32)
        scores = jnp.dot(query, cache, preferred_element_type=jnp.float32) * SOFTMAX_SCALE
        own = jnp.sum(query.astype(jnp.float32) * fresh, axis=1, keepdims=True) * SOFTMAX_SCALE
        positions = lax.broadcasted_iota(jnp.int32, scores.shape, 1)
        scores = jnp.where(positions < length_ref[request], scores, -jnp.inf)
        top = jnp.maximum(jnp.max(scores, axis=1, keepdims=True), own)
        weights = jnp.exp(scores - top)
        own_weight = jnp.exp(own - top)
        summed = jnp.sum(weights, axis=1, keepdims=True) + own_weight
        blended = lax.dot_general(
            weights.astype(jnp.bfloat16),
            cache[:LATENT],
            (((1,), (1,)), ((), ())),
            preferred_element_type=jnp.float32,
        )
        own_rounded = own_weight.astype(jnp.bfloat16).astype(jnp.float32)
        blended = blended + own_rounded * fresh[:, :LATENT]
        out_ref[slot] = (blended / summed).astype(jnp.bfloat16)


def attend(moved, arrival, live, queries, cache, came, fresh):
    count, heads, full = queries.shape
    positions = cache.shape[2]
    group = 4
    return pl.pallas_call(
        functools.partial(attend_body, group),
        grid_spec=pltpu.PrefetchScalarGridSpec(
            num_scalar_prefetch=3,
            grid=(count // group,),
            in_specs=[
                pl.BlockSpec((group, heads, full), lambda i, *_: (i, 0, 0)),
                pl.BlockSpec((group, full, positions), lambda i, *_: (i, 0, 0)),
                pl.BlockSpec(came.shape, lambda i, *_: (0, 0, 0)),
                pl.BlockSpec((group, 1, full), lambda i, *_: (i, 0, 0)),
            ],
            out_specs=pl.BlockSpec((group, heads, LATENT), lambda i, *_: (i, 0, 0)),
        ),
        out_shape=jax.ShapeDtypeStruct((count, heads, LATENT), jnp.bfloat16),
        compiler_params=pltpu.CompilerParams(
            dimension_semantics=("arbitrary",), vmem_limit_bytes=12 << 20
        ),
        cost_estimate=pl.CostEstimate(
            flops=4 * count * heads * full * positions,
            bytes_accessed=2 * count * (heads * (full + LATENT) + full * positions),
            transcendentals=count * heads * positions,
        ),
        name="attend",
    )(moved, arrival, live, queries, cache, came, fresh[:, None, :])


def per_device(
    hidden,
    routes,
    route_weights,
    expert_in,
    expert_out,
    queries,
    fresh_key,
    latent_cache,
    lengths,
    swapped,
):
    dp_count, ep_count = lax.axis_size("dp"), lax.axis_size("ep")
    device_count = dp_count * ep_count
    token_count, width = hidden.shape[1], hidden.shape[2]
    half = width // 2
    me = lax.axis_index(AXES)
    core = me % 2
    dp_bits, ep_bits = dp_count.bit_length() - 1, ep_count.bit_length() - 1
    x_masks = [ep_count << bit for bit in range(dp_bits - Z_BITS)]
    z_unit = ep_count << (dp_bits - Z_BITS)
    y_masks = [1 << bit for bit in range(1, ep_bits)]
    z_masks = [z_unit * step for step in range(1 << Z_BITS)]
    orders = (x_masks + y_masks, y_masks + x_masks)
    level_masks = list(zip(*orders))
    line_count = 1 << len(level_masks)
    sibling = (1, 1)
    spot = jnp.stack([core, me]).astype(jnp.int32)

    meta = meta_columns(jnp.swapaxes(routes, 1, 2), jnp.swapaxes(route_weights, 1, 2))

    own_half = lax.dynamic_slice_in_dim(hidden, core * half, half, axis=2)
    other_half = lax.dynamic_slice_in_dim(hidden, (1 - core) * half, half, axis=2)
    came_half = exchange(other_half, sibling)
    by_core = lambda mine, theirs, axis: jnp.where(
        core == 0,
        jnp.concatenate([mine, theirs], axis=axis),
        jnp.concatenate([theirs, mine], axis=axis),
    )
    pair = by_core(own_half, came_half, 1)
    pair_meta = by_core(meta, jnp.zeros_like(meta), 0)
    line_rows = len(z_masks) * 2 * token_count

    window = lambda *values: lax.optimization_barrier(values)
    far = device_count // 2
    bottom, top_masks = level_masks[:-1], level_masks[-1]

    def send_line(block):
        return [exchange(block, (mask, mask)) for mask in z_masks[1:]]

    def spread(line):
        for masks in bottom:
            line = jnp.concatenate([line, exchange(line, masks)], axis=0)
        return line

    add = lambda terms: functools.reduce(
        lambda total, term: total + term, [term.astype(jnp.float32) for term in terms]
    )
    rounded_sum = lambda terms: add(terms).astype(jnp.bfloat16)
    up = lambda own, sib, with_meta: expert_up(
        spot, own, sib, expert_in[0], line_rows, with_meta
    )
    down = lambda act, scale, side: expert_down(
        spot, act, expert_out[0], scale, line_rows, side
    )
    halves_of = lambda terms: (
        [term[: term.shape[0] // 2] for term in terms],
        [term[term.shape[0] // 2 :] for term in terms],
    )

    def fold(terms):
        for masks in reversed(bottom):
            terms, high = halves_of(terms)
            terms = terms + [exchange(rounded_sum(high), masks)]
        return terms

    def finish_sends(terms):
        block = 2 * token_count
        at = lambda place: [term[place * block : (place + 1) * block] for term in terms]
        return at(0), [rounded_sum(at(place)) for place in range(1, len(z_masks))]

    def finish_line(sends):
        return [exchange(value, (mask, mask)) for value, mask in zip(sends, z_masks[1:])]

    def finish(terms):
        total = rounded_sum(terms).reshape(2, token_count, half)
        kept = lax.dynamic_index_in_dim(total, core, 0, keepdims=False)
        sent = lax.dynamic_index_in_dim(total, 1 - core, 0, keepdims=False)
        return by_core(kept, exchange(sent, sibling), 1)

    block0 = jnp.concatenate([pair[0], pair_meta], axis=1)
    block0, swapped = window(block0, swapped)

    row_count = swapped.shape[0]
    is_moved = swapped == 1
    rank = jnp.cumsum(swapped) - 1
    arrival = jnp.clip(rank, 0, MOVE - 1)
    slots = jnp.arange(row_count, dtype=jnp.int32)
    outgoing = jnp.sum(
        jnp.where(
            is_moved[None, :] & (rank[None, :] == jnp.arange(MOVE, dtype=jnp.int32)[:, None]),
            slots[None, :],
            0,
        ),
        axis=1,
    )
    device_rows = me * row_count + slots
    total_rows = device_count * row_count
    anchor = jnp.where(is_moved, (device_rows + total_rows // 2) % total_rows, device_rows)
    live = lengths[anchor]
    stored = jnp.swapaxes(latent_cache, 1, 2)

    came0 = send_line(block0)
    leaving = pick_caches(outgoing, stored)
    *came0, leaving = window(*came0, leaving)

    low0 = spread(jnp.concatenate([block0] + came0, axis=0))
    low0, block1 = window(low0, pair[1])

    high0 = exchange(low0, top_masks)
    sib_low0 = exchange(low0, sibling)
    came1 = send_line(block1)
    high0, sib_low0, *came1 = window(high0, sib_low0, *came1)

    line1 = jnp.concatenate([block1] + came1, axis=0)
    sib_high0 = exchange(high0, sibling)
    low0, high0, sib_low0, sib_high0, line1, leaving = window(
        low0, high0, sib_low0, sib_high0, line1, leaving
    )

    low1 = spread(line1)
    cache_a = exchange(leaving[: MOVE // 2], (far, far))
    act0, scale0, scale1 = up([low0, high0], [sib_low0, sib_high0], True)
    low1, cache_a, act0, scale0, scale1 = window(low1, cache_a, act0, scale0, scale1)

    part = low1.shape[0] // 2
    high1a = exchange(low1[:part], top_masks)
    sib_low1 = exchange(low1, sibling)
    they_low0, they_high0 = down(act0, scale0, 1)
    low1, high1a, sib_low1, they_low0, they_high0, act0 = window(
        low1, high1a, sib_low1, they_low0, they_high0, act0
    )

    high1b = exchange(low1[part:], top_masks)
    sib_high1a = exchange(high1a, sibling)
    they_low0, they_high0 = exchange(they_low0, sibling), exchange(they_high0, sibling)
    my_low0, my_high0 = down(act0, scale0, 0)
    high1b, sib_high1a, they_low0, they_high0, my_low0, my_high0 = window(
        high1b, sib_high1a, they_low0, they_high0, my_low0, my_high0
    )

    send0 = rounded_sum([my_high0, they_high0])
    sib_high1b = exchange(high1b, sibling)
    send0, sib_high1b, leaving = window(send0, sib_high1b, leaving)

    came = exchange(send0, top_masks)
    cache_b = exchange(leaving[MOVE // 2 :], (far, far))
    (act1,) = up([low1, high1a, high1b], [sib_low1, sib_high1a, sib_high1b], False)
    came, act1, cache_b = window(came, act1, cache_b)

    terms0 = fold([my_low0, they_low0, came])
    they_low1, they_high1 = down(act1, scale1, 1)
    *terms0, they_low1, they_high1 = window(*terms0, they_low1, they_high1)

    kept0, sends0 = finish_sends(terms0)
    *sends0, act1, scale1 = window(*sends0, act1, scale1)
    last0 = finish_line(sends0)
    they_low1, they_high1 = exchange(they_low1, sibling), exchange(they_high1, sibling)
    my_low1, my_high1 = down(act1, scale1, 0)
    they_low1, they_high1, my_low1, my_high1 = window(
        they_low1, they_high1, my_low1, my_high1
    )

    send1 = rounded_sum([my_high1, they_high1])
    send1, queries = window(send1, queries)
    came = exchange(send1, top_masks)
    came_cache = jnp.concatenate([cache_a, cache_b], axis=0)
    context = attend(swapped, arrival, live, queries, stored, came_cache, fresh_key)
    came, context, *last0 = window(came, context, *last0)

    terms1 = fold([my_low1, they_low1, came])
    mixed0 = finish(kept0 + last0)
    kept1, sends1 = finish_sends(terms1)
    mixed1 = finish(kept1 + finish_line(sends1))
    return (jnp.stack([mixed0, mixed1]), context)


def solution(mesh):
    in_specs = (
        P(None, ("dp", "ep"), None),
        P(None, ("dp", "ep"), None),
        P(None, ("dp", "ep"), None),
        P(("dp", "ep"), None, None),
        P(("dp", "ep"), None, None),
        P(("dp", "ep"), None, None),
        P(("dp", "ep"), None),
        P(("dp", "ep"), None, None),
        P(),
        P(("dp", "ep")),
    )
    out_specs = (P(None, ("dp", "ep"), None), P(("dp", "ep"), None, None))
    return jax.shard_map(
        per_device, mesh=mesh, in_specs=in_specs, out_specs=out_specs, check_vma=False
    )
```

time: 238 us -> 159 us (0.67)
  blocking collectives: 44.4 us -> 0 us
  waiting for transfers between devices: 73 us -> 49.5 us
  Pallas kernels: 61.9 us -> 54.3 us
  other arithmetic: 8.6 us -> 13.5 us
  local copies, waits for them, and re-layouts: 10.7 us -> 6.22 us
  starting transfers between devices: 36.8 us -> 34.2 us
    all_gather x1 -> x0, blocking collectives: 44.4 us -> none  [per_device(): all_meta = lax.all_gather(meta, AXES, axis=0, tiled=False)]
    ppermute x44 -> x35, waiting for transfers between devices: 73 us -> 49.5 us  [exchange(): return lax.ppermute(value, AXES, pairs)]
    pallas_call x2 -> x7, Pallas kernels: 52.1 us -> 44.5 us  [the longest x2 28.7 us: expert_up(): pl.pallas_call(functools.partial(up_body, line_rows, piece_counts, with_m...]
    convert_element_type x9 -> x8, other arithmetic: 3.69 us -> 9.11 us  [per_device(): rounded_sum = lambda terms: add(terms).astype(jnp.bfloat16)]
    ppermute x44 -> x35, starting transfers between devices: 36.8 us -> 34.2 us  [exchange(): return lax.ppermute(value, AXES, pairs)]
    unnamed x35 -> x48, local copies, waits for them, and re-layouts: 4.71 us -> 2.23 us
  transfers between devices with their start and end apart: 44 -> 35, of which waited for: 15 -> 14; matrix products, arithmetic and copies ran while one was open for 6% -> 7% of each run, Pallas kernels for 26% -> 34%
where the time goes in v2:
time: 159 us
  Pallas kernels  54.3 us (34%)
  waiting for transfers between devices  49.5 us (31%)
  starting transfers between devices  34.2 us (22%)
  other arithmetic  13.5 us (8%)
  local copies, waits for them, and re-layouts  6.22 us (4%)
    ppermute x35, waiting for transfers between devices, exchange(): return lax.ppermute(value, AXES, pairs)  49.5 us
    ppermute x35, starting transfers between devices, exchange(): return lax.ppermute(value, AXES, pairs)  34.2 us
    pallas_call x2, Pallas kernels, expert_up(): pl.pallas_call(functools.partial(up_body, line_rows, piece_counts, with_m...  28.7 us
    pallas_call x4, Pallas kernels, expert_down(): pl.pallas_call(functools.partial(down_body, line_rows, places), grid_spec...  14.3 us
    convert_element_type x8, other arithmetic, per_device(): rounded_sum = lambda terms: add(terms).astype(jnp.bfloat16)  9.11 us
    pallas_call x1, Pallas kernels, attend(): pl.pallas_call(functools.partial(attend_body, group), grid_spec=pltpu.Pre...  6.03 us
    pallas_call x1, Pallas kernels, pick_caches(): pl.pallas_call(pick_body, grid_spec=pltpu.PrefetchScalarGridSpec(num_scal...  3.84 us
  transfers between devices with their start and end apart: 35, of which 14 were waited for; matrix products, arithmetic and copies ran while one was open for 7% of the time, Pallas kernels for 34%

profile of v2, /device:TPU:0, one launch (start us, length us, event | category | flops | bytes accessed | tf_op | source)
XLA Modules:
  0.0 158.9 jit_solution(17824206377953099883)
XLA Ops:
  2.2 1.5 meta_columns.1
  4.5 2.7 %collective-permute-start.1 = (bf16[32,1920]{1,0:T(8,128)(2,1)S(1)}, bf16[32,1920]{1,0:T(8,128)(2,1)S(1)}, u32[]{:S(2)}, u32[]{:S(2)}) collective-permute-start(bf16[32,1920]{1,0:T(8,128)(2,1)S(1)} %pad_maximum_fusion.5), channel_id=1, source_target_pairs={{0,8},{1,9},{2,10},{3,11},{4,12},{5,13},{6,14},{7,15},{8,0},{9,1},... | collective-permute-start | bytes 368648 | tf_op jit(solution)/shard_map/ppermute | solution.py:24
  7.2 2.6 %collective-permute-start.2 = (bf16[32,1920]{1,0:T(8,128)(2,1)S(1)}, bf16[32,1920]{1,0:T(8,128)(2,1)S(1)}, u32[]{:S(2)}, u32[]{:S(2)}) collective-permute-start(bf16[32,1920]{1,0:T(8,128)(2,1)S(1)} %pad_maximum_fusion.5), channel_id=1, source_target_pairs={{0,16},{1,17},{2,18},{3,19},{4,20},{5,21},{6,22},{7,23},{8,24},{9,... | collective-permute-start | bytes 368648 | tf_op jit(solution)/shard_map/ppermute | solution.py:24
  12.0 3.8 %pick_caches.1 = bf16[4,576,128]{2,1,0:T(8,128)(2,1)} custom-call(s32[4]{0:T(128)} %select_reduce_fusion.index_ref, bf16[16,576,128]{2,1,0:T(8,128)(2,1)} %bitcast.27), custom_call_target="tpu_custom_call" | custom-call | tf_op jit(solution)/shard_map/pick_caches/pallas_call | solution.py:272
  15.8 3.7 %collective-permute-done.2 = bf16[32,1920]{1,0:T(8,128)(2,1)S(1)} collective-permute-done((bf16[32,1920]{1,0:T(8,128)(2,1)S(1)}, bf16[32,1920]{1,0:T(8,128)(2,1)S(1)}, u32[]{:S(2)}, u32[]{:S(2)}) %collective-permute-start.2) | collective-permute-done | bytes 122912 | tf_op jit(solution)/shard_map/ppermute | solution.py:24
  19.6 1.6 collective-permute-start.4
  21.2 7.3 %collective-permute-done.4 = bf16[128,1920]{1,0:T(8,128)(2,1)S(1)} collective-permute-done((bf16[128,1920]{1,0:T(8,128)(2,1)S(1)}, bf16[128,1920]{1,0:T(8,128)(2,1)S(1)}, u32[]{:S(2)}, u32[]{:S(2)}) %collective-permute-start.4) | collective-permute-done | bytes 491552 | tf_op jit(solution)/shard_map/ppermute | solution.py:24
  28.6 1.6 collective-permute-start.5
  30.1 2.5 %collective-permute-start.7 = (bf16[32,1792]{1,0:T(8,128)(2,1)S(1)}, bf16[32,1792]{1,0:T(8,128)(2,1)S(1)}, u32[]{:S(2)}, u32[]{:S(2)}) collective-permute-start(bf16[32,1792]{1,0:T(8,128)(2,1)S(1)} %get-tuple-element.83), channel_id=1, source_target_pairs={{0,8},{1,9},{2,10},{3,11},{4,12},{5,13},{6,14},{7,15},{8,0},{9,1},... | collective-permute-start | bytes 344072 | tf_op jit(solution)/shard_map/ppermute | solution.py:24
  32.6 1.0 collective-permute-start.8
  33.6 1.5 collective-permute-start.9
  35.1 1.4 collective-permute-done.7
  36.4 8.0 %collective-permute-done.8 = bf16[32,1792]{1,0:T(8,128)(2,1)S(1)} collective-permute-done((bf16[32,1792]{1,0:T(8,128)(2,1)S(1)}, bf16[32,1792]{1,0:T(8,128)(2,1)S(1)}, u32[]{:S(2)}, u32[]{:S(2)}) %collective-permute-start.8) | collective-permute-done | bytes 114720 | tf_op jit(solution)/shard_map/ppermute | solution.py:24
  44.7 2.4 %collective-permute-done.10.refs_3_ = bf16[256,1920]{1,0:T(8,128)(2,1)S(1)} collective-permute-done((bf16[256,1920]{1,0:T(8,128)(2,1)S(1)}, bf16[256,1920]{1,0:T(8,128)(2,1)S(1)}, u32[]{:S(2)}, u32[]{:S(2)}) %collective-permute-start.10) | collective-permute-done | bytes 983072 | tf_op jit(solution)/shard_map/ppermute | solution.py:24
  47.1 1.5 collective-permute-start.11
  48.6 3.3 %collective-permute-start.12 = (bf16[2,576,128]{2,1,0:T(8,128)(2,1)S(1)}, bf16[2,576,128]{2,1,0:T(8,128)(2,1)S(1)}, u32[]{:S(2)}, u32[]{:S(2)}) collective-permute-start(bf16[2,576,128]{2,1,0:T(8,128)(2,1)S(1)} %slice.158), channel_id=1, source_target_pairs={{0,16},{1,17},{2,18},{3,19},{4,20},{5,21},{6,22},{7,23},{8,24},{9,... | collective-permute-start | bytes 884744 | tf_op jit(solution)/shard_map/ppermute | solution.py:24
  51.9 14.5 %expert_up.2 = (bf16[512,1024]{1,0:T(8,128)(2,1)}, f32[512,128]{1,0:T(8,128)S(1)}, f32[512,128]{1,0:T(8,128)S(1)}) custom-call(s32[2]{0:T(128)S(1)} %pad_add_fusion.spot_ref, bf16[256,1920]{1,0:T(8,128)(2,1)S(1)} %constant_dynamic-update-slice_fusion.refs_0_, bf16[256,1920]{1,0:T(8,128)(2,1)S(1)} %collective-permute-done.5.refs_1_, ...), custom_call_target="tpu_custom_call" | custom-call | flops 7516192768 | bytes 19660800 | tf_op jit(solution)/shard_map/expert_up/pallas_call | solution.py:152
  67.8 3.6 %expert_down.4 = (bf16[256,1792]{1,0:T(8,128)(2,1)S(1)}, bf16[256,1792]{1,0:T(8,128)(2,1)S(1)}) custom-call(s32[2]{0:T(128)S(1)} %pad_add_fusion.spot_ref, bf16[512,1024]{1,0:T(8,128)(2,1)S(1)} %copy-done.2, bf16[1024,3584]{1,0:T(8,128)(2,1)S(1)} %bitcast.23, f32[512,128]{1,0:T(8,128)S(1)} %get-tuple-element.101.scale_ref), custom_call_target="tpu_custom_call" | custom-call | flops 1879048192 | bytes 6553600 | tf_op jit(solution)/shard_map/expert_down/pallas_call | solution.py:207
  71.4 4.4 %collective-permute-done.13.refs_1_ = bf16[128,1792]{1,0:T(8,128)(2,1)S(1)} collective-permute-done((bf16[128,1792]{1,0:T(8,128)(2,1)S(1)}, bf16[128,1792]{1,0:T(8,128)(2,1)S(1)}, u32[]{:S(2)}, u32[]{:S(2)}) %collective-permute-start.13) | collective-permute-done | bytes 458784 | tf_op jit(solution)/shard_map/ppermute | solution.py:24
  76.9 3.6 %expert_down.5 = (bf16[256,1792]{1,0:T(8,128)(2,1)S(1)}, bf16[256,1792]{1,0:T(8,128)(2,1)S(1)}) custom-call(s32[2]{0:T(128)S(1)} %pad_add_fusion.spot_ref, bf16[512,1024]{1,0:T(8,128)(2,1)S(1)} %copy-done.2, bf16[1024,3584]{1,0:T(8,128)(2,1)S(1)} %bitcast.24, f32[512,128]{1,0:T(8,128)S(1)} %get-tuple-element.101.scale_ref), custom_call_target="tpu_custom_call" | custom-call | flops 1879048192 | bytes 6553600 | tf_op jit(solution)/shard_map/expert_down/pallas_call | solution.py:207
  80.5 4.4 %collective-permute-done.15.refs_2_ = bf16[128,1792]{1,0:T(8,128)(2,1)S(1)} collective-permute-done((bf16[128,1792]{1,0:T(8,128)(2,1)S(1)}, bf16[128,1792]{1,0:T(8,128)(2,1)S(1)}, u32[]{:S(2)}, u32[]{:S(2)}) %collective-permute-start.15) | collective-permute-done | bytes 458784 | tf_op jit(solution)/shard_map/ppermute | solution.py:24
  85.0 1.1 add_convert_fusion.1
  87.4 14.2 %expert_up.3.act_ref = bf16[512,1024]{1,0:T(8,128)(2,1)} custom-call(s32[2]{0:T(128)S(1)} %pad_add_fusion.spot_ref, bf16[256,1792]{1,0:T(8,128)(2,1)S(1)} %pad_maximum_fusion.refs_0_, bf16[128,1792]{1,0:T(8,128)(2,1)S(1)} %collective-permute-done.13.refs_1_, bf16[128,1792]{1,0:T(8,128)(2,1)S(1)} %collective-permute-done.15.refs_2_, ...), custom_call_target="tpu_custom_call" | custom-call | flops 7516192768 | bytes 19398656 | tf_op jit(solution)/shard_map/expert_up/pallas_call | solution.py:152
  101.6 1.0 collective-permute-done.21
  102.6 1.3 add_convert_fusion.3
  104.0 1.6 collective-permute-start.22
  105.6 1.3 slice.164
  107.0 3.6 %expert_down.6 = (bf16[256,1792]{1,0:T(8,128)(2,1)S(1)}, bf16[256,1792]{1,0:T(8,128)(2,1)S(1)}) custom-call(s32[2]{0:T(128)S(1)} %pad_add_fusion.spot_ref, bf16[512,1024]{1,0:T(8,128)(2,1)S(1)} %copy-done.3, bf16[1024,3584]{1,0:T(8,128)(2,1)S(1)} %bitcast.25, f32[512,128]{1,0:T(8,128)S(1)} %get-tuple-element.133.scale_ref), custom_call_target="tpu_custom_call" | custom-call | flops 1879048192 | bytes 6553600 | tf_op jit(solution)/shard_map/expert_down/pallas_call | solution.py:207
  110.6 1.9 %collective-permute-done.22 = bf16[128,1792]{1,0:T(8,128)(2,1)S(1)} collective-permute-done((bf16[128,1792]{1,0:T(8,128)(2,1)S(1)}, bf16[128,1792]{1,0:T(8,128)(2,1)S(1)}, u32[]{:S(2)}, u32[]{:S(2)}) %collective-permute-start.22) | collective-permute-done | bytes 458784 | tf_op jit(solution)/shard_map/ppermute | solution.py:24
  113.9 3.6 %expert_down.7 = (bf16[256,1792]{1,0:T(8,128)(2,1)S(1)}, bf16[256,1792]{1,0:T(8,128)(2,1)S(1)}) custom-call(s32[2]{0:T(128)S(1)} %pad_add_fusion.spot_ref, bf16[512,1024]{1,0:T(8,128)(2,1)S(1)} %copy-done.3, bf16[1024,3584]{1,0:T(8,128)(2,1)S(1)} %bitcast.26, f32[512,128]{1,0:T(8,128)S(1)} %get-tuple-element.133.scale_ref), custom_call_target="tpu_custom_call" | custom-call | flops 1879048192 | bytes 6553600 | tf_op jit(solution)/shard_map/expert_down/pallas_call | solution.py:207
  117.6 1.1 add_convert_fusion
  118.8 1.1 collective-permute-start.25
  120.6 1.5 collective-permute-start.26
  122.1 1.1 collective-permute-start.27
  123.2 1.8 %collective-permute-start.28 = (bf16[32,1792]{1,0:T(8,128)(2,1)S(1)}, bf16[32,1792]{1,0:T(8,128)(2,1)S(1)}, u32[]{:S(2)}, u32[]{:S(2)}) collective-permute-start(bf16[32,1792]{1,0:T(8,128)(2,1)S(1)} %get-tuple-element.144), channel_id=1, source_target_pairs={{0,24},{1,25},{2,26},{3,27},{4,28},{5,29},{6,30},{7,31},{8,16},{9,... | collective-permute-start | bytes 344072 | tf_op jit(solution)/shard_map/ppermute | solution.py:24
  125.1 1.1 pad_maximum_fusion.1.came_ref
  126.2 1.3 copy-done.4
  127.5 6.0 %attend.1 = bf16[16,64,512]{2,1,0:T(8,128)(2,1)} custom-call(s32[16]{0:T(128)S(1)} %copy-done.5, s32[16]{0:T(128)S(1)} %broadcast_clamp_fusion.arrival_ref, s32[16]{0:T(128)S(1)} %gather_fusion, bf16[16,64,576]{2,1,0:T(8,128)(2,1)S(1)} %copy-done.4, bf16[16,576,128]{2,1,0:T(8,128)(2,1)S(1)} %bitcast.28, bf16[4,576,128]{2,1,0:T(8,128)(2,1)S(1)} %pad_maximum_fusion.1.came_ref, ...), custom_call_target="tpu_custom_call" | custom-call | flops 301989888 | bytes 4587520 | tf_op jit(solution)/shard_map/attend/pallas_call | solution.py:315
  133.6 1.2 add_convert_fusion.2
  135.8 1.2 add_convert_fusion.8
  137.0 6.4 %collective-permute-done.30 = bf16[128,1792]{1,0:T(8,128)(2,1)S(1)} collective-permute-done((bf16[128,1792]{1,0:T(8,128)(2,1)S(1)}, bf16[128,1792]{1,0:T(8,128)(2,1)S(1)}, u32[]{:S(2)}, u32[]{:S(2)}) %collective-permute-start.30) | collective-permute-done | bytes 458784 | tf_op jit(solution)/shard_map/ppermute | solution.py:24
  143.3 1.2 add_convert_fusion.7
  144.6 1.7 %collective-permute-start.31 = (bf16[32,1792]{1,0:T(8,128)(2,1)S(1)}, bf16[32,1792]{1,0:T(8,128)(2,1)S(1)}, u32[]{:S(2)}, u32[]{:S(2)}) collective-permute-start(bf16[32,1792]{1,0:T(8,128)(2,1)S(1)} %get-tuple-element.152), channel_id=1, source_target_pairs={{0,8},{1,9},{2,10},{3,11},{4,12},{5,13},{6,14},{7,15},{8,0},{9,1},... | collective-permute-start | bytes 344072 | tf_op jit(solution)/shard_map/ppermute | solution.py:24
  146.3 1.2 collective-permute-start.32
  147.5 1.6 collective-permute-start.33
  149.5 6.3 %collective-permute-done.32 = bf16[32,1792]{1,0:T(8,128)(2,1)S(1)} collective-permute-done((bf16[32,1792]{1,0:T(8,128)(2,1)S(1)}, bf16[32,1792]{1,0:T(8,128)(2,1)S(1)}, u32[]{:S(2)}, u32[]{:S(2)}) %collective-permute-start.32) | collective-permute-done | bytes 114720 | tf_op jit(solution)/shard_map/ppermute | solution.py:24
  155.8 1.0 add_convert_fusion.4
  157.0 1.2 collective-permute-done.34
  (121 shorter events, 13.4 us)
Async XLA Ops:
  0.6 119.3 %copy-start = (s32[512]{0:T(512)S(1)}, s32[512]{0:T(512)}, u32[]{:S(2)}) copy-start(s32[512]{0:T(512)} %param.18) | copy-start | bytes 6148
  1.6 2.8 %collective-permute-start = (bf16[2,16,1792]{2,1,0:T(8,128)(2,1)S(1)}, bf16[2,16,1792]{2,1,0:T(8,128)(2,1)S(1)}, u32[]{:S(2)}, u32[]{:S(2)}) collective-permute-start(bf16[2,16,1792]{2,1,0:T(8,128)(2,1)S(1)} %get-tuple-element.161), channel_id=1, source_target_pairs={{0,1},{1,0},{2,3},{3,2},{4,5},{5,4},{6,7},{7,6},{8,9},{9,8},{10,11... | collective-permute-start | bytes 344072 | tf_op jit(solution)/shard_map/ppermute | solution.py:24
  4.5 11.3 %collective-permute-start.1 = (bf16[32,1920]{1,0:T(8,128)(2,1)S(1)}, bf16[32,1920]{1,0:T(8,128)(2,1)S(1)}, u32[]{:S(2)}, u32[]{:S(2)}) collective-permute-start(bf16[32,1920]{1,0:T(8,128)(2,1)S(1)} %pad_maximum_fusion.5), channel_id=1, source_target_pairs={{0,8},{1,9},{2,10},{3,11},{4,12},{5,13},{6,14},{7,15},{8,0},{9,1},... | collective-permute-start | bytes 368648 | tf_op jit(solution)/shard_map/ppermute | solution.py:24
  7.2 12.4 %collective-permute-start.2 = (bf16[32,1920]{1,0:T(8,128)(2,1)S(1)}, bf16[32,1920]{1,0:T(8,128)(2,1)S(1)}, u32[]{:S(2)}, u32[]{:S(2)}) collective-permute-start(bf16[32,1920]{1,0:T(8,128)(2,1)S(1)} %pad_maximum_fusion.5), channel_id=1, source_target_pairs={{0,16},{1,17},{2,18},{3,19},{4,20},{5,21},{6,22},{7,23},{8,24},{9,... | collective-permute-start | bytes 368648 | tf_op jit(solution)/shard_map/ppermute | solution.py:24
  9.8 9.8 %collective-permute-start.3 = (bf16[32,1920]{1,0:T(8,128)(2,1)S(1)}, bf16[32,1920]{1,0:T(8,128)(2,1)S(1)}, u32[]{:S(2)}, u32[]{:S(2)}) collective-permute-start(bf16[32,1920]{1,0:T(8,128)(2,1)S(1)} %pad_maximum_fusion.5), channel_id=1, source_target_pairs={{0,24},{1,25},{2,26},{3,27},{4,28},{5,29},{6,30},{7,31},{8,16},{9,... | collective-permute-start | bytes 368648 | tf_op jit(solution)/shard_map/ppermute | solution.py:24
  15.8 32.8 %copy-start.6 = (bf16[4,576,128]{2,1,0:T(8,128)(2,1)S(1)}, bf16[4,576,128]{2,1,0:T(8,128)(2,1)}, u32[]{:S(2)}) copy-start(bf16[4,576,128]{2,1,0:T(8,128)(2,1)} %pick_caches.1) | copy-start | bytes 1769476
  19.6 8.9 %collective-permute-start.4 = (bf16[128,1920]{1,0:T(8,128)(2,1)S(1)}, bf16[128,1920]{1,0:T(8,128)(2,1)S(1)}, u32[]{:S(2)}, u32[]{:S(2)}) collective-permute-start(bf16[128,1920]{1,0:T(8,128)(2,1)S(1)} %pad_maximum_fusion.2), channel_id=1, source_target_pairs={{0,4},{1,3},{2,6},{3,1},{4,0},{5,7},{6,2},{7,5},{8,12},{9,11},{10,... | collective-permute-start | bytes 1474568 | tf_op jit(solution)/shard_map/ppermute | solution.py:24
  28.6 15.9 %collective-permute-start.5 = (bf16[256,1920]{1,0:T(8,128)(2,1)S(1)}, bf16[256,1920]{1,0:T(8,128)(2,1)S(1)}, u32[]{:S(2)}, u32[]{:S(2)}) collective-permute-start(bf16[256,1920]{1,0:T(8,128)(2,1)S(1)} %constant_dynamic-update-slice_fusion.refs_0_), channel_id=1, source_target_pairs={{0,2},{1,5},{2,0},{3,7},{4,6},{5,1},{6,4},{7,3},{8,10},{9,13},{10,... | collective-permute-start | bytes 2949128 | tf_op jit(solution)/shard_map/ppermute | solution.py:24
  30.1 14.3 %collective-permute-start.6 = (bf16[256,1920]{1,0:T(8,128)(2,1)S(1)}, bf16[256,1920]{1,0:T(8,128)(2,1)S(1)}, u32[]{:S(2)}, u32[]{:S(2)}) collective-permute-start(bf16[256,1920]{1,0:T(8,128)(2,1)S(1)} %constant_dynamic-update-slice_fusion.refs_0_), channel_id=1, source_target_pairs={{0,1},{1,0},{2,3},{3,2},{4,5},{5,4},{6,7},{7,6},{8,9},{9,8},{10,11... | collective-permute-start | bytes 2949128 | tf_op jit(solution)/shard_map/ppermute | solution.py:24
  30.1 6.3 %collective-permute-start.7 = (bf16[32,1792]{1,0:T(8,128)(2,1)S(1)}, bf16[32,1792]{1,0:T(8,128)(2,1)S(1)}, u32[]{:S(2)}, u32[]{:S(2)}) collective-permute-start(bf16[32,1792]{1,0:T(8,128)(2,1)S(1)} %get-tuple-element.83), channel_id=1, source_target_pairs={{0,8},{1,9},{2,10},{3,11},{4,12},{5,13},{6,14},{7,15},{8,0},{9,1},... | collective-permute-start | bytes 344072 | tf_op jit(solution)/shard_map/ppermute | solution.py:24
  32.6 11.8 %collective-permute-start.8 = (bf16[32,1792]{1,0:T(8,128)(2,1)S(1)}, bf16[32,1792]{1,0:T(8,128)(2,1)S(1)}, u32[]{:S(2)}, u32[]{:S(2)}) collective-permute-start(bf16[32,1792]{1,0:T(8,128)(2,1)S(1)} %get-tuple-element.83), channel_id=1, source_target_pairs={{0,16},{1,17},{2,18},{3,19},{4,20},{5,21},{6,22},{7,23},{8,24},{9,... | collective-permute-start | bytes 344072 | tf_op jit(solution)/shard_map/ppermute | solution.py:24
  33.6 10.8 %collective-permute-start.9 = (bf16[32,1792]{1,0:T(8,128)(2,1)S(1)}, bf16[32,1792]{1,0:T(8,128)(2,1)S(1)}, u32[]{:S(2)}, u32[]{:S(2)}) collective-permute-start(bf16[32,1792]{1,0:T(8,128)(2,1)S(1)} %get-tuple-element.83), channel_id=1, source_target_pairs={{0,24},{1,25},{2,26},{3,27},{4,28},{5,29},{6,30},{7,31},{8,16},{9,... | collective-permute-start | bytes 344072 | tf_op jit(solution)/shard_map/ppermute | solution.py:24
  44.5 2.6 %collective-permute-start.10 = (bf16[256,1920]{1,0:T(8,128)(2,1)S(1)}, bf16[256,1920]{1,0:T(8,128)(2,1)S(1)}, u32[]{:S(2)}, u32[]{:S(2)}) collective-permute-start(bf16[256,1920]{1,0:T(8,128)(2,1)S(1)} %collective-permute-done.5.refs_1_), channel_id=1, source_target_pairs={{0,1},{1,0},{2,3},{3,2},{4,5},{5,4},{6,7},{7,6},{8,9},{9,8},{10,11... | collective-permute-start | bytes 2949128 | tf_op jit(solution)/shard_map/ppermute | solution.py:24
  47.1 4.8 %copy-start.19 = (bf16[256,1920]{1,0:T(8,128)(2,1)}, bf16[256,1920]{1,0:T(8,128)(2,1)S(1)}, u32[]{:S(2)}) copy-start(bf16[256,1920]{1,0:T(8,128)(2,1)S(1)} %collective-permute-done.10.refs_3_) | copy-start | bytes 2949124
  47.1 19.3 %collective-permute-start.11 = (bf16[128,1792]{1,0:T(8,128)(2,1)S(1)}, bf16[128,1792]{1,0:T(8,128)(2,1)S(1)}, u32[]{:S(2)}, u32[]{:S(2)}) collective-permute-start(bf16[128,1792]{1,0:T(8,128)(2,1)S(1)} %pad_maximum_fusion.3), channel_id=1, source_target_pairs={{0,4},{1,3},{2,6},{3,1},{4,0},{5,7},{6,2},{7,5},{8,12},{9,11},{10,... | collective-permute-start | bytes 1376264 | tf_op jit(solution)/shard_map/ppermute | solution.py:24
  48.6 17.9 %collective-permute-start.12 = (bf16[2,576,128]{2,1,0:T(8,128)(2,1)S(1)}, bf16[2,576,128]{2,1,0:T(8,128)(2,1)S(1)}, u32[]{:S(2)}, u32[]{:S(2)}) collective-permute-start(bf16[2,576,128]{2,1,0:T(8,128)(2,1)S(1)} %slice.158), channel_id=1, source_target_pairs={{0,16},{1,17},{2,18},{3,19},{4,20},{5,21},{6,22},{7,23},{8,24},{9,... | collective-permute-start | bytes 884744 | tf_op jit(solution)/shard_map/ppermute | solution.py:24
  51.9 15.9 %slice-start = ((s8[7340032]{0:T(1024)(128)(4,1)}), s8[4194304]{0:T(1024)(128)(4,1)S(1)}, s32[]{:S(2)}) async-start(s8[7340032]{0:T(1024)(128)(4,1)} %bitcast.21), calls=%async_computation | async-start | bytes 8388608
  51.9 15.9 %slice-start.1 = ((s8[7340032]{0:T(1024)(128)(4,1)}), s8[3145728]{0:T(1024)(128)(4,1)S(1)}, s32[]{:S(2)}) async-start(s8[7340032]{0:T(1024)(128)(4,1)} %bitcast.21), calls=%async_computation.1 | async-start | bytes 6291456
  67.2 8.6 %collective-permute-start.14 = (bf16[256,1792]{1,0:T(8,128)(2,1)S(1)}, bf16[256,1792]{1,0:T(8,128)(2,1)S(1)}, u32[]{:S(2)}, u32[]{:S(2)}) collective-permute-start(bf16[256,1792]{1,0:T(8,128)(2,1)S(1)} %pad_maximum_fusion.refs_0_), channel_id=1, source_target_pairs={{0,1},{1,0},{2,3},{3,2},{4,5},{5,4},{6,7},{7,6},{8,9},{9,8},{10,11... | collective-permute-start | bytes 2752520 | tf_op jit(solution)/shard_map/ppermute | solution.py:24
  67.2 8.5 %collective-permute-start.13 = (bf16[128,1792]{1,0:T(8,128)(2,1)S(1)}, bf16[128,1792]{1,0:T(8,128)(2,1)S(1)}, u32[]{:S(2)}, u32[]{:S(2)}) collective-permute-start(bf16[128,1792]{1,0:T(8,128)(2,1)S(1)} %slice.159), channel_id=1, source_target_pairs={{0,2},{1,5},{2,0},{3,7},{4,6},{5,1},{6,4},{7,3},{8,10},{9,13},{10,... | collective-permute-start | bytes 1376264 | tf_op jit(solution)/shard_map/ppermute | solution.py:24
  75.8 9.1 %collective-permute-start.17 = (bf16[256,1792]{1,0:T(8,128)(2,1)S(1)}, bf16[256,1792]{1,0:T(8,128)(2,1)S(1)}, u32[]{:S(2)}, u32[]{:S(2)}) collective-permute-start(bf16[256,1792]{1,0:T(8,128)(2,1)S(1)} %get-tuple-element.106), channel_id=1, source_target_pairs={{0,1},{1,0},{2,3},{3,2},{4,5},{5,4},{6,7},{7,6},{8,9},{9,8},{10,11... | collective-permute-start | bytes 2752520 | tf_op jit(solution)/shard_map/ppermute | solution.py:24
  75.8 9.1 %collective-permute-start.18 = (bf16[256,1792]{1,0:T(8,128)(2,1)S(1)}, bf16[256,1792]{1,0:T(8,128)(2,1)S(1)}, u32[]{:S(2)}, u32[]{:S(2)}) collective-permute-start(bf16[256,1792]{1,0:T(8,128)(2,1)S(1)} %get-tuple-element.107), channel_id=1, source_target_pairs={{0,1},{1,0},{2,3},{3,2},{4,5},{5,4},{6,7},{7,6},{8,9},{9,8},{10,11... | collective-permute-start | bytes 2752520 | tf_op jit(solution)/shard_map/ppermute | solution.py:24
  76.3 8.5 %collective-permute-start.15 = (bf16[128,1792]{1,0:T(8,128)(2,1)S(1)}, bf16[128,1792]{1,0:T(8,128)(2,1)S(1)}, u32[]{:S(2)}, u32[]{:S(2)}) collective-permute-start(bf16[128,1792]{1,0:T(8,128)(2,1)S(1)} %slice.160), channel_id=1, source_target_pairs={{0,2},{1,5},{2,0},{3,7},{4,6},{5,1},{6,4},{7,3},{8,10},{9,13},{10,... | collective-permute-start | bytes 1376264 | tf_op jit(solution)/shard_map/ppermute | solution.py:24
  76.9 8.0 %collective-permute-start.16 = (bf16[128,1792]{1,0:T(8,128)(2,1)S(1)}, bf16[128,1792]{1,0:T(8,128)(2,1)S(1)}, u32[]{:S(2)}, u32[]{:S(2)}) collective-permute-start(bf16[128,1792]{1,0:T(8,128)(2,1)S(1)} %collective-permute-done.13.refs_1_), channel_id=1, source_target_pairs={{0,1},{1,0},{2,3},{3,2},{4,5},{5,4},{6,7},{7,6},{8,9},{9,8},{10,11... | collective-permute-start | bytes 1376264 | tf_op jit(solution)/shard_map/ppermute | solution.py:24
  80.5 6.8 %copy-start.7 = (bf16[4,576,128]{2,1,0:T(8,128)(2,1)S(1)}, bf16[4,576,128]{2,1,0:T(8,128)(2,1)}, u32[]{:S(2)}) copy-start(bf16[4,576,128]{2,1,0:T(8,128)(2,1)} %pick_caches.1) | copy-start | bytes 1769476
  84.9 1.9 %collective-permute-start.19 = (bf16[128,1792]{1,0:T(8,128)(2,1)S(1)}, bf16[128,1792]{1,0:T(8,128)(2,1)S(1)}, u32[]{:S(2)}, u32[]{:S(2)}) collective-permute-start(bf16[128,1792]{1,0:T(8,128)(2,1)S(1)} %collective-permute-done.15.refs_2_), channel_id=1, source_target_pairs={{0,1},{1,0},{2,3},{3,2},{4,5},{5,4},{6,7},{7,6},{8,9},{9,8},{10,11... | collective-permute-start | bytes 1376264 | tf_op jit(solution)/shard_map/ppermute | solution.py:24
  86.8 15.8 %collective-permute-start.20 = (bf16[256,1792]{1,0:T(8,128)(2,1)}, bf16[256,1792]{1,0:T(8,128)(2,1)}, u32[]{:S(2)}, u32[]{:S(2)}) collective-permute-start(bf16[256,1792]{1,0:T(8,128)(2,1)} %add_convert_fusion.1), channel_id=1, source_target_pairs={{0,2},{1,5},{2,0},{3,7},{4,6},{5,1},{6,4},{7,3},{8,10},{9,13},{10,... | collective-permute-start | bytes 2752520 | tf_op jit(solution)/shard_map/ppermute | solution.py:24
  87.3 15.3 %collective-permute-start.21 = (bf16[2,576,128]{2,1,0:T(8,128)(2,1)S(1)}, bf16[2,576,128]{2,1,0:T(8,128)(2,1)S(1)}, u32[]{:S(2)}, u32[]{:S(2)}) collective-permute-start(bf16[2,576,128]{2,1,0:T(8,128)(2,1)S(1)} %slice.163), channel_id=1, source_target_pairs={{0,16},{1,17},{2,18},{3,19},{4,20},{5,21},{6,22},{7,23},{8,24},{9,... | collective-permute-start | bytes 884744 | tf_op jit(solution)/shard_map/ppermute | solution.py:24
  87.4 15.2 %copy-start.14 = (bf16[256,1792]{1,0:T(8,128)(2,1)S(1)}, bf16[256,1792]{1,0:T(8,128)(2,1)}, u32[]{:S(2)}) copy-start(bf16[256,1792]{1,0:T(8,128)(2,1)} %copy-done.13) | copy-start | bytes 2752516
  104.0 8.5 %collective-permute-start.22 = (bf16[128,1792]{1,0:T(8,128)(2,1)S(1)}, bf16[128,1792]{1,0:T(8,128)(2,1)S(1)}, u32[]{:S(2)}, u32[]{:S(2)}) collective-permute-start(bf16[128,1792]{1,0:T(8,128)(2,1)S(1)} %add_convert_fusion.3), channel_id=1, source_target_pairs={{0,4},{1,3},{2,6},{3,1},{4,0},{5,7},{6,2},{7,5},{8,12},{9,11},{10,... | collective-permute-start | bytes 1376264 | tf_op jit(solution)/shard_map/ppermute | solution.py:24
  105.6 7.5 %copy-start.8 = (bf16[128,1792]{1,0:T(8,128)(2,1)}, bf16[128,1792]{1,0:T(8,128)(2,1)S(1)}, u32[]{:S(2)}) copy-start(bf16[128,1792]{1,0:T(8,128)(2,1)S(1)} %slice.161) | copy-start | bytes 1376260
  105.6 7.4 %copy-start.9 = (bf16[128,1792]{1,0:T(8,128)(2,1)}, bf16[128,1792]{1,0:T(8,128)(2,1)S(1)}, u32[]{:S(2)}) copy-start(bf16[128,1792]{1,0:T(8,128)(2,1)S(1)} %slice.162) | copy-start | bytes 1376260
  107.0 6.1 %copy-start.10 = (bf16[128,1792]{1,0:T(8,128)(2,1)}, bf16[128,1792]{1,0:T(8,128)(2,1)S(1)}, u32[]{:S(2)}) copy-start(bf16[128,1792]{1,0:T(8,128)(2,1)S(1)} %slice.164) | copy-start | bytes 1376260
  112.5 5.0 %copy-start.15 = (bf16[128,1792]{1,0:T(8,128)(2,1)}, bf16[128,1792]{1,0:T(8,128)(2,1)S(1)}, u32[]{:S(2)}) copy-start(bf16[128,1792]{1,0:T(8,128)(2,1)S(1)} %collective-permute-done.22) | copy-start | bytes 1376260
  112.5 5.0 %collective-permute-start.23 = (bf16[256,1792]{1,0:T(8,128)(2,1)S(1)}, bf16[256,1792]{1,0:T(8,128)(2,1)S(1)}, u32[]{:S(2)}, u32[]{:S(2)}) collective-permute-start(bf16[256,1792]{1,0:T(8,128)(2,1)S(1)} %get-tuple-element.130), channel_id=1, source_target_pairs={{0,1},{1,0},{2,3},{3,2},{4,5},{5,4},{6,7},{7,6},{8,9},{9,8},{10,11... | collective-permute-start | bytes 2752520 | tf_op jit(solution)/shard_map/ppermute | solution.py:24
  112.5 5.0 %collective-permute-start.24 = (bf16[256,1792]{1,0:T(8,128)(2,1)S(1)}, bf16[256,1792]{1,0:T(8,128)(2,1)S(1)}, u32[]{:S(2)}, u32[]{:S(2)}) collective-permute-start(bf16[256,1792]{1,0:T(8,128)(2,1)S(1)} %get-tuple-element.131), channel_id=1, source_target_pairs={{0,1},{1,0},{2,3},{3,2},{4,5},{5,4},{6,7},{7,6},{8,9},{9,8},{10,11... | collective-permute-start | bytes 2752520 | tf_op jit(solution)/shard_map/ppermute | solution.py:24
  117.6 8.6 %copy-start.1 = (bf16[16,128,576]{1,2,0:T(8,128)(2,1)S(1)}, bf16[16,128,576]{1,2,0:T(8,128)(2,1)}, u32[]{:S(2)}) copy-start(bf16[16,128,576]{1,2,0:T(8,128)(2,1)} %param.17) | copy-start | bytes 7077892
  118.8 14.8 %collective-permute-start.25 = (bf16[256,1792]{1,0:T(8,128)(2,1)}, bf16[256,1792]{1,0:T(8,128)(2,1)}, u32[]{:S(2)}, u32[]{:S(2)}) collective-permute-start(bf16[256,1792]{1,0:T(8,128)(2,1)} %add_convert_fusion), channel_id=1, source_target_pairs={{0,2},{1,5},{2,0},{3,7},{4,6},{5,1},{6,4},{7,3},{8,10},{9,13},{10,... | collective-permute-start | bytes 2752520 | tf_op jit(solution)/shard_map/ppermute | solution.py:24
  120.6 12.9 %collective-permute-start.26 = (bf16[32,1792]{1,0:T(8,128)(2,1)}, bf16[32,1792]{1,0:T(8,128)(2,1)S(1)}, u32[]{:S(2)}, u32[]{:S(2)}) collective-permute-start(bf16[32,1792]{1,0:T(8,128)(2,1)} %get-tuple-element.142), channel_id=1, source_target_pairs={{0,8},{1,9},{2,10},{3,11},{4,12},{5,13},{6,14},{7,15},{8,0},{9,1},... | collective-permute-start | bytes 344072 | tf_op jit(solution)/shard_map/ppermute | solution.py:24
  122.1 11.5 %collective-permute-start.27 = (bf16[32,1792]{1,0:T(8,128)(2,1)}, bf16[32,1792]{1,0:T(8,128)(2,1)S(1)}, u32[]{:S(2)}, u32[]{:S(2)}) collective-permute-start(bf16[32,1792]{1,0:T(8,128)(2,1)} %get-tuple-element.143), channel_id=1, source_target_pairs={{0,16},{1,17},{2,18},{3,19},{4,20},{5,21},{6,22},{7,23},{8,24},{9,... | collective-permute-start | bytes 344072 | tf_op jit(solution)/shard_map/ppermute | solution.py:24
  123.2 10.3 %collective-permute-start.28 = (bf16[32,1792]{1,0:T(8,128)(2,1)S(1)}, bf16[32,1792]{1,0:T(8,128)(2,1)S(1)}, u32[]{:S(2)}, u32[]{:S(2)}) collective-permute-start(bf16[32,1792]{1,0:T(8,128)(2,1)S(1)} %get-tuple-element.144), channel_id=1, source_target_pairs={{0,24},{1,25},{2,26},{3,27},{4,28},{5,29},{6,30},{7,31},{8,16},{9,... | collective-permute-start | bytes 344072 | tf_op jit(solution)/shard_map/ppermute | solution.py:24
  127.5 6.1 %copy-start.12 = (bf16[256,1792]{1,0:T(8,128)(2,1)S(1)}, bf16[256,1792]{1,0:T(8,128)(2,1)}, u32[]{:S(2)}) copy-start(bf16[256,1792]{1,0:T(8,128)(2,1)} %copy-done.11) | copy-start | bytes 2752516
  134.8 8.5 %collective-permute-start.30 = (bf16[128,1792]{1,0:T(8,128)(2,1)S(1)}, bf16[128,1792]{1,0:T(8,128)(2,1)S(1)}, u32[]{:S(2)}, u32[]{:S(2)}) collective-permute-start(bf16[128,1792]{1,0:T(8,128)(2,1)S(1)} %add_convert_fusion.2), channel_id=1, source_target_pairs={{0,4},{1,3},{2,6},{3,1},{4,0},{5,7},{6,2},{7,5},{8,12},{9,11},{10,... | collective-permute-start | bytes 1376264 | tf_op jit(solution)/shard_map/ppermute | solution.py:24
  144.6 5.0 %collective-permute-start.31 = (bf16[32,1792]{1,0:T(8,128)(2,1)S(1)}, bf16[32,1792]{1,0:T(8,128)(2,1)S(1)}, u32[]{:S(2)}, u32[]{:S(2)}) collective-permute-start(bf16[32,1792]{1,0:T(8,128)(2,1)S(1)} %get-tuple-element.152), channel_id=1, source_target_pairs={{0,8},{1,9},{2,10},{3,11},{4,12},{5,13},{6,14},{7,15},{8,0},{9,1},... | collective-permute-start | bytes 344072 | tf_op jit(solution)/shard_map/ppermute | solution.py:24
  146.3 9.5 %collective-permute-start.32 = (bf16[32,1792]{1,0:T(8,128)(2,1)S(1)}, bf16[32,1792]{1,0:T(8,128)(2,1)S(1)}, u32[]{:S(2)}, u32[]{:S(2)}) collective-permute-start(bf16[32,1792]{1,0:T(8,128)(2,1)S(1)} %get-tuple-element.154), channel_id=1, source_target_pairs={{0,16},{1,17},{2,18},{3,19},{4,20},{5,21},{6,22},{7,23},{8,24},{9,... | collective-permute-start | bytes 344072 | tf_op jit(solution)/shard_map/ppermute | solution.py:24
  147.5 8.4 %collective-permute-start.33 = (bf16[32,1792]{1,0:T(8,128)(2,1)S(1)}, bf16[32,1792]{1,0:T(8,128)(2,1)S(1)}, u32[]{:S(2)}, u32[]{:S(2)}) collective-permute-start(bf16[32,1792]{1,0:T(8,128)(2,1)S(1)} %get-tuple-element.153), channel_id=1, source_target_pairs={{0,24},{1,25},{2,26},{3,27},{4,28},{5,29},{6,30},{7,31},{8,16},{9,... | collective-permute-start | bytes 344072 | tf_op jit(solution)/shard_map/ppermute | solution.py:24
  149.0 7.9 %collective-permute-start.29 = (bf16[16,1792]{1,0:T(8,128)(2,1)S(1)}, bf16[16,1792]{1,0:T(8,128)(2,1)S(1)}, u32[]{:S(2)}, u32[]{:S(2)}) collective-permute-start(bf16[16,1792]{1,0:T(8,128)(2,1)S(1)} %get-tuple-element.163), channel_id=1, source_target_pairs={{0,1},{1,0},{2,3},{3,2},{4,5},{5,4},{6,7},{7,6},{8,9},{9,8},{10,11... | collective-permute-start | bytes 172040 | tf_op jit(solution)/shard_map/ppermute | solution.py:24
  156.9 1.3 collective-permute-start.34
  (9 other events, 17.9 us)

commit v3 on v2

--- a/solution.py
+++ b/solution.py
@@ -168,7 +168,7 @@
         ),
         out_shape=out_shape,
         compiler_params=pltpu.CompilerParams(
-            dimension_semantics=("arbitrary",), vmem_limit_bytes=max(50 << 20, held + 24 * rows * block + (4 << 20))
+            dimension_semantics=("arbitrary",), vmem_limit_bytes=max(47 << 20, held + 24 * rows * block + (4 << 20))
         ),
         cost_estimate=pl.CostEstimate(
             flops=8 * rows * half * hidden_units,
@@ -225,8 +225,8 @@
             vmem_limit_bytes=4 * (rows + block) * hidden_units + 24 * rows * block + (2 << 20),
         ),
         cost_estimate=pl.CostEstimate(
-            flops=2 * rows * half * hidden_units,
-            bytes_accessed=2 * half * hidden_units + 2 * rows * (half + hidden_units),
+            flops=1 << 36,
+            bytes_accessed=1 << 27,
             transcendentals=0,
         ),
         name="expert_down",
@@ -474,28 +474,22 @@
     low1, cache_a, act0, scale0, scale1 = window(low1, cache_a, act0, scale0, scale1)
 
     part = low1.shape[0] // 2
-    high1a = exchange(low1[:part], top_masks)
+    high1 = exchange(low1, top_masks)
+    they_low0, they_high0 = down(act0, scale0, 1)
     sib_low1 = exchange(low1, sibling)
-    they_low0, they_high0 = down(act0, scale0, 1)
-    low1, high1a, sib_low1, they_low0, they_high0, act0 = window(
-        low1, high1a, sib_low1, they_low0, they_high0, act0
-    )
-
-    high1b = exchange(low1[part:], top_masks)
-    sib_high1a = exchange(high1a, sibling)
     they_low0, they_high0 = exchange(they_low0, sibling), exchange(they_high0, sibling)
     my_low0, my_high0 = down(act0, scale0, 0)
-    high1b, sib_high1a, they_low0, they_high0, my_low0, my_high0 = window(
-        high1b, sib_high1a, they_low0, they_high0, my_low0, my_high0
+    high1, sib_low1, they_low0, they_high0, my_low0, my_high0 = window(
+        high1, sib_low1, they_low0, they_high0, my_low0, my_high0
     )
 
     send0 = rounded_sum([my_high0, they_high0])
-    sib_high1b = exchange(high1b, sibling)
-    send0, sib_high1b, leaving = window(send0, sib_high1b, leaving)
+    sib_high1 = exchange(high1, sibling)
+    send0, sib_high1, leaving = window(send0, sib_high1, leaving)
 
     came = exchange(send0, top_masks)
     cache_b = exchange(leaving[MOVE // 2 :], (far, far))
-    (act1,) = up([low1, high1a, high1b], [sib_low1, sib_high1a, sib_high1b], False)
+    (act1,) = up([low1, high1], [sib_low1, sib_high1], False)
     came, act1, cache_b = window(came, act1, cache_b)
 
     terms0 = fold([my_low0, they_low0, came])

time: 159 us -> 154 us (0.969)
  waiting for transfers between devices: 49.5 us -> 44.6 us
    ppermute x35 -> x33, waiting for transfers between devices: 49.5 us -> 44.6 us  [exchange(): return lax.ppermute(value, AXES, pairs)]
    unnamed x48, local copies, waits for them, and re-layouts: 2.23 us -> 5.15 us
    ppermute x35 -> x33, starting transfers between devices: 34.2 us -> 33.5 us  [exchange(): return lax.ppermute(value, AXES, pairs)]
  transfers between devices with their start and end apart: 35 -> 33, of which waited for: 14 -> 14; matrix products, arithmetic and copies ran while one was open for 7% -> 6% of each run, Pallas kernels for 34% -> 35%
where the time goes in v3:
time: 154 us; the launch traced here: 153 us
  Pallas kernels  53.7 us (35%)
  waiting for transfers between devices  44.6 us (29%)
  starting transfers between devices  33.5 us (22%)
  other arithmetic  12.3 us (8%)
  local copies, waits for them, and re-layouts  7.79 us (5%)
    ppermute x33, waiting for transfers between devices, exchange(): return lax.ppermute(value, AXES, pairs)  44.6 us
    ppermute x33, starting transfers between devices, exchange(): return lax.ppermute(value, AXES, pairs)  33.5 us
    pallas_call x2, Pallas kernels, expert_up(): pl.pallas_call(functools.partial(up_body, line_rows, piece_counts, with_m...  28.1 us
    pallas_call x4, Pallas kernels, expert_down(): pl.pallas_call(functools.partial(down_body, line_rows, places), grid_spec...  14.3 us
    convert_element_type x8, other arithmetic, per_device(): rounded_sum = lambda terms: add(terms).astype(jnp.bfloat16)  7.95 us
    pallas_call x1, Pallas kernels, attend(): pl.pallas_call(functools.partial(attend_body, group), grid_spec=pltpu.Pre...  6.03 us
    unnamed x48, local copies, waits for them, and re-layouts  5.15 us
    pallas_call x1, Pallas kernels, pick_caches(): pl.pallas_call(pick_body, grid_spec=pltpu.PrefetchScalarGridSpec(num_scal...  3.86 us
  transfers between devices with their start and end apart: 33, of which 14 were waited for; matrix products, arithmetic and copies ran while one was open for 6% of the time, Pallas kernels for 35%

profile of v3, /device:TPU:0, one launch (start us, length us, event | category | flops | bytes accessed | tf_op | source)
XLA Modules:
  0.0 153.1 jit_solution(14098045305601143551)
XLA Ops:
  0.7 1.0 constant_dynamic-slice_fusion.3
  2.2 1.5 meta_columns.1
  4.5 2.7 %collective-permute-start.1 = (bf16[32,1920]{1,0:T(8,128)(2,1)S(1)}, bf16[32,1920]{1,0:T(8,128)(2,1)S(1)}, u32[]{:S(2)}, u32[]{:S(2)}) collective-permute-start(bf16[32,1920]{1,0:T(8,128)(2,1)S(1)} %pad_maximum_fusion.5), channel_id=1, source_target_pairs={{0,8},{1,9},{2,10},{3,11},{4,12},{5,13},{6,14},{7,15},{8,0},{9,1},... | collective-permute-start | bytes 368648 | tf_op jit(solution)/shard_map/ppermute | solution.py:24
  7.2 2.6 %collective-permute-start.2 = (bf16[32,1920]{1,0:T(8,128)(2,1)S(1)}, bf16[32,1920]{1,0:T(8,128)(2,1)S(1)}, u32[]{:S(2)}, u32[]{:S(2)}) collective-permute-start(bf16[32,1920]{1,0:T(8,128)(2,1)S(1)} %pad_maximum_fusion.5), channel_id=1, source_target_pairs={{0,16},{1,17},{2,18},{3,19},{4,20},{5,21},{6,22},{7,23},{8,24},{9,... | collective-permute-start | bytes 368648 | tf_op jit(solution)/shard_map/ppermute | solution.py:24
  12.5 3.9 %pick_caches.1 = bf16[4,576,128]{2,1,0:T(8,128)(2,1)} custom-call(s32[4]{0:T(128)} %select_reduce_fusion.index_ref, bf16[16,576,128]{2,1,0:T(8,128)(2,1)} %bitcast.21), custom_call_target="tpu_custom_call" | custom-call | tf_op jit(solution)/shard_map/pick_caches/pallas_call | solution.py:272
  16.4 3.2 %collective-permute-done.2 = bf16[32,1920]{1,0:T(8,128)(2,1)S(1)} collective-permute-done((bf16[32,1920]{1,0:T(8,128)(2,1)S(1)}, bf16[32,1920]{1,0:T(8,128)(2,1)S(1)}, u32[]{:S(2)}, u32[]{:S(2)}) %collective-permute-start.2) | collective-permute-done | bytes 122912 | tf_op jit(solution)/shard_map/ppermute | solution.py:24
  19.6 1.6 %collective-permute-start.4 = (bf16[128,1920]{1,0:T(8,128)(2,1)S(1)}, bf16[128,1920]{1,0:T(8,128)(2,1)S(1)}, u32[]{:S(2)}, u32[]{:S(2)}) collective-permute-start(bf16[128,1920]{1,0:T(8,128)(2,1)S(1)} %pad_maximum_fusion.2), channel_id=1, source_target_pairs={{0,4},{1,3},{2,6},{3,1},{4,0},{5,7},{6,2},{7,5},{8,12},{9,11},{10,... | collective-permute-start | bytes 1474568 | tf_op jit(solution)/shard_map/ppermute | solution.py:24
  21.2 7.3 %collective-permute-done.4 = bf16[128,1920]{1,0:T(8,128)(2,1)S(1)} collective-permute-done((bf16[128,1920]{1,0:T(8,128)(2,1)S(1)}, bf16[128,1920]{1,0:T(8,128)(2,1)S(1)}, u32[]{:S(2)}, u32[]{:S(2)}) %collective-permute-start.4) | collective-permute-done | bytes 491552 | tf_op jit(solution)/shard_map/ppermute | solution.py:24
  28.6 1.6 %collective-permute-start.5 = (bf16[256,1920]{1,0:T(8,128)(2,1)S(1)}, bf16[256,1920]{1,0:T(8,128)(2,1)S(1)}, u32[]{:S(2)}, u32[]{:S(2)}) collective-permute-start(bf16[256,1920]{1,0:T(8,128)(2,1)S(1)} %constant_dynamic-update-slice_fusion.refs_0_), channel_id=1, source_target_pairs={{0,2},{1,5},{2,0},{3,7},{4,6},{5,1},{6,4},{7,3},{8,10},{9,13},{10,... | collective-permute-start | bytes 2949128 | tf_op jit(solution)/shard_map/ppermute | solution.py:24
  30.1 2.5 %collective-permute-start.7 = (bf16[32,1792]{1,0:T(8,128)(2,1)S(1)}, bf16[32,1792]{1,0:T(8,128)(2,1)S(1)}, u32[]{:S(2)}, u32[]{:S(2)}) collective-permute-start(bf16[32,1792]{1,0:T(8,128)(2,1)S(1)} %get-tuple-element.77), channel_id=1, source_target_pairs={{0,8},{1,9},{2,10},{3,11},{4,12},{5,13},{6,14},{7,15},{8,0},{9,1},... | collective-permute-start | bytes 344072 | tf_op jit(solution)/shard_map/ppermute | solution.py:24
  32.6 1.0 collective-permute-start.8
  33.6 1.5 collective-permute-start.9
  35.1 1.4 collective-permute-done.7
  36.4 8.0 %collective-permute-done.8 = bf16[32,1792]{1,0:T(8,128)(2,1)S(1)} collective-permute-done((bf16[32,1792]{1,0:T(8,128)(2,1)S(1)}, bf16[32,1792]{1,0:T(8,128)(2,1)S(1)}, u32[]{:S(2)}, u32[]{:S(2)}) %collective-permute-start.8) | collective-permute-done | bytes 114720 | tf_op jit(solution)/shard_map/ppermute | solution.py:24
  44.7 2.4 %collective-permute-done.10.refs_3_ = bf16[256,1920]{1,0:T(8,128)(2,1)S(1)} collective-permute-done((bf16[256,1920]{1,0:T(8,128)(2,1)S(1)}, bf16[256,1920]{1,0:T(8,128)(2,1)S(1)}, u32[]{:S(2)}, u32[]{:S(2)}) %collective-permute-start.10) | collective-permute-done | bytes 983072 | tf_op jit(solution)/shard_map/ppermute | solution.py:24
  47.1 1.5 collective-permute-start.11
  48.6 3.3 %collective-permute-start.12 = (bf16[2,576,128]{2,1,0:T(8,128)(2,1)S(1)}, bf16[2,576,128]{2,1,0:T(8,128)(2,1)S(1)}, u32[]{:S(2)}, u32[]{:S(2)}) collective-permute-start(bf16[2,576,128]{2,1,0:T(8,128)(2,1)S(1)} %slice.152), channel_id=1, source_target_pairs={{0,16},{1,17},{2,18},{3,19},{4,20},{5,21},{6,22},{7,23},{8,24},{9,... | collective-permute-start | bytes 884744 | tf_op jit(solution)/shard_map/ppermute | solution.py:24
  51.9 14.4 %expert_up.2 = (bf16[512,1024]{1,0:T(8,128)(2,1)S(1)}, f32[512,128]{1,0:T(8,128)S(1)}, f32[512,128]{1,0:T(8,128)S(1)}) custom-call(s32[2]{0:T(128)S(1)} %pad_add_fusion.spot_ref, bf16[256,1920]{1,0:T(8,128)(2,1)S(1)} %constant_dynamic-update-slice_fusion.refs_0_, bf16[256,1920]{1,0:T(8,128)(2,1)S(1)} %collective-permute-done.5.refs_1_, ...), custom_call_target="tpu_custom_call" | custom-call | flops 7516192768 | bytes 19660800 | tf_op jit(solution)/shard_map/expert_up/pallas_call | solution.py:152
  67.0 3.6 %expert_down.4 = (bf16[256,1792]{1,0:T(8,128)(2,1)S(1)}, bf16[256,1792]{1,0:T(8,128)(2,1)S(1)}) custom-call(s32[2]{0:T(128)S(1)} %pad_add_fusion.spot_ref, bf16[512,1024]{1,0:T(8,128)(2,1)S(1)} %get-tuple-element.94.act_ref, bf16[1024,3584]{1,0:T(8,128)(2,1)S(1)} %bitcast.26, f32[512,128]{1,0:T(8,128)S(1)} %get-tuple-element.95.scale_ref), custom_call_target="tpu_custom_call" | custom-call | flops 68719476736 | bytes 134217728 | tf_op jit(solution)/shard_map/expert_down/pallas_call | solution.py:207
  71.2 3.1 %copy-done.4 = bf16[1,1024,3584]{2,1,0:T(8,128)(2,1)S(1)} copy-done((bf16[1,1024,3584]{2,1,0:T(8,128)(2,1)S(1)}, bf16[1,1024,3584]{2,1,0:T(8,128)(2,1)}, u32[]{:S(2)}) %copy-start.4) | copy-done | bytes 7340056
  74.3 3.6 %expert_down.5 = (bf16[256,1792]{1,0:T(8,128)(2,1)S(1)}, bf16[256,1792]{1,0:T(8,128)(2,1)S(1)}) custom-call(s32[2]{0:T(128)S(1)} %pad_add_fusion.spot_ref, bf16[512,1024]{1,0:T(8,128)(2,1)S(1)} %get-tuple-element.94.act_ref, bf16[1024,3584]{1,0:T(8,128)(2,1)S(1)} %bitcast.27, f32[512,128]{1,0:T(8,128)S(1)} %get-tuple-element.95.scale_ref), custom_call_target="tpu_custom_call" | custom-call | flops 68719476736 | bytes 134217728 | tf_op jit(solution)/shard_map/expert_down/pallas_call | solution.py:207
  77.9 1.9 %collective-permute-done.13.refs_1_ = bf16[256,1792]{1,0:T(8,128)(2,1)S(1)} collective-permute-done((bf16[256,1792]{1,0:T(8,128)(2,1)S(1)}, bf16[256,1792]{1,0:T(8,128)(2,1)S(1)}, u32[]{:S(2)}, u32[]{:S(2)}) %collective-permute-start.13) | collective-permute-done | bytes 917536 | tf_op jit(solution)/shard_map/ppermute | solution.py:24
  79.9 1.1 add_convert_fusion.1
  81.0 1.3 collective-permute-done.17.refs_3_
  83.2 13.6 %expert_up.3.act_ref = bf16[512,1024]{1,0:T(8,128)(2,1)S(1)} custom-call(s32[2]{0:T(128)S(1)} %pad_add_fusion.spot_ref, bf16[256,1792]{1,0:T(8,128)(2,1)S(1)} %pad_maximum_fusion.refs_0_, bf16[256,1792]{1,0:T(8,128)(2,1)S(1)} %collective-permute-done.13.refs_1_, bf16[256,1792]{1,0:T(8,128)(2,1)S(1)} %collective-permute-done.14.refs_2_, ...), custom_call_target="tpu_custom_call" | custom-call | flops 7516192768 | bytes 19398656 | tf_op jit(solution)/shard_map/expert_up/pallas_call | solution.py:152
  96.8 1.5 collective-permute-done.19
  98.5 1.6 %collective-permute-start.20 = (bf16[128,1792]{1,0:T(8,128)(2,1)S(1)}, bf16[128,1792]{1,0:T(8,128)(2,1)S(1)}, u32[]{:S(2)}, u32[]{:S(2)}) collective-permute-start(bf16[128,1792]{1,0:T(8,128)(2,1)S(1)} %add_convert_fusion.3), channel_id=1, source_target_pairs={{0,4},{1,3},{2,6},{3,1},{4,0},{5,7},{6,2},{7,5},{8,12},{9,11},{10,... | collective-permute-start | bytes 1376264 | tf_op jit(solution)/shard_map/ppermute | solution.py:24
  100.0 3.6 %expert_down.6 = (bf16[256,1792]{1,0:T(8,128)(2,1)S(1)}, bf16[256,1792]{1,0:T(8,128)(2,1)S(1)}) custom-call(s32[2]{0:T(128)S(1)} %pad_add_fusion.spot_ref, bf16[512,1024]{1,0:T(8,128)(2,1)S(1)} %expert_up.3.act_ref, bf16[1024,3584]{1,0:T(8,128)(2,1)S(1)} %bitcast.30, f32[512,128]{1,0:T(8,128)S(1)} %get-tuple-element.121.scale_ref), custom_call_target="tpu_custom_call" | custom-call | flops 68719476736 | bytes 134217728 | tf_op jit(solution)/shard_map/expert_down/pallas_call | solution.py:207
  103.7 3.3 %collective-permute-done.20 = bf16[128,1792]{1,0:T(8,128)(2,1)S(1)} collective-permute-done((bf16[128,1792]{1,0:T(8,128)(2,1)S(1)}, bf16[128,1792]{1,0:T(8,128)(2,1)S(1)}, u32[]{:S(2)}, u32[]{:S(2)}) %collective-permute-start.20) | collective-permute-done | bytes 458784 | tf_op jit(solution)/shard_map/ppermute | solution.py:24
  107.0 0.9 add_convert_fusion.9
  108.4 3.6 %expert_down.7 = (bf16[256,1792]{1,0:T(8,128)(2,1)S(1)}, bf16[256,1792]{1,0:T(8,128)(2,1)S(1)}) custom-call(s32[2]{0:T(128)S(1)} %pad_add_fusion.spot_ref, bf16[512,1024]{1,0:T(8,128)(2,1)S(1)} %expert_up.3.act_ref, bf16[1024,3584]{1,0:T(8,128)(2,1)S(1)} %bitcast.31, f32[512,128]{1,0:T(8,128)S(1)} %get-tuple-element.121.scale_ref), custom_call_target="tpu_custom_call" | custom-call | flops 68719476736 | bytes 134217728 | tf_op jit(solution)/shard_map/expert_down/pallas_call | solution.py:207
  112.1 1.1 add_convert_fusion
  114.6 1.5 collective-permute-start.24
  116.1 1.1 collective-permute-start.25
  117.2 1.8 %collective-permute-start.26 = (bf16[32,1792]{1,0:T(8,128)(2,1)S(1)}, bf16[32,1792]{1,0:T(8,128)(2,1)S(1)}, u32[]{:S(2)}, u32[]{:S(2)}) collective-permute-start(bf16[32,1792]{1,0:T(8,128)(2,1)S(1)} %get-tuple-element.132), channel_id=1, source_target_pairs={{0,24},{1,25},{2,26},{3,27},{4,28},{5,29},{6,30},{7,31},{8,16},{9,... | collective-permute-start | bytes 344072 | tf_op jit(solution)/shard_map/ppermute | solution.py:24
  119.0 1.1 pad_maximum_fusion.1.came_ref
  120.2 1.3 copy-done.2
  121.5 6.0 %attend.1 = bf16[16,64,512]{2,1,0:T(8,128)(2,1)} custom-call(s32[16]{0:T(128)S(1)} %copy-done.3, s32[16]{0:T(128)S(1)} %broadcast_clamp_fusion.arrival_ref, s32[16]{0:T(128)S(1)} %gather_fusion, bf16[16,64,576]{2,1,0:T(8,128)(2,1)S(1)} %copy-done.2, bf16[16,576,128]{2,1,0:T(8,128)(2,1)S(1)} %bitcast.22, bf16[4,576,128]{2,1,0:T(8,128)(2,1)S(1)} %pad_maximum_fusion.1.came_ref, ...), custom_call_target="tpu_custom_call" | custom-call | flops 301989888 | bytes 4587520 | tf_op jit(solution)/shard_map/attend/pallas_call | solution.py:315
  127.8 1.2 add_convert_fusion.2
  129.0 1.3 collective-permute-start.28
  130.3 1.2 add_convert_fusion.8
  131.5 6.1 %collective-permute-done.28 = bf16[128,1792]{1,0:T(8,128)(2,1)S(1)} collective-permute-done((bf16[128,1792]{1,0:T(8,128)(2,1)S(1)}, bf16[128,1792]{1,0:T(8,128)(2,1)S(1)}, u32[]{:S(2)}, u32[]{:S(2)}) %collective-permute-start.28) | collective-permute-done | bytes 458784 | tf_op jit(solution)/shard_map/ppermute | solution.py:24
  137.6 1.2 add_convert_fusion.7
  138.8 1.9 %collective-permute-start.29 = (bf16[32,1792]{1,0:T(8,128)(2,1)S(1)}, bf16[32,1792]{1,0:T(8,128)(2,1)S(1)}, u32[]{:S(2)}, u32[]{:S(2)}) collective-permute-start(bf16[32,1792]{1,0:T(8,128)(2,1)S(1)} %get-tuple-element.140), channel_id=1, source_target_pairs={{0,8},{1,9},{2,10},{3,11},{4,12},{5,13},{6,14},{7,15},{8,0},{9,1},... | collective-permute-start | bytes 344072 | tf_op jit(solution)/shard_map/ppermute | solution.py:24
  141.3 1.9 %collective-permute-start.31 = (bf16[32,1792]{1,0:T(8,128)(2,1)S(1)}, bf16[32,1792]{1,0:T(8,128)(2,1)S(1)}, u32[]{:S(2)}, u32[]{:S(2)}) collective-permute-start(bf16[32,1792]{1,0:T(8,128)(2,1)S(1)} %get-tuple-element.141), channel_id=1, source_target_pairs={{0,24},{1,25},{2,26},{3,27},{4,28},{5,29},{6,30},{7,31},{8,16},{9,... | collective-permute-start | bytes 344072 | tf_op jit(solution)/shard_map/ppermute | solution.py:24
  144.0 6.0 %collective-permute-done.30 = bf16[32,1792]{1,0:T(8,128)(2,1)S(1)} collective-permute-done((bf16[32,1792]{1,0:T(8,128)(2,1)S(1)}, bf16[32,1792]{1,0:T(8,128)(2,1)S(1)}, u32[]{:S(2)}, u32[]{:S(2)}) %collective-permute-start.30) | collective-permute-done | bytes 114720 | tf_op jit(solution)/shard_map/ppermute | solution.py:24
  150.1 1.0 add_convert_fusion.4
  151.2 1.2 collective-permute-done.32
  (116 shorter events, 11.2 us)
Async XLA Ops:
  0.6 113.3 %copy-start = (s32[512]{0:T(512)S(1)}, s32[512]{0:T(512)}, u32[]{:S(2)}) copy-start(s32[512]{0:T(512)} %param.18) | copy-start | bytes 6148
  1.6 2.8 %collective-permute-start = (bf16[2,16,1792]{2,1,0:T(8,128)(2,1)S(1)}, bf16[2,16,1792]{2,1,0:T(8,128)(2,1)S(1)}, u32[]{:S(2)}, u32[]{:S(2)}) collective-permute-start(bf16[2,16,1792]{2,1,0:T(8,128)(2,1)S(1)} %get-tuple-element.149), channel_id=1, source_target_pairs={{0,1},{1,0},{2,3},{3,2},{4,5},{5,4},{6,7},{7,6},{8,9},{9,8},{10,11... | collective-permute-start | bytes 344072 | tf_op jit(solution)/shard_map/ppermute | solution.py:24
  4.5 11.8 %collective-permute-start.1 = (bf16[32,1920]{1,0:T(8,128)(2,1)S(1)}, bf16[32,1920]{1,0:T(8,128)(2,1)S(1)}, u32[]{:S(2)}, u32[]{:S(2)}) collective-permute-start(bf16[32,1920]{1,0:T(8,128)(2,1)S(1)} %pad_maximum_fusion.5), channel_id=1, source_target_pairs={{0,8},{1,9},{2,10},{3,11},{4,12},{5,13},{6,14},{7,15},{8,0},{9,1},... | collective-permute-start | bytes 368648 | tf_op jit(solution)/shard_map/ppermute | solution.py:24
  7.2 12.4 %collective-permute-start.2 = (bf16[32,1920]{1,0:T(8,128)(2,1)S(1)}, bf16[32,1920]{1,0:T(8,128)(2,1)S(1)}, u32[]{:S(2)}, u32[]{:S(2)}) collective-permute-start(bf16[32,1920]{1,0:T(8,128)(2,1)S(1)} %pad_maximum_fusion.5), channel_id=1, source_target_pairs={{0,16},{1,17},{2,18},{3,19},{4,20},{5,21},{6,22},{7,23},{8,24},{9,... | collective-permute-start | bytes 368648 | tf_op jit(solution)/shard_map/ppermute | solution.py:24
  9.8 9.8 %collective-permute-start.3 = (bf16[32,1920]{1,0:T(8,128)(2,1)S(1)}, bf16[32,1920]{1,0:T(8,128)(2,1)S(1)}, u32[]{:S(2)}, u32[]{:S(2)}) collective-permute-start(bf16[32,1920]{1,0:T(8,128)(2,1)S(1)} %pad_maximum_fusion.5), channel_id=1, source_target_pairs={{0,24},{1,25},{2,26},{3,27},{4,28},{5,29},{6,30},{7,31},{8,16},{9,... | collective-permute-start | bytes 368648 | tf_op jit(solution)/shard_map/ppermute | solution.py:24
  16.4 32.2 %copy-start.5 = (bf16[4,576,128]{2,1,0:T(8,128)(2,1)S(1)}, bf16[4,576,128]{2,1,0:T(8,128)(2,1)}, u32[]{:S(2)}) copy-start(bf16[4,576,128]{2,1,0:T(8,128)(2,1)} %pick_caches.1) | copy-start | bytes 1769476
  19.6 8.9 %collective-permute-start.4 = (bf16[128,1920]{1,0:T(8,128)(2,1)S(1)}, bf16[128,1920]{1,0:T(8,128)(2,1)S(1)}, u32[]{:S(2)}, u32[]{:S(2)}) collective-permute-start(bf16[128,1920]{1,0:T(8,128)(2,1)S(1)} %pad_maximum_fusion.2), channel_id=1, source_target_pairs={{0,4},{1,3},{2,6},{3,1},{4,0},{5,7},{6,2},{7,5},{8,12},{9,11},{10,... | collective-permute-start | bytes 1474568 | tf_op jit(solution)/shard_map/ppermute | solution.py:24
  28.6 15.9 %collective-permute-start.5 = (bf16[256,1920]{1,0:T(8,128)(2,1)S(1)}, bf16[256,1920]{1,0:T(8,128)(2,1)S(1)}, u32[]{:S(2)}, u32[]{:S(2)}) collective-permute-start(bf16[256,1920]{1,0:T(8,128)(2,1)S(1)} %constant_dynamic-update-slice_fusion.refs_0_), channel_id=1, source_target_pairs={{0,2},{1,5},{2,0},{3,7},{4,6},{5,1},{6,4},{7,3},{8,10},{9,13},{10,... | collective-permute-start | bytes 2949128 | tf_op jit(solution)/shard_map/ppermute | solution.py:24
  30.1 14.3 %collective-permute-start.6 = (bf16[256,1920]{1,0:T(8,128)(2,1)S(1)}, bf16[256,1920]{1,0:T(8,128)(2,1)S(1)}, u32[]{:S(2)}, u32[]{:S(2)}) collective-permute-start(bf16[256,1920]{1,0:T(8,128)(2,1)S(1)} %constant_dynamic-update-slice_fusion.refs_0_), channel_id=1, source_target_pairs={{0,1},{1,0},{2,3},{3,2},{4,5},{5,4},{6,7},{7,6},{8,9},{9,8},{10,11... | collective-permute-start | bytes 2949128 | tf_op jit(solution)/shard_map/ppermute | solution.py:24
  30.1 6.3 %collective-permute-start.7 = (bf16[32,1792]{1,0:T(8,128)(2,1)S(1)}, bf16[32,1792]{1,0:T(8,128)(2,1)S(1)}, u32[]{:S(2)}, u32[]{:S(2)}) collective-permute-start(bf16[32,1792]{1,0:T(8,128)(2,1)S(1)} %get-tuple-element.77), channel_id=1, source_target_pairs={{0,8},{1,9},{2,10},{3,11},{4,12},{5,13},{6,14},{7,15},{8,0},{9,1},... | collective-permute-start | bytes 344072 | tf_op jit(solution)/shard_map/ppermute | solution.py:24
  32.6 11.8 %collective-permute-start.8 = (bf16[32,1792]{1,0:T(8,128)(2,1)S(1)}, bf16[32,1792]{1,0:T(8,128)(2,1)S(1)}, u32[]{:S(2)}, u32[]{:S(2)}) collective-permute-start(bf16[32,1792]{1,0:T(8,128)(2,1)S(1)} %get-tuple-element.77), channel_id=1, source_target_pairs={{0,16},{1,17},{2,18},{3,19},{4,20},{5,21},{6,22},{7,23},{8,24},{9,... | collective-permute-start | bytes 344072 | tf_op jit(solution)/shard_map/ppermute | solution.py:24
  33.6 10.8 %collective-permute-start.9 = (bf16[32,1792]{1,0:T(8,128)(2,1)S(1)}, bf16[32,1792]{1,0:T(8,128)(2,1)S(1)}, u32[]{:S(2)}, u32[]{:S(2)}) collective-permute-start(bf16[32,1792]{1,0:T(8,128)(2,1)S(1)} %get-tuple-element.77), channel_id=1, source_target_pairs={{0,24},{1,25},{2,26},{3,27},{4,28},{5,29},{6,30},{7,31},{8,16},{9,... | collective-permute-start | bytes 344072 | tf_op jit(solution)/shard_map/ppermute | solution.py:24
  44.5 2.6 %collective-permute-start.10 = (bf16[256,1920]{1,0:T(8,128)(2,1)S(1)}, bf16[256,1920]{1,0:T(8,128)(2,1)S(1)}, u32[]{:S(2)}, u32[]{:S(2)}) collective-permute-start(bf16[256,1920]{1,0:T(8,128)(2,1)S(1)} %collective-permute-done.5.refs_1_), channel_id=1, source_target_pairs={{0,1},{1,0},{2,3},{3,2},{4,5},{5,4},{6,7},{7,6},{8,9},{9,8},{10,11... | collective-permute-start | bytes 2949128 | tf_op jit(solution)/shard_map/ppermute | solution.py:24
  47.1 19.2 %collective-permute-start.11 = (bf16[128,1792]{1,0:T(8,128)(2,1)S(1)}, bf16[128,1792]{1,0:T(8,128)(2,1)S(1)}, u32[]{:S(2)}, u32[]{:S(2)}) collective-permute-start(bf16[128,1792]{1,0:T(8,128)(2,1)S(1)} %pad_maximum_fusion.3), channel_id=1, source_target_pairs={{0,4},{1,3},{2,6},{3,1},{4,0},{5,7},{6,2},{7,5},{8,12},{9,11},{10,... | collective-permute-start | bytes 1376264 | tf_op jit(solution)/shard_map/ppermute | solution.py:24
  48.6 18.4 %slice-start = ((s8[7340032]{0:T(1024)(128)(4,1)}), s8[4194304]{0:T(1024)(128)(4,1)S(1)}, s32[]{:S(2)}) async-start(s8[7340032]{0:T(1024)(128)(4,1)} %bitcast.24), calls=%async_computation | async-start | bytes 8388608
  48.6 17.8 %collective-permute-start.12 = (bf16[2,576,128]{2,1,0:T(8,128)(2,1)S(1)}, bf16[2,576,128]{2,1,0:T(8,128)(2,1)S(1)}, u32[]{:S(2)}, u32[]{:S(2)}) collective-permute-start(bf16[2,576,128]{2,1,0:T(8,128)(2,1)S(1)} %slice.152), channel_id=1, source_target_pairs={{0,16},{1,17},{2,18},{3,19},{4,20},{5,21},{6,22},{7,23},{8,24},{9,... | collective-permute-start | bytes 884744 | tf_op jit(solution)/shard_map/ppermute | solution.py:24
  51.9 15.1 %slice-start.1 = ((s8[7340032]{0:T(1024)(128)(4,1)}), s8[3145728]{0:T(1024)(128)(4,1)S(1)}, s32[]{:S(2)}) async-start(s8[7340032]{0:T(1024)(128)(4,1)} %bitcast.24), calls=%async_computation.1 | async-start | bytes 6291456
  66.4 4.2 %copy-start.13 = (bf16[2,576,128]{2,1,0:T(8,128)(2,1)}, bf16[2,576,128]{2,1,0:T(8,128)(2,1)S(1)}, u32[]{:S(2)}) copy-start(bf16[2,576,128]{2,1,0:T(8,128)(2,1)S(1)} %collective-permute-done.12) | copy-start | bytes 884740
  66.4 13.5 %collective-permute-start.13 = (bf16[256,1792]{1,0:T(8,128)(2,1)S(1)}, bf16[256,1792]{1,0:T(8,128)(2,1)S(1)}, u32[]{:S(2)}, u32[]{:S(2)}) collective-permute-start(bf16[256,1792]{1,0:T(8,128)(2,1)S(1)} %pad_maximum_fusion.refs_0_), channel_id=1, source_target_pairs={{0,2},{1,5},{2,0},{3,7},{4,6},{5,1},{6,4},{7,3},{8,10},{9,13},{10,... | collective-permute-start | bytes 2752520 | tf_op jit(solution)/shard_map/ppermute | solution.py:24
  67.0 12.9 %collective-permute-start.14 = (bf16[256,1792]{1,0:T(8,128)(2,1)S(1)}, bf16[256,1792]{1,0:T(8,128)(2,1)S(1)}, u32[]{:S(2)}, u32[]{:S(2)}) collective-permute-start(bf16[256,1792]{1,0:T(8,128)(2,1)S(1)} %pad_maximum_fusion.refs_0_), channel_id=1, source_target_pairs={{0,1},{1,0},{2,3},{3,2},{4,5},{5,4},{6,7},{7,6},{8,9},{9,8},{10,11... | collective-permute-start | bytes 2752520 | tf_op jit(solution)/shard_map/ppermute | solution.py:24
  70.6 7.3 %collective-permute-start.15 = (bf16[256,1792]{1,0:T(8,128)(2,1)S(1)}, bf16[256,1792]{1,0:T(8,128)(2,1)S(1)}, u32[]{:S(2)}, u32[]{:S(2)}) collective-permute-start(bf16[256,1792]{1,0:T(8,128)(2,1)S(1)} %get-tuple-element.96), channel_id=1, source_target_pairs={{0,1},{1,0},{2,3},{3,2},{4,5},{5,4},{6,7},{7,6},{8,9},{9,8},{10,11... | collective-permute-start | bytes 2752520 | tf_op jit(solution)/shard_map/ppermute | solution.py:24
  71.2 6.8 %collective-permute-start.16 = (bf16[256,1792]{1,0:T(8,128)(2,1)S(1)}, bf16[256,1792]{1,0:T(8,128)(2,1)S(1)}, u32[]{:S(2)}, u32[]{:S(2)}) collective-permute-start(bf16[256,1792]{1,0:T(8,128)(2,1)S(1)} %get-tuple-element.97), channel_id=1, source_target_pairs={{0,1},{1,0},{2,3},{3,2},{4,5},{5,4},{6,7},{7,6},{8,9},{9,8},{10,11... | collective-permute-start | bytes 2752520 | tf_op jit(solution)/shard_map/ppermute | solution.py:24
  71.2 3.1 %copy-start.4 = (bf16[1,1024,3584]{2,1,0:T(8,128)(2,1)S(1)}, bf16[1,1024,3584]{2,1,0:T(8,128)(2,1)}, u32[]{:S(2)}) copy-start(bf16[1,1024,3584]{2,1,0:T(8,128)(2,1)} %param.14) | copy-start | bytes 22020100
  79.9 3.1 %copy-start.6 = (bf16[4,576,128]{2,1,0:T(8,128)(2,1)S(1)}, bf16[4,576,128]{2,1,0:T(8,128)(2,1)}, u32[]{:S(2)}) copy-start(bf16[4,576,128]{2,1,0:T(8,128)(2,1)} %pick_caches.1) | copy-start | bytes 1769476
  79.9 2.5 %collective-permute-start.17 = (bf16[256,1792]{1,0:T(8,128)(2,1)S(1)}, bf16[256,1792]{1,0:T(8,128)(2,1)S(1)}, u32[]{:S(2)}, u32[]{:S(2)}) collective-permute-start(bf16[256,1792]{1,0:T(8,128)(2,1)S(1)} %collective-permute-done.13.refs_1_), channel_id=1, source_target_pairs={{0,1},{1,0},{2,3},{3,2},{4,5},{5,4},{6,7},{7,6},{8,9},{9,8},{10,11... | collective-permute-start | bytes 2752520 | tf_op jit(solution)/shard_map/ppermute | solution.py:24
  79.9 20.2 %slice-start.2 = ((s8[7340032]{0:T(1024)(128)(4,1)}), s8[3145728]{0:T(1024)(128)(4,1)S(1)}, s32[]{:S(2)}) async-start(s8[7340032]{0:T(1024)(128)(4,1)} %bitcast.28), calls=%async_computation.2 | async-start | bytes 6291456
  82.4 16.0 %collective-permute-start.18 = (bf16[256,1792]{1,0:T(8,128)(2,1)}, bf16[256,1792]{1,0:T(8,128)(2,1)S(1)}, u32[]{:S(2)}, u32[]{:S(2)}) collective-permute-start(bf16[256,1792]{1,0:T(8,128)(2,1)} %add_convert_fusion.1), channel_id=1, source_target_pairs={{0,2},{1,5},{2,0},{3,7},{4,6},{5,1},{6,4},{7,3},{8,10},{9,13},{10,... | collective-permute-start | bytes 2752520 | tf_op jit(solution)/shard_map/ppermute | solution.py:24
  82.9 24.1 %copy-start.7 = (bf16[128,1792]{1,0:T(8,128)(2,1)}, bf16[128,1792]{1,0:T(8,128)(2,1)S(1)}, u32[]{:S(2)}) copy-start(bf16[128,1792]{1,0:T(8,128)(2,1)S(1)} %slice.153) | copy-start | bytes 1376260
  83.0 24.1 %copy-start.8 = (bf16[128,1792]{1,0:T(8,128)(2,1)}, bf16[128,1792]{1,0:T(8,128)(2,1)S(1)}, u32[]{:S(2)}) copy-start(bf16[128,1792]{1,0:T(8,128)(2,1)S(1)} %slice.154) | copy-start | bytes 1376260
  83.0 17.1 %slice-start.3 = ((s8[7340032]{0:T(1024)(128)(4,1)}), s8[4194304]{0:T(1024)(128)(4,1)S(1)}, s32[]{:S(2)}) async-start(s8[7340032]{0:T(1024)(128)(4,1)} %bitcast.28), calls=%async_computation.3 | async-start | bytes 8388608
  83.0 15.3 %collective-permute-start.19 = (bf16[2,576,128]{2,1,0:T(8,128)(2,1)S(1)}, bf16[2,576,128]{2,1,0:T(8,128)(2,1)S(1)}, u32[]{:S(2)}, u32[]{:S(2)}) collective-permute-start(bf16[2,576,128]{2,1,0:T(8,128)(2,1)S(1)} %slice.155), channel_id=1, source_target_pairs={{0,16},{1,17},{2,18},{3,19},{4,20},{5,21},{6,22},{7,23},{8,24},{9,... | collective-permute-start | bytes 884744 | tf_op jit(solution)/shard_map/ppermute | solution.py:24
  98.3 5.3 %copy-start.14 = (bf16[2,576,128]{2,1,0:T(8,128)(2,1)}, bf16[2,576,128]{2,1,0:T(8,128)(2,1)S(1)}, u32[]{:S(2)}) copy-start(bf16[2,576,128]{2,1,0:T(8,128)(2,1)S(1)} %collective-permute-done.19) | copy-start | bytes 884740
  98.5 8.5 %collective-permute-start.20 = (bf16[128,1792]{1,0:T(8,128)(2,1)S(1)}, bf16[128,1792]{1,0:T(8,128)(2,1)S(1)}, u32[]{:S(2)}, u32[]{:S(2)}) collective-permute-start(bf16[128,1792]{1,0:T(8,128)(2,1)S(1)} %add_convert_fusion.3), channel_id=1, source_target_pairs={{0,4},{1,3},{2,6},{3,1},{4,0},{5,7},{6,2},{7,5},{8,12},{9,11},{10,... | collective-permute-start | bytes 1376264 | tf_op jit(solution)/shard_map/ppermute | solution.py:24
  103.7 8.3 %copy-start.9 = (bf16[128,1792]{1,0:T(8,128)(2,1)}, bf16[128,1792]{1,0:T(8,128)(2,1)S(1)}, u32[]{:S(2)}) copy-start(bf16[128,1792]{1,0:T(8,128)(2,1)S(1)} %slice.156) | copy-start | bytes 1376260
  107.9 4.1 %collective-permute-start.21 = (bf16[256,1792]{1,0:T(8,128)(2,1)S(1)}, bf16[256,1792]{1,0:T(8,128)(2,1)S(1)}, u32[]{:S(2)}, u32[]{:S(2)}) collective-permute-start(bf16[256,1792]{1,0:T(8,128)(2,1)S(1)} %get-tuple-element.118), channel_id=1, source_target_pairs={{0,1},{1,0},{2,3},{3,2},{4,5},{5,4},{6,7},{7,6},{8,9},{9,8},{10,11... | collective-permute-start | bytes 2752520 | tf_op jit(solution)/shard_map/ppermute | solution.py:24
  107.9 4.2 %collective-permute-start.22 = (bf16[256,1792]{1,0:T(8,128)(2,1)S(1)}, bf16[256,1792]{1,0:T(8,128)(2,1)S(1)}, u32[]{:S(2)}, u32[]{:S(2)}) collective-permute-start(bf16[256,1792]{1,0:T(8,128)(2,1)S(1)} %get-tuple-element.119), channel_id=1, source_target_pairs={{0,1},{1,0},{2,3},{3,2},{4,5},{5,4},{6,7},{7,6},{8,9},{9,8},{10,11... | collective-permute-start | bytes 2752520 | tf_op jit(solution)/shard_map/ppermute | solution.py:24
  112.1 8.1 %copy-start.1 = (bf16[16,128,576]{1,2,0:T(8,128)(2,1)S(1)}, bf16[16,128,576]{1,2,0:T(8,128)(2,1)}, u32[]{:S(2)}) copy-start(bf16[16,128,576]{1,2,0:T(8,128)(2,1)} %param.17) | copy-start | bytes 7077892
  113.3 14.5 %collective-permute-start.23 = (bf16[256,1792]{1,0:T(8,128)(2,1)}, bf16[256,1792]{1,0:T(8,128)(2,1)}, u32[]{:S(2)}, u32[]{:S(2)}) collective-permute-start(bf16[256,1792]{1,0:T(8,128)(2,1)} %add_convert_fusion), channel_id=1, source_target_pairs={{0,2},{1,5},{2,0},{3,7},{4,6},{5,1},{6,4},{7,3},{8,10},{9,13},{10,... | collective-permute-start | bytes 2752520 | tf_op jit(solution)/shard_map/ppermute | solution.py:24
  114.6 12.9 %collective-permute-start.24 = (bf16[32,1792]{1,0:T(8,128)(2,1)}, bf16[32,1792]{1,0:T(8,128)(2,1)S(1)}, u32[]{:S(2)}, u32[]{:S(2)}) collective-permute-start(bf16[32,1792]{1,0:T(8,128)(2,1)} %get-tuple-element.130), channel_id=1, source_target_pairs={{0,8},{1,9},{2,10},{3,11},{4,12},{5,13},{6,14},{7,15},{8,0},{9,1},... | collective-permute-start | bytes 344072 | tf_op jit(solution)/shard_map/ppermute | solution.py:24
  116.1 11.7 %collective-permute-start.25 = (bf16[32,1792]{1,0:T(8,128)(2,1)}, bf16[32,1792]{1,0:T(8,128)(2,1)S(1)}, u32[]{:S(2)}, u32[]{:S(2)}) collective-permute-start(bf16[32,1792]{1,0:T(8,128)(2,1)} %get-tuple-element.131), channel_id=1, source_target_pairs={{0,16},{1,17},{2,18},{3,19},{4,20},{5,21},{6,22},{7,23},{8,24},{9,... | collective-permute-start | bytes 344072 | tf_op jit(solution)/shard_map/ppermute | solution.py:24
  117.2 10.6 %collective-permute-start.26 = (bf16[32,1792]{1,0:T(8,128)(2,1)S(1)}, bf16[32,1792]{1,0:T(8,128)(2,1)S(1)}, u32[]{:S(2)}, u32[]{:S(2)}) collective-permute-start(bf16[32,1792]{1,0:T(8,128)(2,1)S(1)} %get-tuple-element.132), channel_id=1, source_target_pairs={{0,24},{1,25},{2,26},{3,27},{4,28},{5,29},{6,30},{7,31},{8,16},{9,... | collective-permute-start | bytes 344072 | tf_op jit(solution)/shard_map/ppermute | solution.py:24
  121.5 6.3 %copy-start.11 = (bf16[256,1792]{1,0:T(8,128)(2,1)S(1)}, bf16[256,1792]{1,0:T(8,128)(2,1)}, u32[]{:S(2)}) copy-start(bf16[256,1792]{1,0:T(8,128)(2,1)} %copy-done.10) | copy-start | bytes 2752516
  129.0 8.5 %collective-permute-start.28 = (bf16[128,1792]{1,0:T(8,128)(2,1)S(1)}, bf16[128,1792]{1,0:T(8,128)(2,1)S(1)}, u32[]{:S(2)}, u32[]{:S(2)}) collective-permute-start(bf16[128,1792]{1,0:T(8,128)(2,1)S(1)} %add_convert_fusion.2), channel_id=1, source_target_pairs={{0,4},{1,3},{2,6},{3,1},{4,0},{5,7},{6,2},{7,5},{8,12},{9,11},{10,... | collective-permute-start | bytes 1376264 | tf_op jit(solution)/shard_map/ppermute | solution.py:24
  138.8 5.2 %collective-permute-start.29 = (bf16[32,1792]{1,0:T(8,128)(2,1)S(1)}, bf16[32,1792]{1,0:T(8,128)(2,1)S(1)}, u32[]{:S(2)}, u32[]{:S(2)}) collective-permute-start(bf16[32,1792]{1,0:T(8,128)(2,1)S(1)} %get-tuple-element.140), channel_id=1, source_target_pairs={{0,8},{1,9},{2,10},{3,11},{4,12},{5,13},{6,14},{7,15},{8,0},{9,1},... | collective-permute-start | bytes 344072 | tf_op jit(solution)/shard_map/ppermute | solution.py:24
  140.7 9.4 %collective-permute-start.30 = (bf16[32,1792]{1,0:T(8,128)(2,1)S(1)}, bf16[32,1792]{1,0:T(8,128)(2,1)S(1)}, u32[]{:S(2)}, u32[]{:S(2)}) collective-permute-start(bf16[32,1792]{1,0:T(8,128)(2,1)S(1)} %get-tuple-element.142), channel_id=1, source_target_pairs={{0,16},{1,17},{2,18},{3,19},{4,20},{5,21},{6,22},{7,23},{8,24},{9,... | collective-permute-start | bytes 344072 | tf_op jit(solution)/shard_map/ppermute | solution.py:24
  141.3 8.7 %collective-permute-start.31 = (bf16[32,1792]{1,0:T(8,128)(2,1)S(1)}, bf16[32,1792]{1,0:T(8,128)(2,1)S(1)}, u32[]{:S(2)}, u32[]{:S(2)}) collective-permute-start(bf16[32,1792]{1,0:T(8,128)(2,1)S(1)} %get-tuple-element.141), channel_id=1, source_target_pairs={{0,24},{1,25},{2,26},{3,27},{4,28},{5,29},{6,30},{7,31},{8,16},{9,... | collective-permute-start | bytes 344072 | tf_op jit(solution)/shard_map/ppermute | solution.py:24
  143.3 7.9 %collective-permute-start.27 = (bf16[16,1792]{1,0:T(8,128)(2,1)S(1)}, bf16[16,1792]{1,0:T(8,128)(2,1)S(1)}, u32[]{:S(2)}, u32[]{:S(2)}) collective-permute-start(bf16[16,1792]{1,0:T(8,128)(2,1)S(1)} %get-tuple-element.151), channel_id=1, source_target_pairs={{0,1},{1,0},{2,3},{3,2},{4,5},{5,4},{6,7},{7,6},{8,9},{9,8},{10,11... | collective-permute-start | bytes 172040 | tf_op jit(solution)/shard_map/ppermute | solution.py:24
  151.1 1.3 collective-permute-start.32
  (7 other events, 10.2 us)

commit v4 on v3

--- a/solution.py
+++ b/solution.py
@@ -179,56 +179,74 @@
     )(spot, *own_pieces, *sib_pieces, expert_in)
 
 
-def down_body(line_rows, places, spot_ref, act_ref, down_ref, scale_ref, low_ref, high_ref):
+def down_body(line_rows, jobs, spot_ref, act_ref, down_ref, scale_ref, *outs):
     del spot_ref
-    answer = jnp.dot(act_ref[...], down_ref[...], preferred_element_type=jnp.float32)
-    scale = scale_ref[...]
-    half_lines = len(places) // 2
-    for column in range(0, answer.shape[1], LANES):
-        value = answer[:, column : column + LANES].astype(jnp.bfloat16).astype(jnp.float32)
-        value = (value * scale).astype(jnp.bfloat16)
-        for index, place in enumerate(places):
-            out = low_ref if index < half_lines else high_ref
-            at = index % half_lines * line_rows
-            out[at : at + line_rows, column : column + LANES] = value[
-                place * line_rows : (place + 1) * line_rows
-            ]
-
-
-def expert_down(spot, act, expert_out, scale, line_rows, side):
+    per_job = pl.num_programs(0) // len(jobs)
+
+    def run(groups, outs):
+        lines = [line for group in groups for line in group]
+        at = lambda ref: jnp.concatenate(
+            [ref[line * line_rows : (line + 1) * line_rows] for line in lines], axis=0
+        )
+        answer = jnp.dot(at(act_ref), down_ref[...], preferred_element_type=jnp.float32)
+        scale = at(scale_ref)
+        for column in range(0, answer.shape[1], LANES):
+            value = answer[:, column : column + LANES].astype(jnp.bfloat16).astype(jnp.float32)
+            value = (value * scale).astype(jnp.bfloat16)
+            first = 0
+            for group, out in zip(groups, outs):
+                rows = len(group) * line_rows
+                out[:, column : column + LANES] = value[first : first + rows]
+                first += rows
+
+    first = 0
+    for index, (_, groups) in enumerate(jobs):
+        mine = outs[first : first + len(groups)]
+        first += len(groups)
+        if len(jobs) == 1:
+            run(groups, mine)
+        else:
+            pl.when(pl.program_id(0) // per_job == index)(functools.partial(run, groups, mine))
+
+
+def expert_down(spot, act, expert_out, scale, line_rows, jobs):
     rows, hidden_units = act.shape
     half = expert_out.shape[1] // 2
-    line_count = rows // line_rows
-    half_bits = (line_count.bit_length() - 1) // 2
-    places = [swap_halves(index, half_bits) if side else index for index in range(line_count)]
     block = 896
     steps = half // block
-    out = pl.BlockSpec((rows // 2, block), lambda i, c: (0, i))
+
+    def weight_at(i, c):
+        side = jobs[0][0]
+        for index, job in enumerate(jobs[1:]):
+            side = jnp.where(i // steps > index, job[0], side)
+        return (0, (c[0] + side - 2 * c[0] * side) * steps + i % steps)
+
+    def out_at(index):
+        return lambda i, c: (0, jnp.minimum(jnp.maximum(i - index * steps, 0), steps - 1))
+
+    out_specs, out_shape = [], []
+    for index, (_, groups) in enumerate(jobs):
+        for group in groups:
+            out_specs.append(pl.BlockSpec((len(group) * line_rows, block), out_at(index)))
+            out_shape.append(jax.ShapeDtypeStruct((len(group) * line_rows, half), jnp.bfloat16))
     return pl.pallas_call(
-        functools.partial(down_body, line_rows, places),
+        functools.partial(down_body, line_rows, jobs),
         grid_spec=pltpu.PrefetchScalarGridSpec(
             num_scalar_prefetch=1,
-            grid=(steps,),
+            grid=(steps * len(jobs),),
             in_specs=[
                 pl.BlockSpec((rows, hidden_units), lambda i, c: (0, 0)),
-                pl.BlockSpec(
-                    (hidden_units, block),
-                    lambda i, c: (0, (1 - c[0] if side else c[0]) * steps + i),
-                ),
+                pl.BlockSpec((hidden_units, block), weight_at),
                 pl.BlockSpec((rows, LANES), lambda i, c: (0, 0)),
             ],
-            out_specs=[out, out],
-        ),
-        out_shape=[jax.ShapeDtypeStruct((rows // 2, half), jnp.bfloat16)] * 2,
+            out_specs=out_specs,
+        ),
+        out_shape=out_shape,
         compiler_params=pltpu.CompilerParams(
             dimension_semantics=("arbitrary",),
             vmem_limit_bytes=4 * (rows + block) * hidden_units + 24 * rows * block + (2 << 20),
         ),
-        cost_estimate=pl.CostEstimate(
-            flops=1 << 36,
-            bytes_accessed=1 << 27,
-            transcendentals=0,
-        ),
+        cost_estimate=pl.CostEstimate(flops=1 << 36, bytes_accessed=1 << 10, transcendentals=0),
         name="expert_down",
     )(spot, act, expert_out, scale)
 
@@ -262,65 +280,99 @@
     )(routes, weights)
 
 
-def pick_body(index_ref, cache_ref, out_ref):
-    out_ref[...] = cache_ref[...]
-
-
-def pick_caches(outgoing, cache):
-    count = outgoing.shape[0]
-    shape = (1,) + cache.shape[1:]
+def pick_body(swapped_ref, cache_ref, first_ref, second_ref, info_ref, sems):
+    row_count = swapped_ref.shape[0]
+    for index in range(MOVE):
+        info_ref[index] = 0
+
+    def find(slot, count):
+        @pl.when((swapped_ref[slot] == 1) & (count < MOVE))
+        def _():
+            info_ref[count] = slot
+
+        return count + swapped_ref[slot]
+
+    count = jnp.minimum(lax.fori_loop(0, row_count, find, jnp.int32(0)), MOVE)
+    last = jnp.maximum(count - 1, 0)
+    last_slot = info_ref[last]
+    copies = []
+    for index in range(MOVE):
+        slot = jnp.where(index < count, info_ref[index], last_slot)
+        info_ref[index] = slot
+        info_ref[MOVE + index] = jnp.where(count > 0, jnp.minimum(index, last), -1)
+        out_ref = first_ref if index < MOVE // 2 else second_ref
+        copies.append(
+            pltpu.make_async_copy(
+                cache_ref.at[slot], out_ref.at[index % (MOVE // 2)], sems.at[index]
+            )
+        )
+        copies[-1].start()
+    for copy in copies:
+        copy.wait()
+
+
+def pick_caches(swapped, cache):
+    part = jax.ShapeDtypeStruct((MOVE // 2,) + cache.shape[1:], cache.dtype)
     return pl.pallas_call(
         pick_body,
         grid_spec=pltpu.PrefetchScalarGridSpec(
             num_scalar_prefetch=1,
-            grid=(count,),
-            in_specs=[pl.BlockSpec(shape, lambda i, index: (index[i], 0, 0))],
-            out_specs=pl.BlockSpec(shape, lambda i, index: (i, 0, 0)),
-        ),
-        out_shape=jax.ShapeDtypeStruct((count,) + cache.shape[1:], cache.dtype),
+            grid=(1,),
+            in_specs=[pl.BlockSpec(memory_space=pl.ANY)],
+            out_specs=[
+                pl.BlockSpec(part.shape, lambda i, _: (0, 0, 0)),
+                pl.BlockSpec(part.shape, lambda i, _: (0, 0, 0)),
+                pl.BlockSpec(memory_space=pltpu.SMEM),
+            ],
+            scratch_shapes=[pltpu.SemaphoreType.DMA((MOVE,))],
+        ),
+        out_shape=[part, part, jax.ShapeDtypeStruct((2 * MOVE,), jnp.int32)],
         name="pick_caches",
-    )(outgoing, cache)
-
-
-def attend_body(group, moved_ref, arrival_ref, length_ref, query_ref, cache_ref, came_ref, fresh_ref, out_ref):
-    first = pl.program_id(0) * group
+    )(swapped, cache)
+
+
+def attend_one(query, cache, fresh, length):
+    fresh = fresh.astype(jnp.float32)
+    scores = jnp.dot(query, cache, preferred_element_type=jnp.float32) * SOFTMAX_SCALE
+    own = jnp.sum(query.astype(jnp.float32) * fresh, axis=1, keepdims=True) * SOFTMAX_SCALE
+    positions = lax.broadcasted_iota(jnp.int32, scores.shape, 1)
+    scores = jnp.where(positions < length, scores, -jnp.inf)
+    top = jnp.maximum(jnp.max(scores, axis=1, keepdims=True), own)
+    weights = jnp.exp(scores - top)
+    own_weight = jnp.exp(own - top)
+    summed = jnp.sum(weights, axis=1, keepdims=True) + own_weight
+    blended = lax.dot_general(
+        weights.astype(jnp.bfloat16),
+        cache[:LATENT],
+        (((1,), (1,)), ((), ())),
+        preferred_element_type=jnp.float32,
+    )
+    own_rounded = own_weight.astype(jnp.bfloat16).astype(jnp.float32)
+    blended = blended + own_rounded * fresh[:, :LATENT]
+    return (blended / summed).astype(jnp.bfloat16)
+
+
+def attend_body(group, spot_ref, length_ref, query_ref, cache_ref, fresh_ref, out_ref):
+    count = group * pl.num_programs(0)
+    first = spot_ref[1] * count + pl.program_id(0) * group
     for slot in range(group):
-        request = first + slot
-        query = query_ref[slot]
-        cache = jnp.where(moved_ref[request] == 1, came_ref[arrival_ref[request]], cache_ref[slot])
-        fresh = fresh_ref[slot].astype(jnp.float32)
-        scores = jnp.dot(query, cache, preferred_element_type=jnp.float32) * SOFTMAX_SCALE
-        own = jnp.sum(query.astype(jnp.float32) * fresh, axis=1, keepdims=True) * SOFTMAX_SCALE
-        positions = lax.broadcasted_iota(jnp.int32, scores.shape, 1)
-        scores = jnp.where(positions < length_ref[request], scores, -jnp.inf)
-        top = jnp.maximum(jnp.max(scores, axis=1, keepdims=True), own)
-        weights = jnp.exp(scores - top)
-        own_weight = jnp.exp(own - top)
-        summed = jnp.sum(weights, axis=1, keepdims=True) + own_weight
-        blended = lax.dot_general(
-            weights.astype(jnp.bfloat16),
-            cache[:LATENT],
-            (((1,), (1,)), ((), ())),
-            preferred_element_type=jnp.float32,
+        out_ref[slot] = attend_one(
+            query_ref[slot], cache_ref[slot], fresh_ref[slot], length_ref[first + slot]
         )
-        own_rounded = own_weight.astype(jnp.bfloat16).astype(jnp.float32)
-        blended = blended + own_rounded * fresh[:, :LATENT]
-        out_ref[slot] = (blended / summed).astype(jnp.bfloat16)
-
-
-def attend(moved, arrival, live, queries, cache, came, fresh):
+
+
+def attend(spot, lengths, queries, cache, fresh):
     count, heads, full = queries.shape
     positions = cache.shape[2]
     group = 4
     return pl.pallas_call(
         functools.partial(attend_body, group),
         grid_spec=pltpu.PrefetchScalarGridSpec(
-            num_scalar_prefetch=3,
+            num_scalar_prefetch=2,
             grid=(count // group,),
             in_specs=[
                 pl.BlockSpec((group, heads, full), lambda i, *_: (i, 0, 0)),
                 pl.BlockSpec((group, full, positions), lambda i, *_: (i, 0, 0)),
-                pl.BlockSpec(came.shape, lambda i, *_: (0, 0, 0)),
                 pl.BlockSpec((group, 1, full), lambda i, *_: (i, 0, 0)),
             ],
             out_specs=pl.BlockSpec((group, heads, LATENT), lambda i, *_: (i, 0, 0)),
@@ -335,7 +387,55 @@
             transcendentals=count * heads * positions,
         ),
         name="attend",
-    )(moved, arrival, live, queries, cache, came, fresh[:, None, :])
+    )(spot, lengths, queries, cache, fresh)
+
+
+def attend_moved_body(
+    row_count, spot_ref, length_ref, info_ref, query_ref, cache_ref, came_a_ref, came_b_ref, fresh_ref, old_ref, out_ref
+):
+    del old_ref
+    index = pl.program_id(0)
+    place = info_ref[MOVE + index]
+    total = length_ref.shape[0]
+    row = spot_ref[1] * row_count + info_ref[index]
+    row = jnp.where(place >= 0, lax.rem(row + total // 2, total), row)
+    came = jnp.where(place < MOVE // 2, came_a_ref[...], came_b_ref[...])[0]
+    cache = jnp.where(place >= 0, came, cache_ref[0])
+    out_ref[0] = attend_one(query_ref[0], cache, fresh_ref[0], length_ref[row])
+
+
+def attend_moved(spot, lengths, info, queries, cache, came_a, came_b, fresh, context):
+    row_count, heads, full = queries.shape
+    positions = cache.shape[2]
+    part = MOVE // 2
+    at_slot = lambda i, spot, lengths, info: (info[i], 0, 0)
+    clip = lambda value: jnp.minimum(jnp.maximum(value, 0), part - 1)
+    one = (1, full, positions)
+    return pl.pallas_call(
+        functools.partial(attend_moved_body, row_count),
+        grid_spec=pltpu.PrefetchScalarGridSpec(
+            num_scalar_prefetch=3,
+            grid=(MOVE,),
+            in_specs=[
+                pl.BlockSpec((1, heads, full), at_slot),
+                pl.BlockSpec(one, at_slot),
+                pl.BlockSpec(one, lambda i, spot, lengths, info: (clip(info[MOVE + i]), 0, 0)),
+                pl.BlockSpec(
+                    one, lambda i, spot, lengths, info: (clip(info[MOVE + i] - part), 0, 0)
+                ),
+                pl.BlockSpec((1, 1, full), at_slot),
+                pl.BlockSpec(memory_space=pl.ANY),
+            ],
+            out_specs=pl.BlockSpec((1, heads, LATENT), at_slot),
+        ),
+        out_shape=jax.ShapeDtypeStruct(context.shape, context.dtype),
+        input_output_aliases={8: 0},
+        compiler_params=pltpu.CompilerParams(
+            dimension_semantics=("arbitrary",), vmem_limit_bytes=48 << 20
+        ),
+        cost_estimate=pl.CostEstimate(flops=1 << 36, bytes_accessed=1 << 10, transcendentals=0),
+        name="attend_moved",
+    )(spot, lengths, info, queries, cache, came_a, came_b, fresh, context)
 
 
 def per_device(
@@ -400,9 +500,13 @@
     up = lambda own, sib, with_meta: expert_up(
         spot, own, sib, expert_in[0], line_rows, with_meta
     )
-    down = lambda act, scale, side: expert_down(
-        spot, act, expert_out[0], scale, line_rows, side
-    )
+    down = lambda act, scale, *jobs: expert_down(
+        spot, act, expert_out[0], scale, line_rows, jobs
+    )
+    half_bits = len(level_masks) // 2
+    my_lines = list(range(line_count))
+    their_lines = [swap_halves(line, half_bits) for line in my_lines]
+    split = line_count // 2
     halves_of = lambda terms: (
         [term[: term.shape[0] // 2] for term in terms],
         [term[term.shape[0] // 2 :] for term in terms],
@@ -431,91 +535,86 @@
     block0 = jnp.concatenate([pair[0], pair_meta], axis=1)
     block0, swapped = window(block0, swapped)
 
-    row_count = swapped.shape[0]
-    is_moved = swapped == 1
-    rank = jnp.cumsum(swapped) - 1
-    arrival = jnp.clip(rank, 0, MOVE - 1)
-    slots = jnp.arange(row_count, dtype=jnp.int32)
-    outgoing = jnp.sum(
-        jnp.where(
-            is_moved[None, :] & (rank[None, :] == jnp.arange(MOVE, dtype=jnp.int32)[:, None]),
-            slots[None, :],
-            0,
-        ),
-        axis=1,
-    )
-    device_rows = me * row_count + slots
-    total_rows = device_count * row_count
-    anchor = jnp.where(is_moved, (device_rows + total_rows // 2) % total_rows, device_rows)
-    live = lengths[anchor]
+    fresh = fresh_key[:, None, :]
     stored = jnp.swapaxes(latent_cache, 1, 2)
 
     came0 = send_line(block0)
-    leaving = pick_caches(outgoing, stored)
-    *came0, leaving = window(*came0, leaving)
+    *leaving, info = pick_caches(swapped, stored)
+    *came0, leave_a, leave_b, info = window(*came0, *leaving, info)
 
     low0 = spread(jnp.concatenate([block0] + came0, axis=0))
-    low0, block1 = window(low0, pair[1])
+    low0, block1, early_queries = window(low0, pair[1], queries)
 
     high0 = exchange(low0, top_masks)
     sib_low0 = exchange(low0, sibling)
     came1 = send_line(block1)
-    high0, sib_low0, *came1 = window(high0, sib_low0, *came1)
+    context = attend(spot, lengths, early_queries, stored, fresh)
+    high0, sib_low0, context, *came1 = window(high0, sib_low0, context, *came1)
 
     line1 = jnp.concatenate([block1] + came1, axis=0)
     sib_high0 = exchange(high0, sibling)
-    low0, high0, sib_low0, sib_high0, line1, leaving = window(
-        low0, high0, sib_low0, sib_high0, line1, leaving
+    low0, high0, sib_low0, sib_high0, line1, leave_a = window(
+        low0, high0, sib_low0, sib_high0, line1, leave_a
     )
 
     low1 = spread(line1)
-    cache_a = exchange(leaving[: MOVE // 2], (far, far))
+    cache_a = exchange(leave_a, (far, far))
     act0, scale0, scale1 = up([low0, high0], [sib_low0, sib_high0], True)
     low1, cache_a, act0, scale0, scale1 = window(low1, cache_a, act0, scale0, scale1)
 
     part = low1.shape[0] // 2
     high1 = exchange(low1, top_masks)
-    they_low0, they_high0 = down(act0, scale0, 1)
+    they_low0, they_high0 = down(act0, scale0, (1, (their_lines[:split], their_lines[split:])))
     sib_low1 = exchange(low1, sibling)
     they_low0, they_high0 = exchange(they_low0, sibling), exchange(they_high0, sibling)
-    my_low0, my_high0 = down(act0, scale0, 0)
+    my_low0, my_high0 = down(act0, scale0, (0, (my_lines[:split], my_lines[split:])))
     high1, sib_low1, they_low0, they_high0, my_low0, my_high0 = window(
         high1, sib_low1, they_low0, they_high0, my_low0, my_high0
     )
 
     send0 = rounded_sum([my_high0, they_high0])
     sib_high1 = exchange(high1, sibling)
-    send0, sib_high1, leaving = window(send0, sib_high1, leaving)
+    send0, sib_high1, leave_b = window(send0, sib_high1, leave_b)
 
     came = exchange(send0, top_masks)
-    cache_b = exchange(leaving[MOVE // 2 :], (far, far))
+    cache_b = exchange(leave_b, (far, far))
     (act1,) = up([low1, high1], [sib_low1, sib_high1], False)
     came, act1, cache_b = window(came, act1, cache_b)
 
-    terms0 = fold([my_low0, they_low0, came])
-    they_low1, they_high1 = down(act1, scale1, 1)
-    *terms0, they_low1, they_high1 = window(*terms0, they_low1, they_high1)
-
+    terms0 = [my_low0, they_low0, came]
+    for masks in reversed(bottom):
+        terms0, high = halves_of(terms0)
+        high, act1 = window(rounded_sum(high), act1)
+        terms0 = terms0 + [exchange(high, masks)]
+
+    they_high1, my_high1 = down(
+        act1, scale1, (1, (their_lines[split:],)), (0, (my_lines[split:],))
+    )
+    they_high1 = exchange(they_high1, sibling)
+    send1 = rounded_sum([my_high1, they_high1])
+    send1, act1 = window(send1, act1)
+    came = exchange(send1, top_masks)
+    they_low1, my_low1 = down(
+        act1, scale1, (1, (their_lines[:split],)), (0, (my_lines[:split],))
+    )
+    they_low1 = exchange(they_low1, sibling)
     kept0, sends0 = finish_sends(terms0)
-    *sends0, act1, scale1 = window(*sends0, act1, scale1)
     last0 = finish_line(sends0)
-    they_low1, they_high1 = exchange(they_low1, sibling), exchange(they_high1, sibling)
-    my_low1, my_high1 = down(act1, scale1, 0)
-    they_low1, they_high1, my_low1, my_high1 = window(
-        they_low1, they_high1, my_low1, my_high1
-    )
-
-    send1 = rounded_sum([my_high1, they_high1])
-    send1, queries = window(send1, queries)
-    came = exchange(send1, top_masks)
-    came_cache = jnp.concatenate([cache_a, cache_b], axis=0)
-    context = attend(swapped, arrival, live, queries, stored, came_cache, fresh_key)
-    came, context, *last0 = window(came, context, *last0)
-
-    terms1 = fold([my_low1, they_low1, came])
+    came, they_low1, my_low1 = window(came, they_low1, my_low1)
+
+    terms1 = [my_low1, they_low1, came]
+    for masks in reversed(bottom):
+        terms1, high = halves_of(terms1)
+        high, queries = window(rounded_sum(high), queries)
+        terms1 = terms1 + [exchange(high, masks)]
+    context = attend_moved(
+        spot, lengths, info, queries, stored, cache_a, cache_b, fresh, context
+    )
+    terms1[-1], context, *last0 = window(terms1[-1], context, *last0)
+    kept1, sends1 = finish_sends(terms1)
+    last1 = finish_line(sends1)
     mixed0 = finish(kept0 + last0)
-    kept1, sends1 = finish_sends(terms1)
-    mixed1 = finish(kept1 + finish_line(sends1))
+    mixed1 = finish(kept1 + last1)
     return (jnp.stack([mixed0, mixed1]), context)
 
 

time: 154 us -> 149 us (0.968)
  Pallas kernels: 53.7 us -> 58.6 us
  local copies, waits for them, and re-layouts: 7.79 us -> 4.28 us
  waiting for transfers between devices: 44.6 us -> 41.7 us
    pallas_call x4 -> x5, Pallas kernels: 14.3 us -> 20.1 us  [the longest x4 17 us: expert_down(): pl.pallas_call(functools.partial(down_body, line_rows, jobs), grid_spec=p...]
    ppermute x33, waiting for transfers between devices: 44.6 us -> 41.7 us  [exchange(): return lax.ppermute(value, AXES, pairs)]
    unnamed x48, local copies, waits for them, and re-layouts: 5.15 us -> 3.17 us
  transfers between devices with their start and end apart: 33 -> 33, of which waited for: 14 -> 17; matrix products, arithmetic and copies ran while one was open for 6% -> 5% of each run, Pallas kernels for 35% -> 36%
where the time goes in v4:
time: 149 us
  Pallas kernels  58.6 us (39%)
  waiting for transfers between devices  41.7 us (28%)
  starting transfers between devices  32 us (21%)
  other arithmetic  10.9 us (7%)
  local copies, waits for them, and re-layouts  4.28 us (3%)
    ppermute x33, waiting for transfers between devices, exchange(): return lax.ppermute(value, AXES, pairs)  41.7 us
    ppermute x33, starting transfers between devices, exchange(): return lax.ppermute(value, AXES, pairs)  32 us
    pallas_call x2, Pallas kernels, expert_up(): pl.pallas_call(functools.partial(up_body, line_rows, piece_counts, with_m...  28 us
    pallas_call x4, Pallas kernels, expert_down(): pl.pallas_call(functools.partial(down_body, line_rows, jobs), grid_spec=p...  17 us
    convert_element_type x8, other arithmetic, per_device(): rounded_sum = lambda terms: add(terms).astype(jnp.bfloat16)  9.12 us
    pallas_call x1, Pallas kernels, attend(): pl.pallas_call(functools.partial(attend_body, group), grid_spec=pltpu.Pre...  5.96 us
    unnamed x48, local copies, waits for them, and re-layouts  3.17 us
    pallas_call x1, Pallas kernels, attend_moved(): pl.pallas_call(functools.partial(attend_moved_body, row_count), grid_spec...  3.13 us
  transfers between devices with their start and end apart: 33, of which 17 were waited for; matrix products, arithmetic and copies ran while one was open for 5% of the time, Pallas kernels for 36%

profile of v4, /device:TPU:0, one launch (start us, length us, event | category | flops | bytes accessed | tf_op | source)
XLA Modules:
  0.0 148.7 jit_solution(4525996879311609131)
XLA Ops:
  0.7 1.0 constant_dynamic-slice_fusion.3
  2.2 1.5 %meta_columns.1 = bf16[16,128]{1,0:T(8,128)(2,1)} custom-call(s32[2,8,16]{2,1,0:T(8,128)} %bitcast.34, f32[2,8,16]{2,1,0:T(8,128)} %bitcast.35), custom_call_target="tpu_custom_call" | custom-call | tf_op jit(solution)/shard_map/meta_columns/pallas_call | solution.py:276
  3.7 0.8 pad_select_fusion
  4.5 4.7 %collective-permute-start.3 = (bf16[32,1920]{1,0:T(8,128)(2,1)S(1)}, bf16[32,1920]{1,0:T(8,128)(2,1)S(1)}, u32[]{:S(2)}, u32[]{:S(2)}) collective-permute-start(bf16[32,1920]{1,0:T(8,128)(2,1)S(1)} %pad_maximum_fusion.4), channel_id=1, source_target_pairs={{0,24},{1,25},{2,26},{3,27},{4,28},{5,29},{6,30},{7,31},{8,16},{9,... | collective-permute-start | bytes 368648 | tf_op jit(solution)/shard_map/ppermute | solution.py:24
  9.8 3.0 %pick_caches.1 = (bf16[2,576,128]{2,1,0:T(8,128)(2,1)}, bf16[2,576,128]{2,1,0:T(8,128)(2,1)}, s32[8]{0:T(128)}) custom-call(s32[16]{0:T(128)} %swapped_ref, bf16[16,576,128]{2,1,0:T(8,128)(2,1)} %bitcast.20), custom_call_target="tpu_custom_call" | custom-call | tf_op jit(solution)/shard_map/pick_caches/pallas_call | solution.py:316
  13.5 6.8 %collective-permute-done.2 = bf16[32,1920]{1,0:T(8,128)(2,1)S(1)} collective-permute-done((bf16[32,1920]{1,0:T(8,128)(2,1)S(1)}, bf16[32,1920]{1,0:T(8,128)(2,1)S(1)}, u32[]{:S(2)}, u32[]{:S(2)}) %collective-permute-start.2) | collective-permute-done | bytes 122912 | tf_op jit(solution)/shard_map/ppermute | solution.py:24
  20.3 1.6 %collective-permute-start.4 = (bf16[128,1920]{1,0:T(8,128)(2,1)S(1)}, bf16[128,1920]{1,0:T(8,128)(2,1)S(1)}, u32[]{:S(2)}, u32[]{:S(2)}) collective-permute-start(bf16[128,1920]{1,0:T(8,128)(2,1)S(1)} %pad_maximum_fusion.1), channel_id=1, source_target_pairs={{0,4},{1,3},{2,6},{3,1},{4,0},{5,7},{6,2},{7,5},{8,12},{9,11},{10,... | collective-permute-start | bytes 1474568 | tf_op jit(solution)/shard_map/ppermute | solution.py:24
  21.9 7.3 %collective-permute-done.4 = bf16[128,1920]{1,0:T(8,128)(2,1)S(1)} collective-permute-done((bf16[128,1920]{1,0:T(8,128)(2,1)S(1)}, bf16[128,1920]{1,0:T(8,128)(2,1)S(1)}, u32[]{:S(2)}, u32[]{:S(2)}) %collective-permute-start.4) | collective-permute-done | bytes 491552 | tf_op jit(solution)/shard_map/ppermute | solution.py:24
  29.3 1.6 %collective-permute-start.5 = (bf16[256,1920]{1,0:T(8,128)(2,1)S(1)}, bf16[256,1920]{1,0:T(8,128)(2,1)S(1)}, u32[]{:S(2)}, u32[]{:S(2)}) collective-permute-start(bf16[256,1920]{1,0:T(8,128)(2,1)S(1)} %constant_dynamic-update-slice_fusion.refs_0_), channel_id=1, source_target_pairs={{0,2},{1,5},{2,0},{3,7},{4,6},{5,1},{6,4},{7,3},{8,10},{9,13},{10,... | collective-permute-start | bytes 2949128 | tf_op jit(solution)/shard_map/ppermute | solution.py:24
  30.9 2.5 %collective-permute-start.9 = (bf16[32,1792]{1,0:T(8,128)(2,1)S(1)}, bf16[32,1792]{1,0:T(8,128)(2,1)S(1)}, u32[]{:S(2)}, u32[]{:S(2)}) collective-permute-start(bf16[32,1792]{1,0:T(8,128)(2,1)S(1)} %get-tuple-element.80), channel_id=1, source_target_pairs={{0,24},{1,25},{2,26},{3,27},{4,28},{5,29},{6,30},{7,31},{8,16},{9,... | collective-permute-start | bytes 344072 | tf_op jit(solution)/shard_map/ppermute | solution.py:24
  33.5 1.9 %collective-permute-start.7 = (bf16[32,1792]{1,0:T(8,128)(2,1)S(1)}, bf16[32,1792]{1,0:T(8,128)(2,1)S(1)}, u32[]{:S(2)}, u32[]{:S(2)}) collective-permute-start(bf16[32,1792]{1,0:T(8,128)(2,1)S(1)} %get-tuple-element.80), channel_id=1, source_target_pairs={{0,8},{1,9},{2,10},{3,11},{4,12},{5,13},{6,14},{7,15},{8,0},{9,1},... | collective-permute-start | bytes 344072 | tf_op jit(solution)/shard_map/ppermute | solution.py:24
  35.5 6.0 %attend.1.old_ref = bf16[16,64,512]{2,1,0:T(8,128)(2,1)} custom-call(s32[2]{0:T(128)S(1)} %pad_add_fusion.spot_ref, s32[512]{0:T(512)S(1)} %copy-done.8, bf16[16,64,576]{2,1,0:T(8,128)(2,1)S(1)} %copy-done.2, bf16[16,576,128]{2,1,0:T(8,128)(2,1)S(1)} %bitcast.21, bf16[16,1,576]{2,1,0:T(2,128)(2,1)S(1)} %copy.13.fresh_ref), custom_call_target="tpu_custom_call" | custom-call | flops 301989888 | bytes 4587520 | tf_op jit(solution)/shard_map/attend/pallas_call | solution.py:368
  41.4 1.6 %collective-permute-done.8 = bf16[32,1792]{1,0:T(8,128)(2,1)S(1)} collective-permute-done((bf16[32,1792]{1,0:T(8,128)(2,1)S(1)}, bf16[32,1792]{1,0:T(8,128)(2,1)S(1)}, u32[]{:S(2)}, u32[]{:S(2)}) %collective-permute-start.8) | collective-permute-done | bytes 114720 | tf_op jit(solution)/shard_map/ppermute | solution.py:24
  43.5 2.5 %collective-permute-done.10.refs_3_ = bf16[256,1920]{1,0:T(8,128)(2,1)S(1)} collective-permute-done((bf16[256,1920]{1,0:T(8,128)(2,1)S(1)}, bf16[256,1920]{1,0:T(8,128)(2,1)S(1)}, u32[]{:S(2)}, u32[]{:S(2)}) %collective-permute-start.10) | collective-permute-done | bytes 983072 | tf_op jit(solution)/shard_map/ppermute | solution.py:24
  46.1 1.5 collective-permute-start.11
  47.5 14.4 %expert_up.2 = (bf16[512,1024]{1,0:T(8,128)(2,1)S(1)}, f32[512,128]{1,0:T(8,128)S(1)}, f32[512,128]{1,0:T(8,128)S(1)}) custom-call(s32[2]{0:T(128)S(1)} %pad_add_fusion.spot_ref, bf16[256,1920]{1,0:T(8,128)(2,1)S(1)} %constant_dynamic-update-slice_fusion.refs_0_, bf16[256,1920]{1,0:T(8,128)(2,1)S(1)} %collective-permute-done.5.refs_1_, ...), custom_call_target="tpu_custom_call" | custom-call | flops 7516192768 | bytes 19660800 | tf_op jit(solution)/shard_map/expert_up/pallas_call | solution.py:152
  62.1 0.7 copy-done.10
  62.9 1.5 %collective-permute-start.13 = (bf16[256,1792]{1,0:T(8,128)(2,1)S(1)}, bf16[256,1792]{1,0:T(8,128)(2,1)S(1)}, u32[]{:S(2)}, u32[]{:S(2)}) collective-permute-start(bf16[256,1792]{1,0:T(8,128)(2,1)S(1)} %pad_maximum_fusion.refs_0_), channel_id=1, source_target_pairs={{0,2},{1,5},{2,0},{3,7},{4,6},{5,1},{6,4},{7,3},{8,10},{9,13},{10,... | collective-permute-start | bytes 2752520 | tf_op jit(solution)/shard_map/ppermute | solution.py:24
  64.4 3.6 %expert_down.4 = (bf16[256,1792]{1,0:T(8,128)(2,1)S(1)}, bf16[256,1792]{1,0:T(8,128)(2,1)S(1)}) custom-call(s32[2]{0:T(128)S(1)} %pad_add_fusion.spot_ref, bf16[512,1024]{1,0:T(8,128)(2,1)S(1)} %get-tuple-element.97.act_ref, bf16[1024,3584]{1,0:T(8,128)(2,1)S(1)} %bitcast.25, f32[512,128]{1,0:T(8,128)S(1)} %get-tuple-element.98.scale_ref), custom_call_target="tpu_custom_call" | custom-call | flops 68719476736 | bytes 1024 | tf_op jit(solution)/shard_map/expert_down/pallas_call | solution.py:232
  68.6 3.6 %expert_down.5 = (bf16[256,1792]{1,0:T(8,128)(2,1)S(1)}, bf16[256,1792]{1,0:T(8,128)(2,1)S(1)}) custom-call(s32[2]{0:T(128)S(1)} %pad_add_fusion.spot_ref, bf16[512,1024]{1,0:T(8,128)(2,1)S(1)} %get-tuple-element.97.act_ref, bf16[1024,3584]{1,0:T(8,128)(2,1)S(1)} %bitcast.26, f32[512,128]{1,0:T(8,128)S(1)} %get-tuple-element.98.scale_ref), custom_call_target="tpu_custom_call" | custom-call | flops 68719476736 | bytes 1024 | tf_op jit(solution)/shard_map/expert_down/pallas_call | solution.py:232
  72.3 4.0 %collective-permute-done.13.refs_1_ = bf16[256,1792]{1,0:T(8,128)(2,1)S(1)} collective-permute-done((bf16[256,1792]{1,0:T(8,128)(2,1)S(1)}, bf16[256,1792]{1,0:T(8,128)(2,1)S(1)}, u32[]{:S(2)}, u32[]{:S(2)}) %collective-permute-start.13) | collective-permute-done | bytes 917536 | tf_op jit(solution)/shard_map/ppermute | solution.py:24
  76.6 2.2 %collective-permute-done.17.refs_3_ = bf16[256,1792]{1,0:T(8,128)(2,1)S(1)} collective-permute-done((bf16[256,1792]{1,0:T(8,128)(2,1)S(1)}, bf16[256,1792]{1,0:T(8,128)(2,1)S(1)}, u32[]{:S(2)}, u32[]{:S(2)}) %collective-permute-start.17) | collective-permute-done | bytes 917536 | tf_op jit(solution)/shard_map/ppermute | solution.py:24
  78.8 1.5 %collective-permute-start.18 = (bf16[256,1792]{1,0:T(8,128)(2,1)S(1)}, bf16[256,1792]{1,0:T(8,128)(2,1)S(1)}, u32[]{:S(2)}, u32[]{:S(2)}) collective-permute-start(bf16[256,1792]{1,0:T(8,128)(2,1)S(1)} %add_convert_fusion.1), channel_id=1, source_target_pairs={{0,2},{1,5},{2,0},{3,7},{4,6},{5,1},{6,4},{7,3},{8,10},{9,13},{10,... | collective-permute-start | bytes 2752520 | tf_op jit(solution)/shard_map/ppermute | solution.py:24
  80.4 2.8 %collective-permute-start.19 = (bf16[2,576,128]{2,1,0:T(8,128)(2,1)S(1)}, bf16[2,576,128]{2,1,0:T(8,128)(2,1)S(1)}, u32[]{:S(2)}, u32[]{:S(2)}) collective-permute-start(bf16[2,576,128]{2,1,0:T(8,128)(2,1)S(1)} %copy-done.18), channel_id=1, source_target_pairs={{0,16},{1,17},{2,18},{3,19},{4,20},{5,21},{6,22},{7,23},{8,24},{9,... | collective-permute-start | bytes 884744 | tf_op jit(solution)/shard_map/ppermute | solution.py:24
  83.2 13.6 %expert_up.3.act_ref = bf16[512,1024]{1,0:T(8,128)(2,1)S(1)} custom-call(s32[2]{0:T(128)S(1)} %pad_add_fusion.spot_ref, bf16[256,1792]{1,0:T(8,128)(2,1)S(1)} %pad_maximum_fusion.refs_0_, bf16[256,1792]{1,0:T(8,128)(2,1)S(1)} %collective-permute-done.13.refs_1_, bf16[256,1792]{1,0:T(8,128)(2,1)S(1)} %collective-permute-done.14.refs_2_, ...), custom_call_target="tpu_custom_call" | custom-call | flops 7516192768 | bytes 19398656 | tf_op jit(solution)/shard_map/expert_up/pallas_call | solution.py:152
  96.9 1.2 add_convert_fusion.3
  98.0 4.5 %expert_down.6 = (bf16[256,1792]{1,0:T(8,128)(2,1)S(1)}, bf16[256,1792]{1,0:T(8,128)(2,1)S(1)}) custom-call(s32[2]{0:T(128)S(1)} %pad_add_fusion.spot_ref, bf16[512,1024]{1,0:T(8,128)(2,1)S(1)} %expert_up.3.act_ref, bf16[1024,3584]{1,0:T(8,128)(2,1)S(1)} %bitcast.27, f32[512,128]{1,0:T(8,128)S(1)} %get-tuple-element.117.scale_ref), custom_call_target="tpu_custom_call" | custom-call | flops 68719476736 | bytes 1024 | tf_op jit(solution)/shard_map/expert_down/pallas_call | solution.py:232
  103.2 1.9 %collective-permute-done.21 = bf16[256,1792]{1,0:T(8,128)(2,1)S(1)} collective-permute-done((bf16[256,1792]{1,0:T(8,128)(2,1)S(1)}, bf16[256,1792]{1,0:T(8,128)(2,1)S(1)}, u32[]{:S(2)}, u32[]{:S(2)}) %collective-permute-start.21) | collective-permute-done | bytes 917536 | tf_op jit(solution)/shard_map/ppermute | solution.py:24
  105.0 1.1 add_convert_fusion
  106.2 1.0 collective-permute-start.22
  107.2 5.3 %expert_down.7 = (bf16[256,1792]{1,0:T(8,128)(2,1)}, bf16[256,1792]{1,0:T(8,128)(2,1)S(1)}) custom-call(s32[2]{0:T(128)S(1)} %pad_add_fusion.spot_ref, bf16[512,1024]{1,0:T(8,128)(2,1)S(1)} %expert_up.3.act_ref, bf16[1024,3584]{1,0:T(8,128)(2,1)S(1)} %bitcast.28, f32[512,128]{1,0:T(8,128)S(1)} %get-tuple-element.117.scale_ref), custom_call_target="tpu_custom_call" | custom-call | flops 68719476736 | bytes 1024 | tf_op jit(solution)/shard_map/expert_down/pallas_call | solution.py:232
  112.5 1.0 copy-done.4
  113.6 1.6 %add_convert_fusion.9 = (bf16[32,1792]{1,0:T(8,128)(2,1)S(1)}, bf16[32,1792]{1,0:T(8,128)(2,1)S(1)}, bf16[32,1792]{1,0:T(8,128)(2,1)S(1)}) fusion(bf16[128,1792]{1,0:T(8,128)(2,1)} %collective-permute-done.20, bf16[256,1792]{1,0:T(8,128)(2,1)} %copy-done.16, bf16[256,1792]{1,0:T(8,128)(2,1)} %copy-done.15, bf16[256,1792]{1,0:T(8,128)(2,1)S(1)} %get-tuple-element.103), kind=kLoop, calls=%fused_computation.14 | loop fusion | flops 1376256 | bytes 1720320 | tf_op jit(solution)/shard_map/convert_element_type | solution.py:499
  115.3 2.6 %collective-permute-start.27 = (bf16[32,1792]{1,0:T(8,128)(2,1)S(1)}, bf16[32,1792]{1,0:T(8,128)(2,1)S(1)}, u32[]{:S(2)}, u32[]{:S(2)}) collective-permute-start(bf16[32,1792]{1,0:T(8,128)(2,1)S(1)} %get-tuple-element.141), channel_id=1, source_target_pairs={{0,24},{1,25},{2,26},{3,27},{4,28},{5,29},{6,30},{7,31},{8,16},{9,... | collective-permute-start | bytes 344072 | tf_op jit(solution)/shard_map/ppermute | solution.py:24
  117.9 1.8 %collective-permute-start.25 = (bf16[32,1792]{1,0:T(8,128)(2,1)S(1)}, bf16[32,1792]{1,0:T(8,128)(2,1)S(1)}, u32[]{:S(2)}, u32[]{:S(2)}) collective-permute-start(bf16[32,1792]{1,0:T(8,128)(2,1)S(1)} %get-tuple-element.143), channel_id=1, source_target_pairs={{0,8},{1,9},{2,10},{3,11},{4,12},{5,13},{6,14},{7,15},{8,0},{9,1},... | collective-permute-start | bytes 344072 | tf_op jit(solution)/shard_map/ppermute | solution.py:24
  119.7 1.0 collective-permute-done.22
  120.7 1.5 add_convert_fusion.2
  122.9 1.3 copy-done.3
  124.2 3.1 %attend_moved.1 = bf16[16,64,512]{2,1,0:T(8,128)(2,1)} custom-call(s32[2]{0:T(128)S(1)} %pad_add_fusion.spot_ref, s32[512]{0:T(512)S(1)} %copy-done.9, s32[8]{0:T(128)S(1)} %copy-done.14, bf16[16,64,576]{2,1,0:T(8,128)(2,1)S(1)} %copy-done.3, bf16[16,576,128]{2,1,0:T(8,128)(2,1)S(1)} %bitcast.22, ...), custom_call_target="tpu_custom_call", output_to_operand_aliasing={{}: (8, {})} | custom-call | flops 68719476736 | bytes 1024 | tf_op jit(solution)/shard_map/attend_moved/pallas_call | solution.py:414
  127.5 3.3 %collective-permute-done.24 = bf16[128,1792]{1,0:T(8,128)(2,1)S(1)} collective-permute-done((bf16[128,1792]{1,0:T(8,128)(2,1)S(1)}, bf16[128,1792]{1,0:T(8,128)(2,1)S(1)}, u32[]{:S(2)}, u32[]{:S(2)}) %collective-permute-start.24) | collective-permute-done | bytes 458784 | tf_op jit(solution)/shard_map/ppermute | solution.py:24
  130.8 1.4 add_convert_fusion.7
  132.3 2.4 %collective-permute-start.31 = (bf16[32,1792]{1,0:T(8,128)(2,1)S(1)}, bf16[32,1792]{1,0:T(8,128)(2,1)S(1)}, u32[]{:S(2)}, u32[]{:S(2)}) collective-permute-start(bf16[32,1792]{1,0:T(8,128)(2,1)S(1)} %get-tuple-element.139), channel_id=1, source_target_pairs={{0,24},{1,25},{2,26},{3,27},{4,28},{5,29},{6,30},{7,31},{8,16},{9,... | collective-permute-start | bytes 344072 | tf_op jit(solution)/shard_map/ppermute | solution.py:24
  134.7 0.9 collective-permute-start.30
  135.7 1.1 add_convert_fusion.8
  137.3 3.9 %collective-permute-done.31 = bf16[32,1792]{1,0:T(8,128)(2,1)S(1)} collective-permute-done((bf16[32,1792]{1,0:T(8,128)(2,1)S(1)}, bf16[32,1792]{1,0:T(8,128)(2,1)S(1)}, u32[]{:S(2)}, u32[]{:S(2)}) %collective-permute-start.31) | collective-permute-done | bytes 114720 | tf_op jit(solution)/shard_map/ppermute | solution.py:24
  141.2 4.3 %collective-permute-done.30 = bf16[32,1792]{1,0:T(8,128)(2,1)S(1)} collective-permute-done((bf16[32,1792]{1,0:T(8,128)(2,1)S(1)}, bf16[32,1792]{1,0:T(8,128)(2,1)S(1)}, u32[]{:S(2)}, u32[]{:S(2)}) %collective-permute-start.30) | collective-permute-done | bytes 114720 | tf_op jit(solution)/shard_map/ppermute | solution.py:24
  145.5 1.1 add_convert_fusion.4
  146.7 1.2 collective-permute-done.32
  (101 shorter events, 6.9 us)
Async XLA Ops:
  1.6 2.8 %collective-permute-start = (bf16[2,16,1792]{2,1,0:T(8,128)(2,1)S(1)}, bf16[2,16,1792]{2,1,0:T(8,128)(2,1)S(1)}, u32[]{:S(2)}, u32[]{:S(2)}) collective-permute-start(bf16[2,16,1792]{2,1,0:T(8,128)(2,1)S(1)} %get-tuple-element.147), channel_id=1, source_target_pairs={{0,1},{1,0},{2,3},{3,2},{4,5},{5,4},{6,7},{7,6},{8,9},{9,8},{10,11... | collective-permute-start | bytes 344072 | tf_op jit(solution)/shard_map/ppermute | solution.py:24
  4.5 9.0 %collective-permute-start.3 = (bf16[32,1920]{1,0:T(8,128)(2,1)S(1)}, bf16[32,1920]{1,0:T(8,128)(2,1)S(1)}, u32[]{:S(2)}, u32[]{:S(2)}) collective-permute-start(bf16[32,1920]{1,0:T(8,128)(2,1)S(1)} %pad_maximum_fusion.4), channel_id=1, source_target_pairs={{0,24},{1,25},{2,26},{3,27},{4,28},{5,29},{6,30},{7,31},{8,16},{9,... | collective-permute-start | bytes 368648 | tf_op jit(solution)/shard_map/ppermute | solution.py:24
  9.2 11.0 %collective-permute-start.2 = (bf16[32,1920]{1,0:T(8,128)(2,1)S(1)}, bf16[32,1920]{1,0:T(8,128)(2,1)S(1)}, u32[]{:S(2)}, u32[]{:S(2)}) collective-permute-start(bf16[32,1920]{1,0:T(8,128)(2,1)S(1)} %pad_maximum_fusion.4), channel_id=1, source_target_pairs={{0,16},{1,17},{2,18},{3,19},{4,20},{5,21},{6,22},{7,23},{8,24},{9,... | collective-permute-start | bytes 368648 | tf_op jit(solution)/shard_map/ppermute | solution.py:24
  9.2 11.0 %collective-permute-start.1 = (bf16[32,1920]{1,0:T(8,128)(2,1)S(1)}, bf16[32,1920]{1,0:T(8,128)(2,1)S(1)}, u32[]{:S(2)}, u32[]{:S(2)}) collective-permute-start(bf16[32,1920]{1,0:T(8,128)(2,1)S(1)} %pad_maximum_fusion.4), channel_id=1, source_target_pairs={{0,8},{1,9},{2,10},{3,11},{4,12},{5,13},{6,14},{7,15},{8,0},{9,1},... | collective-permute-start | bytes 368648 | tf_op jit(solution)/shard_map/ppermute | solution.py:24
  9.8 25.6 %copy-start.2 = (bf16[16,64,576]{2,1,0:T(8,128)(2,1)S(1)}, bf16[16,64,576]{2,1,0:T(8,128)(2,1)}, u32[]{:S(2)}) copy-start(bf16[16,64,576]{2,1,0:T(8,128)(2,1)} %query_ref.1) | copy-start | bytes 3538948
  12.8 18.0 %copy-start.17 = (bf16[16,576]{1,0:T(8,128)(2,1)S(1)}, bf16[16,576]{1,0:T(8,128)(2,1)}, u32[]{:S(2)}) copy-start(bf16[16,576]{1,0:T(8,128)(2,1)} %param.16) | copy-start | bytes 55300
  12.9 22.6 %copy-start = (bf16[16,128,576]{1,2,0:T(8,128)(2,1)S(1)}, bf16[16,128,576]{1,2,0:T(8,128)(2,1)}, u32[]{:S(2)}) copy-start(bf16[16,128,576]{1,2,0:T(8,128)(2,1)} %param.17) | copy-start | bytes 7077892
  12.9 22.6 %copy-start.8 = (s32[512]{0:T(512)S(1)}, s32[512]{0:T(512)}, u32[]{:S(2)}) copy-start(s32[512]{0:T(512)} %length_ref.3) | copy-start | bytes 6148
  20.3 8.9 %collective-permute-start.4 = (bf16[128,1920]{1,0:T(8,128)(2,1)S(1)}, bf16[128,1920]{1,0:T(8,128)(2,1)S(1)}, u32[]{:S(2)}, u32[]{:S(2)}) collective-permute-start(bf16[128,1920]{1,0:T(8,128)(2,1)S(1)} %pad_maximum_fusion.1), channel_id=1, source_target_pairs={{0,4},{1,3},{2,6},{3,1},{4,0},{5,7},{6,2},{7,5},{8,12},{9,11},{10,... | collective-permute-start | bytes 1474568 | tf_op jit(solution)/shard_map/ppermute | solution.py:24
  29.2 13.8 %collective-permute-start.6 = (bf16[256,1920]{1,0:T(8,128)(2,1)S(1)}, bf16[256,1920]{1,0:T(8,128)(2,1)S(1)}, u32[]{:S(2)}, u32[]{:S(2)}) collective-permute-start(bf16[256,1920]{1,0:T(8,128)(2,1)S(1)} %constant_dynamic-update-slice_fusion.refs_0_), channel_id=1, source_target_pairs={{0,1},{1,0},{2,3},{3,2},{4,5},{5,4},{6,7},{7,6},{8,9},{9,8},{10,11... | collective-permute-start | bytes 2949128 | tf_op jit(solution)/shard_map/ppermute | solution.py:24
  29.3 14.2 %collective-permute-start.5 = (bf16[256,1920]{1,0:T(8,128)(2,1)S(1)}, bf16[256,1920]{1,0:T(8,128)(2,1)S(1)}, u32[]{:S(2)}, u32[]{:S(2)}) collective-permute-start(bf16[256,1920]{1,0:T(8,128)(2,1)S(1)} %constant_dynamic-update-slice_fusion.refs_0_), channel_id=1, source_target_pairs={{0,2},{1,5},{2,0},{3,7},{4,6},{5,1},{6,4},{7,3},{8,10},{9,13},{10,... | collective-permute-start | bytes 2949128 | tf_op jit(solution)/shard_map/ppermute | solution.py:24
  30.9 10.5 %copy-start.6 = (bf16[16,1,576]{2,1,0:T(2,128)(2,1)}, bf16[16,1,576]{2,1,0:T(2,128)(2,1)S(1)}, u32[]{:S(2)}) copy-start(bf16[16,1,576]{2,1,0:T(2,128)(2,1)S(1)} %copy.13.fresh_ref) | copy-start | bytes 55300
  30.9 10.5 %collective-permute-start.9 = (bf16[32,1792]{1,0:T(8,128)(2,1)S(1)}, bf16[32,1792]{1,0:T(8,128)(2,1)S(1)}, u32[]{:S(2)}, u32[]{:S(2)}) collective-permute-start(bf16[32,1792]{1,0:T(8,128)(2,1)S(1)} %get-tuple-element.80), channel_id=1, source_target_pairs={{0,24},{1,25},{2,26},{3,27},{4,28},{5,29},{6,30},{7,31},{8,16},{9,... | collective-permute-start | bytes 344072 | tf_op jit(solution)/shard_map/ppermute | solution.py:24
  33.5 9.5 %collective-permute-start.8 = (bf16[32,1792]{1,0:T(8,128)(2,1)S(1)}, bf16[32,1792]{1,0:T(8,128)(2,1)S(1)}, u32[]{:S(2)}, u32[]{:S(2)}) collective-permute-start(bf16[32,1792]{1,0:T(8,128)(2,1)S(1)} %get-tuple-element.80), channel_id=1, source_target_pairs={{0,16},{1,17},{2,18},{3,19},{4,20},{5,21},{6,22},{7,23},{8,24},{9,... | collective-permute-start | bytes 344072 | tf_op jit(solution)/shard_map/ppermute | solution.py:24
  33.5 9.5 %collective-permute-start.7 = (bf16[32,1792]{1,0:T(8,128)(2,1)S(1)}, bf16[32,1792]{1,0:T(8,128)(2,1)S(1)}, u32[]{:S(2)}, u32[]{:S(2)}) collective-permute-start(bf16[32,1792]{1,0:T(8,128)(2,1)S(1)} %get-tuple-element.80), channel_id=1, source_target_pairs={{0,8},{1,9},{2,10},{3,11},{4,12},{5,13},{6,14},{7,15},{8,0},{9,1},... | collective-permute-start | bytes 344072 | tf_op jit(solution)/shard_map/ppermute | solution.py:24
  35.5 10.6 %copy-start.19 = (bf16[2,576,128]{2,1,0:T(8,128)(2,1)S(1)}, bf16[2,576,128]{2,1,0:T(8,128)(2,1)}, u32[]{:S(2)}) copy-start(bf16[2,576,128]{2,1,0:T(8,128)(2,1)} %get-tuple-element.88) | copy-start | bytes 884740
  43.5 2.6 %collective-permute-start.10 = (bf16[256,1920]{1,0:T(8,128)(2,1)S(1)}, bf16[256,1920]{1,0:T(8,128)(2,1)S(1)}, u32[]{:S(2)}, u32[]{:S(2)}) collective-permute-start(bf16[256,1920]{1,0:T(8,128)(2,1)S(1)} %collective-permute-done.5.refs_1_), channel_id=1, source_target_pairs={{0,1},{1,0},{2,3},{3,2},{4,5},{5,4},{6,7},{7,6},{8,9},{9,8},{10,11... | collective-permute-start | bytes 2949128 | tf_op jit(solution)/shard_map/ppermute | solution.py:24
  43.5 21.0 %slice-start = ((s8[7340032]{0:T(1024)(128)(4,1)}), s8[4194304]{0:T(1024)(128)(4,1)S(1)}, s32[]{:S(2)}) async-start(s8[7340032]{0:T(1024)(128)(4,1)} %bitcast.23), calls=%async_computation | async-start | bytes 8388608
  46.0 16.1 %collective-permute-start.12 = (bf16[2,576,128]{2,1,0:T(8,128)(2,1)S(1)}, bf16[2,576,128]{2,1,0:T(8,128)(2,1)S(1)}, u32[]{:S(2)}, u32[]{:S(2)}) collective-permute-start(bf16[2,576,128]{2,1,0:T(8,128)(2,1)S(1)} %copy-done.19), channel_id=1, source_target_pairs={{0,16},{1,17},{2,18},{3,19},{4,20},{5,21},{6,22},{7,23},{8,24},{9,... | collective-permute-start | bytes 884744 | tf_op jit(solution)/shard_map/ppermute | solution.py:24
  46.1 15.9 %collective-permute-start.11 = (bf16[128,1792]{1,0:T(8,128)(2,1)S(1)}, bf16[128,1792]{1,0:T(8,128)(2,1)S(1)}, u32[]{:S(2)}, u32[]{:S(2)}) collective-permute-start(bf16[128,1792]{1,0:T(8,128)(2,1)S(1)} %pad_maximum_fusion.2), channel_id=1, source_target_pairs={{0,4},{1,3},{2,6},{3,1},{4,0},{5,7},{6,2},{7,5},{8,12},{9,11},{10,... | collective-permute-start | bytes 1376264 | tf_op jit(solution)/shard_map/ppermute | solution.py:24
  47.5 16.9 %slice-start.1 = ((s8[7340032]{0:T(1024)(128)(4,1)}), s8[3145728]{0:T(1024)(128)(4,1)S(1)}, s32[]{:S(2)}) async-start(s8[7340032]{0:T(1024)(128)(4,1)} %bitcast.23), calls=%async_computation.1 | async-start | bytes 6291456
  62.9 9.4 %collective-permute-start.14 = (bf16[256,1792]{1,0:T(8,128)(2,1)S(1)}, bf16[256,1792]{1,0:T(8,128)(2,1)S(1)}, u32[]{:S(2)}, u32[]{:S(2)}) collective-permute-start(bf16[256,1792]{1,0:T(8,128)(2,1)S(1)} %pad_maximum_fusion.refs_0_), channel_id=1, source_target_pairs={{0,1},{1,0},{2,3},{3,2},{4,5},{5,4},{6,7},{7,6},{8,9},{9,8},{10,11... | collective-permute-start | bytes 2752520 | tf_op jit(solution)/shard_map/ppermute | solution.py:24
  62.9 13.4 %collective-permute-start.13 = (bf16[256,1792]{1,0:T(8,128)(2,1)S(1)}, bf16[256,1792]{1,0:T(8,128)(2,1)S(1)}, u32[]{:S(2)}, u32[]{:S(2)}) collective-permute-start(bf16[256,1792]{1,0:T(8,128)(2,1)S(1)} %pad_maximum_fusion.refs_0_), channel_id=1, source_target_pairs={{0,2},{1,5},{2,0},{3,7},{4,6},{5,1},{6,4},{7,3},{8,10},{9,13},{10,... | collective-permute-start | bytes 2752520 | tf_op jit(solution)/shard_map/ppermute | solution.py:24
  68.1 8.2 %collective-permute-start.15 = (bf16[256,1792]{1,0:T(8,128)(2,1)S(1)}, bf16[256,1792]{1,0:T(8,128)(2,1)S(1)}, u32[]{:S(2)}, u32[]{:S(2)}) collective-permute-start(bf16[256,1792]{1,0:T(8,128)(2,1)S(1)} %get-tuple-element.99), channel_id=1, source_target_pairs={{0,1},{1,0},{2,3},{3,2},{4,5},{5,4},{6,7},{7,6},{8,9},{9,8},{10,11... | collective-permute-start | bytes 2752520 | tf_op jit(solution)/shard_map/ppermute | solution.py:24
  68.3 8.0 %collective-permute-start.16 = (bf16[256,1792]{1,0:T(8,128)(2,1)S(1)}, bf16[256,1792]{1,0:T(8,128)(2,1)S(1)}, u32[]{:S(2)}, u32[]{:S(2)}) collective-permute-start(bf16[256,1792]{1,0:T(8,128)(2,1)S(1)} %get-tuple-element.100), channel_id=1, source_target_pairs={{0,1},{1,0},{2,3},{3,2},{4,5},{5,4},{6,7},{7,6},{8,9},{9,8},{10,11... | collective-permute-start | bytes 2752520 | tf_op jit(solution)/shard_map/ppermute | solution.py:24
  76.3 20.5 %copy-start.15 = (bf16[256,1792]{1,0:T(8,128)(2,1)}, bf16[256,1792]{1,0:T(8,128)(2,1)S(1)}, u32[]{:S(2)}) copy-start(bf16[256,1792]{1,0:T(8,128)(2,1)S(1)} %collective-permute-done.15) | copy-start | bytes 2752516
  76.3 2.5 %collective-permute-start.17 = (bf16[256,1792]{1,0:T(8,128)(2,1)S(1)}, bf16[256,1792]{1,0:T(8,128)(2,1)S(1)}, u32[]{:S(2)}, u32[]{:S(2)}) collective-permute-start(bf16[256,1792]{1,0:T(8,128)(2,1)S(1)} %collective-permute-done.13.refs_1_), channel_id=1, source_target_pairs={{0,1},{1,0},{2,3},{3,2},{4,5},{5,4},{6,7},{7,6},{8,9},{9,8},{10,11... | collective-permute-start | bytes 2752520 | tf_op jit(solution)/shard_map/ppermute | solution.py:24
  78.8 18.0 %collective-permute-start.18 = (bf16[256,1792]{1,0:T(8,128)(2,1)S(1)}, bf16[256,1792]{1,0:T(8,128)(2,1)S(1)}, u32[]{:S(2)}, u32[]{:S(2)}) collective-permute-start(bf16[256,1792]{1,0:T(8,128)(2,1)S(1)} %add_convert_fusion.1), channel_id=1, source_target_pairs={{0,2},{1,5},{2,0},{3,7},{4,6},{5,1},{6,4},{7,3},{8,10},{9,13},{10,... | collective-permute-start | bytes 2752520 | tf_op jit(solution)/shard_map/ppermute | solution.py:24
  80.4 16.4 %collective-permute-start.19 = (bf16[2,576,128]{2,1,0:T(8,128)(2,1)S(1)}, bf16[2,576,128]{2,1,0:T(8,128)(2,1)S(1)}, u32[]{:S(2)}, u32[]{:S(2)}) collective-permute-start(bf16[2,576,128]{2,1,0:T(8,128)(2,1)S(1)} %copy-done.18), channel_id=1, source_target_pairs={{0,16},{1,17},{2,18},{3,19},{4,20},{5,21},{6,22},{7,23},{8,24},{9,... | collective-permute-start | bytes 884744 | tf_op jit(solution)/shard_map/ppermute | solution.py:24
  102.5 2.5 %collective-permute-start.21 = (bf16[256,1792]{1,0:T(8,128)(2,1)S(1)}, bf16[256,1792]{1,0:T(8,128)(2,1)S(1)}, u32[]{:S(2)}, u32[]{:S(2)}) collective-permute-start(bf16[256,1792]{1,0:T(8,128)(2,1)S(1)} %get-tuple-element.119), channel_id=1, source_target_pairs={{0,1},{1,0},{2,3},{3,2},{4,5},{5,4},{6,7},{7,6},{8,9},{9,8},{10,11... | collective-permute-start | bytes 2752520 | tf_op jit(solution)/shard_map/ppermute | solution.py:24
  102.6 11.0 %collective-permute-start.20 = (bf16[128,1792]{1,0:T(8,128)(2,1)}, bf16[128,1792]{1,0:T(8,128)(2,1)}, u32[]{:S(2)}, u32[]{:S(2)}) collective-permute-start(bf16[128,1792]{1,0:T(8,128)(2,1)} %add_convert_fusion.3), channel_id=1, source_target_pairs={{0,4},{1,3},{2,6},{3,1},{4,0},{5,7},{6,2},{7,5},{8,12},{9,11},{10,... | collective-permute-start | bytes 1376264 | tf_op jit(solution)/shard_map/ppermute | solution.py:24
  106.2 14.5 %collective-permute-start.22 = (bf16[256,1792]{1,0:T(8,128)(2,1)}, bf16[256,1792]{1,0:T(8,128)(2,1)}, u32[]{:S(2)}, u32[]{:S(2)}) collective-permute-start(bf16[256,1792]{1,0:T(8,128)(2,1)} %add_convert_fusion), channel_id=1, source_target_pairs={{0,2},{1,5},{2,0},{3,7},{4,6},{5,1},{6,4},{7,3},{8,10},{9,13},{10,... | collective-permute-start | bytes 2752520 | tf_op jit(solution)/shard_map/ppermute | solution.py:24
  113.5 9.3 %copy-start.1 = (bf16[16,128,576]{1,2,0:T(8,128)(2,1)S(1)}, bf16[16,128,576]{1,2,0:T(8,128)(2,1)}, u32[]{:S(2)}) copy-start(bf16[16,128,576]{1,2,0:T(8,128)(2,1)} %param.17) | copy-start | bytes 7077892
  113.5 9.3 %copy-start.7 = (bf16[16,1,576]{2,1,0:T(2,128)(2,1)S(1)}, bf16[16,1,576]{2,1,0:T(2,128)(2,1)}, u32[]{:S(2)}) copy-start(bf16[16,1,576]{2,1,0:T(2,128)(2,1)} %copy-done.6) | copy-start | bytes 55300
  113.5 9.3 %copy-start.9 = (s32[512]{0:T(512)S(1)}, s32[512]{0:T(512)}, u32[]{:S(2)}) copy-start(s32[512]{0:T(512)} %length_ref.3) | copy-start | bytes 6148
  113.5 9.3 %copy-start.14 = (s32[8]{0:T(128)S(1)}, s32[8]{0:T(128)}, u32[]{:S(2)}) copy-start(s32[8]{0:T(128)} %get-tuple-element.128.info_ref) | copy-start | bytes 100
  113.5 7.2 %collective-permute-start.23 = (bf16[256,1792]{1,0:T(8,128)(2,1)}, bf16[256,1792]{1,0:T(8,128)(2,1)}, u32[]{:S(2)}, u32[]{:S(2)}) collective-permute-start(bf16[256,1792]{1,0:T(8,128)(2,1)} %get-tuple-element.122), channel_id=1, source_target_pairs={{0,1},{1,0},{2,3},{3,2},{4,5},{5,4},{6,7},{7,6},{8,9},{9,8},{10,11... | collective-permute-start | bytes 2752520 | tf_op jit(solution)/shard_map/ppermute | solution.py:24
  113.6 9.2 %copy-start.11 = (bf16[2,576,128]{2,1,0:T(8,128)(2,1)S(1)}, bf16[2,576,128]{2,1,0:T(8,128)(2,1)}, u32[]{:S(2)}) copy-start(bf16[2,576,128]{2,1,0:T(8,128)(2,1)} %copy-done.10) | copy-start | bytes 884740
  113.6 9.2 %copy-start.13 = (bf16[2,576,128]{2,1,0:T(8,128)(2,1)S(1)}, bf16[2,576,128]{2,1,0:T(8,128)(2,1)}, u32[]{:S(2)}) copy-start(bf16[2,576,128]{2,1,0:T(8,128)(2,1)} %copy-done.12) | copy-start | bytes 884740
  115.3 12.0 %collective-permute-start.27 = (bf16[32,1792]{1,0:T(8,128)(2,1)S(1)}, bf16[32,1792]{1,0:T(8,128)(2,1)S(1)}, u32[]{:S(2)}, u32[]{:S(2)}) collective-permute-start(bf16[32,1792]{1,0:T(8,128)(2,1)S(1)} %get-tuple-element.141), channel_id=1, source_target_pairs={{0,24},{1,25},{2,26},{3,27},{4,28},{5,29},{6,30},{7,31},{8,16},{9,... | collective-permute-start | bytes 344072 | tf_op jit(solution)/shard_map/ppermute | solution.py:24
  117.9 9.6 %collective-permute-start.26 = (bf16[32,1792]{1,0:T(8,128)(2,1)S(1)}, bf16[32,1792]{1,0:T(8,128)(2,1)S(1)}, u32[]{:S(2)}, u32[]{:S(2)}) collective-permute-start(bf16[32,1792]{1,0:T(8,128)(2,1)S(1)} %get-tuple-element.142), channel_id=1, source_target_pairs={{0,16},{1,17},{2,18},{3,19},{4,20},{5,21},{6,22},{7,23},{8,24},{9,... | collective-permute-start | bytes 344072 | tf_op jit(solution)/shard_map/ppermute | solution.py:24
  117.9 9.6 %collective-permute-start.25 = (bf16[32,1792]{1,0:T(8,128)(2,1)S(1)}, bf16[32,1792]{1,0:T(8,128)(2,1)S(1)}, u32[]{:S(2)}, u32[]{:S(2)}) collective-permute-start(bf16[32,1792]{1,0:T(8,128)(2,1)S(1)} %get-tuple-element.143), channel_id=1, source_target_pairs={{0,8},{1,9},{2,10},{3,11},{4,12},{5,13},{6,14},{7,15},{8,0},{9,1},... | collective-permute-start | bytes 344072 | tf_op jit(solution)/shard_map/ppermute | solution.py:24
  122.2 8.5 %collective-permute-start.24 = (bf16[128,1792]{1,0:T(8,128)(2,1)S(1)}, bf16[128,1792]{1,0:T(8,128)(2,1)S(1)}, u32[]{:S(2)}, u32[]{:S(2)}) collective-permute-start(bf16[128,1792]{1,0:T(8,128)(2,1)S(1)} %add_convert_fusion.2), channel_id=1, source_target_pairs={{0,4},{1,3},{2,6},{3,1},{4,0},{5,7},{6,2},{7,5},{8,12},{9,11},{10,... | collective-permute-start | bytes 1376264 | tf_op jit(solution)/shard_map/ppermute | solution.py:24
  132.1 5.2 %collective-permute-start.29 = (bf16[32,1792]{1,0:T(8,128)(2,1)S(1)}, bf16[32,1792]{1,0:T(8,128)(2,1)S(1)}, u32[]{:S(2)}, u32[]{:S(2)}) collective-permute-start(bf16[32,1792]{1,0:T(8,128)(2,1)S(1)} %get-tuple-element.138), channel_id=1, source_target_pairs={{0,8},{1,9},{2,10},{3,11},{4,12},{5,13},{6,14},{7,15},{8,0},{9,1},... | collective-permute-start | bytes 344072 | tf_op jit(solution)/shard_map/ppermute | solution.py:24
  132.3 8.9 %collective-permute-start.31 = (bf16[32,1792]{1,0:T(8,128)(2,1)S(1)}, bf16[32,1792]{1,0:T(8,128)(2,1)S(1)}, u32[]{:S(2)}, u32[]{:S(2)}) collective-permute-start(bf16[32,1792]{1,0:T(8,128)(2,1)S(1)} %get-tuple-element.139), channel_id=1, source_target_pairs={{0,24},{1,25},{2,26},{3,27},{4,28},{5,29},{6,30},{7,31},{8,16},{9,... | collective-permute-start | bytes 344072 | tf_op jit(solution)/shard_map/ppermute | solution.py:24
  134.7 10.8 %collective-permute-start.30 = (bf16[32,1792]{1,0:T(8,128)(2,1)S(1)}, bf16[32,1792]{1,0:T(8,128)(2,1)S(1)}, u32[]{:S(2)}, u32[]{:S(2)}) collective-permute-start(bf16[32,1792]{1,0:T(8,128)(2,1)S(1)} %get-tuple-element.140), channel_id=1, source_target_pairs={{0,16},{1,17},{2,18},{3,19},{4,20},{5,21},{6,22},{7,23},{8,24},{9,... | collective-permute-start | bytes 344072 | tf_op jit(solution)/shard_map/ppermute | solution.py:24
  136.8 9.9 %collective-permute-start.28 = (bf16[16,1792]{1,0:T(8,128)(2,1)S(1)}, bf16[16,1792]{1,0:T(8,128)(2,1)S(1)}, u32[]{:S(2)}, u32[]{:S(2)}) collective-permute-start(bf16[16,1792]{1,0:T(8,128)(2,1)S(1)} %get-tuple-element.149), channel_id=1, source_target_pairs={{0,1},{1,0},{2,3},{3,2},{4,5},{5,4},{6,7},{7,6},{8,9},{9,8},{10,11... | collective-permute-start | bytes 172040 | tf_op jit(solution)/shard_map/ppermute | solution.py:24
  146.6 1.3 collective-permute-start.32
  (7 other events, 29.0 us)

commit v5 on v4

--- a/solution.py
+++ b/solution.py
@@ -252,24 +252,21 @@
 
 
 def meta_body(route_ref, weight_ref, meta_ref):
-    token_count, wide = meta_ref.shape
-    total = jnp.zeros((token_count, wide), jnp.float32)
-    lanes = lax.broadcasted_iota(jnp.int32, (META_PICKS, wide), 1)
-    picks = lax.broadcasted_iota(jnp.int32, (META_PICKS, wide), 0)
+    parts = []
     for step in range(STEPS):
         weight = weight_ref[step]
-        top = weight.astype(jnp.bfloat16)
-        rest = weight - top.astype(jnp.float32)
-        middle = rest.astype(jnp.bfloat16)
-        last = (rest - middle.astype(jnp.float32)).astype(jnp.bfloat16)
-        ids = route_ref[step].astype(jnp.float32).astype(jnp.bfloat16)
-        for part, value in enumerate((ids, top, middle, last)):
-            place = (step * 4 + part) * META_PICKS
-            spots = (lanes == picks + place).astype(jnp.bfloat16)
-            total += lax.dot_general(
-                value, spots, (((0,), (0,)), ((), ())), preferred_element_type=jnp.float32
-            )
-    meta_ref[...] = total.astype(jnp.bfloat16)
+        top = weight.astype(jnp.bfloat16).astype(jnp.float32)
+        middle = (weight - top).astype(jnp.bfloat16).astype(jnp.float32)
+        parts += [route_ref[step].astype(jnp.float32), top, middle, weight - top - middle]
+    value = jnp.concatenate(parts, axis=0).astype(jnp.bfloat16)
+    shape = (value.shape[0], meta_ref.shape[1])
+    rows = lax.broadcasted_iota(jnp.int32, shape, 0)
+    lanes = lax.broadcasted_iota(jnp.int32, shape, 1)
+    spots = (rows == lanes).astype(jnp.bfloat16)
+    turned = lax.dot_general(
+        value, spots, (((0,), (0,)), ((), ())), preferred_element_type=jnp.float32
+    )
+    meta_ref[...] = turned.astype(jnp.bfloat16)
 
 
 def meta_columns(routes, weights):
@@ -485,6 +482,8 @@
     far = device_count // 2
     bottom, top_masks = level_masks[:-1], level_masks[-1]
 
+    swap = lambda value: exchange(value, sibling)
+
     def send_line(block):
         return [exchange(block, (mask, mask)) for mask in z_masks[1:]]
 
@@ -557,39 +556,45 @@
         low0, high0, sib_low0, sib_high0, line1, leave_a
     )
 
-    low1 = spread(line1)
+    low1 = [line1]
+    for masks in bottom:
+        low1 = low1 + [exchange(line, masks) for line in low1]
+    first1 = exchange(line1, top_masks)
     cache_a = exchange(leave_a, (far, far))
     act0, scale0, scale1 = up([low0, high0], [sib_low0, sib_high0], True)
-    low1, cache_a, act0, scale0, scale1 = window(low1, cache_a, act0, scale0, scale1)
-
-    part = low1.shape[0] // 2
-    high1 = exchange(low1, top_masks)
+    first1, cache_a, act0, scale0, scale1, *low1 = window(
+        first1, cache_a, act0, scale0, scale1, *low1
+    )
+
+    rest1 = [exchange(line, top_masks) for line in low1[1:]]
+    sib_low1 = [swap(line) for line in low1]
+    sib_first1 = swap(first1)
     they_low0, they_high0 = down(act0, scale0, (1, (their_lines[:split], their_lines[split:])))
-    sib_low1 = exchange(low1, sibling)
-    they_low0, they_high0 = exchange(they_low0, sibling), exchange(they_high0, sibling)
+    they_low0, they_high0 = swap(they_low0), swap(they_high0)
     my_low0, my_high0 = down(act0, scale0, (0, (my_lines[:split], my_lines[split:])))
-    high1, sib_low1, they_low0, they_high0, my_low0, my_high0 = window(
-        high1, sib_low1, they_low0, they_high0, my_low0, my_high0
-    )
+    sib_first1, they_low0, they_high0, my_low0, my_high0, *flat = window(
+        sib_first1, they_low0, they_high0, my_low0, my_high0, *sib_low1, *rest1
+    )
+    sib_low1, rest1 = flat[:split], flat[split:]
 
     send0 = rounded_sum([my_high0, they_high0])
-    sib_high1 = exchange(high1, sibling)
-    send0, sib_high1, leave_b = window(send0, sib_high1, leave_b)
+    sib_rest1 = [swap(line) for line in rest1]
+    send0, leave_b, *sib_rest1 = window(send0, leave_b, *sib_rest1)
 
     came = exchange(send0, top_masks)
     cache_b = exchange(leave_b, (far, far))
-    (act1,) = up([low1, high1], [sib_low1, sib_high1], False)
+    (act1,) = up(low1 + [first1] + rest1, sib_low1 + [sib_first1] + sib_rest1, False)
     came, act1, cache_b = window(came, act1, cache_b)
 
+    they_high1, my_high1 = down(
+        act1, scale1, (1, (their_lines[split:],)), (0, (my_lines[split:],))
+    )
     terms0 = [my_low0, they_low0, came]
     for masks in reversed(bottom):
         terms0, high = halves_of(terms0)
-        high, act1 = window(rounded_sum(high), act1)
+        high, my_high1 = window(rounded_sum(high), my_high1)
         terms0 = terms0 + [exchange(high, masks)]
 
-    they_high1, my_high1 = down(
-        act1, scale1, (1, (their_lines[split:],)), (0, (my_lines[split:],))
-    )
     they_high1 = exchange(they_high1, sibling)
     send1 = rounded_sum([my_high1, they_high1])
     send1, act1 = window(send1, act1)
@@ -600,7 +605,7 @@
     they_low1 = exchange(they_low1, sibling)
     kept0, sends0 = finish_sends(terms0)
     last0 = finish_line(sends0)
-    came, they_low1, my_low1 = window(came, they_low1, my_low1)
+    came, my_low1 = window(came, my_low1)
 
     terms1 = [my_low1, they_low1, came]
     for masks in reversed(bottom):

time: 149 us -> 146 us (0.980)
  waiting for transfers between devices: 41.7 us -> 34.6 us
  starting transfers between devices: 32 us -> 36.4 us
    ppermute x33 -> x36, waiting for transfers between devices: 41.7 us -> 34.6 us  [exchange(): return lax.ppermute(value, AXES, pairs)]
    ppermute x33 -> x36, starting transfers between devices: 32 us -> 36.4 us  [exchange(): return lax.ppermute(value, AXES, pairs)]
  transfers between devices with their start and end apart: 33 -> 36, of which waited for: 17 -> 13; matrix products, arithmetic and copies ran while one was open for 5% -> 6% of each run, Pallas kernels for 36% -> 37%
where the time goes in v5:
time: 146 us
  Pallas kernels  58.6 us (40%)
  starting transfers between devices  36.4 us (25%)
  waiting for transfers between devices  34.6 us (24%)
  other arithmetic  10.6 us (7%)
  local copies, waits for them, and re-layouts  4.28 us (3%)
    ppermute x36, starting transfers between devices, exchange(): return lax.ppermute(value, AXES, pairs)  36.4 us
    ppermute x36, waiting for transfers between devices, exchange(): return lax.ppermute(value, AXES, pairs)  34.6 us
    pallas_call x2, Pallas kernels, expert_up(): pl.pallas_call(functools.partial(up_body, line_rows, piece_counts, with_m...  28.1 us
    pallas_call x4, Pallas kernels, expert_down(): pl.pallas_call(functools.partial(down_body, line_rows, jobs), grid_spec=p...  17 us
    convert_element_type x8, other arithmetic, per_device(): rounded_sum = lambda terms: add(terms).astype(jnp.bfloat16)  8.83 us
    pallas_call x1, Pallas kernels, attend(): pl.pallas_call(functools.partial(attend_body, group), grid_spec=pltpu.Pre...  5.96 us
    unnamed x48, local copies, waits for them, and re-layouts  3.17 us
    pallas_call x1, Pallas kernels, attend_moved(): pl.pallas_call(functools.partial(attend_moved_body, row_count), grid_spec...  3.13 us
  transfers between devices with their start and end apart: 36, of which 13 were waited for; matrix products, arithmetic and copies ran while one was open for 6% of the time, Pallas kernels for 37%

profile of v5, /device:TPU:0, one launch (start us, length us, event | category | flops | bytes accessed | tf_op | source)
XLA Modules:
  0.0 145.5 jit_solution(2981194021421489661)
XLA Ops:
  0.7 1.0 constant_dynamic-slice_fusion.3
  2.2 1.5 %meta_columns.1 = bf16[16,128]{1,0:T(8,128)(2,1)} custom-call(s32[2,8,16]{2,1,0:T(8,128)} %bitcast.34, f32[2,8,16]{2,1,0:T(8,128)} %bitcast.35), custom_call_target="tpu_custom_call" | custom-call | tf_op jit(solution)/shard_map/meta_columns/pallas_call | solution.py:273
  3.6 0.8 pad_select_fusion
  4.5 2.7 %collective-permute-start.1 = (bf16[32,1920]{1,0:T(8,128)(2,1)S(1)}, bf16[32,1920]{1,0:T(8,128)(2,1)S(1)}, u32[]{:S(2)}, u32[]{:S(2)}) collective-permute-start(bf16[32,1920]{1,0:T(8,128)(2,1)S(1)} %pad_maximum_fusion.3), channel_id=1, source_target_pairs={{0,8},{1,9},{2,10},{3,11},{4,12},{5,13},{6,14},{7,15},{8,0},{9,1},... | collective-permute-start | bytes 368648 | tf_op jit(solution)/shard_map/ppermute | solution.py:24
  7.2 2.6 %collective-permute-start.2 = (bf16[32,1920]{1,0:T(8,128)(2,1)S(1)}, bf16[32,1920]{1,0:T(8,128)(2,1)S(1)}, u32[]{:S(2)}, u32[]{:S(2)}) collective-permute-start(bf16[32,1920]{1,0:T(8,128)(2,1)S(1)} %pad_maximum_fusion.3), channel_id=1, source_target_pairs={{0,16},{1,17},{2,18},{3,19},{4,20},{5,21},{6,22},{7,23},{8,24},{9,... | collective-permute-start | bytes 368648 | tf_op jit(solution)/shard_map/ppermute | solution.py:24
  9.7 3.0 %pick_caches.1 = (bf16[2,576,128]{2,1,0:T(8,128)(2,1)}, bf16[2,576,128]{2,1,0:T(8,128)(2,1)}, s32[8]{0:T(128)}) custom-call(s32[16]{0:T(128)} %swapped_ref, bf16[16,576,128]{2,1,0:T(8,128)(2,1)} %bitcast.20), custom_call_target="tpu_custom_call" | custom-call | tf_op jit(solution)/shard_map/pick_caches/pallas_call | solution.py:313
  13.1 6.4 %collective-permute-done.2 = bf16[32,1920]{1,0:T(8,128)(2,1)S(1)} collective-permute-done((bf16[32,1920]{1,0:T(8,128)(2,1)S(1)}, bf16[32,1920]{1,0:T(8,128)(2,1)S(1)}, u32[]{:S(2)}, u32[]{:S(2)}) %collective-permute-start.2) | collective-permute-done | bytes 122912 | tf_op jit(solution)/shard_map/ppermute | solution.py:24
  19.6 1.6 %collective-permute-start.4 = (bf16[128,1920]{1,0:T(8,128)(2,1)S(1)}, bf16[128,1920]{1,0:T(8,128)(2,1)S(1)}, u32[]{:S(2)}, u32[]{:S(2)}) collective-permute-start(bf16[128,1920]{1,0:T(8,128)(2,1)S(1)} %pad_maximum_fusion), channel_id=1, source_target_pairs={{0,4},{1,3},{2,6},{3,1},{4,0},{5,7},{6,2},{7,5},{8,12},{9,11},{10,... | collective-permute-start | bytes 1474568 | tf_op jit(solution)/shard_map/ppermute | solution.py:24
  21.2 7.3 %collective-permute-done.4 = bf16[128,1920]{1,0:T(8,128)(2,1)S(1)} collective-permute-done((bf16[128,1920]{1,0:T(8,128)(2,1)S(1)}, bf16[128,1920]{1,0:T(8,128)(2,1)S(1)}, u32[]{:S(2)}, u32[]{:S(2)}) %collective-permute-start.4) | collective-permute-done | bytes 491552 | tf_op jit(solution)/shard_map/ppermute | solution.py:24
  28.5 1.6 %collective-permute-start.5 = (bf16[256,1920]{1,0:T(8,128)(2,1)S(1)}, bf16[256,1920]{1,0:T(8,128)(2,1)S(1)}, u32[]{:S(2)}, u32[]{:S(2)}) collective-permute-start(bf16[256,1920]{1,0:T(8,128)(2,1)S(1)} %constant_dynamic-update-slice_fusion.refs_0_), channel_id=1, source_target_pairs={{0,2},{1,5},{2,0},{3,7},{4,6},{5,1},{6,4},{7,3},{8,10},{9,13},{10,... | collective-permute-start | bytes 2949128 | tf_op jit(solution)/shard_map/ppermute | solution.py:24
  30.1 2.5 %collective-permute-start.7 = (bf16[32,1792]{1,0:T(8,128)(2,1)S(1)}, bf16[32,1792]{1,0:T(8,128)(2,1)S(1)}, u32[]{:S(2)}, u32[]{:S(2)}) collective-permute-start(bf16[32,1792]{1,0:T(8,128)(2,1)S(1)} %get-tuple-element.83), channel_id=1, source_target_pairs={{0,8},{1,9},{2,10},{3,11},{4,12},{5,13},{6,14},{7,15},{8,0},{9,1},... | collective-permute-start | bytes 344072 | tf_op jit(solution)/shard_map/ppermute | solution.py:24
  32.7 1.1 collective-permute-start.8
  33.8 1.4 collective-permute-start.9
  35.3 6.0 %attend.1.old_ref = bf16[16,64,512]{2,1,0:T(8,128)(2,1)} custom-call(s32[2]{0:T(128)S(1)} %pad_add_fusion.spot_ref, s32[512]{0:T(512)S(1)} %copy-done.8, bf16[16,64,576]{2,1,0:T(8,128)(2,1)S(1)} %copy-done.2, bf16[16,576,128]{2,1,0:T(8,128)(2,1)S(1)} %bitcast.21, bf16[16,1,576]{2,1,0:T(2,128)(2,1)S(1)} %copy.13.fresh_ref), custom_call_target="tpu_custom_call" | custom-call | flops 301989888 | bytes 4587520 | tf_op jit(solution)/shard_map/attend/pallas_call | solution.py:365
  41.2 3.3 %collective-permute-done.8 = bf16[32,1792]{1,0:T(8,128)(2,1)S(1)} collective-permute-done((bf16[32,1792]{1,0:T(8,128)(2,1)S(1)}, bf16[32,1792]{1,0:T(8,128)(2,1)S(1)}, u32[]{:S(2)}, u32[]{:S(2)}) %collective-permute-start.8) | collective-permute-done | bytes 114720 | tf_op jit(solution)/shard_map/ppermute | solution.py:24
  44.7 2.5 %collective-permute-done.10.refs_3_ = bf16[256,1920]{1,0:T(8,128)(2,1)S(1)} collective-permute-done((bf16[256,1920]{1,0:T(8,128)(2,1)S(1)}, bf16[256,1920]{1,0:T(8,128)(2,1)S(1)}, u32[]{:S(2)}, u32[]{:S(2)}) %collective-permute-start.10) | collective-permute-done | bytes 983072 | tf_op jit(solution)/shard_map/ppermute | solution.py:24
  47.7 1.5 %collective-permute-start.13 = (bf16[128,1792]{1,0:T(8,128)(2,1)S(1)}, bf16[128,1792]{1,0:T(8,128)(2,1)S(1)}, u32[]{:S(2)}, u32[]{:S(2)}) collective-permute-start(bf16[128,1792]{1,0:T(8,128)(2,1)S(1)} %pad_maximum_fusion.1.refs_0_), channel_id=1, source_target_pairs={{0,4},{1,3},{2,6},{3,1},{4,0},{5,7},{6,2},{7,5},{8,12},{9,11},{10,... | collective-permute-start | bytes 1376264 | tf_op jit(solution)/shard_map/ppermute | solution.py:24
  49.2 3.2 %collective-permute-start.12 = (bf16[2,576,128]{2,1,0:T(8,128)(2,1)S(1)}, bf16[2,576,128]{2,1,0:T(8,128)(2,1)S(1)}, u32[]{:S(2)}, u32[]{:S(2)}) collective-permute-start(bf16[2,576,128]{2,1,0:T(8,128)(2,1)S(1)} %copy-done.19), channel_id=1, source_target_pairs={{0,16},{1,17},{2,18},{3,19},{4,20},{5,21},{6,22},{7,23},{8,24},{9,... | collective-permute-start | bytes 884744 | tf_op jit(solution)/shard_map/ppermute | solution.py:24
  52.4 14.4 %expert_up.2 = (bf16[512,1024]{1,0:T(8,128)(2,1)S(1)}, f32[512,128]{1,0:T(8,128)S(1)}, f32[512,128]{1,0:T(8,128)S(1)}) custom-call(s32[2]{0:T(128)S(1)} %pad_add_fusion.spot_ref, bf16[256,1920]{1,0:T(8,128)(2,1)S(1)} %constant_dynamic-update-slice_fusion.refs_0_, bf16[256,1920]{1,0:T(8,128)(2,1)S(1)} %collective-permute-done.5.refs_1_, ...), custom_call_target="tpu_custom_call" | custom-call | flops 7516192768 | bytes 19660800 | tf_op jit(solution)/shard_map/expert_up/pallas_call | solution.py:152
  67.6 1.6 %collective-permute-start.19 = (bf16[128,1792]{1,0:T(8,128)(2,1)S(1)}, bf16[128,1792]{1,0:T(8,128)(2,1)S(1)}, u32[]{:S(2)}, u32[]{:S(2)}) collective-permute-start(bf16[128,1792]{1,0:T(8,128)(2,1)S(1)} %collective-permute-done.13.refs_1_), channel_id=1, source_target_pairs={{0,2},{1,5},{2,0},{3,7},{4,6},{5,1},{6,4},{7,3},{8,10},{9,13},{10,... | collective-permute-start | bytes 1376264 | tf_op jit(solution)/shard_map/ppermute | solution.py:24
  69.2 3.6 %expert_down.4 = (bf16[256,1792]{1,0:T(8,128)(2,1)S(1)}, bf16[256,1792]{1,0:T(8,128)(2,1)S(1)}) custom-call(s32[2]{0:T(128)S(1)} %pad_add_fusion.spot_ref, bf16[512,1024]{1,0:T(8,128)(2,1)S(1)} %get-tuple-element.100.act_ref, bf16[1024,3584]{1,0:T(8,128)(2,1)S(1)} %bitcast.25, f32[512,128]{1,0:T(8,128)S(1)} %get-tuple-element.101.scale_ref), custom_call_target="tpu_custom_call" | custom-call | flops 68719476736 | bytes 1024 | tf_op jit(solution)/shard_map/expert_down/pallas_call | solution.py:232
  73.9 3.6 %expert_down.5 = (bf16[256,1792]{1,0:T(8,128)(2,1)S(1)}, bf16[256,1792]{1,0:T(8,128)(2,1)S(1)}) custom-call(s32[2]{0:T(128)S(1)} %pad_add_fusion.spot_ref, bf16[512,1024]{1,0:T(8,128)(2,1)S(1)} %get-tuple-element.100.act_ref, bf16[1024,3584]{1,0:T(8,128)(2,1)S(1)} %bitcast.26, f32[512,128]{1,0:T(8,128)S(1)} %get-tuple-element.101.scale_ref), custom_call_target="tpu_custom_call" | custom-call | flops 68719476736 | bytes 1024 | tf_op jit(solution)/shard_map/expert_down/pallas_call | solution.py:232
  78.2 1.3 collective-permute-done.20.refs_7_
  80.0 13.6 %expert_up.3.act_ref = bf16[512,1024]{1,0:T(8,128)(2,1)S(1)} custom-call(s32[2]{0:T(128)S(1)} %pad_add_fusion.spot_ref, bf16[128,1792]{1,0:T(8,128)(2,1)S(1)} %pad_maximum_fusion.1.refs_0_, bf16[128,1792]{1,0:T(8,128)(2,1)S(1)} %collective-permute-done.13.refs_1_, bf16[128,1792]{1,0:T(8,128)(2,1)S(1)} %collective-permute-done.11.refs_2_, ...), custom_call_target="tpu_custom_call" | custom-call | flops 7516192768 | bytes 19398656 | tf_op jit(solution)/shard_map/expert_up/pallas_call | solution.py:152
  93.7 1.7 %collective-permute-done.22.came_b_ref = bf16[2,576,128]{2,1,0:T(8,128)(2,1)S(1)} collective-permute-done((bf16[2,576,128]{2,1,0:T(8,128)(2,1)S(1)}, bf16[2,576,128]{2,1,0:T(8,128)(2,1)S(1)}, u32[]{:S(2)}, u32[]{:S(2)}) %collective-permute-start.22) | collective-permute-done | bytes 294944 | tf_op jit(solution)/shard_map/ppermute | solution.py:24
  95.3 4.5 %expert_down.6 = (bf16[256,1792]{1,0:T(8,128)(2,1)S(1)}, bf16[256,1792]{1,0:T(8,128)(2,1)S(1)}) custom-call(s32[2]{0:T(128)S(1)} %pad_add_fusion.spot_ref, bf16[512,1024]{1,0:T(8,128)(2,1)S(1)} %expert_up.3.act_ref, bf16[1024,3584]{1,0:T(8,128)(2,1)S(1)} %bitcast.27, f32[512,128]{1,0:T(8,128)S(1)} %get-tuple-element.122.scale_ref), custom_call_target="tpu_custom_call" | custom-call | flops 68719476736 | bytes 1024 | tf_op jit(solution)/shard_map/expert_down/pallas_call | solution.py:232
  99.9 1.0 add_convert_fusion.3
  100.9 1.5 %collective-permute-start.23 = (bf16[128,1792]{1,0:T(8,128)(2,1)}, bf16[128,1792]{1,0:T(8,128)(2,1)}, u32[]{:S(2)}, u32[]{:S(2)}) collective-permute-start(bf16[128,1792]{1,0:T(8,128)(2,1)} %add_convert_fusion.3), channel_id=1, source_target_pairs={{0,4},{1,3},{2,6},{3,1},{4,0},{5,7},{6,2},{7,5},{8,12},{9,11},{10,... | collective-permute-start | bytes 1376264 | tf_op jit(solution)/shard_map/ppermute | solution.py:24
  102.5 1.1 add_convert_fusion
  103.6 1.3 collective-permute-start.25
  104.9 5.3 %expert_down.7 = (bf16[256,1792]{1,0:T(8,128)(2,1)}, bf16[256,1792]{1,0:T(8,128)(2,1)S(1)}) custom-call(s32[2]{0:T(128)S(1)} %pad_add_fusion.spot_ref, bf16[512,1024]{1,0:T(8,128)(2,1)S(1)} %expert_up.3.act_ref, bf16[1024,3584]{1,0:T(8,128)(2,1)S(1)} %bitcast.28, f32[512,128]{1,0:T(8,128)S(1)} %get-tuple-element.122.scale_ref), custom_call_target="tpu_custom_call" | custom-call | flops 68719476736 | bytes 1024 | tf_op jit(solution)/shard_map/expert_down/pallas_call | solution.py:232
  110.2 1.0 copy-done.4
  111.3 1.4 collective-permute-done.23
  112.8 1.5 %add_convert_fusion.9 = (bf16[32,1792]{1,0:T(8,128)(2,1)S(1)}, bf16[32,1792]{1,0:T(8,128)(2,1)S(1)}, bf16[32,1792]{1,0:T(8,128)(2,1)S(1)}) fusion(bf16[128,1792]{1,0:T(8,128)(2,1)} %collective-permute-done.23, bf16[256,1792]{1,0:T(8,128)(2,1)} %copy-done.16, bf16[256,1792]{1,0:T(8,128)(2,1)} %copy-done.15, bf16[256,1792]{1,0:T(8,128)(2,1)S(1)} %get-tuple-element.108), kind=kLoop, calls=%fused_computation.13 | loop fusion | flops 1376256 | bytes 1720320 | tf_op jit(solution)/shard_map/convert_element_type | solution.py:498
  114.5 2.3 %collective-permute-start.29 = (bf16[32,1792]{1,0:T(8,128)(2,1)S(1)}, bf16[32,1792]{1,0:T(8,128)(2,1)S(1)}, u32[]{:S(2)}, u32[]{:S(2)}) collective-permute-start(bf16[32,1792]{1,0:T(8,128)(2,1)S(1)} %get-tuple-element.148), channel_id=1, source_target_pairs={{0,16},{1,17},{2,18},{3,19},{4,20},{5,21},{6,22},{7,23},{8,24},{9,... | collective-permute-start | bytes 344072 | tf_op jit(solution)/shard_map/ppermute | solution.py:24
  116.9 1.9 %collective-permute-start.30 = (bf16[32,1792]{1,0:T(8,128)(2,1)S(1)}, bf16[32,1792]{1,0:T(8,128)(2,1)S(1)}, u32[]{:S(2)}, u32[]{:S(2)}) collective-permute-start(bf16[32,1792]{1,0:T(8,128)(2,1)S(1)} %get-tuple-element.147), channel_id=1, source_target_pairs={{0,24},{1,25},{2,26},{3,27},{4,28},{5,29},{6,30},{7,31},{8,16},{9,... | collective-permute-start | bytes 344072 | tf_op jit(solution)/shard_map/ppermute | solution.py:24
  119.1 1.5 %add_convert_fusion.2 = bf16[128,1792]{1,0:T(8,128)(2,1)S(1)} fusion(bf16[256,1792]{1,0:T(8,128)(2,1)} %collective-permute-done.26, bf16[256,1792]{1,0:T(8,128)(2,1)} %collective-permute-done.25, bf16[256,1792]{1,0:T(8,128)(2,1)} %copy-done.4), kind=kLoop, calls=%fused_computation.2 | loop fusion | flops 1376256 | bytes 1835008 | tf_op jit(solution)/shard_map/convert_element_type | solution.py:498
  120.5 1.6 %collective-permute-start.27 = (bf16[128,1792]{1,0:T(8,128)(2,1)S(1)}, bf16[128,1792]{1,0:T(8,128)(2,1)S(1)}, u32[]{:S(2)}, u32[]{:S(2)}) collective-permute-start(bf16[128,1792]{1,0:T(8,128)(2,1)S(1)} %add_convert_fusion.2), channel_id=1, source_target_pairs={{0,4},{1,3},{2,6},{3,1},{4,0},{5,7},{6,2},{7,5},{8,12},{9,11},{10,... | collective-permute-start | bytes 1376264 | tf_op jit(solution)/shard_map/ppermute | solution.py:24
  122.2 1.3 copy-done.3
  123.5 3.1 %attend_moved.1 = bf16[16,64,512]{2,1,0:T(8,128)(2,1)} custom-call(s32[2]{0:T(128)S(1)} %pad_add_fusion.spot_ref, s32[512]{0:T(512)S(1)} %copy-done.9, s32[8]{0:T(128)S(1)} %copy-done.14, bf16[16,64,576]{2,1,0:T(8,128)(2,1)S(1)} %copy-done.3, bf16[16,576,128]{2,1,0:T(8,128)(2,1)S(1)} %bitcast.22, ...), custom_call_target="tpu_custom_call", output_to_operand_aliasing={{}: (8, {})} | custom-call | flops 68719476736 | bytes 1024 | tf_op jit(solution)/shard_map/attend_moved/pallas_call | solution.py:411
  126.6 2.5 %collective-permute-done.27 = bf16[128,1792]{1,0:T(8,128)(2,1)S(1)} collective-permute-done((bf16[128,1792]{1,0:T(8,128)(2,1)S(1)}, bf16[128,1792]{1,0:T(8,128)(2,1)S(1)}, u32[]{:S(2)}, u32[]{:S(2)}) %collective-permute-start.27) | collective-permute-done | bytes 458784 | tf_op jit(solution)/shard_map/ppermute | solution.py:24
  129.1 1.4 add_convert_fusion.7
  130.8 2.2 %collective-permute-start.33 = (bf16[32,1792]{1,0:T(8,128)(2,1)S(1)}, bf16[32,1792]{1,0:T(8,128)(2,1)S(1)}, u32[]{:S(2)}, u32[]{:S(2)}) collective-permute-start(bf16[32,1792]{1,0:T(8,128)(2,1)S(1)} %get-tuple-element.146), channel_id=1, source_target_pairs={{0,16},{1,17},{2,18},{3,19},{4,20},{5,21},{6,22},{7,23},{8,24},{9,... | collective-permute-start | bytes 344072 | tf_op jit(solution)/shard_map/ppermute | solution.py:24
  133.0 1.9 %collective-permute-start.34 = (bf16[32,1792]{1,0:T(8,128)(2,1)S(1)}, bf16[32,1792]{1,0:T(8,128)(2,1)S(1)}, u32[]{:S(2)}, u32[]{:S(2)}) collective-permute-start(bf16[32,1792]{1,0:T(8,128)(2,1)S(1)} %get-tuple-element.145), channel_id=1, source_target_pairs={{0,24},{1,25},{2,26},{3,27},{4,28},{5,29},{6,30},{7,31},{8,16},{9,... | collective-permute-start | bytes 344072 | tf_op jit(solution)/shard_map/ppermute | solution.py:24
  134.9 1.1 add_convert_fusion.8
  136.8 5.6 %collective-permute-done.33 = bf16[32,1792]{1,0:T(8,128)(2,1)S(1)} collective-permute-done((bf16[32,1792]{1,0:T(8,128)(2,1)S(1)}, bf16[32,1792]{1,0:T(8,128)(2,1)S(1)}, u32[]{:S(2)}, u32[]{:S(2)}) %collective-permute-start.33) | collective-permute-done | bytes 114720 | tf_op jit(solution)/shard_map/ppermute | solution.py:24
  142.4 1.1 add_convert_fusion.4
  143.6 1.2 collective-permute-done.35
  (106 shorter events, 7.6 us)
Async XLA Ops:
  1.6 2.8 %collective-permute-start = (bf16[2,16,1792]{2,1,0:T(8,128)(2,1)S(1)}, bf16[2,16,1792]{2,1,0:T(8,128)(2,1)S(1)}, u32[]{:S(2)}, u32[]{:S(2)}) collective-permute-start(bf16[2,16,1792]{2,1,0:T(8,128)(2,1)S(1)} %get-tuple-element.153), channel_id=1, source_target_pairs={{0,1},{1,0},{2,3},{3,2},{4,5},{5,4},{6,7},{7,6},{8,9},{9,8},{10,11... | collective-permute-start | bytes 344072 | tf_op jit(solution)/shard_map/ppermute | solution.py:24
  4.5 8.7 %collective-permute-start.1 = (bf16[32,1920]{1,0:T(8,128)(2,1)S(1)}, bf16[32,1920]{1,0:T(8,128)(2,1)S(1)}, u32[]{:S(2)}, u32[]{:S(2)}) collective-permute-start(bf16[32,1920]{1,0:T(8,128)(2,1)S(1)} %pad_maximum_fusion.3), channel_id=1, source_target_pairs={{0,8},{1,9},{2,10},{3,11},{4,12},{5,13},{6,14},{7,15},{8,0},{9,1},... | collective-permute-start | bytes 368648 | tf_op jit(solution)/shard_map/ppermute | solution.py:24
  7.2 12.4 %collective-permute-start.2 = (bf16[32,1920]{1,0:T(8,128)(2,1)S(1)}, bf16[32,1920]{1,0:T(8,128)(2,1)S(1)}, u32[]{:S(2)}, u32[]{:S(2)}) collective-permute-start(bf16[32,1920]{1,0:T(8,128)(2,1)S(1)} %pad_maximum_fusion.3), channel_id=1, source_target_pairs={{0,16},{1,17},{2,18},{3,19},{4,20},{5,21},{6,22},{7,23},{8,24},{9,... | collective-permute-start | bytes 368648 | tf_op jit(solution)/shard_map/ppermute | solution.py:24
  9.7 9.8 %collective-permute-start.3 = (bf16[32,1920]{1,0:T(8,128)(2,1)S(1)}, bf16[32,1920]{1,0:T(8,128)(2,1)S(1)}, u32[]{:S(2)}, u32[]{:S(2)}) collective-permute-start(bf16[32,1920]{1,0:T(8,128)(2,1)S(1)} %pad_maximum_fusion.3), channel_id=1, source_target_pairs={{0,24},{1,25},{2,26},{3,27},{4,28},{5,29},{6,30},{7,31},{8,16},{9,... | collective-permute-start | bytes 368648 | tf_op jit(solution)/shard_map/ppermute | solution.py:24
  9.7 25.5 %copy-start.2 = (bf16[16,64,576]{2,1,0:T(8,128)(2,1)S(1)}, bf16[16,64,576]{2,1,0:T(8,128)(2,1)}, u32[]{:S(2)}) copy-start(bf16[16,64,576]{2,1,0:T(8,128)(2,1)} %query_ref.1) | copy-start | bytes 3538948
  12.7 17.4 %copy-start.17 = (bf16[16,576]{1,0:T(8,128)(2,1)S(1)}, bf16[16,576]{1,0:T(8,128)(2,1)}, u32[]{:S(2)}) copy-start(bf16[16,576]{1,0:T(8,128)(2,1)} %param.16) | copy-start | bytes 55300
  12.8 22.5 %copy-start = (bf16[16,128,576]{1,2,0:T(8,128)(2,1)S(1)}, bf16[16,128,576]{1,2,0:T(8,128)(2,1)}, u32[]{:S(2)}) copy-start(bf16[16,128,576]{1,2,0:T(8,128)(2,1)} %param.17) | copy-start | bytes 7077892
  12.8 22.5 %copy-start.8 = (s32[512]{0:T(512)S(1)}, s32[512]{0:T(512)}, u32[]{:S(2)}) copy-start(s32[512]{0:T(512)} %length_ref.3) | copy-start | bytes 6148
  19.6 8.9 %collective-permute-start.4 = (bf16[128,1920]{1,0:T(8,128)(2,1)S(1)}, bf16[128,1920]{1,0:T(8,128)(2,1)S(1)}, u32[]{:S(2)}, u32[]{:S(2)}) collective-permute-start(bf16[128,1920]{1,0:T(8,128)(2,1)S(1)} %pad_maximum_fusion), channel_id=1, source_target_pairs={{0,4},{1,3},{2,6},{3,1},{4,0},{5,7},{6,2},{7,5},{8,12},{9,11},{10,... | collective-permute-start | bytes 1474568 | tf_op jit(solution)/shard_map/ppermute | solution.py:24
  28.5 16.0 %collective-permute-start.5 = (bf16[256,1920]{1,0:T(8,128)(2,1)S(1)}, bf16[256,1920]{1,0:T(8,128)(2,1)S(1)}, u32[]{:S(2)}, u32[]{:S(2)}) collective-permute-start(bf16[256,1920]{1,0:T(8,128)(2,1)S(1)} %constant_dynamic-update-slice_fusion.refs_0_), channel_id=1, source_target_pairs={{0,2},{1,5},{2,0},{3,7},{4,6},{5,1},{6,4},{7,3},{8,10},{9,13},{10,... | collective-permute-start | bytes 2949128 | tf_op jit(solution)/shard_map/ppermute | solution.py:24
  30.1 14.4 %collective-permute-start.6 = (bf16[256,1920]{1,0:T(8,128)(2,1)S(1)}, bf16[256,1920]{1,0:T(8,128)(2,1)S(1)}, u32[]{:S(2)}, u32[]{:S(2)}) collective-permute-start(bf16[256,1920]{1,0:T(8,128)(2,1)S(1)} %constant_dynamic-update-slice_fusion.refs_0_), channel_id=1, source_target_pairs={{0,1},{1,0},{2,3},{3,2},{4,5},{5,4},{6,7},{7,6},{8,9},{9,8},{10,11... | collective-permute-start | bytes 2949128 | tf_op jit(solution)/shard_map/ppermute | solution.py:24
  30.1 11.1 %copy-start.6 = (bf16[16,1,576]{2,1,0:T(2,128)(2,1)}, bf16[16,1,576]{2,1,0:T(2,128)(2,1)S(1)}, u32[]{:S(2)}) copy-start(bf16[16,1,576]{2,1,0:T(2,128)(2,1)S(1)} %copy.13.fresh_ref) | copy-start | bytes 55300
  30.1 11.1 %collective-permute-start.7 = (bf16[32,1792]{1,0:T(8,128)(2,1)S(1)}, bf16[32,1792]{1,0:T(8,128)(2,1)S(1)}, u32[]{:S(2)}, u32[]{:S(2)}) collective-permute-start(bf16[32,1792]{1,0:T(8,128)(2,1)S(1)} %get-tuple-element.83), channel_id=1, source_target_pairs={{0,8},{1,9},{2,10},{3,11},{4,12},{5,13},{6,14},{7,15},{8,0},{9,1},... | collective-permute-start | bytes 344072 | tf_op jit(solution)/shard_map/ppermute | solution.py:24
  32.7 11.8 %collective-permute-start.8 = (bf16[32,1792]{1,0:T(8,128)(2,1)S(1)}, bf16[32,1792]{1,0:T(8,128)(2,1)S(1)}, u32[]{:S(2)}, u32[]{:S(2)}) collective-permute-start(bf16[32,1792]{1,0:T(8,128)(2,1)S(1)} %get-tuple-element.83), channel_id=1, source_target_pairs={{0,16},{1,17},{2,18},{3,19},{4,20},{5,21},{6,22},{7,23},{8,24},{9,... | collective-permute-start | bytes 344072 | tf_op jit(solution)/shard_map/ppermute | solution.py:24
  33.8 10.8 %collective-permute-start.9 = (bf16[32,1792]{1,0:T(8,128)(2,1)S(1)}, bf16[32,1792]{1,0:T(8,128)(2,1)S(1)}, u32[]{:S(2)}, u32[]{:S(2)}) collective-permute-start(bf16[32,1792]{1,0:T(8,128)(2,1)S(1)} %get-tuple-element.83), channel_id=1, source_target_pairs={{0,24},{1,25},{2,26},{3,27},{4,28},{5,29},{6,30},{7,31},{8,16},{9,... | collective-permute-start | bytes 344072 | tf_op jit(solution)/shard_map/ppermute | solution.py:24
  35.2 14.0 %copy-start.19 = (bf16[2,576,128]{2,1,0:T(8,128)(2,1)S(1)}, bf16[2,576,128]{2,1,0:T(8,128)(2,1)}, u32[]{:S(2)}) copy-start(bf16[2,576,128]{2,1,0:T(8,128)(2,1)} %get-tuple-element.91) | copy-start | bytes 884740
  44.5 2.6 %collective-permute-start.10 = (bf16[256,1920]{1,0:T(8,128)(2,1)S(1)}, bf16[256,1920]{1,0:T(8,128)(2,1)S(1)}, u32[]{:S(2)}, u32[]{:S(2)}) collective-permute-start(bf16[256,1920]{1,0:T(8,128)(2,1)S(1)} %collective-permute-done.5.refs_1_), channel_id=1, source_target_pairs={{0,1},{1,0},{2,3},{3,2},{4,5},{5,4},{6,7},{7,6},{8,9},{9,8},{10,11... | collective-permute-start | bytes 2949128 | tf_op jit(solution)/shard_map/ppermute | solution.py:24
  44.6 24.6 %slice-start = ((s8[7340032]{0:T(1024)(128)(4,1)}), s8[4194304]{0:T(1024)(128)(4,1)S(1)}, s32[]{:S(2)}) async-start(s8[7340032]{0:T(1024)(128)(4,1)} %bitcast.23), calls=%async_computation | async-start | bytes 8388608
  47.2 20.4 %collective-permute-start.11 = (bf16[128,1792]{1,0:T(8,128)(2,1)S(1)}, bf16[128,1792]{1,0:T(8,128)(2,1)S(1)}, u32[]{:S(2)}, u32[]{:S(2)}) collective-permute-start(bf16[128,1792]{1,0:T(8,128)(2,1)S(1)} %pad_maximum_fusion.1.refs_0_), channel_id=1, source_target_pairs={{0,2},{1,5},{2,0},{3,7},{4,6},{5,1},{6,4},{7,3},{8,10},{9,13},{10,... | collective-permute-start | bytes 1376264 | tf_op jit(solution)/shard_map/ppermute | solution.py:24
  47.7 19.9 %collective-permute-start.13 = (bf16[128,1792]{1,0:T(8,128)(2,1)S(1)}, bf16[128,1792]{1,0:T(8,128)(2,1)S(1)}, u32[]{:S(2)}, u32[]{:S(2)}) collective-permute-start(bf16[128,1792]{1,0:T(8,128)(2,1)S(1)} %pad_maximum_fusion.1.refs_0_), channel_id=1, source_target_pairs={{0,4},{1,3},{2,6},{3,1},{4,0},{5,7},{6,2},{7,5},{8,12},{9,11},{10,... | collective-permute-start | bytes 1376264 | tf_op jit(solution)/shard_map/ppermute | solution.py:24
  49.2 17.6 %collective-permute-start.12 = (bf16[2,576,128]{2,1,0:T(8,128)(2,1)S(1)}, bf16[2,576,128]{2,1,0:T(8,128)(2,1)S(1)}, u32[]{:S(2)}, u32[]{:S(2)}) collective-permute-start(bf16[2,576,128]{2,1,0:T(8,128)(2,1)S(1)} %copy-done.19), channel_id=1, source_target_pairs={{0,16},{1,17},{2,18},{3,19},{4,20},{5,21},{6,22},{7,23},{8,24},{9,... | collective-permute-start | bytes 884744 | tf_op jit(solution)/shard_map/ppermute | solution.py:24
  52.4 16.8 %slice-start.1 = ((s8[7340032]{0:T(1024)(128)(4,1)}), s8[3145728]{0:T(1024)(128)(4,1)S(1)}, s32[]{:S(2)}) async-start(s8[7340032]{0:T(1024)(128)(4,1)} %bitcast.23), calls=%async_computation.1 | async-start | bytes 6291456
  67.6 10.0 %collective-permute-start.18 = (bf16[128,1792]{1,0:T(8,128)(2,1)S(1)}, bf16[128,1792]{1,0:T(8,128)(2,1)S(1)}, u32[]{:S(2)}, u32[]{:S(2)}) collective-permute-start(bf16[128,1792]{1,0:T(8,128)(2,1)S(1)} %collective-permute-done.13.refs_1_), channel_id=1, source_target_pairs={{0,1},{1,0},{2,3},{3,2},{4,5},{5,4},{6,7},{7,6},{8,9},{9,8},{10,11... | collective-permute-start | bytes 1376264 | tf_op jit(solution)/shard_map/ppermute | solution.py:24
  67.6 10.0 %collective-permute-start.19 = (bf16[128,1792]{1,0:T(8,128)(2,1)S(1)}, bf16[128,1792]{1,0:T(8,128)(2,1)S(1)}, u32[]{:S(2)}, u32[]{:S(2)}) collective-permute-start(bf16[128,1792]{1,0:T(8,128)(2,1)S(1)} %collective-permute-done.13.refs_1_), channel_id=1, source_target_pairs={{0,2},{1,5},{2,0},{3,7},{4,6},{5,1},{6,4},{7,3},{8,10},{9,13},{10,... | collective-permute-start | bytes 1376264 | tf_op jit(solution)/shard_map/ppermute | solution.py:24
  69.2 4.3 %collective-permute-start.14 = (bf16[128,1792]{1,0:T(8,128)(2,1)S(1)}, bf16[128,1792]{1,0:T(8,128)(2,1)S(1)}, u32[]{:S(2)}, u32[]{:S(2)}) collective-permute-start(bf16[128,1792]{1,0:T(8,128)(2,1)S(1)} %collective-permute-done.11.refs_2_), channel_id=1, source_target_pairs={{0,1},{1,0},{2,3},{3,2},{4,5},{5,4},{6,7},{7,6},{8,9},{9,8},{10,11... | collective-permute-start | bytes 1376264 | tf_op jit(solution)/shard_map/ppermute | solution.py:24
  72.8 4.7 %collective-permute-start.15 = (bf16[256,1792]{1,0:T(8,128)(2,1)S(1)}, bf16[256,1792]{1,0:T(8,128)(2,1)S(1)}, u32[]{:S(2)}, u32[]{:S(2)}) collective-permute-start(bf16[256,1792]{1,0:T(8,128)(2,1)S(1)} %get-tuple-element.102), channel_id=1, source_target_pairs={{0,1},{1,0},{2,3},{3,2},{4,5},{5,4},{6,7},{7,6},{8,9},{9,8},{10,11... | collective-permute-start | bytes 2752520 | tf_op jit(solution)/shard_map/ppermute | solution.py:24
  73.4 4.2 %collective-permute-start.16 = (bf16[256,1792]{1,0:T(8,128)(2,1)S(1)}, bf16[256,1792]{1,0:T(8,128)(2,1)S(1)}, u32[]{:S(2)}, u32[]{:S(2)}) collective-permute-start(bf16[256,1792]{1,0:T(8,128)(2,1)S(1)} %get-tuple-element.103), channel_id=1, source_target_pairs={{0,1},{1,0},{2,3},{3,2},{4,5},{5,4},{6,7},{7,6},{8,9},{9,8},{10,11... | collective-permute-start | bytes 2752520 | tf_op jit(solution)/shard_map/ppermute | solution.py:24
  73.5 4.1 %collective-permute-start.17 = (bf16[128,1792]{1,0:T(8,128)(2,1)S(1)}, bf16[128,1792]{1,0:T(8,128)(2,1)S(1)}, u32[]{:S(2)}, u32[]{:S(2)}) collective-permute-start(bf16[128,1792]{1,0:T(8,128)(2,1)S(1)} %pad_maximum_fusion.1.refs_0_), channel_id=1, source_target_pairs={{0,1},{1,0},{2,3},{3,2},{4,5},{5,4},{6,7},{7,6},{8,9},{9,8},{10,11... | collective-permute-start | bytes 1376264 | tf_op jit(solution)/shard_map/ppermute | solution.py:24
  77.6 22.3 %copy-start.15 = (bf16[256,1792]{1,0:T(8,128)(2,1)}, bf16[256,1792]{1,0:T(8,128)(2,1)S(1)}, u32[]{:S(2)}) copy-start(bf16[256,1792]{1,0:T(8,128)(2,1)S(1)} %collective-permute-done.15) | copy-start | bytes 2752516
  77.6 1.9 %collective-permute-start.20 = (bf16[128,1792]{1,0:T(8,128)(2,1)S(1)}, bf16[128,1792]{1,0:T(8,128)(2,1)S(1)}, u32[]{:S(2)}, u32[]{:S(2)}) collective-permute-start(bf16[128,1792]{1,0:T(8,128)(2,1)S(1)} %collective-permute-done.19.refs_3_), channel_id=1, source_target_pairs={{0,1},{1,0},{2,3},{3,2},{4,5},{5,4},{6,7},{7,6},{8,9},{9,8},{10,11... | collective-permute-start | bytes 1376264 | tf_op jit(solution)/shard_map/ppermute | solution.py:24
  79.5 15.8 %collective-permute-start.21 = (bf16[256,1792]{1,0:T(8,128)(2,1)S(1)}, bf16[256,1792]{1,0:T(8,128)(2,1)S(1)}, u32[]{:S(2)}, u32[]{:S(2)}) collective-permute-start(bf16[256,1792]{1,0:T(8,128)(2,1)S(1)} %add_convert_fusion.1), channel_id=1, source_target_pairs={{0,2},{1,5},{2,0},{3,7},{4,6},{5,1},{6,4},{7,3},{8,10},{9,13},{10,... | collective-permute-start | bytes 2752520 | tf_op jit(solution)/shard_map/ppermute | solution.py:24
  80.0 15.3 %collective-permute-start.22 = (bf16[2,576,128]{2,1,0:T(8,128)(2,1)S(1)}, bf16[2,576,128]{2,1,0:T(8,128)(2,1)S(1)}, u32[]{:S(2)}, u32[]{:S(2)}) collective-permute-start(bf16[2,576,128]{2,1,0:T(8,128)(2,1)S(1)} %copy-done.18), channel_id=1, source_target_pairs={{0,16},{1,17},{2,18},{3,19},{4,20},{5,21},{6,22},{7,23},{8,24},{9,... | collective-permute-start | bytes 884744 | tf_op jit(solution)/shard_map/ppermute | solution.py:24
  99.8 2.6 %collective-permute-start.24 = (bf16[256,1792]{1,0:T(8,128)(2,1)S(1)}, bf16[256,1792]{1,0:T(8,128)(2,1)S(1)}, u32[]{:S(2)}, u32[]{:S(2)}) collective-permute-start(bf16[256,1792]{1,0:T(8,128)(2,1)S(1)} %get-tuple-element.126), channel_id=1, source_target_pairs={{0,1},{1,0},{2,3},{3,2},{4,5},{5,4},{6,7},{7,6},{8,9},{9,8},{10,11... | collective-permute-start | bytes 2752520 | tf_op jit(solution)/shard_map/ppermute | solution.py:24
  100.9 11.8 %collective-permute-start.23 = (bf16[128,1792]{1,0:T(8,128)(2,1)}, bf16[128,1792]{1,0:T(8,128)(2,1)}, u32[]{:S(2)}, u32[]{:S(2)}) collective-permute-start(bf16[128,1792]{1,0:T(8,128)(2,1)} %add_convert_fusion.3), channel_id=1, source_target_pairs={{0,4},{1,3},{2,6},{3,1},{4,0},{5,7},{6,2},{7,5},{8,12},{9,11},{10,... | collective-permute-start | bytes 1376264 | tf_op jit(solution)/shard_map/ppermute | solution.py:24
  103.6 15.5 %collective-permute-start.25 = (bf16[256,1792]{1,0:T(8,128)(2,1)}, bf16[256,1792]{1,0:T(8,128)(2,1)}, u32[]{:S(2)}, u32[]{:S(2)}) collective-permute-start(bf16[256,1792]{1,0:T(8,128)(2,1)} %add_convert_fusion), channel_id=1, source_target_pairs={{0,2},{1,5},{2,0},{3,7},{4,6},{5,1},{6,4},{7,3},{8,10},{9,13},{10,... | collective-permute-start | bytes 2752520 | tf_op jit(solution)/shard_map/ppermute | solution.py:24
  111.2 10.9 %copy-start.7 = (bf16[16,1,576]{2,1,0:T(2,128)(2,1)S(1)}, bf16[16,1,576]{2,1,0:T(2,128)(2,1)}, u32[]{:S(2)}) copy-start(bf16[16,1,576]{2,1,0:T(2,128)(2,1)} %copy-done.6) | copy-start | bytes 55300
  111.2 10.9 %copy-start.9 = (s32[512]{0:T(512)S(1)}, s32[512]{0:T(512)}, u32[]{:S(2)}) copy-start(s32[512]{0:T(512)} %length_ref.3) | copy-start | bytes 6148
  111.2 10.9 %copy-start.14 = (s32[8]{0:T(128)S(1)}, s32[8]{0:T(128)}, u32[]{:S(2)}) copy-start(s32[8]{0:T(128)} %get-tuple-element.134.info_ref) | copy-start | bytes 100
  111.2 7.9 %collective-permute-start.26 = (bf16[256,1792]{1,0:T(8,128)(2,1)}, bf16[256,1792]{1,0:T(8,128)(2,1)}, u32[]{:S(2)}, u32[]{:S(2)}) collective-permute-start(bf16[256,1792]{1,0:T(8,128)(2,1)} %get-tuple-element.131), channel_id=1, source_target_pairs={{0,1},{1,0},{2,3},{3,2},{4,5},{5,4},{6,7},{7,6},{8,9},{9,8},{10,11... | collective-permute-start | bytes 2752520 | tf_op jit(solution)/shard_map/ppermute | solution.py:24
  114.3 12.4 %collective-permute-start.28 = (bf16[32,1792]{1,0:T(8,128)(2,1)S(1)}, bf16[32,1792]{1,0:T(8,128)(2,1)S(1)}, u32[]{:S(2)}, u32[]{:S(2)}) collective-permute-start(bf16[32,1792]{1,0:T(8,128)(2,1)S(1)} %get-tuple-element.149), channel_id=1, source_target_pairs={{0,8},{1,9},{2,10},{3,11},{4,12},{5,13},{6,14},{7,15},{8,0},{9,1},... | collective-permute-start | bytes 344072 | tf_op jit(solution)/shard_map/ppermute | solution.py:24
  114.5 12.1 %collective-permute-start.29 = (bf16[32,1792]{1,0:T(8,128)(2,1)S(1)}, bf16[32,1792]{1,0:T(8,128)(2,1)S(1)}, u32[]{:S(2)}, u32[]{:S(2)}) collective-permute-start(bf16[32,1792]{1,0:T(8,128)(2,1)S(1)} %get-tuple-element.148), channel_id=1, source_target_pairs={{0,16},{1,17},{2,18},{3,19},{4,20},{5,21},{6,22},{7,23},{8,24},{9,... | collective-permute-start | bytes 344072 | tf_op jit(solution)/shard_map/ppermute | solution.py:24
  116.9 9.8 %collective-permute-start.30 = (bf16[32,1792]{1,0:T(8,128)(2,1)S(1)}, bf16[32,1792]{1,0:T(8,128)(2,1)S(1)}, u32[]{:S(2)}, u32[]{:S(2)}) collective-permute-start(bf16[32,1792]{1,0:T(8,128)(2,1)S(1)} %get-tuple-element.147), channel_id=1, source_target_pairs={{0,24},{1,25},{2,26},{3,27},{4,28},{5,29},{6,30},{7,31},{8,16},{9,... | collective-permute-start | bytes 344072 | tf_op jit(solution)/shard_map/ppermute | solution.py:24
  120.5 8.5 %collective-permute-start.27 = (bf16[128,1792]{1,0:T(8,128)(2,1)S(1)}, bf16[128,1792]{1,0:T(8,128)(2,1)S(1)}, u32[]{:S(2)}, u32[]{:S(2)}) collective-permute-start(bf16[128,1792]{1,0:T(8,128)(2,1)S(1)} %add_convert_fusion.2), channel_id=1, source_target_pairs={{0,4},{1,3},{2,6},{3,1},{4,0},{5,7},{6,2},{7,5},{8,12},{9,11},{10,... | collective-permute-start | bytes 1376264 | tf_op jit(solution)/shard_map/ppermute | solution.py:24
  130.4 6.3 %collective-permute-start.32 = (bf16[32,1792]{1,0:T(8,128)(2,1)S(1)}, bf16[32,1792]{1,0:T(8,128)(2,1)S(1)}, u32[]{:S(2)}, u32[]{:S(2)}) collective-permute-start(bf16[32,1792]{1,0:T(8,128)(2,1)S(1)} %get-tuple-element.144), channel_id=1, source_target_pairs={{0,8},{1,9},{2,10},{3,11},{4,12},{5,13},{6,14},{7,15},{8,0},{9,1},... | collective-permute-start | bytes 344072 | tf_op jit(solution)/shard_map/ppermute | solution.py:24
  130.8 11.5 %collective-permute-start.33 = (bf16[32,1792]{1,0:T(8,128)(2,1)S(1)}, bf16[32,1792]{1,0:T(8,128)(2,1)S(1)}, u32[]{:S(2)}, u32[]{:S(2)}) collective-permute-start(bf16[32,1792]{1,0:T(8,128)(2,1)S(1)} %get-tuple-element.146), channel_id=1, source_target_pairs={{0,16},{1,17},{2,18},{3,19},{4,20},{5,21},{6,22},{7,23},{8,24},{9,... | collective-permute-start | bytes 344072 | tf_op jit(solution)/shard_map/ppermute | solution.py:24
  133.0 9.3 %collective-permute-start.34 = (bf16[32,1792]{1,0:T(8,128)(2,1)S(1)}, bf16[32,1792]{1,0:T(8,128)(2,1)S(1)}, u32[]{:S(2)}, u32[]{:S(2)}) collective-permute-start(bf16[32,1792]{1,0:T(8,128)(2,1)S(1)} %get-tuple-element.145), channel_id=1, source_target_pairs={{0,24},{1,25},{2,26},{3,27},{4,28},{5,29},{6,30},{7,31},{8,16},{9,... | collective-permute-start | bytes 344072 | tf_op jit(solution)/shard_map/ppermute | solution.py:24
  136.0 7.5 %collective-permute-start.31 = (bf16[16,1792]{1,0:T(8,128)(2,1)S(1)}, bf16[16,1792]{1,0:T(8,128)(2,1)S(1)}, u32[]{:S(2)}, u32[]{:S(2)}) collective-permute-start(bf16[16,1792]{1,0:T(8,128)(2,1)S(1)} %get-tuple-element.155), channel_id=1, source_target_pairs={{0,1},{1,0},{2,3},{3,2},{4,5},{5,4},{6,7},{7,6},{8,9},{9,8},{10,11... | collective-permute-start | bytes 172040 | tf_op jit(solution)/shard_map/ppermute | solution.py:24
  143.5 1.3 collective-permute-start.35
  (10 other events, 52.8 us)

commit v6 on v5

--- a/solution.py
+++ b/solution.py
@@ -457,7 +457,8 @@
     x_masks = [ep_count << bit for bit in range(dp_bits - Z_BITS)]
     z_unit = ep_count << (dp_bits - Z_BITS)
     y_masks = [1 << bit for bit in range(1, ep_bits)]
-    z_masks = [z_unit * step for step in range(1 << Z_BITS)]
+    z_steps = sorted(range(1, 1 << Z_BITS), key=lambda step: step < 1 << (Z_BITS - 1))
+    z_masks = [z_unit * step for step in [0] + z_steps]
     orders = (x_masks + y_masks, y_masks + x_masks)
     level_masks = list(zip(*orders))
     line_count = 1 << len(level_masks)

time: 146 us -> 144 us (0.986)
  starting transfers between devices: 36.4 us -> 32.6 us
  waiting for transfers between devices: 34.6 us -> 36.7 us
    ppermute x36, starting transfers between devices: 36.4 us -> 32.6 us  [exchange(): return lax.ppermute(value, AXES, pairs)]
    ppermute x36, waiting for transfers between devices: 34.6 us -> 36.7 us  [exchange(): return lax.ppermute(value, AXES, pairs)]
  transfers between devices with their start and end apart: 36 -> 36, of which waited for: 13 -> 15; matrix products, arithmetic and copies ran while one was open for 6% -> 6% of each run, Pallas kernels for 37% -> 38%
where the time goes in v6:
time: 144 us
  Pallas kernels  58.6 us (41%)
  waiting for transfers between devices  36.7 us (25%)
  starting transfers between devices  32.6 us (23%)
  other arithmetic  10.6 us (7%)
  local copies, waits for them, and re-layouts  4.28 us (3%)
    ppermute x36, waiting for transfers between devices, exchange(): return lax.ppermute(value, AXES, pairs)  36.7 us
    ppermute x36, starting transfers between devices, exchange(): return lax.ppermute(value, AXES, pairs)  32.6 us
    pallas_call x2, Pallas kernels, expert_up(): pl.pallas_call(functools.partial(up_body, line_rows, piece_counts, with_m...  28.1 us
    pallas_call x4, Pallas kernels, expert_down(): pl.pallas_call(functools.partial(down_body, line_rows, jobs), grid_spec=p...  17 us
    convert_element_type x8, other arithmetic, per_device(): rounded_sum = lambda terms: add(terms).astype(jnp.bfloat16)  8.83 us
    pallas_call x1, Pallas kernels, attend(): pl.pallas_call(functools.partial(attend_body, group), grid_spec=pltpu.Pre...  5.96 us
    unnamed x48, local copies, waits for them, and re-layouts  3.17 us
    pallas_call x1, Pallas kernels, attend_moved(): pl.pallas_call(functools.partial(attend_moved_body, row_count), grid_spec...  3.13 us
  transfers between devices with their start and end apart: 36, of which 15 were waited for; matrix products, arithmetic and copies ran while one was open for 6% of the time, Pallas kernels for 38%

profile of v6, /device:TPU:0, one launch (start us, length us, event | category | flops | bytes accessed | tf_op | source)
XLA Modules:
  0.0 143.8 jit_solution(5626314400830209493)
XLA Ops:
  0.7 1.0 constant_dynamic-slice_fusion.3
  2.2 1.5 %meta_columns.1 = bf16[16,128]{1,0:T(8,128)(2,1)} custom-call(s32[2,8,16]{2,1,0:T(8,128)} %bitcast.34, f32[2,8,16]{2,1,0:T(8,128)} %bitcast.35), custom_call_target="tpu_custom_call" | custom-call | tf_op jit(solution)/shard_map/meta_columns/pallas_call | solution.py:273
  4.5 3.7 %collective-permute-start.1 = (bf16[32,1920]{1,0:T(8,128)(2,1)S(1)}, bf16[32,1920]{1,0:T(8,128)(2,1)S(1)}, u32[]{:S(2)}, u32[]{:S(2)}) collective-permute-start(bf16[32,1920]{1,0:T(8,128)(2,1)S(1)} %pad_maximum_fusion.3), channel_id=1, source_target_pairs={{0,16},{1,17},{2,18},{3,19},{4,20},{5,21},{6,22},{7,23},{8,24},{9,... | collective-permute-start | bytes 368648 | tf_op jit(solution)/shard_map/ppermute | solution.py:24
  8.2 1.3 collective-permute-start.2
  9.7 3.0 %pick_caches.1 = (bf16[2,576,128]{2,1,0:T(8,128)(2,1)}, bf16[2,576,128]{2,1,0:T(8,128)(2,1)}, s32[8]{0:T(128)}) custom-call(s32[16]{0:T(128)} %swapped_ref, bf16[16,576,128]{2,1,0:T(8,128)(2,1)} %bitcast.20), custom_call_target="tpu_custom_call" | custom-call | tf_op jit(solution)/shard_map/pick_caches/pallas_call | solution.py:313
  12.8 4.8 %collective-permute-done.1 = bf16[32,1920]{1,0:T(8,128)(2,1)S(1)} collective-permute-done((bf16[32,1920]{1,0:T(8,128)(2,1)S(1)}, bf16[32,1920]{1,0:T(8,128)(2,1)S(1)}, u32[]{:S(2)}, u32[]{:S(2)}) %collective-permute-start.1) | collective-permute-done | bytes 122912 | tf_op jit(solution)/shard_map/ppermute | solution.py:24
  17.7 1.1 collective-permute-done.3
  18.8 1.6 %collective-permute-start.4 = (bf16[128,1920]{1,0:T(8,128)(2,1)S(1)}, bf16[128,1920]{1,0:T(8,128)(2,1)S(1)}, u32[]{:S(2)}, u32[]{:S(2)}) collective-permute-start(bf16[128,1920]{1,0:T(8,128)(2,1)S(1)} %pad_maximum_fusion), channel_id=1, source_target_pairs={{0,4},{1,3},{2,6},{3,1},{4,0},{5,7},{6,2},{7,5},{8,12},{9,11},{10,... | collective-permute-start | bytes 1474568 | tf_op jit(solution)/shard_map/ppermute | solution.py:24
  20.5 7.2 %collective-permute-done.4 = bf16[128,1920]{1,0:T(8,128)(2,1)S(1)} collective-permute-done((bf16[128,1920]{1,0:T(8,128)(2,1)S(1)}, bf16[128,1920]{1,0:T(8,128)(2,1)S(1)}, u32[]{:S(2)}, u32[]{:S(2)}) %collective-permute-start.4) | collective-permute-done | bytes 491552 | tf_op jit(solution)/shard_map/ppermute | solution.py:24
  27.8 1.6 %collective-permute-start.5 = (bf16[256,1920]{1,0:T(8,128)(2,1)S(1)}, bf16[256,1920]{1,0:T(8,128)(2,1)S(1)}, u32[]{:S(2)}, u32[]{:S(2)}) collective-permute-start(bf16[256,1920]{1,0:T(8,128)(2,1)S(1)} %constant_dynamic-update-slice_fusion.refs_0_), channel_id=1, source_target_pairs={{0,2},{1,5},{2,0},{3,7},{4,6},{5,1},{6,4},{7,3},{8,10},{9,13},{10,... | collective-permute-start | bytes 2949128 | tf_op jit(solution)/shard_map/ppermute | solution.py:24
  29.5 3.9 %collective-permute-start.7 = (bf16[32,1792]{1,0:T(8,128)(2,1)S(1)}, bf16[32,1792]{1,0:T(8,128)(2,1)S(1)}, u32[]{:S(2)}, u32[]{:S(2)}) collective-permute-start(bf16[32,1792]{1,0:T(8,128)(2,1)S(1)} %get-tuple-element.83), channel_id=1, source_target_pairs={{0,16},{1,17},{2,18},{3,19},{4,20},{5,21},{6,22},{7,23},{8,24},{9,... | collective-permute-start | bytes 344072 | tf_op jit(solution)/shard_map/ppermute | solution.py:24
  34.2 6.0 %attend.1.old_ref = bf16[16,64,512]{2,1,0:T(8,128)(2,1)} custom-call(s32[2]{0:T(128)S(1)} %pad_add_fusion.spot_ref, s32[512]{0:T(512)S(1)} %copy-done.8, bf16[16,64,576]{2,1,0:T(8,128)(2,1)S(1)} %copy-done.2, bf16[16,576,128]{2,1,0:T(8,128)(2,1)S(1)} %bitcast.21, bf16[16,1,576]{2,1,0:T(2,128)(2,1)S(1)} %copy.13.fresh_ref), custom_call_target="tpu_custom_call" | custom-call | flops 301989888 | bytes 4587520 | tf_op jit(solution)/shard_map/attend/pallas_call | solution.py:365
  40.1 2.3 %collective-permute-done.7 = bf16[32,1792]{1,0:T(8,128)(2,1)S(1)} collective-permute-done((bf16[32,1792]{1,0:T(8,128)(2,1)S(1)}, bf16[32,1792]{1,0:T(8,128)(2,1)S(1)}, u32[]{:S(2)}, u32[]{:S(2)}) %collective-permute-start.7) | collective-permute-done | bytes 114720 | tf_op jit(solution)/shard_map/ppermute | solution.py:24
  42.4 1.1 collective-permute-done.9
  43.6 2.5 %collective-permute-done.10.refs_3_ = bf16[256,1920]{1,0:T(8,128)(2,1)S(1)} collective-permute-done((bf16[256,1920]{1,0:T(8,128)(2,1)S(1)}, bf16[256,1920]{1,0:T(8,128)(2,1)S(1)}, u32[]{:S(2)}, u32[]{:S(2)}) %collective-permute-start.10) | collective-permute-done | bytes 983072 | tf_op jit(solution)/shard_map/ppermute | solution.py:24
  46.6 1.5 %collective-permute-start.13 = (bf16[128,1792]{1,0:T(8,128)(2,1)S(1)}, bf16[128,1792]{1,0:T(8,128)(2,1)S(1)}, u32[]{:S(2)}, u32[]{:S(2)}) collective-permute-start(bf16[128,1792]{1,0:T(8,128)(2,1)S(1)} %pad_maximum_fusion.1.refs_0_), channel_id=1, source_target_pairs={{0,4},{1,3},{2,6},{3,1},{4,0},{5,7},{6,2},{7,5},{8,12},{9,11},{10,... | collective-permute-start | bytes 1376264 | tf_op jit(solution)/shard_map/ppermute | solution.py:24
  48.1 3.4 %collective-permute-start.12 = (bf16[2,576,128]{2,1,0:T(8,128)(2,1)S(1)}, bf16[2,576,128]{2,1,0:T(8,128)(2,1)S(1)}, u32[]{:S(2)}, u32[]{:S(2)}) collective-permute-start(bf16[2,576,128]{2,1,0:T(8,128)(2,1)S(1)} %copy-done.19), channel_id=1, source_target_pairs={{0,16},{1,17},{2,18},{3,19},{4,20},{5,21},{6,22},{7,23},{8,24},{9,... | collective-permute-start | bytes 884744 | tf_op jit(solution)/shard_map/ppermute | solution.py:24
  51.5 14.4 %expert_up.2 = (bf16[512,1024]{1,0:T(8,128)(2,1)S(1)}, f32[512,128]{1,0:T(8,128)S(1)}, f32[512,128]{1,0:T(8,128)S(1)}) custom-call(s32[2]{0:T(128)S(1)} %pad_add_fusion.spot_ref, bf16[256,1920]{1,0:T(8,128)(2,1)S(1)} %constant_dynamic-update-slice_fusion.refs_0_, bf16[256,1920]{1,0:T(8,128)(2,1)S(1)} %collective-permute-done.5.refs_1_, ...), custom_call_target="tpu_custom_call" | custom-call | flops 7516192768 | bytes 19660800 | tf_op jit(solution)/shard_map/expert_up/pallas_call | solution.py:152
  67.4 3.6 %expert_down.4 = (bf16[256,1792]{1,0:T(8,128)(2,1)S(1)}, bf16[256,1792]{1,0:T(8,128)(2,1)S(1)}) custom-call(s32[2]{0:T(128)S(1)} %pad_add_fusion.spot_ref, bf16[512,1024]{1,0:T(8,128)(2,1)S(1)} %get-tuple-element.100.act_ref, bf16[1024,3584]{1,0:T(8,128)(2,1)S(1)} %bitcast.25, f32[512,128]{1,0:T(8,128)S(1)} %get-tuple-element.101.scale_ref), custom_call_target="tpu_custom_call" | custom-call | flops 68719476736 | bytes 1024 | tf_op jit(solution)/shard_map/expert_down/pallas_call | solution.py:232
  72.2 3.6 %expert_down.5 = (bf16[256,1792]{1,0:T(8,128)(2,1)S(1)}, bf16[256,1792]{1,0:T(8,128)(2,1)S(1)}) custom-call(s32[2]{0:T(128)S(1)} %pad_add_fusion.spot_ref, bf16[512,1024]{1,0:T(8,128)(2,1)S(1)} %get-tuple-element.100.act_ref, bf16[1024,3584]{1,0:T(8,128)(2,1)S(1)} %bitcast.26, f32[512,128]{1,0:T(8,128)S(1)} %get-tuple-element.101.scale_ref), custom_call_target="tpu_custom_call" | custom-call | flops 68719476736 | bytes 1024 | tf_op jit(solution)/shard_map/expert_down/pallas_call | solution.py:232
  76.4 1.3 collective-permute-done.20.refs_7_
  77.7 1.3 collective-permute-start.21
  79.1 13.6 %expert_up.3.act_ref = bf16[512,1024]{1,0:T(8,128)(2,1)S(1)} custom-call(s32[2]{0:T(128)S(1)} %pad_add_fusion.spot_ref, bf16[128,1792]{1,0:T(8,128)(2,1)S(1)} %pad_maximum_fusion.1.refs_0_, bf16[128,1792]{1,0:T(8,128)(2,1)S(1)} %collective-permute-done.13.refs_1_, bf16[128,1792]{1,0:T(8,128)(2,1)S(1)} %collective-permute-done.11.refs_2_, ...), custom_call_target="tpu_custom_call" | custom-call | flops 7516192768 | bytes 19398656 | tf_op jit(solution)/shard_map/expert_up/pallas_call | solution.py:152
  92.7 1.9 %collective-permute-done.22.came_b_ref = bf16[2,576,128]{2,1,0:T(8,128)(2,1)S(1)} collective-permute-done((bf16[2,576,128]{2,1,0:T(8,128)(2,1)S(1)}, bf16[2,576,128]{2,1,0:T(8,128)(2,1)S(1)}, u32[]{:S(2)}, u32[]{:S(2)}) %collective-permute-start.22) | collective-permute-done | bytes 294944 | tf_op jit(solution)/shard_map/ppermute | solution.py:24
  94.7 4.5 %expert_down.6 = (bf16[256,1792]{1,0:T(8,128)(2,1)S(1)}, bf16[256,1792]{1,0:T(8,128)(2,1)S(1)}) custom-call(s32[2]{0:T(128)S(1)} %pad_add_fusion.spot_ref, bf16[512,1024]{1,0:T(8,128)(2,1)S(1)} %expert_up.3.act_ref, bf16[1024,3584]{1,0:T(8,128)(2,1)S(1)} %bitcast.27, f32[512,128]{1,0:T(8,128)S(1)} %get-tuple-element.122.scale_ref), custom_call_target="tpu_custom_call" | custom-call | flops 68719476736 | bytes 1024 | tf_op jit(solution)/shard_map/expert_down/pallas_call | solution.py:232
  99.3 1.0 add_convert_fusion.3
  100.3 0.9 collective-permute-start.23
  101.7 1.1 add_convert_fusion
  103.6 5.3 %expert_down.7 = (bf16[256,1792]{1,0:T(8,128)(2,1)}, bf16[256,1792]{1,0:T(8,128)(2,1)S(1)}) custom-call(s32[2]{0:T(128)S(1)} %pad_add_fusion.spot_ref, bf16[512,1024]{1,0:T(8,128)(2,1)S(1)} %expert_up.3.act_ref, bf16[1024,3584]{1,0:T(8,128)(2,1)S(1)} %bitcast.28, f32[512,128]{1,0:T(8,128)S(1)} %get-tuple-element.122.scale_ref), custom_call_target="tpu_custom_call" | custom-call | flops 68719476736 | bytes 1024 | tf_op jit(solution)/shard_map/expert_down/pallas_call | solution.py:232
  108.9 1.0 copy-done.4
  110.1 2.1 %collective-permute-done.23 = bf16[128,1792]{1,0:T(8,128)(2,1)} collective-permute-done((bf16[128,1792]{1,0:T(8,128)(2,1)}, bf16[128,1792]{1,0:T(8,128)(2,1)}, u32[]{:S(2)}, u32[]{:S(2)}) %collective-permute-start.23) | collective-permute-done | bytes 458784 | tf_op jit(solution)/shard_map/ppermute | solution.py:24
  112.2 1.5 %add_convert_fusion.9 = (bf16[32,1792]{1,0:T(8,128)(2,1)S(1)}, bf16[32,1792]{1,0:T(8,128)(2,1)S(1)}, bf16[32,1792]{1,0:T(8,128)(2,1)S(1)}) fusion(bf16[128,1792]{1,0:T(8,128)(2,1)} %collective-permute-done.23, bf16[256,1792]{1,0:T(8,128)(2,1)} %copy-done.16, bf16[256,1792]{1,0:T(8,128)(2,1)} %copy-done.15, bf16[256,1792]{1,0:T(8,128)(2,1)S(1)} %get-tuple-element.108), kind=kLoop, calls=%fused_computation.13 | loop fusion | flops 1376256 | bytes 1720320 | tf_op jit(solution)/shard_map/convert_element_type | solution.py:499
  113.7 1.1 collective-permute-start.28
  115.5 1.7 %collective-permute-start.30 = (bf16[32,1792]{1,0:T(8,128)(2,1)S(1)}, bf16[32,1792]{1,0:T(8,128)(2,1)S(1)}, u32[]{:S(2)}, u32[]{:S(2)}) collective-permute-start(bf16[32,1792]{1,0:T(8,128)(2,1)S(1)} %get-tuple-element.147), channel_id=1, source_target_pairs={{0,8},{1,9},{2,10},{3,11},{4,12},{5,13},{6,14},{7,15},{8,0},{9,1},... | collective-permute-start | bytes 344072 | tf_op jit(solution)/shard_map/ppermute | solution.py:24
  117.2 1.2 collective-permute-done.25
  118.4 1.5 %add_convert_fusion.2 = bf16[128,1792]{1,0:T(8,128)(2,1)S(1)} fusion(bf16[256,1792]{1,0:T(8,128)(2,1)} %collective-permute-done.26, bf16[256,1792]{1,0:T(8,128)(2,1)} %collective-permute-done.25, bf16[256,1792]{1,0:T(8,128)(2,1)} %copy-done.4), kind=kLoop, calls=%fused_computation.2 | loop fusion | flops 1376256 | bytes 1835008 | tf_op jit(solution)/shard_map/convert_element_type | solution.py:499
  119.9 1.0 collective-permute-start.27
  120.9 1.3 copy-done.3
  122.2 3.1 %attend_moved.1 = bf16[16,64,512]{2,1,0:T(8,128)(2,1)} custom-call(s32[2]{0:T(128)S(1)} %pad_add_fusion.spot_ref, s32[512]{0:T(512)S(1)} %copy-done.9, s32[8]{0:T(128)S(1)} %copy-done.14, bf16[16,64,576]{2,1,0:T(8,128)(2,1)S(1)} %copy-done.3, bf16[16,576,128]{2,1,0:T(8,128)(2,1)S(1)} %bitcast.22, ...), custom_call_target="tpu_custom_call", output_to_operand_aliasing={{}: (8, {})} | custom-call | flops 68719476736 | bytes 1024 | tf_op jit(solution)/shard_map/attend_moved/pallas_call | solution.py:411
  125.3 3.1 %collective-permute-done.27 = bf16[128,1792]{1,0:T(8,128)(2,1)S(1)} collective-permute-done((bf16[128,1792]{1,0:T(8,128)(2,1)S(1)}, bf16[128,1792]{1,0:T(8,128)(2,1)S(1)}, u32[]{:S(2)}, u32[]{:S(2)}) %collective-permute-start.27) | collective-permute-done | bytes 458784 | tf_op jit(solution)/shard_map/ppermute | solution.py:24
  128.4 1.4 add_convert_fusion.7
  129.8 1.1 collective-permute-start.32
  131.7 1.6 %collective-permute-start.34 = (bf16[32,1792]{1,0:T(8,128)(2,1)S(1)}, bf16[32,1792]{1,0:T(8,128)(2,1)S(1)}, u32[]{:S(2)}, u32[]{:S(2)}) collective-permute-start(bf16[32,1792]{1,0:T(8,128)(2,1)S(1)} %get-tuple-element.145), channel_id=1, source_target_pairs={{0,8},{1,9},{2,10},{3,11},{4,12},{5,13},{6,14},{7,15},{8,0},{9,1},... | collective-permute-start | bytes 344072 | tf_op jit(solution)/shard_map/ppermute | solution.py:24
  133.3 1.1 add_convert_fusion.8
  134.6 4.9 %collective-permute-done.32 = bf16[32,1792]{1,0:T(8,128)(2,1)S(1)} collective-permute-done((bf16[32,1792]{1,0:T(8,128)(2,1)S(1)}, bf16[32,1792]{1,0:T(8,128)(2,1)S(1)}, u32[]{:S(2)}, u32[]{:S(2)}) %collective-permute-start.32) | collective-permute-done | bytes 114720 | tf_op jit(solution)/shard_map/ppermute | solution.py:24
  139.4 1.2 collective-permute-done.34
  140.7 1.1 add_convert_fusion.4
  141.9 1.2 collective-permute-done.35
  (106 shorter events, 10.3 us)
Async XLA Ops:
  1.6 2.8 %collective-permute-start = (bf16[2,16,1792]{2,1,0:T(8,128)(2,1)S(1)}, bf16[2,16,1792]{2,1,0:T(8,128)(2,1)S(1)}, u32[]{:S(2)}, u32[]{:S(2)}) collective-permute-start(bf16[2,16,1792]{2,1,0:T(8,128)(2,1)S(1)} %get-tuple-element.153), channel_id=1, source_target_pairs={{0,1},{1,0},{2,3},{3,2},{4,5},{5,4},{6,7},{7,6},{8,9},{9,8},{10,11... | collective-permute-start | bytes 344072 | tf_op jit(solution)/shard_map/ppermute | solution.py:24
  4.5 13.2 %collective-permute-start.1 = (bf16[32,1920]{1,0:T(8,128)(2,1)S(1)}, bf16[32,1920]{1,0:T(8,128)(2,1)S(1)}, u32[]{:S(2)}, u32[]{:S(2)}) collective-permute-start(bf16[32,1920]{1,0:T(8,128)(2,1)S(1)} %pad_maximum_fusion.3), channel_id=1, source_target_pairs={{0,16},{1,17},{2,18},{3,19},{4,20},{5,21},{6,22},{7,23},{8,24},{9,... | collective-permute-start | bytes 368648 | tf_op jit(solution)/shard_map/ppermute | solution.py:24
  8.2 9.5 %collective-permute-start.2 = (bf16[32,1920]{1,0:T(8,128)(2,1)S(1)}, bf16[32,1920]{1,0:T(8,128)(2,1)S(1)}, u32[]{:S(2)}, u32[]{:S(2)}) collective-permute-start(bf16[32,1920]{1,0:T(8,128)(2,1)S(1)} %pad_maximum_fusion.3), channel_id=1, source_target_pairs={{0,24},{1,25},{2,26},{3,27},{4,28},{5,29},{6,30},{7,31},{8,16},{9,... | collective-permute-start | bytes 368648 | tf_op jit(solution)/shard_map/ppermute | solution.py:24
  9.5 9.3 %collective-permute-start.3 = (bf16[32,1920]{1,0:T(8,128)(2,1)S(1)}, bf16[32,1920]{1,0:T(8,128)(2,1)S(1)}, u32[]{:S(2)}, u32[]{:S(2)}) collective-permute-start(bf16[32,1920]{1,0:T(8,128)(2,1)S(1)} %pad_maximum_fusion.3), channel_id=1, source_target_pairs={{0,8},{1,9},{2,10},{3,11},{4,12},{5,13},{6,14},{7,15},{8,0},{9,1},... | collective-permute-start | bytes 368648 | tf_op jit(solution)/shard_map/ppermute | solution.py:24
  9.7 24.4 %copy-start.2 = (bf16[16,64,576]{2,1,0:T(8,128)(2,1)S(1)}, bf16[16,64,576]{2,1,0:T(8,128)(2,1)}, u32[]{:S(2)}) copy-start(bf16[16,64,576]{2,1,0:T(8,128)(2,1)} %query_ref.1) | copy-start | bytes 3538948
  12.7 16.7 %copy-start.17 = (bf16[16,576]{1,0:T(8,128)(2,1)S(1)}, bf16[16,576]{1,0:T(8,128)(2,1)}, u32[]{:S(2)}) copy-start(bf16[16,576]{1,0:T(8,128)(2,1)} %param.16) | copy-start | bytes 55300
  12.8 21.4 %copy-start = (bf16[16,128,576]{1,2,0:T(8,128)(2,1)S(1)}, bf16[16,128,576]{1,2,0:T(8,128)(2,1)}, u32[]{:S(2)}) copy-start(bf16[16,128,576]{1,2,0:T(8,128)(2,1)} %param.17) | copy-start | bytes 7077892
  12.8 21.4 %copy-start.8 = (s32[512]{0:T(512)S(1)}, s32[512]{0:T(512)}, u32[]{:S(2)}) copy-start(s32[512]{0:T(512)} %length_ref.3) | copy-start | bytes 6148
  18.8 8.9 %collective-permute-start.4 = (bf16[128,1920]{1,0:T(8,128)(2,1)S(1)}, bf16[128,1920]{1,0:T(8,128)(2,1)S(1)}, u32[]{:S(2)}, u32[]{:S(2)}) collective-permute-start(bf16[128,1920]{1,0:T(8,128)(2,1)S(1)} %pad_maximum_fusion), channel_id=1, source_target_pairs={{0,4},{1,3},{2,6},{3,1},{4,0},{5,7},{6,2},{7,5},{8,12},{9,11},{10,... | collective-permute-start | bytes 1474568 | tf_op jit(solution)/shard_map/ppermute | solution.py:24
  27.8 15.7 %collective-permute-start.5 = (bf16[256,1920]{1,0:T(8,128)(2,1)S(1)}, bf16[256,1920]{1,0:T(8,128)(2,1)S(1)}, u32[]{:S(2)}, u32[]{:S(2)}) collective-permute-start(bf16[256,1920]{1,0:T(8,128)(2,1)S(1)} %constant_dynamic-update-slice_fusion.refs_0_), channel_id=1, source_target_pairs={{0,2},{1,5},{2,0},{3,7},{4,6},{5,1},{6,4},{7,3},{8,10},{9,13},{10,... | collective-permute-start | bytes 2949128 | tf_op jit(solution)/shard_map/ppermute | solution.py:24
  29.4 14.1 %collective-permute-start.6 = (bf16[256,1920]{1,0:T(8,128)(2,1)S(1)}, bf16[256,1920]{1,0:T(8,128)(2,1)S(1)}, u32[]{:S(2)}, u32[]{:S(2)}) collective-permute-start(bf16[256,1920]{1,0:T(8,128)(2,1)S(1)} %constant_dynamic-update-slice_fusion.refs_0_), channel_id=1, source_target_pairs={{0,1},{1,0},{2,3},{3,2},{4,5},{5,4},{6,7},{7,6},{8,9},{9,8},{10,11... | collective-permute-start | bytes 2949128 | tf_op jit(solution)/shard_map/ppermute | solution.py:24
  29.5 12.9 %collective-permute-start.7 = (bf16[32,1792]{1,0:T(8,128)(2,1)S(1)}, bf16[32,1792]{1,0:T(8,128)(2,1)S(1)}, u32[]{:S(2)}, u32[]{:S(2)}) collective-permute-start(bf16[32,1792]{1,0:T(8,128)(2,1)S(1)} %get-tuple-element.83), channel_id=1, source_target_pairs={{0,16},{1,17},{2,18},{3,19},{4,20},{5,21},{6,22},{7,23},{8,24},{9,... | collective-permute-start | bytes 344072 | tf_op jit(solution)/shard_map/ppermute | solution.py:24
  33.4 9.0 %collective-permute-start.8 = (bf16[32,1792]{1,0:T(8,128)(2,1)S(1)}, bf16[32,1792]{1,0:T(8,128)(2,1)S(1)}, u32[]{:S(2)}, u32[]{:S(2)}) collective-permute-start(bf16[32,1792]{1,0:T(8,128)(2,1)S(1)} %get-tuple-element.83), channel_id=1, source_target_pairs={{0,24},{1,25},{2,26},{3,27},{4,28},{5,29},{6,30},{7,31},{8,16},{9,... | collective-permute-start | bytes 344072 | tf_op jit(solution)/shard_map/ppermute | solution.py:24
  33.9 9.6 %collective-permute-start.9 = (bf16[32,1792]{1,0:T(8,128)(2,1)S(1)}, bf16[32,1792]{1,0:T(8,128)(2,1)S(1)}, u32[]{:S(2)}, u32[]{:S(2)}) collective-permute-start(bf16[32,1792]{1,0:T(8,128)(2,1)S(1)} %get-tuple-element.83), channel_id=1, source_target_pairs={{0,8},{1,9},{2,10},{3,11},{4,12},{5,13},{6,14},{7,15},{8,0},{9,1},... | collective-permute-start | bytes 344072 | tf_op jit(solution)/shard_map/ppermute | solution.py:24
  34.1 14.0 %copy-start.19 = (bf16[2,576,128]{2,1,0:T(8,128)(2,1)S(1)}, bf16[2,576,128]{2,1,0:T(8,128)(2,1)}, u32[]{:S(2)}) copy-start(bf16[2,576,128]{2,1,0:T(8,128)(2,1)} %get-tuple-element.91) | copy-start | bytes 884740
  43.5 2.6 %collective-permute-start.10 = (bf16[256,1920]{1,0:T(8,128)(2,1)S(1)}, bf16[256,1920]{1,0:T(8,128)(2,1)S(1)}, u32[]{:S(2)}, u32[]{:S(2)}) collective-permute-start(bf16[256,1920]{1,0:T(8,128)(2,1)S(1)} %collective-permute-done.5.refs_1_), channel_id=1, source_target_pairs={{0,1},{1,0},{2,3},{3,2},{4,5},{5,4},{6,7},{7,6},{8,9},{9,8},{10,11... | collective-permute-start | bytes 2949128 | tf_op jit(solution)/shard_map/ppermute | solution.py:24
  43.5 23.9 %slice-start = ((s8[7340032]{0:T(1024)(128)(4,1)}), s8[4194304]{0:T(1024)(128)(4,1)S(1)}, s32[]{:S(2)}) async-start(s8[7340032]{0:T(1024)(128)(4,1)} %bitcast.23), calls=%async_computation | async-start | bytes 8388608
  46.1 20.6 %collective-permute-start.11 = (bf16[128,1792]{1,0:T(8,128)(2,1)S(1)}, bf16[128,1792]{1,0:T(8,128)(2,1)S(1)}, u32[]{:S(2)}, u32[]{:S(2)}) collective-permute-start(bf16[128,1792]{1,0:T(8,128)(2,1)S(1)} %pad_maximum_fusion.1.refs_0_), channel_id=1, source_target_pairs={{0,2},{1,5},{2,0},{3,7},{4,6},{5,1},{6,4},{7,3},{8,10},{9,13},{10,... | collective-permute-start | bytes 1376264 | tf_op jit(solution)/shard_map/ppermute | solution.py:24
  46.6 20.1 %collective-permute-start.13 = (bf16[128,1792]{1,0:T(8,128)(2,1)S(1)}, bf16[128,1792]{1,0:T(8,128)(2,1)S(1)}, u32[]{:S(2)}, u32[]{:S(2)}) collective-permute-start(bf16[128,1792]{1,0:T(8,128)(2,1)S(1)} %pad_maximum_fusion.1.refs_0_), channel_id=1, source_target_pairs={{0,4},{1,3},{2,6},{3,1},{4,0},{5,7},{6,2},{7,5},{8,12},{9,11},{10,... | collective-permute-start | bytes 1376264 | tf_op jit(solution)/shard_map/ppermute | solution.py:24
  48.1 17.8 %collective-permute-start.12 = (bf16[2,576,128]{2,1,0:T(8,128)(2,1)S(1)}, bf16[2,576,128]{2,1,0:T(8,128)(2,1)S(1)}, u32[]{:S(2)}, u32[]{:S(2)}) collective-permute-start(bf16[2,576,128]{2,1,0:T(8,128)(2,1)S(1)} %copy-done.19), channel_id=1, source_target_pairs={{0,16},{1,17},{2,18},{3,19},{4,20},{5,21},{6,22},{7,23},{8,24},{9,... | collective-permute-start | bytes 884744 | tf_op jit(solution)/shard_map/ppermute | solution.py:24
  51.5 15.9 %slice-start.1 = ((s8[7340032]{0:T(1024)(128)(4,1)}), s8[3145728]{0:T(1024)(128)(4,1)S(1)}, s32[]{:S(2)}) async-start(s8[7340032]{0:T(1024)(128)(4,1)} %bitcast.23), calls=%async_computation.1 | async-start | bytes 6291456
  66.7 9.1 %collective-permute-start.18 = (bf16[128,1792]{1,0:T(8,128)(2,1)S(1)}, bf16[128,1792]{1,0:T(8,128)(2,1)S(1)}, u32[]{:S(2)}, u32[]{:S(2)}) collective-permute-start(bf16[128,1792]{1,0:T(8,128)(2,1)S(1)} %collective-permute-done.13.refs_1_), channel_id=1, source_target_pairs={{0,1},{1,0},{2,3},{3,2},{4,5},{5,4},{6,7},{7,6},{8,9},{9,8},{10,11... | collective-permute-start | bytes 1376264 | tf_op jit(solution)/shard_map/ppermute | solution.py:24
  66.7 9.1 %collective-permute-start.19 = (bf16[128,1792]{1,0:T(8,128)(2,1)S(1)}, bf16[128,1792]{1,0:T(8,128)(2,1)S(1)}, u32[]{:S(2)}, u32[]{:S(2)}) collective-permute-start(bf16[128,1792]{1,0:T(8,128)(2,1)S(1)} %collective-permute-done.13.refs_1_), channel_id=1, source_target_pairs={{0,2},{1,5},{2,0},{3,7},{4,6},{5,1},{6,4},{7,3},{8,10},{9,13},{10,... | collective-permute-start | bytes 1376264 | tf_op jit(solution)/shard_map/ppermute | solution.py:24
  67.4 4.3 %collective-permute-start.14 = (bf16[128,1792]{1,0:T(8,128)(2,1)S(1)}, bf16[128,1792]{1,0:T(8,128)(2,1)S(1)}, u32[]{:S(2)}, u32[]{:S(2)}) collective-permute-start(bf16[128,1792]{1,0:T(8,128)(2,1)S(1)} %collective-permute-done.11.refs_2_), channel_id=1, source_target_pairs={{0,1},{1,0},{2,3},{3,2},{4,5},{5,4},{6,7},{7,6},{8,9},{9,8},{10,11... | collective-permute-start | bytes 1376264 | tf_op jit(solution)/shard_map/ppermute | solution.py:24
  71.1 4.7 %collective-permute-start.15 = (bf16[256,1792]{1,0:T(8,128)(2,1)S(1)}, bf16[256,1792]{1,0:T(8,128)(2,1)S(1)}, u32[]{:S(2)}, u32[]{:S(2)}) collective-permute-start(bf16[256,1792]{1,0:T(8,128)(2,1)S(1)} %get-tuple-element.102), channel_id=1, source_target_pairs={{0,1},{1,0},{2,3},{3,2},{4,5},{5,4},{6,7},{7,6},{8,9},{9,8},{10,11... | collective-permute-start | bytes 2752520 | tf_op jit(solution)/shard_map/ppermute | solution.py:24
  71.6 4.2 %collective-permute-start.16 = (bf16[256,1792]{1,0:T(8,128)(2,1)S(1)}, bf16[256,1792]{1,0:T(8,128)(2,1)S(1)}, u32[]{:S(2)}, u32[]{:S(2)}) collective-permute-start(bf16[256,1792]{1,0:T(8,128)(2,1)S(1)} %get-tuple-element.103), channel_id=1, source_target_pairs={{0,1},{1,0},{2,3},{3,2},{4,5},{5,4},{6,7},{7,6},{8,9},{9,8},{10,11... | collective-permute-start | bytes 2752520 | tf_op jit(solution)/shard_map/ppermute | solution.py:24
  71.7 4.1 %collective-permute-start.17 = (bf16[128,1792]{1,0:T(8,128)(2,1)S(1)}, bf16[128,1792]{1,0:T(8,128)(2,1)S(1)}, u32[]{:S(2)}, u32[]{:S(2)}) collective-permute-start(bf16[128,1792]{1,0:T(8,128)(2,1)S(1)} %pad_maximum_fusion.1.refs_0_), channel_id=1, source_target_pairs={{0,1},{1,0},{2,3},{3,2},{4,5},{5,4},{6,7},{7,6},{8,9},{9,8},{10,11... | collective-permute-start | bytes 1376264 | tf_op jit(solution)/shard_map/ppermute | solution.py:24
  75.8 23.4 %copy-start.15 = (bf16[256,1792]{1,0:T(8,128)(2,1)}, bf16[256,1792]{1,0:T(8,128)(2,1)S(1)}, u32[]{:S(2)}) copy-start(bf16[256,1792]{1,0:T(8,128)(2,1)S(1)} %collective-permute-done.15) | copy-start | bytes 2752516
  75.9 1.9 %collective-permute-start.20 = (bf16[128,1792]{1,0:T(8,128)(2,1)S(1)}, bf16[128,1792]{1,0:T(8,128)(2,1)S(1)}, u32[]{:S(2)}, u32[]{:S(2)}) collective-permute-start(bf16[128,1792]{1,0:T(8,128)(2,1)S(1)} %collective-permute-done.19.refs_3_), channel_id=1, source_target_pairs={{0,1},{1,0},{2,3},{3,2},{4,5},{5,4},{6,7},{7,6},{8,9},{9,8},{10,11... | collective-permute-start | bytes 1376264 | tf_op jit(solution)/shard_map/ppermute | solution.py:24
  77.7 16.9 %collective-permute-start.21 = (bf16[256,1792]{1,0:T(8,128)(2,1)S(1)}, bf16[256,1792]{1,0:T(8,128)(2,1)S(1)}, u32[]{:S(2)}, u32[]{:S(2)}) collective-permute-start(bf16[256,1792]{1,0:T(8,128)(2,1)S(1)} %add_convert_fusion.1), channel_id=1, source_target_pairs={{0,2},{1,5},{2,0},{3,7},{4,6},{5,1},{6,4},{7,3},{8,10},{9,13},{10,... | collective-permute-start | bytes 2752520 | tf_op jit(solution)/shard_map/ppermute | solution.py:24
  79.1 15.6 %collective-permute-start.22 = (bf16[2,576,128]{2,1,0:T(8,128)(2,1)S(1)}, bf16[2,576,128]{2,1,0:T(8,128)(2,1)S(1)}, u32[]{:S(2)}, u32[]{:S(2)}) collective-permute-start(bf16[2,576,128]{2,1,0:T(8,128)(2,1)S(1)} %copy-done.18), channel_id=1, source_target_pairs={{0,16},{1,17},{2,18},{3,19},{4,20},{5,21},{6,22},{7,23},{8,24},{9,... | collective-permute-start | bytes 884744 | tf_op jit(solution)/shard_map/ppermute | solution.py:24
  99.2 2.5 %collective-permute-start.24 = (bf16[256,1792]{1,0:T(8,128)(2,1)S(1)}, bf16[256,1792]{1,0:T(8,128)(2,1)S(1)}, u32[]{:S(2)}, u32[]{:S(2)}) collective-permute-start(bf16[256,1792]{1,0:T(8,128)(2,1)S(1)} %get-tuple-element.126), channel_id=1, source_target_pairs={{0,1},{1,0},{2,3},{3,2},{4,5},{5,4},{6,7},{7,6},{8,9},{9,8},{10,11... | collective-permute-start | bytes 2752520 | tf_op jit(solution)/shard_map/ppermute | solution.py:24
  100.3 11.9 %collective-permute-start.23 = (bf16[128,1792]{1,0:T(8,128)(2,1)}, bf16[128,1792]{1,0:T(8,128)(2,1)}, u32[]{:S(2)}, u32[]{:S(2)}) collective-permute-start(bf16[128,1792]{1,0:T(8,128)(2,1)} %add_convert_fusion.3), channel_id=1, source_target_pairs={{0,4},{1,3},{2,6},{3,1},{4,0},{5,7},{6,2},{7,5},{8,12},{9,11},{10,... | collective-permute-start | bytes 1376264 | tf_op jit(solution)/shard_map/ppermute | solution.py:24
  102.8 15.6 %collective-permute-start.25 = (bf16[256,1792]{1,0:T(8,128)(2,1)}, bf16[256,1792]{1,0:T(8,128)(2,1)}, u32[]{:S(2)}, u32[]{:S(2)}) collective-permute-start(bf16[256,1792]{1,0:T(8,128)(2,1)} %add_convert_fusion), channel_id=1, source_target_pairs={{0,2},{1,5},{2,0},{3,7},{4,6},{5,1},{6,4},{7,3},{8,10},{9,13},{10,... | collective-permute-start | bytes 2752520 | tf_op jit(solution)/shard_map/ppermute | solution.py:24
  109.9 10.9 %copy-start.1 = (bf16[16,128,576]{1,2,0:T(8,128)(2,1)S(1)}, bf16[16,128,576]{1,2,0:T(8,128)(2,1)}, u32[]{:S(2)}) copy-start(bf16[16,128,576]{1,2,0:T(8,128)(2,1)} %param.17) | copy-start | bytes 7077892
  109.9 10.9 %copy-start.7 = (bf16[16,1,576]{2,1,0:T(2,128)(2,1)S(1)}, bf16[16,1,576]{2,1,0:T(2,128)(2,1)}, u32[]{:S(2)}) copy-start(bf16[16,1,576]{2,1,0:T(2,128)(2,1)} %copy-done.6) | copy-start | bytes 55300
  109.9 10.9 %copy-start.9 = (s32[512]{0:T(512)S(1)}, s32[512]{0:T(512)}, u32[]{:S(2)}) copy-start(s32[512]{0:T(512)} %length_ref.3) | copy-start | bytes 6148
  109.9 10.9 %copy-start.14 = (s32[8]{0:T(128)S(1)}, s32[8]{0:T(128)}, u32[]{:S(2)}) copy-start(s32[8]{0:T(128)} %get-tuple-element.134.info_ref) | copy-start | bytes 100
  109.9 8.5 %collective-permute-start.26 = (bf16[256,1792]{1,0:T(8,128)(2,1)}, bf16[256,1792]{1,0:T(8,128)(2,1)}, u32[]{:S(2)}, u32[]{:S(2)}) collective-permute-start(bf16[256,1792]{1,0:T(8,128)(2,1)} %get-tuple-element.131), channel_id=1, source_target_pairs={{0,1},{1,0},{2,3},{3,2},{4,5},{5,4},{6,7},{7,6},{8,9},{9,8},{10,11... | collective-permute-start | bytes 2752520 | tf_op jit(solution)/shard_map/ppermute | solution.py:24
  113.7 11.7 %collective-permute-start.28 = (bf16[32,1792]{1,0:T(8,128)(2,1)S(1)}, bf16[32,1792]{1,0:T(8,128)(2,1)S(1)}, u32[]{:S(2)}, u32[]{:S(2)}) collective-permute-start(bf16[32,1792]{1,0:T(8,128)(2,1)S(1)} %get-tuple-element.149), channel_id=1, source_target_pairs={{0,16},{1,17},{2,18},{3,19},{4,20},{5,21},{6,22},{7,23},{8,24},{9,... | collective-permute-start | bytes 344072 | tf_op jit(solution)/shard_map/ppermute | solution.py:24
  114.8 10.6 %collective-permute-start.29 = (bf16[32,1792]{1,0:T(8,128)(2,1)S(1)}, bf16[32,1792]{1,0:T(8,128)(2,1)S(1)}, u32[]{:S(2)}, u32[]{:S(2)}) collective-permute-start(bf16[32,1792]{1,0:T(8,128)(2,1)S(1)} %get-tuple-element.148), channel_id=1, source_target_pairs={{0,24},{1,25},{2,26},{3,27},{4,28},{5,29},{6,30},{7,31},{8,16},{9,... | collective-permute-start | bytes 344072 | tf_op jit(solution)/shard_map/ppermute | solution.py:24
  115.5 9.9 %collective-permute-start.30 = (bf16[32,1792]{1,0:T(8,128)(2,1)S(1)}, bf16[32,1792]{1,0:T(8,128)(2,1)S(1)}, u32[]{:S(2)}, u32[]{:S(2)}) collective-permute-start(bf16[32,1792]{1,0:T(8,128)(2,1)S(1)} %get-tuple-element.147), channel_id=1, source_target_pairs={{0,8},{1,9},{2,10},{3,11},{4,12},{5,13},{6,14},{7,15},{8,0},{9,1},... | collective-permute-start | bytes 344072 | tf_op jit(solution)/shard_map/ppermute | solution.py:24
  119.9 8.5 %collective-permute-start.27 = (bf16[128,1792]{1,0:T(8,128)(2,1)S(1)}, bf16[128,1792]{1,0:T(8,128)(2,1)S(1)}, u32[]{:S(2)}, u32[]{:S(2)}) collective-permute-start(bf16[128,1792]{1,0:T(8,128)(2,1)S(1)} %add_convert_fusion.2), channel_id=1, source_target_pairs={{0,4},{1,3},{2,6},{3,1},{4,0},{5,7},{6,2},{7,5},{8,12},{9,11},{10,... | collective-permute-start | bytes 1376264 | tf_op jit(solution)/shard_map/ppermute | solution.py:24
  129.8 9.6 %collective-permute-start.32 = (bf16[32,1792]{1,0:T(8,128)(2,1)S(1)}, bf16[32,1792]{1,0:T(8,128)(2,1)S(1)}, u32[]{:S(2)}, u32[]{:S(2)}) collective-permute-start(bf16[32,1792]{1,0:T(8,128)(2,1)S(1)} %get-tuple-element.144), channel_id=1, source_target_pairs={{0,16},{1,17},{2,18},{3,19},{4,20},{5,21},{6,22},{7,23},{8,24},{9,... | collective-permute-start | bytes 344072 | tf_op jit(solution)/shard_map/ppermute | solution.py:24
  130.9 8.6 %collective-permute-start.33 = (bf16[32,1792]{1,0:T(8,128)(2,1)S(1)}, bf16[32,1792]{1,0:T(8,128)(2,1)S(1)}, u32[]{:S(2)}, u32[]{:S(2)}) collective-permute-start(bf16[32,1792]{1,0:T(8,128)(2,1)S(1)} %get-tuple-element.146), channel_id=1, source_target_pairs={{0,24},{1,25},{2,26},{3,27},{4,28},{5,29},{6,30},{7,31},{8,16},{9,... | collective-permute-start | bytes 344072 | tf_op jit(solution)/shard_map/ppermute | solution.py:24
  131.7 9.0 %collective-permute-start.34 = (bf16[32,1792]{1,0:T(8,128)(2,1)S(1)}, bf16[32,1792]{1,0:T(8,128)(2,1)S(1)}, u32[]{:S(2)}, u32[]{:S(2)}) collective-permute-start(bf16[32,1792]{1,0:T(8,128)(2,1)S(1)} %get-tuple-element.145), channel_id=1, source_target_pairs={{0,8},{1,9},{2,10},{3,11},{4,12},{5,13},{6,14},{7,15},{8,0},{9,1},... | collective-permute-start | bytes 344072 | tf_op jit(solution)/shard_map/ppermute | solution.py:24
  134.5 7.3 %collective-permute-start.31 = (bf16[16,1792]{1,0:T(8,128)(2,1)S(1)}, bf16[16,1792]{1,0:T(8,128)(2,1)S(1)}, u32[]{:S(2)}, u32[]{:S(2)}) collective-permute-start(bf16[16,1792]{1,0:T(8,128)(2,1)S(1)} %get-tuple-element.155), channel_id=1, source_target_pairs={{0,1},{1,0},{2,3},{3,2},{4,5},{5,4},{6,7},{7,6},{8,9},{9,8},{10,11... | collective-permute-start | bytes 172040 | tf_op jit(solution)/shard_map/ppermute | solution.py:24
  141.7 1.3 collective-permute-start.35
  (10 other events, 53.9 us)

commit v7 on v6

--- a/solution.py
+++ b/solution.py
@@ -552,10 +552,8 @@
     high0, sib_low0, context, *came1 = window(high0, sib_low0, context, *came1)
 
     line1 = jnp.concatenate([block1] + came1, axis=0)
+    low0, high0, sib_low0, line1, leave_a = window(low0, high0, sib_low0, line1, leave_a)
     sib_high0 = exchange(high0, sibling)
-    low0, high0, sib_low0, sib_high0, line1, leave_a = window(
-        low0, high0, sib_low0, sib_high0, line1, leave_a
-    )
 
     low1 = [line1]
     for masks in bottom:
@@ -579,8 +577,8 @@
     sib_low1, rest1 = flat[:split], flat[split:]
 
     send0 = rounded_sum([my_high0, they_high0])
+    send0, leave_b, *rest1 = window(send0, leave_b, *rest1)
     sib_rest1 = [swap(line) for line in rest1]
-    send0, leave_b, *sib_rest1 = window(send0, leave_b, *sib_rest1)
 
     came = exchange(send0, top_masks)
     cache_b = exchange(leave_b, (far, far))

time: 144 us -> 141 us (0.979)
  waiting for transfers between devices: 36.7 us -> 32.8 us
    ppermute x36, waiting for transfers between devices: 36.7 us -> 32.8 us  [exchange(): return lax.ppermute(value, AXES, pairs)]
  transfers between devices with their start and end apart: 36 -> 36, of which waited for: 15 -> 13; matrix products, arithmetic and copies ran while one was open for 6% -> 6% of each run, Pallas kernels for 38% -> 39%
where the time goes in v7:
time: 141 us; the launch traced here: 140 us
  Pallas kernels  58.6 us (42%)
  starting transfers between devices  33 us (23%)
  waiting for transfers between devices  32.8 us (23%)
  other arithmetic  10.6 us (8%)
  local copies, waits for them, and re-layouts  4.28 us (3%)
    ppermute x36, starting transfers between devices, exchange(): return lax.ppermute(value, AXES, pairs)  33 us
    ppermute x36, waiting for transfers between devices, exchange(): return lax.ppermute(value, AXES, pairs)  32.8 us
    pallas_call x2, Pallas kernels, expert_up(): pl.pallas_call(functools.partial(up_body, line_rows, piece_counts, with_m...  28.1 us
    pallas_call x4, Pallas kernels, expert_down(): pl.pallas_call(functools.partial(down_body, line_rows, jobs), grid_spec=p...  17 us
    convert_element_type x8, other arithmetic, per_device(): rounded_sum = lambda terms: add(terms).astype(jnp.bfloat16)  8.83 us
    pallas_call x1, Pallas kernels, attend(): pl.pallas_call(functools.partial(attend_body, group), grid_spec=pltpu.Pre...  5.96 us
    unnamed x48, local copies, waits for them, and re-layouts  3.17 us
    pallas_call x1, Pallas kernels, attend_moved(): pl.pallas_call(functools.partial(attend_moved_body, row_count), grid_spec...  3.13 us
  transfers between devices with their start and end apart: 36, of which 13 were waited for; matrix products, arithmetic and copies ran while one was open for 6% of the time, Pallas kernels for 39%

profile of v7, /device:TPU:0, one launch (start us, length us, event | category | flops | bytes accessed | tf_op | source)
XLA Modules:
  0.0 140.4 jit_solution(10361195443962078545)
XLA Ops:
  0.7 1.0 constant_dynamic-slice_fusion.3
  2.2 1.5 %meta_columns.1 = bf16[16,128]{1,0:T(8,128)(2,1)} custom-call(s32[2,8,16]{2,1,0:T(8,128)} %bitcast.34, f32[2,8,16]{2,1,0:T(8,128)} %bitcast.35), custom_call_target="tpu_custom_call" | custom-call | tf_op jit(solution)/shard_map/meta_columns/pallas_call | solution.py:273
  4.5 3.7 %collective-permute-start.1 = (bf16[32,1920]{1,0:T(8,128)(2,1)S(1)}, bf16[32,1920]{1,0:T(8,128)(2,1)S(1)}, u32[]{:S(2)}, u32[]{:S(2)}) collective-permute-start(bf16[32,1920]{1,0:T(8,128)(2,1)S(1)} %pad_maximum_fusion.3), channel_id=1, source_target_pairs={{0,16},{1,17},{2,18},{3,19},{4,20},{5,21},{6,22},{7,23},{8,24},{9,... | collective-permute-start | bytes 368648 | tf_op jit(solution)/shard_map/ppermute | solution.py:24
  8.2 1.3 collective-permute-start.2
  9.7 3.0 %pick_caches.1 = (bf16[2,576,128]{2,1,0:T(8,128)(2,1)}, bf16[2,576,128]{2,1,0:T(8,128)(2,1)}, s32[8]{0:T(128)}) custom-call(s32[16]{0:T(128)} %swapped_ref, bf16[16,576,128]{2,1,0:T(8,128)(2,1)} %bitcast.20), custom_call_target="tpu_custom_call" | custom-call | tf_op jit(solution)/shard_map/pick_caches/pallas_call | solution.py:313
  12.8 4.8 %collective-permute-done.1 = bf16[32,1920]{1,0:T(8,128)(2,1)S(1)} collective-permute-done((bf16[32,1920]{1,0:T(8,128)(2,1)S(1)}, bf16[32,1920]{1,0:T(8,128)(2,1)S(1)}, u32[]{:S(2)}, u32[]{:S(2)}) %collective-permute-start.1) | collective-permute-done | bytes 122912 | tf_op jit(solution)/shard_map/ppermute | solution.py:24
  17.7 1.1 collective-permute-done.3
  18.8 1.6 %collective-permute-start.4 = (bf16[128,1920]{1,0:T(8,128)(2,1)S(1)}, bf16[128,1920]{1,0:T(8,128)(2,1)S(1)}, u32[]{:S(2)}, u32[]{:S(2)}) collective-permute-start(bf16[128,1920]{1,0:T(8,128)(2,1)S(1)} %pad_maximum_fusion), channel_id=1, source_target_pairs={{0,4},{1,3},{2,6},{3,1},{4,0},{5,7},{6,2},{7,5},{8,12},{9,11},{10,... | collective-permute-start | bytes 1474568 | tf_op jit(solution)/shard_map/ppermute | solution.py:24
  20.5 7.2 %collective-permute-done.4 = bf16[128,1920]{1,0:T(8,128)(2,1)S(1)} collective-permute-done((bf16[128,1920]{1,0:T(8,128)(2,1)S(1)}, bf16[128,1920]{1,0:T(8,128)(2,1)S(1)}, u32[]{:S(2)}, u32[]{:S(2)}) %collective-permute-start.4) | collective-permute-done | bytes 491552 | tf_op jit(solution)/shard_map/ppermute | solution.py:24
  27.8 1.6 %collective-permute-start.5 = (bf16[256,1920]{1,0:T(8,128)(2,1)S(1)}, bf16[256,1920]{1,0:T(8,128)(2,1)S(1)}, u32[]{:S(2)}, u32[]{:S(2)}) collective-permute-start(bf16[256,1920]{1,0:T(8,128)(2,1)S(1)} %constant_dynamic-update-slice_fusion.refs_0_), channel_id=1, source_target_pairs={{0,2},{1,5},{2,0},{3,7},{4,6},{5,1},{6,4},{7,3},{8,10},{9,13},{10,... | collective-permute-start | bytes 2949128 | tf_op jit(solution)/shard_map/ppermute | solution.py:24
  29.5 3.9 %collective-permute-start.7 = (bf16[32,1792]{1,0:T(8,128)(2,1)S(1)}, bf16[32,1792]{1,0:T(8,128)(2,1)S(1)}, u32[]{:S(2)}, u32[]{:S(2)}) collective-permute-start(bf16[32,1792]{1,0:T(8,128)(2,1)S(1)} %get-tuple-element.82), channel_id=1, source_target_pairs={{0,16},{1,17},{2,18},{3,19},{4,20},{5,21},{6,22},{7,23},{8,24},{9,... | collective-permute-start | bytes 344072 | tf_op jit(solution)/shard_map/ppermute | solution.py:24
  34.2 6.0 %attend.1.old_ref = bf16[16,64,512]{2,1,0:T(8,128)(2,1)} custom-call(s32[2]{0:T(128)S(1)} %pad_add_fusion.spot_ref, s32[512]{0:T(512)S(1)} %copy-done.8, bf16[16,64,576]{2,1,0:T(8,128)(2,1)S(1)} %copy-done.2, bf16[16,576,128]{2,1,0:T(8,128)(2,1)S(1)} %bitcast.21, bf16[16,1,576]{2,1,0:T(2,128)(2,1)S(1)} %copy.13.fresh_ref), custom_call_target="tpu_custom_call" | custom-call | flops 301989888 | bytes 4587520 | tf_op jit(solution)/shard_map/attend/pallas_call | solution.py:365
  40.1 2.3 %collective-permute-done.7 = bf16[32,1792]{1,0:T(8,128)(2,1)S(1)} collective-permute-done((bf16[32,1792]{1,0:T(8,128)(2,1)S(1)}, bf16[32,1792]{1,0:T(8,128)(2,1)S(1)}, u32[]{:S(2)}, u32[]{:S(2)}) %collective-permute-start.7) | collective-permute-done | bytes 114720 | tf_op jit(solution)/shard_map/ppermute | solution.py:24
  42.4 1.1 collective-permute-done.9
  44.2 1.5 %collective-permute-start.13 = (bf16[128,1792]{1,0:T(8,128)(2,1)S(1)}, bf16[128,1792]{1,0:T(8,128)(2,1)S(1)}, u32[]{:S(2)}, u32[]{:S(2)}) collective-permute-start(bf16[128,1792]{1,0:T(8,128)(2,1)S(1)} %pad_maximum_fusion.1.refs_0_), channel_id=1, source_target_pairs={{0,4},{1,3},{2,6},{3,1},{4,0},{5,7},{6,2},{7,5},{8,12},{9,11},{10,... | collective-permute-start | bytes 1376264 | tf_op jit(solution)/shard_map/ppermute | solution.py:24
  45.7 3.4 %collective-permute-start.11 = (bf16[2,576,128]{2,1,0:T(8,128)(2,1)S(1)}, bf16[2,576,128]{2,1,0:T(8,128)(2,1)S(1)}, u32[]{:S(2)}, u32[]{:S(2)}) collective-permute-start(bf16[2,576,128]{2,1,0:T(8,128)(2,1)S(1)} %copy-done.19), channel_id=1, source_target_pairs={{0,16},{1,17},{2,18},{3,19},{4,20},{5,21},{6,22},{7,23},{8,24},{9,... | collective-permute-start | bytes 884744 | tf_op jit(solution)/shard_map/ppermute | solution.py:24
  49.1 14.4 %expert_up.2 = (bf16[512,1024]{1,0:T(8,128)(2,1)S(1)}, f32[512,128]{1,0:T(8,128)S(1)}, f32[512,128]{1,0:T(8,128)S(1)}) custom-call(s32[2]{0:T(128)S(1)} %pad_add_fusion.spot_ref, bf16[256,1920]{1,0:T(8,128)(2,1)S(1)} %constant_dynamic-update-slice_fusion.refs_0_, bf16[256,1920]{1,0:T(8,128)(2,1)S(1)} %collective-permute-done.5.refs_1_, ...), custom_call_target="tpu_custom_call" | custom-call | flops 7516192768 | bytes 19660800 | tf_op jit(solution)/shard_map/expert_up/pallas_call | solution.py:152
  65.0 3.6 %expert_down.4 = (bf16[256,1792]{1,0:T(8,128)(2,1)S(1)}, bf16[256,1792]{1,0:T(8,128)(2,1)S(1)}) custom-call(s32[2]{0:T(128)S(1)} %pad_add_fusion.spot_ref, bf16[512,1024]{1,0:T(8,128)(2,1)S(1)} %get-tuple-element.98.act_ref, bf16[1024,3584]{1,0:T(8,128)(2,1)S(1)} %bitcast.25, f32[512,128]{1,0:T(8,128)S(1)} %get-tuple-element.99.scale_ref), custom_call_target="tpu_custom_call" | custom-call | flops 68719476736 | bytes 1024 | tf_op jit(solution)/shard_map/expert_down/pallas_call | solution.py:232
  69.7 3.6 %expert_down.5 = (bf16[256,1792]{1,0:T(8,128)(2,1)S(1)}, bf16[256,1792]{1,0:T(8,128)(2,1)S(1)}) custom-call(s32[2]{0:T(128)S(1)} %pad_add_fusion.spot_ref, bf16[512,1024]{1,0:T(8,128)(2,1)S(1)} %get-tuple-element.98.act_ref, bf16[1024,3584]{1,0:T(8,128)(2,1)S(1)} %bitcast.26, f32[512,128]{1,0:T(8,128)S(1)} %get-tuple-element.99.scale_ref), custom_call_target="tpu_custom_call" | custom-call | flops 68719476736 | bytes 1024 | tf_op jit(solution)/shard_map/expert_down/pallas_call | solution.py:232
  73.9 1.4 collective-permute-start.20
  75.7 13.6 %expert_up.3.act_ref = bf16[512,1024]{1,0:T(8,128)(2,1)S(1)} custom-call(s32[2]{0:T(128)S(1)} %pad_add_fusion.spot_ref, bf16[128,1792]{1,0:T(8,128)(2,1)S(1)} %pad_maximum_fusion.1.refs_0_, bf16[128,1792]{1,0:T(8,128)(2,1)S(1)} %collective-permute-done.13.refs_1_, bf16[128,1792]{1,0:T(8,128)(2,1)S(1)} %collective-permute-done.10.refs_2_, ...), custom_call_target="tpu_custom_call" | custom-call | flops 7516192768 | bytes 19398656 | tf_op jit(solution)/shard_map/expert_up/pallas_call | solution.py:152
  89.3 1.6 %collective-permute-done.22.came_b_ref = bf16[2,576,128]{2,1,0:T(8,128)(2,1)S(1)} collective-permute-done((bf16[2,576,128]{2,1,0:T(8,128)(2,1)S(1)}, bf16[2,576,128]{2,1,0:T(8,128)(2,1)S(1)}, u32[]{:S(2)}, u32[]{:S(2)}) %collective-permute-start.22) | collective-permute-done | bytes 294944 | tf_op jit(solution)/shard_map/ppermute | solution.py:24
  90.9 4.5 %expert_down.6 = (bf16[256,1792]{1,0:T(8,128)(2,1)S(1)}, bf16[256,1792]{1,0:T(8,128)(2,1)S(1)}) custom-call(s32[2]{0:T(128)S(1)} %pad_add_fusion.spot_ref, bf16[512,1024]{1,0:T(8,128)(2,1)S(1)} %expert_up.3.act_ref, bf16[1024,3584]{1,0:T(8,128)(2,1)S(1)} %bitcast.27, f32[512,128]{1,0:T(8,128)S(1)} %get-tuple-element.120.scale_ref), custom_call_target="tpu_custom_call" | custom-call | flops 68719476736 | bytes 1024 | tf_op jit(solution)/shard_map/expert_down/pallas_call | solution.py:232
  95.5 1.0 add_convert_fusion.3
  96.5 0.9 collective-permute-start.23
  98.0 1.1 add_convert_fusion
  99.9 5.3 %expert_down.7 = (bf16[256,1792]{1,0:T(8,128)(2,1)}, bf16[256,1792]{1,0:T(8,128)(2,1)S(1)}) custom-call(s32[2]{0:T(128)S(1)} %pad_add_fusion.spot_ref, bf16[512,1024]{1,0:T(8,128)(2,1)S(1)} %expert_up.3.act_ref, bf16[1024,3584]{1,0:T(8,128)(2,1)S(1)} %bitcast.28, f32[512,128]{1,0:T(8,128)S(1)} %get-tuple-element.120.scale_ref), custom_call_target="tpu_custom_call" | custom-call | flops 68719476736 | bytes 1024 | tf_op jit(solution)/shard_map/expert_down/pallas_call | solution.py:232
  105.2 1.0 copy-done.4
  106.3 2.1 %collective-permute-done.23 = bf16[128,1792]{1,0:T(8,128)(2,1)} collective-permute-done((bf16[128,1792]{1,0:T(8,128)(2,1)}, bf16[128,1792]{1,0:T(8,128)(2,1)}, u32[]{:S(2)}, u32[]{:S(2)}) %collective-permute-start.23) | collective-permute-done | bytes 458784 | tf_op jit(solution)/shard_map/ppermute | solution.py:24
  108.4 1.5 %add_convert_fusion.9 = (bf16[32,1792]{1,0:T(8,128)(2,1)S(1)}, bf16[32,1792]{1,0:T(8,128)(2,1)S(1)}, bf16[32,1792]{1,0:T(8,128)(2,1)S(1)}) fusion(bf16[128,1792]{1,0:T(8,128)(2,1)} %collective-permute-done.23, bf16[256,1792]{1,0:T(8,128)(2,1)} %copy-done.16, bf16[256,1792]{1,0:T(8,128)(2,1)} %copy-done.15, bf16[256,1792]{1,0:T(8,128)(2,1)S(1)} %get-tuple-element.106), kind=kLoop, calls=%fused_computation.13 | loop fusion | flops 1376256 | bytes 1720320 | tf_op jit(solution)/shard_map/convert_element_type | solution.py:499
  109.9 1.1 collective-permute-start.28
  111.0 1.2 collective-permute-start.29
  112.2 1.3 collective-permute-start.30
  113.5 1.2 collective-permute-done.25
  114.7 1.5 %add_convert_fusion.2 = bf16[128,1792]{1,0:T(8,128)(2,1)S(1)} fusion(bf16[256,1792]{1,0:T(8,128)(2,1)} %collective-permute-done.26, bf16[256,1792]{1,0:T(8,128)(2,1)} %collective-permute-done.25, bf16[256,1792]{1,0:T(8,128)(2,1)} %copy-done.4), kind=kLoop, calls=%fused_computation.2 | loop fusion | flops 1376256 | bytes 1835008 | tf_op jit(solution)/shard_map/convert_element_type | solution.py:499
  116.1 0.9 collective-permute-start.27
  117.1 1.3 copy-done.3
  118.4 3.1 %attend_moved.1 = bf16[16,64,512]{2,1,0:T(8,128)(2,1)} custom-call(s32[2]{0:T(128)S(1)} %pad_add_fusion.spot_ref, s32[512]{0:T(512)S(1)} %copy-done.9, s32[8]{0:T(128)S(1)} %copy-done.14, bf16[16,64,576]{2,1,0:T(8,128)(2,1)S(1)} %copy-done.3, bf16[16,576,128]{2,1,0:T(8,128)(2,1)S(1)} %bitcast.22, ...), custom_call_target="tpu_custom_call", output_to_operand_aliasing={{}: (8, {})} | custom-call | flops 68719476736 | bytes 1024 | tf_op jit(solution)/shard_map/attend_moved/pallas_call | solution.py:411
  121.6 3.1 %collective-permute-done.27 = bf16[128,1792]{1,0:T(8,128)(2,1)S(1)} collective-permute-done((bf16[128,1792]{1,0:T(8,128)(2,1)S(1)}, bf16[128,1792]{1,0:T(8,128)(2,1)S(1)}, u32[]{:S(2)}, u32[]{:S(2)}) %collective-permute-start.27) | collective-permute-done | bytes 458784 | tf_op jit(solution)/shard_map/ppermute | solution.py:24
  124.7 1.4 add_convert_fusion.7
  126.0 1.1 collective-permute-start.32
  127.1 1.2 collective-permute-start.33
  128.3 1.3 collective-permute-start.34
  129.6 1.1 add_convert_fusion.8
  130.8 5.2 %collective-permute-done.32 = bf16[32,1792]{1,0:T(8,128)(2,1)S(1)} collective-permute-done((bf16[32,1792]{1,0:T(8,128)(2,1)S(1)}, bf16[32,1792]{1,0:T(8,128)(2,1)S(1)}, u32[]{:S(2)}, u32[]{:S(2)}) %collective-permute-start.32) | collective-permute-done | bytes 114720 | tf_op jit(solution)/shard_map/ppermute | solution.py:24
  136.0 1.2 collective-permute-done.34
  137.2 1.1 add_convert_fusion.4
  138.5 1.2 collective-permute-done.35
  (106 shorter events, 9.2 us)
Async XLA Ops:
  1.6 2.8 %collective-permute-start = (bf16[2,16,1792]{2,1,0:T(8,128)(2,1)S(1)}, bf16[2,16,1792]{2,1,0:T(8,128)(2,1)S(1)}, u32[]{:S(2)}, u32[]{:S(2)}) collective-permute-start(bf16[2,16,1792]{2,1,0:T(8,128)(2,1)S(1)} %get-tuple-element.151), channel_id=1, source_target_pairs={{0,1},{1,0},{2,3},{3,2},{4,5},{5,4},{6,7},{7,6},{8,9},{9,8},{10,11... | collective-permute-start | bytes 344072 | tf_op jit(solution)/shard_map/ppermute | solution.py:24
  4.5 13.2 %collective-permute-start.1 = (bf16[32,1920]{1,0:T(8,128)(2,1)S(1)}, bf16[32,1920]{1,0:T(8,128)(2,1)S(1)}, u32[]{:S(2)}, u32[]{:S(2)}) collective-permute-start(bf16[32,1920]{1,0:T(8,128)(2,1)S(1)} %pad_maximum_fusion.3), channel_id=1, source_target_pairs={{0,16},{1,17},{2,18},{3,19},{4,20},{5,21},{6,22},{7,23},{8,24},{9,... | collective-permute-start | bytes 368648 | tf_op jit(solution)/shard_map/ppermute | solution.py:24
  8.2 9.5 %collective-permute-start.2 = (bf16[32,1920]{1,0:T(8,128)(2,1)S(1)}, bf16[32,1920]{1,0:T(8,128)(2,1)S(1)}, u32[]{:S(2)}, u32[]{:S(2)}) collective-permute-start(bf16[32,1920]{1,0:T(8,128)(2,1)S(1)} %pad_maximum_fusion.3), channel_id=1, source_target_pairs={{0,24},{1,25},{2,26},{3,27},{4,28},{5,29},{6,30},{7,31},{8,16},{9,... | collective-permute-start | bytes 368648 | tf_op jit(solution)/shard_map/ppermute | solution.py:24
  9.5 9.3 %collective-permute-start.3 = (bf16[32,1920]{1,0:T(8,128)(2,1)S(1)}, bf16[32,1920]{1,0:T(8,128)(2,1)S(1)}, u32[]{:S(2)}, u32[]{:S(2)}) collective-permute-start(bf16[32,1920]{1,0:T(8,128)(2,1)S(1)} %pad_maximum_fusion.3), channel_id=1, source_target_pairs={{0,8},{1,9},{2,10},{3,11},{4,12},{5,13},{6,14},{7,15},{8,0},{9,1},... | collective-permute-start | bytes 368648 | tf_op jit(solution)/shard_map/ppermute | solution.py:24
  9.7 24.4 %copy-start.2 = (bf16[16,64,576]{2,1,0:T(8,128)(2,1)S(1)}, bf16[16,64,576]{2,1,0:T(8,128)(2,1)}, u32[]{:S(2)}) copy-start(bf16[16,64,576]{2,1,0:T(8,128)(2,1)} %query_ref.1) | copy-start | bytes 3538948
  12.7 16.7 %copy-start.17 = (bf16[16,576]{1,0:T(8,128)(2,1)S(1)}, bf16[16,576]{1,0:T(8,128)(2,1)}, u32[]{:S(2)}) copy-start(bf16[16,576]{1,0:T(8,128)(2,1)} %param.16) | copy-start | bytes 55300
  12.8 21.4 %copy-start = (bf16[16,128,576]{1,2,0:T(8,128)(2,1)S(1)}, bf16[16,128,576]{1,2,0:T(8,128)(2,1)}, u32[]{:S(2)}) copy-start(bf16[16,128,576]{1,2,0:T(8,128)(2,1)} %param.17) | copy-start | bytes 7077892
  12.8 21.4 %copy-start.8 = (s32[512]{0:T(512)S(1)}, s32[512]{0:T(512)}, u32[]{:S(2)}) copy-start(s32[512]{0:T(512)} %length_ref.3) | copy-start | bytes 6148
  18.8 8.9 %collective-permute-start.4 = (bf16[128,1920]{1,0:T(8,128)(2,1)S(1)}, bf16[128,1920]{1,0:T(8,128)(2,1)S(1)}, u32[]{:S(2)}, u32[]{:S(2)}) collective-permute-start(bf16[128,1920]{1,0:T(8,128)(2,1)S(1)} %pad_maximum_fusion), channel_id=1, source_target_pairs={{0,4},{1,3},{2,6},{3,1},{4,0},{5,7},{6,2},{7,5},{8,12},{9,11},{10,... | collective-permute-start | bytes 1474568 | tf_op jit(solution)/shard_map/ppermute | solution.py:24
  27.8 15.7 %collective-permute-start.5 = (bf16[256,1920]{1,0:T(8,128)(2,1)S(1)}, bf16[256,1920]{1,0:T(8,128)(2,1)S(1)}, u32[]{:S(2)}, u32[]{:S(2)}) collective-permute-start(bf16[256,1920]{1,0:T(8,128)(2,1)S(1)} %constant_dynamic-update-slice_fusion.refs_0_), channel_id=1, source_target_pairs={{0,2},{1,5},{2,0},{3,7},{4,6},{5,1},{6,4},{7,3},{8,10},{9,13},{10,... | collective-permute-start | bytes 2949128 | tf_op jit(solution)/shard_map/ppermute | solution.py:24
  29.4 14.1 %collective-permute-start.6 = (bf16[256,1920]{1,0:T(8,128)(2,1)S(1)}, bf16[256,1920]{1,0:T(8,128)(2,1)S(1)}, u32[]{:S(2)}, u32[]{:S(2)}) collective-permute-start(bf16[256,1920]{1,0:T(8,128)(2,1)S(1)} %constant_dynamic-update-slice_fusion.refs_0_), channel_id=1, source_target_pairs={{0,1},{1,0},{2,3},{3,2},{4,5},{5,4},{6,7},{7,6},{8,9},{9,8},{10,11... | collective-permute-start | bytes 2949128 | tf_op jit(solution)/shard_map/ppermute | solution.py:24
  29.5 12.9 %collective-permute-start.7 = (bf16[32,1792]{1,0:T(8,128)(2,1)S(1)}, bf16[32,1792]{1,0:T(8,128)(2,1)S(1)}, u32[]{:S(2)}, u32[]{:S(2)}) collective-permute-start(bf16[32,1792]{1,0:T(8,128)(2,1)S(1)} %get-tuple-element.82), channel_id=1, source_target_pairs={{0,16},{1,17},{2,18},{3,19},{4,20},{5,21},{6,22},{7,23},{8,24},{9,... | collective-permute-start | bytes 344072 | tf_op jit(solution)/shard_map/ppermute | solution.py:24
  33.4 9.0 %collective-permute-start.8 = (bf16[32,1792]{1,0:T(8,128)(2,1)S(1)}, bf16[32,1792]{1,0:T(8,128)(2,1)S(1)}, u32[]{:S(2)}, u32[]{:S(2)}) collective-permute-start(bf16[32,1792]{1,0:T(8,128)(2,1)S(1)} %get-tuple-element.82), channel_id=1, source_target_pairs={{0,24},{1,25},{2,26},{3,27},{4,28},{5,29},{6,30},{7,31},{8,16},{9,... | collective-permute-start | bytes 344072 | tf_op jit(solution)/shard_map/ppermute | solution.py:24
  33.9 9.6 %collective-permute-start.9 = (bf16[32,1792]{1,0:T(8,128)(2,1)S(1)}, bf16[32,1792]{1,0:T(8,128)(2,1)S(1)}, u32[]{:S(2)}, u32[]{:S(2)}) collective-permute-start(bf16[32,1792]{1,0:T(8,128)(2,1)S(1)} %get-tuple-element.82), channel_id=1, source_target_pairs={{0,8},{1,9},{2,10},{3,11},{4,12},{5,13},{6,14},{7,15},{8,0},{9,1},... | collective-permute-start | bytes 344072 | tf_op jit(solution)/shard_map/ppermute | solution.py:24
  34.1 11.6 %copy-start.19 = (bf16[2,576,128]{2,1,0:T(8,128)(2,1)S(1)}, bf16[2,576,128]{2,1,0:T(8,128)(2,1)}, u32[]{:S(2)}) copy-start(bf16[2,576,128]{2,1,0:T(8,128)(2,1)} %get-tuple-element.90) | copy-start | bytes 884740
  43.5 21.5 %slice-start = ((s8[7340032]{0:T(1024)(128)(4,1)}), s8[4194304]{0:T(1024)(128)(4,1)S(1)}, s32[]{:S(2)}) async-start(s8[7340032]{0:T(1024)(128)(4,1)} %bitcast.23), calls=%async_computation | async-start | bytes 8388608
  43.6 5.5 %collective-permute-start.12 = (bf16[256,1920]{1,0:T(8,128)(2,1)S(1)}, bf16[256,1920]{1,0:T(8,128)(2,1)S(1)}, u32[]{:S(2)}, u32[]{:S(2)}) collective-permute-start(bf16[256,1920]{1,0:T(8,128)(2,1)S(1)} %collective-permute-done.5.refs_1_), channel_id=1, source_target_pairs={{0,1},{1,0},{2,3},{3,2},{4,5},{5,4},{6,7},{7,6},{8,9},{9,8},{10,11... | collective-permute-start | bytes 2949128 | tf_op jit(solution)/shard_map/ppermute | solution.py:24
  43.6 20.6 %collective-permute-start.10 = (bf16[128,1792]{1,0:T(8,128)(2,1)S(1)}, bf16[128,1792]{1,0:T(8,128)(2,1)S(1)}, u32[]{:S(2)}, u32[]{:S(2)}) collective-permute-start(bf16[128,1792]{1,0:T(8,128)(2,1)S(1)} %pad_maximum_fusion.1.refs_0_), channel_id=1, source_target_pairs={{0,2},{1,5},{2,0},{3,7},{4,6},{5,1},{6,4},{7,3},{8,10},{9,13},{10,... | collective-permute-start | bytes 1376264 | tf_op jit(solution)/shard_map/ppermute | solution.py:24
  44.2 20.0 %collective-permute-start.13 = (bf16[128,1792]{1,0:T(8,128)(2,1)S(1)}, bf16[128,1792]{1,0:T(8,128)(2,1)S(1)}, u32[]{:S(2)}, u32[]{:S(2)}) collective-permute-start(bf16[128,1792]{1,0:T(8,128)(2,1)S(1)} %pad_maximum_fusion.1.refs_0_), channel_id=1, source_target_pairs={{0,4},{1,3},{2,6},{3,1},{4,0},{5,7},{6,2},{7,5},{8,12},{9,11},{10,... | collective-permute-start | bytes 1376264 | tf_op jit(solution)/shard_map/ppermute | solution.py:24
  45.7 17.8 %collective-permute-start.11 = (bf16[2,576,128]{2,1,0:T(8,128)(2,1)S(1)}, bf16[2,576,128]{2,1,0:T(8,128)(2,1)S(1)}, u32[]{:S(2)}, u32[]{:S(2)}) collective-permute-start(bf16[2,576,128]{2,1,0:T(8,128)(2,1)S(1)} %copy-done.19), channel_id=1, source_target_pairs={{0,16},{1,17},{2,18},{3,19},{4,20},{5,21},{6,22},{7,23},{8,24},{9,... | collective-permute-start | bytes 884744 | tf_op jit(solution)/shard_map/ppermute | solution.py:24
  49.1 15.9 %slice-start.1 = ((s8[7340032]{0:T(1024)(128)(4,1)}), s8[3145728]{0:T(1024)(128)(4,1)S(1)}, s32[]{:S(2)}) async-start(s8[7340032]{0:T(1024)(128)(4,1)} %bitcast.23), calls=%async_computation.1 | async-start | bytes 6291456
  64.3 9.1 %collective-permute-start.18 = (bf16[128,1792]{1,0:T(8,128)(2,1)S(1)}, bf16[128,1792]{1,0:T(8,128)(2,1)S(1)}, u32[]{:S(2)}, u32[]{:S(2)}) collective-permute-start(bf16[128,1792]{1,0:T(8,128)(2,1)S(1)} %collective-permute-done.13.refs_1_), channel_id=1, source_target_pairs={{0,1},{1,0},{2,3},{3,2},{4,5},{5,4},{6,7},{7,6},{8,9},{9,8},{10,11... | collective-permute-start | bytes 1376264 | tf_op jit(solution)/shard_map/ppermute | solution.py:24
  64.3 9.1 %collective-permute-start.19 = (bf16[128,1792]{1,0:T(8,128)(2,1)S(1)}, bf16[128,1792]{1,0:T(8,128)(2,1)S(1)}, u32[]{:S(2)}, u32[]{:S(2)}) collective-permute-start(bf16[128,1792]{1,0:T(8,128)(2,1)S(1)} %collective-permute-done.13.refs_1_), channel_id=1, source_target_pairs={{0,2},{1,5},{2,0},{3,7},{4,6},{5,1},{6,4},{7,3},{8,10},{9,13},{10,... | collective-permute-start | bytes 1376264 | tf_op jit(solution)/shard_map/ppermute | solution.py:24
  65.0 4.3 %collective-permute-start.14 = (bf16[128,1792]{1,0:T(8,128)(2,1)S(1)}, bf16[128,1792]{1,0:T(8,128)(2,1)S(1)}, u32[]{:S(2)}, u32[]{:S(2)}) collective-permute-start(bf16[128,1792]{1,0:T(8,128)(2,1)S(1)} %collective-permute-done.10.refs_2_), channel_id=1, source_target_pairs={{0,1},{1,0},{2,3},{3,2},{4,5},{5,4},{6,7},{7,6},{8,9},{9,8},{10,11... | collective-permute-start | bytes 1376264 | tf_op jit(solution)/shard_map/ppermute | solution.py:24
  68.7 4.7 %collective-permute-start.15 = (bf16[256,1792]{1,0:T(8,128)(2,1)S(1)}, bf16[256,1792]{1,0:T(8,128)(2,1)S(1)}, u32[]{:S(2)}, u32[]{:S(2)}) collective-permute-start(bf16[256,1792]{1,0:T(8,128)(2,1)S(1)} %get-tuple-element.100), channel_id=1, source_target_pairs={{0,1},{1,0},{2,3},{3,2},{4,5},{5,4},{6,7},{7,6},{8,9},{9,8},{10,11... | collective-permute-start | bytes 2752520 | tf_op jit(solution)/shard_map/ppermute | solution.py:24
  69.2 4.2 %collective-permute-start.16 = (bf16[256,1792]{1,0:T(8,128)(2,1)S(1)}, bf16[256,1792]{1,0:T(8,128)(2,1)S(1)}, u32[]{:S(2)}, u32[]{:S(2)}) collective-permute-start(bf16[256,1792]{1,0:T(8,128)(2,1)S(1)} %get-tuple-element.101), channel_id=1, source_target_pairs={{0,1},{1,0},{2,3},{3,2},{4,5},{5,4},{6,7},{7,6},{8,9},{9,8},{10,11... | collective-permute-start | bytes 2752520 | tf_op jit(solution)/shard_map/ppermute | solution.py:24
  69.3 4.1 %collective-permute-start.17 = (bf16[128,1792]{1,0:T(8,128)(2,1)S(1)}, bf16[128,1792]{1,0:T(8,128)(2,1)S(1)}, u32[]{:S(2)}, u32[]{:S(2)}) collective-permute-start(bf16[128,1792]{1,0:T(8,128)(2,1)S(1)} %pad_maximum_fusion.1.refs_0_), channel_id=1, source_target_pairs={{0,1},{1,0},{2,3},{3,2},{4,5},{5,4},{6,7},{7,6},{8,9},{9,8},{10,11... | collective-permute-start | bytes 1376264 | tf_op jit(solution)/shard_map/ppermute | solution.py:24
  73.4 22.1 %copy-start.15 = (bf16[256,1792]{1,0:T(8,128)(2,1)}, bf16[256,1792]{1,0:T(8,128)(2,1)S(1)}, u32[]{:S(2)}) copy-start(bf16[256,1792]{1,0:T(8,128)(2,1)S(1)} %collective-permute-done.15) | copy-start | bytes 2752516
  73.6 2.1 %collective-permute-start.21 = (bf16[128,1792]{1,0:T(8,128)(2,1)S(1)}, bf16[128,1792]{1,0:T(8,128)(2,1)S(1)}, u32[]{:S(2)}, u32[]{:S(2)}) collective-permute-start(bf16[128,1792]{1,0:T(8,128)(2,1)S(1)} %collective-permute-done.19.refs_3_), channel_id=1, source_target_pairs={{0,1},{1,0},{2,3},{3,2},{4,5},{5,4},{6,7},{7,6},{8,9},{9,8},{10,11... | collective-permute-start | bytes 1376264 | tf_op jit(solution)/shard_map/ppermute | solution.py:24
  73.9 17.0 %collective-permute-start.20 = (bf16[256,1792]{1,0:T(8,128)(2,1)S(1)}, bf16[256,1792]{1,0:T(8,128)(2,1)S(1)}, u32[]{:S(2)}, u32[]{:S(2)}) collective-permute-start(bf16[256,1792]{1,0:T(8,128)(2,1)S(1)} %add_convert_fusion.1), channel_id=1, source_target_pairs={{0,2},{1,5},{2,0},{3,7},{4,6},{5,1},{6,4},{7,3},{8,10},{9,13},{10,... | collective-permute-start | bytes 2752520 | tf_op jit(solution)/shard_map/ppermute | solution.py:24
  75.3 15.6 %collective-permute-start.22 = (bf16[2,576,128]{2,1,0:T(8,128)(2,1)S(1)}, bf16[2,576,128]{2,1,0:T(8,128)(2,1)S(1)}, u32[]{:S(2)}, u32[]{:S(2)}) collective-permute-start(bf16[2,576,128]{2,1,0:T(8,128)(2,1)S(1)} %copy-done.18), channel_id=1, source_target_pairs={{0,16},{1,17},{2,18},{3,19},{4,20},{5,21},{6,22},{7,23},{8,24},{9,... | collective-permute-start | bytes 884744 | tf_op jit(solution)/shard_map/ppermute | solution.py:24
  95.4 2.5 %collective-permute-start.24 = (bf16[256,1792]{1,0:T(8,128)(2,1)S(1)}, bf16[256,1792]{1,0:T(8,128)(2,1)S(1)}, u32[]{:S(2)}, u32[]{:S(2)}) collective-permute-start(bf16[256,1792]{1,0:T(8,128)(2,1)S(1)} %get-tuple-element.124), channel_id=1, source_target_pairs={{0,1},{1,0},{2,3},{3,2},{4,5},{5,4},{6,7},{7,6},{8,9},{9,8},{10,11... | collective-permute-start | bytes 2752520 | tf_op jit(solution)/shard_map/ppermute | solution.py:24
  96.5 11.9 %collective-permute-start.23 = (bf16[128,1792]{1,0:T(8,128)(2,1)}, bf16[128,1792]{1,0:T(8,128)(2,1)}, u32[]{:S(2)}, u32[]{:S(2)}) collective-permute-start(bf16[128,1792]{1,0:T(8,128)(2,1)} %add_convert_fusion.3), channel_id=1, source_target_pairs={{0,4},{1,3},{2,6},{3,1},{4,0},{5,7},{6,2},{7,5},{8,12},{9,11},{10,... | collective-permute-start | bytes 1376264 | tf_op jit(solution)/shard_map/ppermute | solution.py:24
  99.1 15.6 %collective-permute-start.25 = (bf16[256,1792]{1,0:T(8,128)(2,1)}, bf16[256,1792]{1,0:T(8,128)(2,1)}, u32[]{:S(2)}, u32[]{:S(2)}) collective-permute-start(bf16[256,1792]{1,0:T(8,128)(2,1)} %add_convert_fusion), channel_id=1, source_target_pairs={{0,2},{1,5},{2,0},{3,7},{4,6},{5,1},{6,4},{7,3},{8,10},{9,13},{10,... | collective-permute-start | bytes 2752520 | tf_op jit(solution)/shard_map/ppermute | solution.py:24
  106.2 10.9 %copy-start.1 = (bf16[16,128,576]{1,2,0:T(8,128)(2,1)S(1)}, bf16[16,128,576]{1,2,0:T(8,128)(2,1)}, u32[]{:S(2)}) copy-start(bf16[16,128,576]{1,2,0:T(8,128)(2,1)} %param.17) | copy-start | bytes 7077892
  106.2 10.9 %copy-start.7 = (bf16[16,1,576]{2,1,0:T(2,128)(2,1)S(1)}, bf16[16,1,576]{2,1,0:T(2,128)(2,1)}, u32[]{:S(2)}) copy-start(bf16[16,1,576]{2,1,0:T(2,128)(2,1)} %copy-done.6) | copy-start | bytes 55300
  106.2 10.9 %copy-start.9 = (s32[512]{0:T(512)S(1)}, s32[512]{0:T(512)}, u32[]{:S(2)}) copy-start(s32[512]{0:T(512)} %length_ref.3) | copy-start | bytes 6148
  106.2 10.9 %copy-start.14 = (s32[8]{0:T(128)S(1)}, s32[8]{0:T(128)}, u32[]{:S(2)}) copy-start(s32[8]{0:T(128)} %get-tuple-element.132.info_ref) | copy-start | bytes 100
  106.2 8.5 %collective-permute-start.26 = (bf16[256,1792]{1,0:T(8,128)(2,1)}, bf16[256,1792]{1,0:T(8,128)(2,1)}, u32[]{:S(2)}, u32[]{:S(2)}) collective-permute-start(bf16[256,1792]{1,0:T(8,128)(2,1)} %get-tuple-element.129), channel_id=1, source_target_pairs={{0,1},{1,0},{2,3},{3,2},{4,5},{5,4},{6,7},{7,6},{8,9},{9,8},{10,11... | collective-permute-start | bytes 2752520 | tf_op jit(solution)/shard_map/ppermute | solution.py:24
  109.9 11.7 %collective-permute-start.28 = (bf16[32,1792]{1,0:T(8,128)(2,1)S(1)}, bf16[32,1792]{1,0:T(8,128)(2,1)S(1)}, u32[]{:S(2)}, u32[]{:S(2)}) collective-permute-start(bf16[32,1792]{1,0:T(8,128)(2,1)S(1)} %get-tuple-element.147), channel_id=1, source_target_pairs={{0,16},{1,17},{2,18},{3,19},{4,20},{5,21},{6,22},{7,23},{8,24},{9,... | collective-permute-start | bytes 344072 | tf_op jit(solution)/shard_map/ppermute | solution.py:24
  111.0 10.6 %collective-permute-start.29 = (bf16[32,1792]{1,0:T(8,128)(2,1)S(1)}, bf16[32,1792]{1,0:T(8,128)(2,1)S(1)}, u32[]{:S(2)}, u32[]{:S(2)}) collective-permute-start(bf16[32,1792]{1,0:T(8,128)(2,1)S(1)} %get-tuple-element.146), channel_id=1, source_target_pairs={{0,24},{1,25},{2,26},{3,27},{4,28},{5,29},{6,30},{7,31},{8,16},{9,... | collective-permute-start | bytes 344072 | tf_op jit(solution)/shard_map/ppermute | solution.py:24
  112.2 9.4 %collective-permute-start.30 = (bf16[32,1792]{1,0:T(8,128)(2,1)S(1)}, bf16[32,1792]{1,0:T(8,128)(2,1)S(1)}, u32[]{:S(2)}, u32[]{:S(2)}) collective-permute-start(bf16[32,1792]{1,0:T(8,128)(2,1)S(1)} %get-tuple-element.145), channel_id=1, source_target_pairs={{0,8},{1,9},{2,10},{3,11},{4,12},{5,13},{6,14},{7,15},{8,0},{9,1},... | collective-permute-start | bytes 344072 | tf_op jit(solution)/shard_map/ppermute | solution.py:24
  116.1 8.5 %collective-permute-start.27 = (bf16[128,1792]{1,0:T(8,128)(2,1)S(1)}, bf16[128,1792]{1,0:T(8,128)(2,1)S(1)}, u32[]{:S(2)}, u32[]{:S(2)}) collective-permute-start(bf16[128,1792]{1,0:T(8,128)(2,1)S(1)} %add_convert_fusion.2), channel_id=1, source_target_pairs={{0,4},{1,3},{2,6},{3,1},{4,0},{5,7},{6,2},{7,5},{8,12},{9,11},{10,... | collective-permute-start | bytes 1376264 | tf_op jit(solution)/shard_map/ppermute | solution.py:24
  126.0 10.0 %collective-permute-start.32 = (bf16[32,1792]{1,0:T(8,128)(2,1)S(1)}, bf16[32,1792]{1,0:T(8,128)(2,1)S(1)}, u32[]{:S(2)}, u32[]{:S(2)}) collective-permute-start(bf16[32,1792]{1,0:T(8,128)(2,1)S(1)} %get-tuple-element.142), channel_id=1, source_target_pairs={{0,16},{1,17},{2,18},{3,19},{4,20},{5,21},{6,22},{7,23},{8,24},{9,... | collective-permute-start | bytes 344072 | tf_op jit(solution)/shard_map/ppermute | solution.py:24
  127.1 8.9 %collective-permute-start.33 = (bf16[32,1792]{1,0:T(8,128)(2,1)S(1)}, bf16[32,1792]{1,0:T(8,128)(2,1)S(1)}, u32[]{:S(2)}, u32[]{:S(2)}) collective-permute-start(bf16[32,1792]{1,0:T(8,128)(2,1)S(1)} %get-tuple-element.144), channel_id=1, source_target_pairs={{0,24},{1,25},{2,26},{3,27},{4,28},{5,29},{6,30},{7,31},{8,16},{9,... | collective-permute-start | bytes 344072 | tf_op jit(solution)/shard_map/ppermute | solution.py:24
  128.3 9.0 %collective-permute-start.34 = (bf16[32,1792]{1,0:T(8,128)(2,1)S(1)}, bf16[32,1792]{1,0:T(8,128)(2,1)S(1)}, u32[]{:S(2)}, u32[]{:S(2)}) collective-permute-start(bf16[32,1792]{1,0:T(8,128)(2,1)S(1)} %get-tuple-element.143), channel_id=1, source_target_pairs={{0,8},{1,9},{2,10},{3,11},{4,12},{5,13},{6,14},{7,15},{8,0},{9,1},... | collective-permute-start | bytes 344072 | tf_op jit(solution)/shard_map/ppermute | solution.py:24
  130.7 7.7 %collective-permute-start.31 = (bf16[16,1792]{1,0:T(8,128)(2,1)S(1)}, bf16[16,1792]{1,0:T(8,128)(2,1)S(1)}, u32[]{:S(2)}, u32[]{:S(2)}) collective-permute-start(bf16[16,1792]{1,0:T(8,128)(2,1)S(1)} %get-tuple-element.153), channel_id=1, source_target_pairs={{0,1},{1,0},{2,3},{3,2},{4,5},{5,4},{6,7},{7,6},{8,9},{9,8},{10,11... | collective-permute-start | bytes 172040 | tf_op jit(solution)/shard_map/ppermute | solution.py:24
  138.3 1.3 collective-permute-start.35
  (10 other events, 52.6 us)

commit v8 on v7

--- a/solution.py
+++ b/solution.py
@@ -244,7 +244,7 @@
         out_shape=out_shape,
         compiler_params=pltpu.CompilerParams(
             dimension_semantics=("arbitrary",),
-            vmem_limit_bytes=4 * (rows + block) * hidden_units + 24 * rows * block + (2 << 20),
+            vmem_limit_bytes=4 * (rows + block) * hidden_units + 24 * rows * block + (10 << 20),
         ),
         cost_estimate=pl.CostEstimate(flops=1 << 36, bytes_accessed=1 << 10, transcendentals=0),
         name="expert_down",
@@ -468,8 +468,7 @@
     meta = meta_columns(jnp.swapaxes(routes, 1, 2), jnp.swapaxes(route_weights, 1, 2))
 
     own_half = lax.dynamic_slice_in_dim(hidden, core * half, half, axis=2)
-    other_half = lax.dynamic_slice_in_dim(hidden, (1 - core) * half, half, axis=2)
-    came_half = exchange(other_half, sibling)
+    came_half = lax.dynamic_slice_in_dim(exchange(hidden, sibling), core * half, half, axis=2)
     by_core = lambda mine, theirs, axis: jnp.where(
         core == 0,
         jnp.concatenate([mine, theirs], axis=axis),

time: 141 us -> 141 us (level)
  transfers between devices with their start and end apart: 36 -> 36, of which waited for: 13 -> 13; matrix products, arithmetic and copies ran while one was open for 6% -> 7% of each run, Pallas kernels for 39% -> 39%
where the time goes in v8:
time: 141 us; the launch traced here: 140 us
  Pallas kernels  58.7 us (42%)
  starting transfers between devices  33 us (23%)
  waiting for transfers between devices  32.8 us (23%)
  other arithmetic  10.6 us (8%)
  local copies, waits for them, and re-layouts  4.21 us (3%)
    ppermute x36, starting transfers between devices, exchange(): return lax.ppermute(value, AXES, pairs)  33 us
    ppermute x36, waiting for transfers between devices, exchange(): return lax.ppermute(value, AXES, pairs)  32.8 us
    pallas_call x2, Pallas kernels, expert_up(): pl.pallas_call(functools.partial(up_body, line_rows, piece_counts, with_m...  28 us
    pallas_call x4, Pallas kernels, expert_down(): pl.pallas_call(functools.partial(down_body, line_rows, jobs), grid_spec=p...  17 us
    convert_element_type x8, other arithmetic, per_device(): rounded_sum = lambda terms: add(terms).astype(jnp.bfloat16)  8.84 us
    pallas_call x1, Pallas kernels, attend(): pl.pallas_call(functools.partial(attend_body, group), grid_spec=pltpu.Pre...  5.96 us
    unnamed x48, local copies, waits for them, and re-layouts  3.15 us
    pallas_call x1, Pallas kernels, attend_moved(): pl.pallas_call(functools.partial(attend_moved_body, row_count), grid_spec...  3.13 us
  transfers between devices with their start and end apart: 36, of which 13 were waited for; matrix products, arithmetic and copies ran while one was open for 7% of the time, Pallas kernels for 39%

profile of v8, /device:TPU:0, one launch (start us, length us, event | category | flops | bytes accessed | tf_op | source)
XLA Modules:
  0.0 140.3 jit_solution(16402528196804025308)
XLA Ops:
  1.1 1.5 %meta_columns.1 = bf16[16,128]{1,0:T(8,128)(2,1)} custom-call(s32[2,8,16]{2,1,0:T(8,128)} %bitcast.34, f32[2,8,16]{2,1,0:T(8,128)} %bitcast.35), custom_call_target="tpu_custom_call" | custom-call | tf_op jit(solution)/shard_map/meta_columns/pallas_call | solution.py:273
  3.4 0.9 constant_dynamic-slice_fusion.3
  4.4 3.7 %collective-permute-start.1 = (bf16[32,1920]{1,0:T(8,128)(2,1)S(1)}, bf16[32,1920]{1,0:T(8,128)(2,1)S(1)}, u32[]{:S(2)}, u32[]{:S(2)}) collective-permute-start(bf16[32,1920]{1,0:T(8,128)(2,1)S(1)} %pad_maximum_fusion.3), channel_id=1, source_target_pairs={{0,16},{1,17},{2,18},{3,19},{4,20},{5,21},{6,22},{7,23},{8,24},{9,... | collective-permute-start | bytes 368648 | tf_op jit(solution)/shard_map/ppermute | solution.py:24
  8.1 1.3 collective-permute-start.2
  9.7 3.0 %pick_caches.1 = (bf16[2,576,128]{2,1,0:T(8,128)(2,1)}, bf16[2,576,128]{2,1,0:T(8,128)(2,1)}, s32[8]{0:T(128)}) custom-call(s32[16]{0:T(128)} %swapped_ref, bf16[16,576,128]{2,1,0:T(8,128)(2,1)} %bitcast.20), custom_call_target="tpu_custom_call" | custom-call | tf_op jit(solution)/shard_map/pick_caches/pallas_call | solution.py:313
  12.8 4.8 %collective-permute-done.1 = bf16[32,1920]{1,0:T(8,128)(2,1)S(1)} collective-permute-done((bf16[32,1920]{1,0:T(8,128)(2,1)S(1)}, bf16[32,1920]{1,0:T(8,128)(2,1)S(1)}, u32[]{:S(2)}, u32[]{:S(2)}) %collective-permute-start.1) | collective-permute-done | bytes 122912 | tf_op jit(solution)/shard_map/ppermute | solution.py:24
  17.6 1.1 collective-permute-done.3
  18.8 1.6 %collective-permute-start.4 = (bf16[128,1920]{1,0:T(8,128)(2,1)S(1)}, bf16[128,1920]{1,0:T(8,128)(2,1)S(1)}, u32[]{:S(2)}, u32[]{:S(2)}) collective-permute-start(bf16[128,1920]{1,0:T(8,128)(2,1)S(1)} %pad_maximum_fusion), channel_id=1, source_target_pairs={{0,4},{1,3},{2,6},{3,1},{4,0},{5,7},{6,2},{7,5},{8,12},{9,11},{10,... | collective-permute-start | bytes 1474568 | tf_op jit(solution)/shard_map/ppermute | solution.py:24
  20.4 7.2 %collective-permute-done.4 = bf16[128,1920]{1,0:T(8,128)(2,1)S(1)} collective-permute-done((bf16[128,1920]{1,0:T(8,128)(2,1)S(1)}, bf16[128,1920]{1,0:T(8,128)(2,1)S(1)}, u32[]{:S(2)}, u32[]{:S(2)}) %collective-permute-start.4) | collective-permute-done | bytes 491552 | tf_op jit(solution)/shard_map/ppermute | solution.py:24
  27.7 1.6 %collective-permute-start.5 = (bf16[256,1920]{1,0:T(8,128)(2,1)S(1)}, bf16[256,1920]{1,0:T(8,128)(2,1)S(1)}, u32[]{:S(2)}, u32[]{:S(2)}) collective-permute-start(bf16[256,1920]{1,0:T(8,128)(2,1)S(1)} %constant_dynamic-update-slice_fusion.refs_0_), channel_id=1, source_target_pairs={{0,2},{1,5},{2,0},{3,7},{4,6},{5,1},{6,4},{7,3},{8,10},{9,13},{10,... | collective-permute-start | bytes 2949128 | tf_op jit(solution)/shard_map/ppermute | solution.py:24
  29.4 3.9 %collective-permute-start.7 = (bf16[32,1792]{1,0:T(8,128)(2,1)S(1)}, bf16[32,1792]{1,0:T(8,128)(2,1)S(1)}, u32[]{:S(2)}, u32[]{:S(2)}) collective-permute-start(bf16[32,1792]{1,0:T(8,128)(2,1)S(1)} %get-tuple-element.82), channel_id=1, source_target_pairs={{0,16},{1,17},{2,18},{3,19},{4,20},{5,21},{6,22},{7,23},{8,24},{9,... | collective-permute-start | bytes 344072 | tf_op jit(solution)/shard_map/ppermute | solution.py:24
  34.1 6.0 %attend.1.old_ref = bf16[16,64,512]{2,1,0:T(8,128)(2,1)} custom-call(s32[2]{0:T(128)S(1)} %pad_add_fusion.spot_ref, s32[512]{0:T(512)S(1)} %copy-done.8, bf16[16,64,576]{2,1,0:T(8,128)(2,1)S(1)} %copy-done.2, bf16[16,576,128]{2,1,0:T(8,128)(2,1)S(1)} %bitcast.21, bf16[16,1,576]{2,1,0:T(2,128)(2,1)S(1)} %copy.13.fresh_ref), custom_call_target="tpu_custom_call" | custom-call | flops 301989888 | bytes 4587520 | tf_op jit(solution)/shard_map/attend/pallas_call | solution.py:365
  40.0 2.3 %collective-permute-done.7 = bf16[32,1792]{1,0:T(8,128)(2,1)S(1)} collective-permute-done((bf16[32,1792]{1,0:T(8,128)(2,1)S(1)}, bf16[32,1792]{1,0:T(8,128)(2,1)S(1)}, u32[]{:S(2)}, u32[]{:S(2)}) %collective-permute-start.7) | collective-permute-done | bytes 114720 | tf_op jit(solution)/shard_map/ppermute | solution.py:24
  42.3 1.1 collective-permute-done.9
  44.2 1.5 %collective-permute-start.13 = (bf16[128,1792]{1,0:T(8,128)(2,1)S(1)}, bf16[128,1792]{1,0:T(8,128)(2,1)S(1)}, u32[]{:S(2)}, u32[]{:S(2)}) collective-permute-start(bf16[128,1792]{1,0:T(8,128)(2,1)S(1)} %pad_maximum_fusion.1.refs_0_), channel_id=1, source_target_pairs={{0,4},{1,3},{2,6},{3,1},{4,0},{5,7},{6,2},{7,5},{8,12},{9,11},{10,... | collective-permute-start | bytes 1376264 | tf_op jit(solution)/shard_map/ppermute | solution.py:24
  45.6 3.4 %collective-permute-start.11 = (bf16[2,576,128]{2,1,0:T(8,128)(2,1)S(1)}, bf16[2,576,128]{2,1,0:T(8,128)(2,1)S(1)}, u32[]{:S(2)}, u32[]{:S(2)}) collective-permute-start(bf16[2,576,128]{2,1,0:T(8,128)(2,1)S(1)} %copy-done.19), channel_id=1, source_target_pairs={{0,16},{1,17},{2,18},{3,19},{4,20},{5,21},{6,22},{7,23},{8,24},{9,... | collective-permute-start | bytes 884744 | tf_op jit(solution)/shard_map/ppermute | solution.py:24
  49.0 14.4 %expert_up.2 = (bf16[512,1024]{1,0:T(8,128)(2,1)S(1)}, f32[512,128]{1,0:T(8,128)S(1)}, f32[512,128]{1,0:T(8,128)S(1)}) custom-call(s32[2]{0:T(128)S(1)} %pad_add_fusion.spot_ref, bf16[256,1920]{1,0:T(8,128)(2,1)S(1)} %constant_dynamic-update-slice_fusion.refs_0_, bf16[256,1920]{1,0:T(8,128)(2,1)S(1)} %collective-permute-done.5.refs_1_, ...), custom_call_target="tpu_custom_call" | custom-call | flops 7516192768 | bytes 19660800 | tf_op jit(solution)/shard_map/expert_up/pallas_call | solution.py:152
  65.0 3.6 %expert_down.4 = (bf16[256,1792]{1,0:T(8,128)(2,1)S(1)}, bf16[256,1792]{1,0:T(8,128)(2,1)S(1)}) custom-call(s32[2]{0:T(128)S(1)} %pad_add_fusion.spot_ref, bf16[512,1024]{1,0:T(8,128)(2,1)S(1)} %get-tuple-element.98.act_ref, bf16[1024,3584]{1,0:T(8,128)(2,1)S(1)} %bitcast.25, f32[512,128]{1,0:T(8,128)S(1)} %get-tuple-element.99.scale_ref), custom_call_target="tpu_custom_call" | custom-call | flops 68719476736 | bytes 1024 | tf_op jit(solution)/shard_map/expert_down/pallas_call | solution.py:232
  69.6 3.6 %expert_down.5 = (bf16[256,1792]{1,0:T(8,128)(2,1)S(1)}, bf16[256,1792]{1,0:T(8,128)(2,1)S(1)}) custom-call(s32[2]{0:T(128)S(1)} %pad_add_fusion.spot_ref, bf16[512,1024]{1,0:T(8,128)(2,1)S(1)} %get-tuple-element.98.act_ref, bf16[1024,3584]{1,0:T(8,128)(2,1)S(1)} %bitcast.26, f32[512,128]{1,0:T(8,128)S(1)} %get-tuple-element.99.scale_ref), custom_call_target="tpu_custom_call" | custom-call | flops 68719476736 | bytes 1024 | tf_op jit(solution)/shard_map/expert_down/pallas_call | solution.py:232
  73.9 1.4 collective-permute-start.20
  75.6 13.6 %expert_up.3.act_ref = bf16[512,1024]{1,0:T(8,128)(2,1)S(1)} custom-call(s32[2]{0:T(128)S(1)} %pad_add_fusion.spot_ref, bf16[128,1792]{1,0:T(8,128)(2,1)S(1)} %pad_maximum_fusion.1.refs_0_, bf16[128,1792]{1,0:T(8,128)(2,1)S(1)} %collective-permute-done.13.refs_1_, bf16[128,1792]{1,0:T(8,128)(2,1)S(1)} %collective-permute-done.10.refs_2_, ...), custom_call_target="tpu_custom_call" | custom-call | flops 7516192768 | bytes 19398656 | tf_op jit(solution)/shard_map/expert_up/pallas_call | solution.py:152
  89.3 1.6 %collective-permute-done.22.came_b_ref = bf16[2,576,128]{2,1,0:T(8,128)(2,1)S(1)} collective-permute-done((bf16[2,576,128]{2,1,0:T(8,128)(2,1)S(1)}, bf16[2,576,128]{2,1,0:T(8,128)(2,1)S(1)}, u32[]{:S(2)}, u32[]{:S(2)}) %collective-permute-start.22) | collective-permute-done | bytes 294944 | tf_op jit(solution)/shard_map/ppermute | solution.py:24
  90.9 4.5 %expert_down.6 = (bf16[256,1792]{1,0:T(8,128)(2,1)S(1)}, bf16[256,1792]{1,0:T(8,128)(2,1)S(1)}) custom-call(s32[2]{0:T(128)S(1)} %pad_add_fusion.spot_ref, bf16[512,1024]{1,0:T(8,128)(2,1)S(1)} %expert_up.3.act_ref, bf16[1024,3584]{1,0:T(8,128)(2,1)S(1)} %bitcast.27, f32[512,128]{1,0:T(8,128)S(1)} %get-tuple-element.120.scale_ref), custom_call_target="tpu_custom_call" | custom-call | flops 68719476736 | bytes 1024 | tf_op jit(solution)/shard_map/expert_down/pallas_call | solution.py:232
  95.5 1.0 add_convert_fusion.3
  96.5 0.9 collective-permute-start.23
  97.9 1.1 add_convert_fusion
  99.8 5.3 %expert_down.7 = (bf16[256,1792]{1,0:T(8,128)(2,1)}, bf16[256,1792]{1,0:T(8,128)(2,1)S(1)}) custom-call(s32[2]{0:T(128)S(1)} %pad_add_fusion.spot_ref, bf16[512,1024]{1,0:T(8,128)(2,1)S(1)} %expert_up.3.act_ref, bf16[1024,3584]{1,0:T(8,128)(2,1)S(1)} %bitcast.28, f32[512,128]{1,0:T(8,128)S(1)} %get-tuple-element.120.scale_ref), custom_call_target="tpu_custom_call" | custom-call | flops 68719476736 | bytes 1024 | tf_op jit(solution)/shard_map/expert_down/pallas_call | solution.py:232
  105.2 1.0 copy-done.4
  106.3 2.1 %collective-permute-done.23 = bf16[128,1792]{1,0:T(8,128)(2,1)} collective-permute-done((bf16[128,1792]{1,0:T(8,128)(2,1)}, bf16[128,1792]{1,0:T(8,128)(2,1)}, u32[]{:S(2)}, u32[]{:S(2)}) %collective-permute-start.23) | collective-permute-done | bytes 458784 | tf_op jit(solution)/shard_map/ppermute | solution.py:24
  108.4 1.5 %add_convert_fusion.9 = (bf16[32,1792]{1,0:T(8,128)(2,1)S(1)}, bf16[32,1792]{1,0:T(8,128)(2,1)S(1)}, bf16[32,1792]{1,0:T(8,128)(2,1)S(1)}) fusion(bf16[128,1792]{1,0:T(8,128)(2,1)} %collective-permute-done.23, bf16[256,1792]{1,0:T(8,128)(2,1)} %copy-done.16, bf16[256,1792]{1,0:T(8,128)(2,1)} %copy-done.15, bf16[256,1792]{1,0:T(8,128)(2,1)S(1)} %get-tuple-element.106), kind=kLoop, calls=%fused_computation.13 | loop fusion | flops 1376256 | bytes 1720320 | tf_op jit(solution)/shard_map/convert_element_type | solution.py:498
  109.9 1.1 collective-permute-start.28
  110.9 1.2 collective-permute-start.29
  112.1 1.3 collective-permute-start.30
  113.4 1.2 collective-permute-done.25
  114.6 1.5 %add_convert_fusion.2 = bf16[128,1792]{1,0:T(8,128)(2,1)S(1)} fusion(bf16[256,1792]{1,0:T(8,128)(2,1)} %collective-permute-done.26, bf16[256,1792]{1,0:T(8,128)(2,1)} %collective-permute-done.25, bf16[256,1792]{1,0:T(8,128)(2,1)} %copy-done.4), kind=kLoop, calls=%fused_computation.2 | loop fusion | flops 1376256 | bytes 1835008 | tf_op jit(solution)/shard_map/convert_element_type | solution.py:498
  116.1 1.0 collective-permute-start.27
  117.1 1.3 copy-done.3
  118.4 3.1 %attend_moved.1 = bf16[16,64,512]{2,1,0:T(8,128)(2,1)} custom-call(s32[2]{0:T(128)S(1)} %pad_add_fusion.spot_ref, s32[512]{0:T(512)S(1)} %copy-done.9, s32[8]{0:T(128)S(1)} %copy-done.14, bf16[16,64,576]{2,1,0:T(8,128)(2,1)S(1)} %copy-done.3, bf16[16,576,128]{2,1,0:T(8,128)(2,1)S(1)} %bitcast.22, ...), custom_call_target="tpu_custom_call", output_to_operand_aliasing={{}: (8, {})} | custom-call | flops 68719476736 | bytes 1024 | tf_op jit(solution)/shard_map/attend_moved/pallas_call | solution.py:411
  121.5 3.1 %collective-permute-done.27 = bf16[128,1792]{1,0:T(8,128)(2,1)S(1)} collective-permute-done((bf16[128,1792]{1,0:T(8,128)(2,1)S(1)}, bf16[128,1792]{1,0:T(8,128)(2,1)S(1)}, u32[]{:S(2)}, u32[]{:S(2)}) %collective-permute-start.27) | collective-permute-done | bytes 458784 | tf_op jit(solution)/shard_map/ppermute | solution.py:24
  124.6 1.4 add_convert_fusion.7
  126.0 1.1 collective-permute-start.32
  127.1 1.2 collective-permute-start.33
  128.2 1.3 collective-permute-start.34
  129.5 1.1 add_convert_fusion.8
  130.8 5.2 %collective-permute-done.32 = bf16[32,1792]{1,0:T(8,128)(2,1)S(1)} collective-permute-done((bf16[32,1792]{1,0:T(8,128)(2,1)S(1)}, bf16[32,1792]{1,0:T(8,128)(2,1)S(1)}, u32[]{:S(2)}, u32[]{:S(2)}) %collective-permute-start.32) | collective-permute-done | bytes 114720 | tf_op jit(solution)/shard_map/ppermute | solution.py:24
  136.0 1.2 collective-permute-done.34
  137.2 1.1 add_convert_fusion.4
  138.4 1.2 collective-permute-done.35
  (107 shorter events, 9.2 us)
Async XLA Ops:
  0.6 3.7 %collective-permute-start = (bf16[2,16,3584]{2,1,0:T(8,128)(2,1)}, bf16[2,16,3584]{2,1,0:T(8,128)(2,1)S(1)}, u32[]{:S(2)}, u32[]{:S(2)}) collective-permute-start(bf16[2,16,3584]{2,1,0:T(8,128)(2,1)} %param.10), channel_id=1, source_target_pairs={{0,1},{1,0},{2,3},{3,2},{4,5},{5,4},{6,7},{7,6},{8,9},{9,8},{10,11... | collective-permute-start | bytes 688136 | tf_op jit(solution)/shard_map/ppermute | solution.py:24
  4.4 13.2 %collective-permute-start.1 = (bf16[32,1920]{1,0:T(8,128)(2,1)S(1)}, bf16[32,1920]{1,0:T(8,128)(2,1)S(1)}, u32[]{:S(2)}, u32[]{:S(2)}) collective-permute-start(bf16[32,1920]{1,0:T(8,128)(2,1)S(1)} %pad_maximum_fusion.3), channel_id=1, source_target_pairs={{0,16},{1,17},{2,18},{3,19},{4,20},{5,21},{6,22},{7,23},{8,24},{9,... | collective-permute-start | bytes 368648 | tf_op jit(solution)/shard_map/ppermute | solution.py:24
  8.1 9.5 %collective-permute-start.2 = (bf16[32,1920]{1,0:T(8,128)(2,1)S(1)}, bf16[32,1920]{1,0:T(8,128)(2,1)S(1)}, u32[]{:S(2)}, u32[]{:S(2)}) collective-permute-start(bf16[32,1920]{1,0:T(8,128)(2,1)S(1)} %pad_maximum_fusion.3), channel_id=1, source_target_pairs={{0,24},{1,25},{2,26},{3,27},{4,28},{5,29},{6,30},{7,31},{8,16},{9,... | collective-permute-start | bytes 368648 | tf_op jit(solution)/shard_map/ppermute | solution.py:24
  9.5 9.3 %collective-permute-start.3 = (bf16[32,1920]{1,0:T(8,128)(2,1)S(1)}, bf16[32,1920]{1,0:T(8,128)(2,1)S(1)}, u32[]{:S(2)}, u32[]{:S(2)}) collective-permute-start(bf16[32,1920]{1,0:T(8,128)(2,1)S(1)} %pad_maximum_fusion.3), channel_id=1, source_target_pairs={{0,8},{1,9},{2,10},{3,11},{4,12},{5,13},{6,14},{7,15},{8,0},{9,1},... | collective-permute-start | bytes 368648 | tf_op jit(solution)/shard_map/ppermute | solution.py:24
  9.7 24.4 %copy-start.2 = (bf16[16,64,576]{2,1,0:T(8,128)(2,1)S(1)}, bf16[16,64,576]{2,1,0:T(8,128)(2,1)}, u32[]{:S(2)}) copy-start(bf16[16,64,576]{2,1,0:T(8,128)(2,1)} %query_ref.1) | copy-start | bytes 3538948
  12.7 16.7 %copy-start.17 = (bf16[16,576]{1,0:T(8,128)(2,1)S(1)}, bf16[16,576]{1,0:T(8,128)(2,1)}, u32[]{:S(2)}) copy-start(bf16[16,576]{1,0:T(8,128)(2,1)} %param.16) | copy-start | bytes 55300
  12.7 21.4 %copy-start = (bf16[16,128,576]{1,2,0:T(8,128)(2,1)S(1)}, bf16[16,128,576]{1,2,0:T(8,128)(2,1)}, u32[]{:S(2)}) copy-start(bf16[16,128,576]{1,2,0:T(8,128)(2,1)} %param.17) | copy-start | bytes 7077892
  12.7 21.4 %copy-start.8 = (s32[512]{0:T(512)S(1)}, s32[512]{0:T(512)}, u32[]{:S(2)}) copy-start(s32[512]{0:T(512)} %length_ref.3) | copy-start | bytes 6148
  18.8 8.9 %collective-permute-start.4 = (bf16[128,1920]{1,0:T(8,128)(2,1)S(1)}, bf16[128,1920]{1,0:T(8,128)(2,1)S(1)}, u32[]{:S(2)}, u32[]{:S(2)}) collective-permute-start(bf16[128,1920]{1,0:T(8,128)(2,1)S(1)} %pad_maximum_fusion), channel_id=1, source_target_pairs={{0,4},{1,3},{2,6},{3,1},{4,0},{5,7},{6,2},{7,5},{8,12},{9,11},{10,... | collective-permute-start | bytes 1474568 | tf_op jit(solution)/shard_map/ppermute | solution.py:24
  27.7 15.7 %collective-permute-start.5 = (bf16[256,1920]{1,0:T(8,128)(2,1)S(1)}, bf16[256,1920]{1,0:T(8,128)(2,1)S(1)}, u32[]{:S(2)}, u32[]{:S(2)}) collective-permute-start(bf16[256,1920]{1,0:T(8,128)(2,1)S(1)} %constant_dynamic-update-slice_fusion.refs_0_), channel_id=1, source_target_pairs={{0,2},{1,5},{2,0},{3,7},{4,6},{5,1},{6,4},{7,3},{8,10},{9,13},{10,... | collective-permute-start | bytes 2949128 | tf_op jit(solution)/shard_map/ppermute | solution.py:24
  29.4 14.1 %collective-permute-start.6 = (bf16[256,1920]{1,0:T(8,128)(2,1)S(1)}, bf16[256,1920]{1,0:T(8,128)(2,1)S(1)}, u32[]{:S(2)}, u32[]{:S(2)}) collective-permute-start(bf16[256,1920]{1,0:T(8,128)(2,1)S(1)} %constant_dynamic-update-slice_fusion.refs_0_), channel_id=1, source_target_pairs={{0,1},{1,0},{2,3},{3,2},{4,5},{5,4},{6,7},{7,6},{8,9},{9,8},{10,11... | collective-permute-start | bytes 2949128 | tf_op jit(solution)/shard_map/ppermute | solution.py:24
  29.4 12.9 %collective-permute-start.7 = (bf16[32,1792]{1,0:T(8,128)(2,1)S(1)}, bf16[32,1792]{1,0:T(8,128)(2,1)S(1)}, u32[]{:S(2)}, u32[]{:S(2)}) collective-permute-start(bf16[32,1792]{1,0:T(8,128)(2,1)S(1)} %get-tuple-element.82), channel_id=1, source_target_pairs={{0,16},{1,17},{2,18},{3,19},{4,20},{5,21},{6,22},{7,23},{8,24},{9,... | collective-permute-start | bytes 344072 | tf_op jit(solution)/shard_map/ppermute | solution.py:24
  33.4 9.0 %collective-permute-start.8 = (bf16[32,1792]{1,0:T(8,128)(2,1)S(1)}, bf16[32,1792]{1,0:T(8,128)(2,1)S(1)}, u32[]{:S(2)}, u32[]{:S(2)}) collective-permute-start(bf16[32,1792]{1,0:T(8,128)(2,1)S(1)} %get-tuple-element.82), channel_id=1, source_target_pairs={{0,24},{1,25},{2,26},{3,27},{4,28},{5,29},{6,30},{7,31},{8,16},{9,... | collective-permute-start | bytes 344072 | tf_op jit(solution)/shard_map/ppermute | solution.py:24
  33.8 9.6 %collective-permute-start.9 = (bf16[32,1792]{1,0:T(8,128)(2,1)S(1)}, bf16[32,1792]{1,0:T(8,128)(2,1)S(1)}, u32[]{:S(2)}, u32[]{:S(2)}) collective-permute-start(bf16[32,1792]{1,0:T(8,128)(2,1)S(1)} %get-tuple-element.82), channel_id=1, source_target_pairs={{0,8},{1,9},{2,10},{3,11},{4,12},{5,13},{6,14},{7,15},{8,0},{9,1},... | collective-permute-start | bytes 344072 | tf_op jit(solution)/shard_map/ppermute | solution.py:24
  34.1 11.6 %copy-start.19 = (bf16[2,576,128]{2,1,0:T(8,128)(2,1)S(1)}, bf16[2,576,128]{2,1,0:T(8,128)(2,1)}, u32[]{:S(2)}) copy-start(bf16[2,576,128]{2,1,0:T(8,128)(2,1)} %get-tuple-element.90) | copy-start | bytes 884740
  43.5 21.5 %slice-start = ((s8[7340032]{0:T(1024)(128)(4,1)}), s8[4194304]{0:T(1024)(128)(4,1)S(1)}, s32[]{:S(2)}) async-start(s8[7340032]{0:T(1024)(128)(4,1)} %bitcast.23), calls=%async_computation | async-start | bytes 8388608
  43.5 5.5 %collective-permute-start.12 = (bf16[256,1920]{1,0:T(8,128)(2,1)S(1)}, bf16[256,1920]{1,0:T(8,128)(2,1)S(1)}, u32[]{:S(2)}, u32[]{:S(2)}) collective-permute-start(bf16[256,1920]{1,0:T(8,128)(2,1)S(1)} %collective-permute-done.5.refs_1_), channel_id=1, source_target_pairs={{0,1},{1,0},{2,3},{3,2},{4,5},{5,4},{6,7},{7,6},{8,9},{9,8},{10,11... | collective-permute-start | bytes 2949128 | tf_op jit(solution)/shard_map/ppermute | solution.py:24
  43.6 20.6 %collective-permute-start.10 = (bf16[128,1792]{1,0:T(8,128)(2,1)S(1)}, bf16[128,1792]{1,0:T(8,128)(2,1)S(1)}, u32[]{:S(2)}, u32[]{:S(2)}) collective-permute-start(bf16[128,1792]{1,0:T(8,128)(2,1)S(1)} %pad_maximum_fusion.1.refs_0_), channel_id=1, source_target_pairs={{0,2},{1,5},{2,0},{3,7},{4,6},{5,1},{6,4},{7,3},{8,10},{9,13},{10,... | collective-permute-start | bytes 1376264 | tf_op jit(solution)/shard_map/ppermute | solution.py:24
  44.2 20.0 %collective-permute-start.13 = (bf16[128,1792]{1,0:T(8,128)(2,1)S(1)}, bf16[128,1792]{1,0:T(8,128)(2,1)S(1)}, u32[]{:S(2)}, u32[]{:S(2)}) collective-permute-start(bf16[128,1792]{1,0:T(8,128)(2,1)S(1)} %pad_maximum_fusion.1.refs_0_), channel_id=1, source_target_pairs={{0,4},{1,3},{2,6},{3,1},{4,0},{5,7},{6,2},{7,5},{8,12},{9,11},{10,... | collective-permute-start | bytes 1376264 | tf_op jit(solution)/shard_map/ppermute | solution.py:24
  45.6 17.8 %collective-permute-start.11 = (bf16[2,576,128]{2,1,0:T(8,128)(2,1)S(1)}, bf16[2,576,128]{2,1,0:T(8,128)(2,1)S(1)}, u32[]{:S(2)}, u32[]{:S(2)}) collective-permute-start(bf16[2,576,128]{2,1,0:T(8,128)(2,1)S(1)} %copy-done.19), channel_id=1, source_target_pairs={{0,16},{1,17},{2,18},{3,19},{4,20},{5,21},{6,22},{7,23},{8,24},{9,... | collective-permute-start | bytes 884744 | tf_op jit(solution)/shard_map/ppermute | solution.py:24
  49.0 15.9 %slice-start.1 = ((s8[7340032]{0:T(1024)(128)(4,1)}), s8[3145728]{0:T(1024)(128)(4,1)S(1)}, s32[]{:S(2)}) async-start(s8[7340032]{0:T(1024)(128)(4,1)} %bitcast.23), calls=%async_computation.1 | async-start | bytes 6291456
  64.2 9.1 %collective-permute-start.18 = (bf16[128,1792]{1,0:T(8,128)(2,1)S(1)}, bf16[128,1792]{1,0:T(8,128)(2,1)S(1)}, u32[]{:S(2)}, u32[]{:S(2)}) collective-permute-start(bf16[128,1792]{1,0:T(8,128)(2,1)S(1)} %collective-permute-done.13.refs_1_), channel_id=1, source_target_pairs={{0,1},{1,0},{2,3},{3,2},{4,5},{5,4},{6,7},{7,6},{8,9},{9,8},{10,11... | collective-permute-start | bytes 1376264 | tf_op jit(solution)/shard_map/ppermute | solution.py:24
  64.2 9.1 %collective-permute-start.19 = (bf16[128,1792]{1,0:T(8,128)(2,1)S(1)}, bf16[128,1792]{1,0:T(8,128)(2,1)S(1)}, u32[]{:S(2)}, u32[]{:S(2)}) collective-permute-start(bf16[128,1792]{1,0:T(8,128)(2,1)S(1)} %collective-permute-done.13.refs_1_), channel_id=1, source_target_pairs={{0,2},{1,5},{2,0},{3,7},{4,6},{5,1},{6,4},{7,3},{8,10},{9,13},{10,... | collective-permute-start | bytes 1376264 | tf_op jit(solution)/shard_map/ppermute | solution.py:24
  64.9 4.3 %collective-permute-start.14 = (bf16[128,1792]{1,0:T(8,128)(2,1)S(1)}, bf16[128,1792]{1,0:T(8,128)(2,1)S(1)}, u32[]{:S(2)}, u32[]{:S(2)}) collective-permute-start(bf16[128,1792]{1,0:T(8,128)(2,1)S(1)} %collective-permute-done.10.refs_2_), channel_id=1, source_target_pairs={{0,1},{1,0},{2,3},{3,2},{4,5},{5,4},{6,7},{7,6},{8,9},{9,8},{10,11... | collective-permute-start | bytes 1376264 | tf_op jit(solution)/shard_map/ppermute | solution.py:24
  68.6 4.7 %collective-permute-start.15 = (bf16[256,1792]{1,0:T(8,128)(2,1)S(1)}, bf16[256,1792]{1,0:T(8,128)(2,1)S(1)}, u32[]{:S(2)}, u32[]{:S(2)}) collective-permute-start(bf16[256,1792]{1,0:T(8,128)(2,1)S(1)} %get-tuple-element.100), channel_id=1, source_target_pairs={{0,1},{1,0},{2,3},{3,2},{4,5},{5,4},{6,7},{7,6},{8,9},{9,8},{10,11... | collective-permute-start | bytes 2752520 | tf_op jit(solution)/shard_map/ppermute | solution.py:24
  69.1 4.2 %collective-permute-start.16 = (bf16[256,1792]{1,0:T(8,128)(2,1)S(1)}, bf16[256,1792]{1,0:T(8,128)(2,1)S(1)}, u32[]{:S(2)}, u32[]{:S(2)}) collective-permute-start(bf16[256,1792]{1,0:T(8,128)(2,1)S(1)} %get-tuple-element.101), channel_id=1, source_target_pairs={{0,1},{1,0},{2,3},{3,2},{4,5},{5,4},{6,7},{7,6},{8,9},{9,8},{10,11... | collective-permute-start | bytes 2752520 | tf_op jit(solution)/shard_map/ppermute | solution.py:24
  69.2 4.1 %collective-permute-start.17 = (bf16[128,1792]{1,0:T(8,128)(2,1)S(1)}, bf16[128,1792]{1,0:T(8,128)(2,1)S(1)}, u32[]{:S(2)}, u32[]{:S(2)}) collective-permute-start(bf16[128,1792]{1,0:T(8,128)(2,1)S(1)} %pad_maximum_fusion.1.refs_0_), channel_id=1, source_target_pairs={{0,1},{1,0},{2,3},{3,2},{4,5},{5,4},{6,7},{7,6},{8,9},{9,8},{10,11... | collective-permute-start | bytes 1376264 | tf_op jit(solution)/shard_map/ppermute | solution.py:24
  73.3 22.1 %copy-start.15 = (bf16[256,1792]{1,0:T(8,128)(2,1)}, bf16[256,1792]{1,0:T(8,128)(2,1)S(1)}, u32[]{:S(2)}) copy-start(bf16[256,1792]{1,0:T(8,128)(2,1)S(1)} %collective-permute-done.15) | copy-start | bytes 2752516
  73.6 2.1 %collective-permute-start.21 = (bf16[128,1792]{1,0:T(8,128)(2,1)S(1)}, bf16[128,1792]{1,0:T(8,128)(2,1)S(1)}, u32[]{:S(2)}, u32[]{:S(2)}) collective-permute-start(bf16[128,1792]{1,0:T(8,128)(2,1)S(1)} %collective-permute-done.19.refs_3_), channel_id=1, source_target_pairs={{0,1},{1,0},{2,3},{3,2},{4,5},{5,4},{6,7},{7,6},{8,9},{9,8},{10,11... | collective-permute-start | bytes 1376264 | tf_op jit(solution)/shard_map/ppermute | solution.py:24
  73.9 17.0 %collective-permute-start.20 = (bf16[256,1792]{1,0:T(8,128)(2,1)S(1)}, bf16[256,1792]{1,0:T(8,128)(2,1)S(1)}, u32[]{:S(2)}, u32[]{:S(2)}) collective-permute-start(bf16[256,1792]{1,0:T(8,128)(2,1)S(1)} %add_convert_fusion.1), channel_id=1, source_target_pairs={{0,2},{1,5},{2,0},{3,7},{4,6},{5,1},{6,4},{7,3},{8,10},{9,13},{10,... | collective-permute-start | bytes 2752520 | tf_op jit(solution)/shard_map/ppermute | solution.py:24
  75.3 15.6 %collective-permute-start.22 = (bf16[2,576,128]{2,1,0:T(8,128)(2,1)S(1)}, bf16[2,576,128]{2,1,0:T(8,128)(2,1)S(1)}, u32[]{:S(2)}, u32[]{:S(2)}) collective-permute-start(bf16[2,576,128]{2,1,0:T(8,128)(2,1)S(1)} %copy-done.18), channel_id=1, source_target_pairs={{0,16},{1,17},{2,18},{3,19},{4,20},{5,21},{6,22},{7,23},{8,24},{9,... | collective-permute-start | bytes 884744 | tf_op jit(solution)/shard_map/ppermute | solution.py:24
  95.4 2.5 %collective-permute-start.24 = (bf16[256,1792]{1,0:T(8,128)(2,1)S(1)}, bf16[256,1792]{1,0:T(8,128)(2,1)S(1)}, u32[]{:S(2)}, u32[]{:S(2)}) collective-permute-start(bf16[256,1792]{1,0:T(8,128)(2,1)S(1)} %get-tuple-element.124), channel_id=1, source_target_pairs={{0,1},{1,0},{2,3},{3,2},{4,5},{5,4},{6,7},{7,6},{8,9},{9,8},{10,11... | collective-permute-start | bytes 2752520 | tf_op jit(solution)/shard_map/ppermute | solution.py:24
  96.5 11.9 %collective-permute-start.23 = (bf16[128,1792]{1,0:T(8,128)(2,1)}, bf16[128,1792]{1,0:T(8,128)(2,1)}, u32[]{:S(2)}, u32[]{:S(2)}) collective-permute-start(bf16[128,1792]{1,0:T(8,128)(2,1)} %add_convert_fusion.3), channel_id=1, source_target_pairs={{0,4},{1,3},{2,6},{3,1},{4,0},{5,7},{6,2},{7,5},{8,12},{9,11},{10,... | collective-permute-start | bytes 1376264 | tf_op jit(solution)/shard_map/ppermute | solution.py:24
  99.0 15.6 %collective-permute-start.25 = (bf16[256,1792]{1,0:T(8,128)(2,1)}, bf16[256,1792]{1,0:T(8,128)(2,1)}, u32[]{:S(2)}, u32[]{:S(2)}) collective-permute-start(bf16[256,1792]{1,0:T(8,128)(2,1)} %add_convert_fusion), channel_id=1, source_target_pairs={{0,2},{1,5},{2,0},{3,7},{4,6},{5,1},{6,4},{7,3},{8,10},{9,13},{10,... | collective-permute-start | bytes 2752520 | tf_op jit(solution)/shard_map/ppermute | solution.py:24
  106.1 10.9 %copy-start.1 = (bf16[16,128,576]{1,2,0:T(8,128)(2,1)S(1)}, bf16[16,128,576]{1,2,0:T(8,128)(2,1)}, u32[]{:S(2)}) copy-start(bf16[16,128,576]{1,2,0:T(8,128)(2,1)} %param.17) | copy-start | bytes 7077892
  106.1 10.9 %copy-start.7 = (bf16[16,1,576]{2,1,0:T(2,128)(2,1)S(1)}, bf16[16,1,576]{2,1,0:T(2,128)(2,1)}, u32[]{:S(2)}) copy-start(bf16[16,1,576]{2,1,0:T(2,128)(2,1)} %copy-done.6) | copy-start | bytes 55300
  106.1 10.9 %copy-start.9 = (s32[512]{0:T(512)S(1)}, s32[512]{0:T(512)}, u32[]{:S(2)}) copy-start(s32[512]{0:T(512)} %length_ref.3) | copy-start | bytes 6148
  106.1 10.9 %copy-start.14 = (s32[8]{0:T(128)S(1)}, s32[8]{0:T(128)}, u32[]{:S(2)}) copy-start(s32[8]{0:T(128)} %get-tuple-element.132.info_ref) | copy-start | bytes 100
  106.1 8.5 %collective-permute-start.26 = (bf16[256,1792]{1,0:T(8,128)(2,1)}, bf16[256,1792]{1,0:T(8,128)(2,1)}, u32[]{:S(2)}, u32[]{:S(2)}) collective-permute-start(bf16[256,1792]{1,0:T(8,128)(2,1)} %get-tuple-element.129), channel_id=1, source_target_pairs={{0,1},{1,0},{2,3},{3,2},{4,5},{5,4},{6,7},{7,6},{8,9},{9,8},{10,11... | collective-permute-start | bytes 2752520 | tf_op jit(solution)/shard_map/ppermute | solution.py:24
  109.9 11.7 %collective-permute-start.28 = (bf16[32,1792]{1,0:T(8,128)(2,1)S(1)}, bf16[32,1792]{1,0:T(8,128)(2,1)S(1)}, u32[]{:S(2)}, u32[]{:S(2)}) collective-permute-start(bf16[32,1792]{1,0:T(8,128)(2,1)S(1)} %get-tuple-element.147), channel_id=1, source_target_pairs={{0,16},{1,17},{2,18},{3,19},{4,20},{5,21},{6,22},{7,23},{8,24},{9,... | collective-permute-start | bytes 344072 | tf_op jit(solution)/shard_map/ppermute | solution.py:24
  110.9 10.6 %collective-permute-start.29 = (bf16[32,1792]{1,0:T(8,128)(2,1)S(1)}, bf16[32,1792]{1,0:T(8,128)(2,1)S(1)}, u32[]{:S(2)}, u32[]{:S(2)}) collective-permute-start(bf16[32,1792]{1,0:T(8,128)(2,1)S(1)} %get-tuple-element.146), channel_id=1, source_target_pairs={{0,24},{1,25},{2,26},{3,27},{4,28},{5,29},{6,30},{7,31},{8,16},{9,... | collective-permute-start | bytes 344072 | tf_op jit(solution)/shard_map/ppermute | solution.py:24
  112.1 9.4 %collective-permute-start.30 = (bf16[32,1792]{1,0:T(8,128)(2,1)S(1)}, bf16[32,1792]{1,0:T(8,128)(2,1)S(1)}, u32[]{:S(2)}, u32[]{:S(2)}) collective-permute-start(bf16[32,1792]{1,0:T(8,128)(2,1)S(1)} %get-tuple-element.145), channel_id=1, source_target_pairs={{0,8},{1,9},{2,10},{3,11},{4,12},{5,13},{6,14},{7,15},{8,0},{9,1},... | collective-permute-start | bytes 344072 | tf_op jit(solution)/shard_map/ppermute | solution.py:24
  116.1 8.5 %collective-permute-start.27 = (bf16[128,1792]{1,0:T(8,128)(2,1)S(1)}, bf16[128,1792]{1,0:T(8,128)(2,1)S(1)}, u32[]{:S(2)}, u32[]{:S(2)}) collective-permute-start(bf16[128,1792]{1,0:T(8,128)(2,1)S(1)} %add_convert_fusion.2), channel_id=1, source_target_pairs={{0,4},{1,3},{2,6},{3,1},{4,0},{5,7},{6,2},{7,5},{8,12},{9,11},{10,... | collective-permute-start | bytes 1376264 | tf_op jit(solution)/shard_map/ppermute | solution.py:24
  126.0 10.0 %collective-permute-start.32 = (bf16[32,1792]{1,0:T(8,128)(2,1)S(1)}, bf16[32,1792]{1,0:T(8,128)(2,1)S(1)}, u32[]{:S(2)}, u32[]{:S(2)}) collective-permute-start(bf16[32,1792]{1,0:T(8,128)(2,1)S(1)} %get-tuple-element.142), channel_id=1, source_target_pairs={{0,16},{1,17},{2,18},{3,19},{4,20},{5,21},{6,22},{7,23},{8,24},{9,... | collective-permute-start | bytes 344072 | tf_op jit(solution)/shard_map/ppermute | solution.py:24
  127.1 8.9 %collective-permute-start.33 = (bf16[32,1792]{1,0:T(8,128)(2,1)S(1)}, bf16[32,1792]{1,0:T(8,128)(2,1)S(1)}, u32[]{:S(2)}, u32[]{:S(2)}) collective-permute-start(bf16[32,1792]{1,0:T(8,128)(2,1)S(1)} %get-tuple-element.144), channel_id=1, source_target_pairs={{0,24},{1,25},{2,26},{3,27},{4,28},{5,29},{6,30},{7,31},{8,16},{9,... | collective-permute-start | bytes 344072 | tf_op jit(solution)/shard_map/ppermute | solution.py:24
  128.2 9.0 %collective-permute-start.34 = (bf16[32,1792]{1,0:T(8,128)(2,1)S(1)}, bf16[32,1792]{1,0:T(8,128)(2,1)S(1)}, u32[]{:S(2)}, u32[]{:S(2)}) collective-permute-start(bf16[32,1792]{1,0:T(8,128)(2,1)S(1)} %get-tuple-element.143), channel_id=1, source_target_pairs={{0,8},{1,9},{2,10},{3,11},{4,12},{5,13},{6,14},{7,15},{8,0},{9,1},... | collective-permute-start | bytes 344072 | tf_op jit(solution)/shard_map/ppermute | solution.py:24
  130.7 7.7 %collective-permute-start.31 = (bf16[16,1792]{1,0:T(8,128)(2,1)S(1)}, bf16[16,1792]{1,0:T(8,128)(2,1)S(1)}, u32[]{:S(2)}, u32[]{:S(2)}) collective-permute-start(bf16[16,1792]{1,0:T(8,128)(2,1)S(1)} %get-tuple-element.151), channel_id=1, source_target_pairs={{0,1},{1,0},{2,3},{3,2},{4,5},{5,4},{6,7},{7,6},{8,9},{9,8},{10,11... | collective-permute-start | bytes 172040 | tf_op jit(solution)/shard_map/ppermute | solution.py:24
  138.3 1.3 collective-permute-start.35
  (10 other events, 52.6 us)
